TPU v7x, 32 devices: a whole 2x2x4 slice. The times are simulated.
32 devices in a mesh: mem: 4 (over y, x), tok: 8 (over z, core).
Axes of the slice: x: 2, y: 2, z: 4, core: 2. Of those that a mesh axis runs over, the one named last changes fastest.
Arguments:
- ens_state: bfloat16 [16, 4096, 256], P('mem', 'tok'), may hold values from -8 to 8
- attn_gain: float32 [256], replicated, may hold values from 0.1 to 1.9
- ffn_gain: float32 [256], replicated, may hold values from 0.1 to 1.9
- w_query: bfloat16 [256, 256], replicated, may hold values from -2 to 2
- w_key: bfloat16 [256, 256], replicated, may hold values from -2 to 2
- w_value: bfloat16 [256, 256], replicated, may hold values from -0.375 to 0.375
- w_out: bfloat16 [256, 256], replicated, may hold values from -0.375 to 0.375
- w_gate: bfloat16 [256, 1024], replicated, may hold values from -0.375 to 0.375
- w_up: bfloat16 [256, 1024], replicated, may hold values from -0.375 to 0.375
- down_weight: bfloat16 [1024, 256], replicated, may hold values from -0.1875 to 0.1875
- head_window: int32 [4], replicated, may hold values from 32 to 256, as said below
- obs_token: int32 [32768], P('tok'), may hold values from 0 to 4095, as said below
- obs_channel: int32 [32768], P('tok'), may hold values from 0 to 255
- obs_value: float32 [32768], P('tok'), may hold values from -6 to 6
- obs_var: float32 [32768], P('tok'), may hold values from 1 to 16
Outputs:
- analysis: bfloat16 [16, 4096, 256], P('mem', 'tok')
Inputs may be any that keep to these rules, and one draw needn't show every extreme that they name: `head_window`: one head's window is exactly 256. `obs_token`: sample o lies on a token of block o // 4096, that is between (o // 4096) * 512 and that plus 512 - 1; the first sample is on token 0 and the last on token 4095.
All inputs are finite; a program needn't handle non-finite values.
Results may differ from a plain program's by a relative error of at most 0.012.
Values may be sent and summed in bfloat16 or wider, within the bound.
No kernel may reach another device: no remote copies, remote signals or barrier semaphores. Data moves between devices by JAX's collectives and lax.ppermute only.
A program may use at most 128 MiB of HBM per device.

v0:
```python
import math

import jax
import jax.numpy as jnp
from jax import lax
from jax.sharding import PartitionSpec as P

WIN = 256
NS_STEPS = 8


EPS = 1e-05


def padded_2(cells, sides, width):
    for axis, dim in sides:
        count = lax.axis_size(axis)
        ends = count - 1
        head = lax.slice_in_dim(cells, 0, width, axis=dim)
        tail = lax.slice_in_dim(cells, cells.shape[dim] - width, cells.shape[dim], axis=dim)
        cells = jnp.concatenate(
            [
                lax.ppermute(tail, axis, [(i, (i + 1) % count) for i in range(ends)]),
                cells,
                lax.ppermute(head, axis, [((i + 1) % count, i) for i in range(ends)]),
            ],
            axis=dim,
        )
    return cells


def rms_scaled(values, gain):
    return values * lax.rsqrt(jnp.mean(values * values, axis=-1, keepdims=True) + EPS) * gain


def apply_projection(values, matrix):
    return jnp.einsum("gsd,de->gse", values, matrix, preferred_element_type=jnp.float32)


def attend(queries, key_rows, value_rows, head_window, first_pos, total_len, reach):
    groups, row_count, feat_width = queries.shape
    head_count = head_window.shape[0]
    head_size = feat_width // head_count
    block_rows = min(512, row_count)
    key_count = block_rows + 2 * reach
    logit_scale = 1.0 / math.sqrt(head_size)

    def one_block(block_index):
        block_start = block_index * block_rows
        q_pos = first_pos + block_start + jnp.arange(block_rows, dtype=jnp.int32)
        k_pos = first_pos - reach + block_start + jnp.arange(key_count, dtype=jnp.int32)
        apart = jnp.abs(q_pos[:, None] - k_pos[None, :])
        inside = (k_pos >= 0) & (k_pos < total_len)
        head_outputs = []
        for head in range(head_count):
            lower_column = head * head_size
            upper_column = lower_column + head_size
            score_matrix = (
                jnp.einsum(
                    "alx,adx->ald",
                    queries[:, :, lower_column:upper_column],
                    key_rows[:, :, lower_column:upper_column],
                    preferred_element_type=jnp.float32,
                )
                * logit_scale
            )
            allowed = (apart <= head_window[head]) & inside[None, :]
            score_matrix = jnp.where(allowed[None], score_matrix, -1e30)
            row_top = jnp.max(score_matrix, axis=-1, keepdims=True)
            expo = jnp.exp(score_matrix - row_top)
            row_total = jnp.sum(expo, axis=-1, keepdims=True)
            softmax_weights = (expo / row_total).astype(jnp.bfloat16)
            head_outputs.append(
                jnp.einsum(
                    "pol,plj->poj",
                    softmax_weights,
                    value_rows[:, :, lower_column:upper_column],
                    preferred_element_type=jnp.float32,
                )
            )
        return jnp.concatenate(head_outputs, axis=-1).astype(jnp.bfloat16)

    pieces = lax.map(one_block, jnp.arange(row_count // block_rows, dtype=jnp.int32))
    return jnp.moveaxis(pieces, 0, 1).reshape(groups, row_count, feat_width)


def ensemble_transform(gram, proj):
    ensemble_fields = gram.shape[0]
    identity = jnp.eye(ensemble_fields, dtype=jnp.float32)
    mean_mat = jnp.full(
        (ensemble_fields, ensemble_fields), 1.0 / ensemble_fields, dtype=jnp.float32
    )
    system = gram + (ensemble_fields - 1.0) * identity
    factor = jnp.linalg.cholesky(system)
    mean_weights = jax.scipy.linalg.cho_solve((factor, True), proj)
    mean_level = jnp.trace(system) / ensemble_fields
    lifted = system + (mean_level - (ensemble_fields - 1.0)) * mean_mat
    frobenius = jnp.sqrt(jnp.sum(lifted * lifted))
    root_iter = lifted / frobenius
    inv_iter = identity
    for sweep in range(NS_STEPS):
        correction = 1.5 * identity - 0.5 * jnp.dot(
            inv_iter, root_iter, precision=lax.Precision.HIGHEST
        )
        root_iter = jnp.dot(root_iter, correction, precision=lax.Precision.HIGHEST)
        inv_iter = jnp.dot(correction, inv_iter, precision=lax.Precision.HIGHEST)
    inv_root = (
        inv_iter / jnp.sqrt(frobenius)
        + (1.0 / math.sqrt(ensemble_fields - 1.0) - 1.0 / jnp.sqrt(mean_level)) * mean_mat
    )
    spread_part = math.sqrt(ensemble_fields - 1.0) * inv_root
    return mean_mat + jnp.dot(
        identity - mean_mat, mean_weights[:, None] + spread_part, precision=lax.Precision.HIGHEST
    )


def gram_terms(measurement_vector, obs_value, obs_var, owned):
    seen_mean = jnp.mean(measurement_vector, axis=0)
    inv_err = lax.rsqrt(obs_var)
    scaled = jnp.where(
        owned[None, :], (measurement_vector - seen_mean[None, :]) * inv_err[None, :], 0.0
    )
    innovation = jnp.where(owned, (obs_value - seen_mean) * inv_err, 0.0)
    gram = jnp.dot(scaled, scaled.T, precision=lax.Precision.HIGHEST)
    proj = jnp.dot(scaled, innovation, precision=lax.Precision.HIGHEST)
    return (gram, proj)


def local(
    ens_state,
    attn_gain,
    ffn_gain,
    w_query,
    w_key,
    w_value,
    w_out,
    w_gate,
    w_up,
    down_weight,
    head_window,
    obs_token,
    obs_channel,
    obs_value,
    obs_var,
):
    nearby_ensemble, row_count, feat_width = ens_state.shape
    mem_count = lax.axis_size("mem")
    first_pos = lax.axis_index("tok") * row_count
    total_len = row_count * lax.axis_size("tok")
    normed_in = rms_scaled(ens_state.astype(jnp.float32), attn_gain).astype(jnp.bfloat16)
    queries = apply_projection(normed_in, w_query).astype(jnp.bfloat16)
    key_here = apply_projection(normed_in, w_key).astype(jnp.bfloat16)
    value_here = apply_projection(normed_in, w_value).astype(jnp.bfloat16)
    joined = jnp.concatenate([key_here, value_here], axis=-1)
    padded = padded_2(joined, (("tok", 1),), WIN)
    key_rows = padded[:, :, :feat_width]
    value_rows = padded[:, :, feat_width:]
    mixed_heads = attend(queries, key_rows, value_rows, head_window, first_pos, total_len, WIN)
    after_attention_state = (
        ens_state.astype(jnp.float32) + apply_projection(mixed_heads, w_out)
    ).astype(jnp.bfloat16)
    normed_mid = rms_scaled(after_attention_state.astype(jnp.float32), ffn_gain).astype(
        jnp.bfloat16
    )
    hidden_neurons = (
        jax.nn.silu(apply_projection(normed_mid, w_gate)) * apply_projection(normed_mid, w_up)
    ).astype(jnp.bfloat16)
    prior_field = (
        after_attention_state.astype(jnp.float32) + apply_projection(hidden_neurons, down_weight)
    ).astype(jnp.bfloat16)
    local_token = obs_token - first_pos
    widened_field = lax.all_to_all(prior_field, "mem", split_axis=1, concat_axis=0, tiled=True)
    mem_index = lax.axis_index("mem")
    serial_position = local_token * feat_width + obs_channel
    nearby_measurements = prior_field.reshape(nearby_ensemble, -1)[:, serial_position]
    measurement_vector = lax.all_to_all(
        nearby_measurements, "mem", split_axis=1, concat_axis=0, tiled=True
    ).astype(jnp.float32)
    share_size = obs_token.shape[0] // mem_count
    value_share = lax.dynamic_slice_in_dim(obs_value, mem_index * share_size, share_size)
    var_share = lax.dynamic_slice_in_dim(obs_var, mem_index * share_size, share_size)
    owned = jnp.ones((share_size,), dtype=bool)
    gram, proj = gram_terms(measurement_vector, value_share, var_share, owned)
    gram, proj = lax.psum((gram, proj), ("mem", "tok"))
    analysis_operator = ensemble_transform(gram, proj)
    mixed_result = jnp.einsum(
        "ts,tnm->snm",
        analysis_operator,
        widened_field.astype(jnp.float32),
        precision=lax.Precision.HIGHEST,
    )
    return lax.all_to_all(
        mixed_result.astype(jnp.bfloat16), "mem", split_axis=0, concat_axis=1, tiled=True
    )


def solution(mesh):
    in_specs = (
        P("mem", "tok", None),
        P(),
        P(),
        P(),
        P(),
        P(),
        P(),
        P(),
        P(),
        P(),
        P(),
        P("tok"),
        P("tok"),
        P("tok"),
        P("tok"),
    )
    out_specs = P("mem", "tok", None)
    return jax.shard_map(local, mesh=mesh, in_specs=in_specs, out_specs=out_specs, check_vma=False)
```

profile of v0, /device:TPU:0, one launch (start us, length us, event | category | flops | bytes accessed | tf_op | source)
XLA Modules:
  0.0 243.8 jit_solution(17233606575558458351)
XLA Ops:
  0.0 1.6 copy.45
  1.9 1.5 convolution_convert_fusion.2
  3.9 1.0 copy-done.1
  5.0 1.5 fusion.59
  6.4 3.3 %collective-permute-start = (bf16[4,256,512]{1,2,0:T(8,128)(2,1)}, bf16[4,256,512]{1,2,0:T(8,128)(2,1)}, u32[]{:S(2)}, u32[]{:S(2)}) collective-permute-start(bf16[4,256,512]{1,2,0:T(8,128)(2,1)} %get-tuple-element.19), channel_id=1, source_target_pairs={{0,1},{1,2},{2,3},{3,4},{4,5},{5,6},{6,7},{8,9},{9,10},{10,11},{11... | collective-permute-start | bytes 3145736 | tf_op jit(solution)/shard_map/ppermute | solution.py:23
  9.8 1.3 collective-permute-start.1
  11.8 1.5 convolution_convert_fusion.3
  13.3 5.2 %fusion.39 = (pred[512,1024]{1,0:T(8,128)(4,1)}, pred[512,1024]{1,0:T(8,128)(4,1)}, pred[512,1024]{1,0:T(8,128)(4,1)}, pred[512,1024]{1,0:T(8,128)(4,1)S(1)}) fusion(s32[]{:T(128)} %bitcast, s32[1024]{0:T(1024)S(1)} %iota_add_fusion, s32[512]{0:T(512)S(1)} %iota_add_fusion.1, pred[1024]{0:T(1024)(128)(4,1)S(1)} %compare_and_fusion, s32[]{:T(128)} %bitcast.4, ...), kind=kLoop, calls=%fused_computation.62 | loop fusion | flops 5242880 | bytes 2104336 | tf_op jit(solution)/shard_map/while/body/eval_jaxpr/and | solution.py:67
  18.6 3.5 %pad_maximum_fusion = bf16[4,1024,512]{1,2,0:T(8,128)(2,1)} fusion(bf16[4,256,512]{1,2,0:T(8,128)(2,1)} %collective-permute-done.1, bf16[4,512,256]{1,2,0:T(8,128)(2,1)S(1)} %copy-done.2, bf16[4,512,256]{1,2,0:T(8,128)(2,1)S(1)} %convolution_convert_fusion.2, bf16[4,256,512]{1,2,0:T(8,128)(2,1)} %collective-permute-done), kind=kLoop, calls=%fused_computation.22 | loop fusion | flops 16777216 | bytes 8388608 | tf_op jit(solution)/shard_map/concatenate | solution.py:21
  22.1 7.5 %fusion.194 = (f32[4,512]{1,0:T(4,128)S(1)}, f32[4,512,1024]{2,1,0:T(8,128)}) fusion(pred[512,1024]{1,0:T(8,128)(4,1)} %get-tuple-element.34, bf16[4,1024,512]{1,2,0:T(8,128)(2,1)} %pad_maximum_fusion, bf16[4,512,256]{1,2,0:T(8,128)(2,1)} %convolution_convert_fusion.3), kind=kOutput, calls=%fused_computation.199 | convolution fusion | flops 276825088 | bytes 9707520 | tf_op jit(solution)/shard_map/while/body/eval_jaxpr/sub | solution.py:70
  29.6 7.3 %fusion.185 = (f32[4,512]{1,0:T(4,128)S(1)}, f32[4,512,1024]{2,1,0:T(8,128)}) fusion(pred[512,1024]{1,0:T(8,128)(4,1)S(1)} %copy-done.4, bf16[4,1024,512]{1,2,0:T(8,128)(2,1)} %pad_maximum_fusion, bf16[4,512,256]{1,2,0:T(8,128)(2,1)} %convolution_convert_fusion.3), kind=kOutput, calls=%fused_computation.198 | convolution fusion | flops 276825088 | bytes 9707520 | tf_op jit(solution)/shard_map/while/body/eval_jaxpr/sub | solution.py:70
  37.0 7.3 %fusion.176 = (f32[4,512]{1,0:T(4,128)S(1)}, f32[4,512,1024]{2,1,0:T(8,128)}) fusion(pred[512,1024]{1,0:T(8,128)(4,1)S(1)} %copy-done.3, bf16[4,1024,512]{1,2,0:T(8,128)(2,1)} %pad_maximum_fusion, bf16[4,512,256]{1,2,0:T(8,128)(2,1)} %convolution_convert_fusion.3), kind=kOutput, calls=%fused_computation.197 | convolution fusion | flops 276825088 | bytes 9707520 | tf_op jit(solution)/shard_map/while/body/eval_jaxpr/sub | solution.py:70
  44.3 7.3 %fusion.167 = (f32[4,512]{1,0:T(4,128)S(1)}, f32[4,512,1024]{2,1,0:T(8,128)}) fusion(pred[512,1024]{1,0:T(8,128)(4,1)S(1)} %get-tuple-element.37, bf16[4,1024,512]{1,2,0:T(8,128)(2,1)} %pad_maximum_fusion, bf16[4,512,256]{1,2,0:T(8,128)(2,1)} %convolution_convert_fusion.3), kind=kOutput, calls=%fused_computation.196 | convolution fusion | flops 276825088 | bytes 9707520 | tf_op jit(solution)/shard_map/while/body/eval_jaxpr/sub | solution.py:70
  51.6 5.0 %fusion.46 = bf16[4,512,64]{1,2,0:T(8,128)(2,1)S(1)} fusion(f32[4,512,1024]{2,1,0:T(8,128)} %get-tuple-element.50, f32[4,512]{1,0:T(4,128)S(1)} %get-tuple-element.49, bf16[4,1024,512]{1,2,0:T(8,128)(2,1)} %pad_maximum_fusion), kind=kOutput, calls=%fused_computation.73 | convolution fusion | flops 272760832 | bytes 9183232 | tf_op jit(solution)/shard_map/while/body/eval_jaxpr/pol,plj->poj/dot_general | solution.py:74
  56.6 5.0 %fusion.45 = bf16[4,512,64]{1,2,0:T(8,128)(2,1)S(1)} fusion(f32[4,512,1024]{2,1,0:T(8,128)} %get-tuple-element.48, f32[4,512]{1,0:T(4,128)S(1)} %get-tuple-element.47, bf16[4,1024,512]{1,2,0:T(8,128)(2,1)} %pad_maximum_fusion), kind=kOutput, calls=%fused_computation.72 | convolution fusion | flops 272760832 | bytes 9183232 | tf_op jit(solution)/shard_map/while/body/eval_jaxpr/pol,plj->poj/dot_general | solution.py:74
  61.7 2.7 %fusion.44 = bf16[4,512,64]{1,2,0:T(8,128)(2,1)S(1)} fusion(f32[4,512,1024]{2,1,0:T(8,128)S(1)} %bitcast.126, f32[4,512]{1,0:T(4,128)S(1)} %get-tuple-element.45, bf16[4,1024,512]{1,2,0:T(8,128)(2,1)} %pad_maximum_fusion), kind=kOutput, calls=%fused_computation.71 | convolution fusion | flops 272760832 | bytes 9183232 | tf_op jit(solution)/shard_map/while/body/eval_jaxpr/pol,plj->poj/dot_general | solution.py:74
  64.4 2.5 %fusion.43 = bf16[4,512,64]{1,2,0:T(8,128)(2,1)S(1)} fusion(f32[4,512,1024]{2,1,0:T(8,128)S(1)} %bitcast.128, f32[4,512]{1,0:T(4,128)S(1)} %get-tuple-element.43, bf16[4,1024,512]{1,2,0:T(8,128)(2,1)} %pad_maximum_fusion), kind=kOutput, calls=%fused_computation.70 | convolution fusion | flops 272760832 | bytes 9183232 | tf_op jit(solution)/shard_map/while/body/eval_jaxpr/pol,plj->poj/dot_general | solution.py:74
  67.7 4.6 %fusion.77 = f32[4,512,1024]{2,1,0:T(8,128)} fusion(bf16[4,512,256]{1,2,0:T(8,128)(2,1)S(1)} %get-tuple-element.52, f32[256]{0:T(256)S(1)} %copy-done.8, f32[4,512]{1,0:T(4,128)S(1)} %add_rsqrt_fusion, bf16[256,1024]{1,0:T(8,128)(2,1)S(1)} %copy-done), kind=kOutput, calls=%fused_computation.113 | convolution fusion | flops 1075838976 | bytes 9970688 | tf_op jit(solution)/shard_map/gsd,de->gse/dot_general | solution.py:37
  72.3 6.9 %fusion.34 = bf16[4,512,256]{1,2,0:T(8,128)(2,1)S(1)} fusion(bf16[4,512,256]{1,2,0:T(8,128)(2,1)S(1)} %get-tuple-element.52, f32[4,512,1024]{2,1,0:T(8,128)} %fusion.77, f32[256]{0:T(256)S(1)} %copy-done.8, f32[4,512]{1,0:T(4,128)S(1)} %add_rsqrt_fusion, bf16[1024,256]{1,0:T(8,128)(2,1)} %param.24, bf16[256,1024]{1,0:T(8,128)(2,1)} %param.23), kind=kOutput, calls=%fused_computation.54 | convolution fusion | flops 2163736576 | bytes 11543552 | tf_op jit(solution)/shard_map/gsd,de->gse/dot_general | solution.py:37
  79.2 24.6 %copy.82 = bf16[4,512,256]{0,2,1:T(8,128)(2,1)} copy(bf16[4,512,256]{1,2,0:T(8,128)(2,1)S(1)} %fusion.34) | data formatting | bytes 2097152 | tf_op jit(solution)/shard_map/reshape | solution.py:175
  103.8 42.8 %gather_fusion = bf16[4096,4]{1,0:T(8,128)(2,1)S(1)} fusion(bf16[4,131072]{0,1:T(8,128)(2,1)} %bitcast.119, s32[4096]{0:T(1024)S(1)} %fusion.141), kind=kCustom, calls=%fused_computation | custom fusion | bytes 81920 | tf_op jit(solution)/shard_map/gather | solution.py:175
  146.6 1.0 copy.59
  147.5 4.6 %all-to-all-start = ((bf16[4,4,1024]{2,0,1:T(4,128)(2,1)}), bf16[4,4,1024]{2,0,1:T(4,128)(2,1)S(1)}, u32[]{:S(2)}, u32[]{:S(2)}) async-start(bf16[4,4,1024]{2,0,1:T(4,128)(2,1)} %copy.59), calls=%async_computation | async-start | bytes 65536 | tf_op jit(solution)/shard_map/all_to_all | solution.py:176
  152.1 1.4 copy.61
  153.5 3.3 %all-to-all-done = bf16[4,4,1024]{2,0,1:T(4,128)(2,1)S(1)} async-done(((bf16[4,4,1024]{2,0,1:T(4,128)(2,1)}), bf16[4,4,1024]{2,0,1:T(4,128)(2,1)S(1)}, u32[]{:S(2)}, u32[]{:S(2)}) %all-to-all-start) | async-done | bytes 32800 | tf_op jit(solution)/shard_map/all_to_all | solution.py:176
  156.9 3.5 %all-to-all-start.1 = ((bf16[4,512,256]{2,0,1:T(4,128)(2,1)}), bf16[4,512,256]{2,0,1:T(4,128)(2,1)S(1)}, u32[]{:S(2)}, u32[]{:S(2)}) async-start(bf16[4,512,256]{2,0,1:T(4,128)(2,1)} %copy.61), calls=%async_computation.1 | async-start | bytes 2097152 | tf_op jit(solution)/shard_map/all_to_all | solution.py:172
  161.6 51.7 %all-reduce = (f32[16,16]{1,0:T(8,128)S(1)}, f32[16]{0:T(128)S(1)}) all-reduce(f32[16,16]{1,0:T(8,128)S(1)} %fusion.203, f32[16]{0:T(128)S(1)} %convolution_bitcast_fusion.2), channel_id=1, replica_groups=mesh['mem'=4,'tok'=8] {'mem','tok'}, use_global_device_ids=true, to_apply=%region_11.12 | all-reduce | flops 272 | bytes 2176 | tf_op jit(solution)/shard_map/psum | solution.py:184
  218.7 1.5 cholesky.13
  221.7 1.2 custom-call.10
  224.7 1.0 convolution_convert_fusion
  226.1 16.7 %all_to_all.49 = bf16[16,128,256]{2,1,0:T(8,128)(2,1)S(1)} all-to-all(bf16[16,128,256]{2,1,0:T(8,128)(2,1)S(1)} %copy.64), channel_id=1, replica_groups=mesh['mem'=4,'tok'=8] {'mem'}, dimensions={0} | all-to-all | bytes 2097152 | tf_op jit(solution)/shard_map/all_to_all | solution.py:192
  242.7 1.0 copy.65
  (92 shorter events, 10.9 us)
Async XLA Ops:
  0.0 67.6 %copy-start = (bf16[256,1024]{1,0:T(8,128)(2,1)S(1)}, bf16[256,1024]{1,0:T(8,128)(2,1)}, u32[]{:S(2)}) copy-start(bf16[256,1024]{1,0:T(8,128)(2,1)} %param.22) | copy-start | bytes 1572868
  0.0 3.4 %copy-start.12 = (f32[256]{0:T(256)S(1)}, f32[256]{0:T(256)}, u32[]{:S(2)}) copy-start(f32[256]{0:T(256)} %param.16) | copy-start | bytes 3076
  0.0 3.4 %copy-start.9 = (bf16[256,256]{1,0:T(8,128)(2,1)S(1)}, bf16[256,256]{1,0:T(8,128)(2,1)}, u32[]{:S(2)}) copy-start(bf16[256,256]{1,0:T(8,128)(2,1)} %param.20) | copy-start | bytes 393220
  1.8 9.3 %copy-start.7 = (s32[4]{0:T(128)S(1)}, s32[4]{0:T(128)}, u32[]{:S(2)}) copy-start(s32[4]{0:T(128)} %param.25) | copy-start | bytes 52
  1.8 10.0 %copy-start.5 = (s32[4096]{0:T(1024)S(1)}, s32[4096]{0:T(1024)}, u32[]{:S(2)}) copy-start(s32[4096]{0:T(1024)} %param.27) | copy-start | bytes 49156
  1.8 10.0 %copy-start.6 = (s32[4096]{0:T(1024)S(1)}, s32[4096]{0:T(1024)}, u32[]{:S(2)}) copy-start(s32[4096]{0:T(1024)} %param.26) | copy-start | bytes 49156
  1.9 10.0 %copy-start.10 = (bf16[256,256]{1,0:T(8,128)(2,1)S(1)}, bf16[256,256]{1,0:T(8,128)(2,1)}, u32[]{:S(2)}) copy-start(bf16[256,256]{1,0:T(8,128)(2,1)} %param.18) | copy-start | bytes 393220
  3.9 1.0 copy-start.1
  6.4 12.1 %collective-permute-start = (bf16[4,256,512]{1,2,0:T(8,128)(2,1)}, bf16[4,256,512]{1,2,0:T(8,128)(2,1)}, u32[]{:S(2)}, u32[]{:S(2)}) collective-permute-start(bf16[4,256,512]{1,2,0:T(8,128)(2,1)} %get-tuple-element.19), channel_id=1, source_target_pairs={{0,1},{1,2},{2,3},{3,4},{4,5},{5,6},{6,7},{8,9},{9,10},{10,11},{11... | collective-permute-start | bytes 3145736 | tf_op jit(solution)/shard_map/ppermute | solution.py:23
  9.8 8.8 %collective-permute-start.1 = (bf16[4,256,512]{1,2,0:T(8,128)(2,1)}, bf16[4,256,512]{1,2,0:T(8,128)(2,1)}, u32[]{:S(2)}, u32[]{:S(2)}) collective-permute-start(bf16[4,256,512]{1,2,0:T(8,128)(2,1)} %get-tuple-element.20), channel_id=1, source_target_pairs={{1,0},{2,1},{3,2},{4,3},{5,4},{6,5},{7,6},{9,8},{10,9},{11,10},{12... | collective-permute-start | bytes 3145736 | tf_op jit(solution)/shard_map/ppermute | solution.py:25
  11.1 7.5 %copy-start.2 = (bf16[4,512,256]{1,2,0:T(8,128)(2,1)S(1)}, bf16[4,512,256]{1,2,0:T(8,128)(2,1)}, u32[]{:S(2)}) copy-start(bf16[4,512,256]{1,2,0:T(8,128)(2,1)} %copy-done.1) | copy-start | bytes 3145732
  22.1 7.5 %copy-start.4 = (pred[512,1024]{1,0:T(8,128)(4,1)S(1)}, pred[512,1024]{1,0:T(8,128)(4,1)}, u32[]{:S(2)}) copy-start(pred[512,1024]{1,0:T(8,128)(4,1)} %get-tuple-element.35) | copy-start | bytes 1572868
  29.6 7.4 %copy-start.3 = (pred[512,1024]{1,0:T(8,128)(4,1)S(1)}, pred[512,1024]{1,0:T(8,128)(4,1)}, u32[]{:S(2)}) copy-start(pred[512,1024]{1,0:T(8,128)(4,1)} %get-tuple-element.36) | copy-start | bytes 1572868
  51.6 10.1 %slice-start = ((s8[8388608]{0:T(1024)(128)(4,1)}), s8[4194304]{0:T(1024)(128)(4,1)S(1)}, s32[]{:S(2)}) async-start(s8[8388608]{0:T(1024)(128)(4,1)} %bitcast.125), calls=%async_computation.3 | async-start | bytes 8388608
  56.6 5.1 %slice-start.1 = ((s8[8388608]{0:T(1024)(128)(4,1)}), s8[4194304]{0:T(1024)(128)(4,1)S(1)}, s32[]{:S(2)}) async-start(s8[8388608]{0:T(1024)(128)(4,1)} %bitcast.125), calls=%async_computation.4 | async-start | bytes 8388608
  56.6 7.8 %slice-start.2 = ((s8[8388608]{0:T(1024)(128)(4,1)}), s8[4194304]{0:T(1024)(128)(4,1)S(1)}, s32[]{:S(2)}) async-start(s8[8388608]{0:T(1024)(128)(4,1)} %bitcast.127), calls=%async_computation.5 | async-start | bytes 8388608
  61.7 2.7 %slice-start.3 = ((s8[8388608]{0:T(1024)(128)(4,1)}), s8[4194304]{0:T(1024)(128)(4,1)S(1)}, s32[]{:S(2)}) async-start(s8[8388608]{0:T(1024)(128)(4,1)} %bitcast.127), calls=%async_computation.6 | async-start | bytes 8388608
  64.4 2.6 %copy-start.11 = (bf16[256,256]{1,0:T(8,128)(2,1)S(1)}, bf16[256,256]{1,0:T(8,128)(2,1)}, u32[]{:S(2)}) copy-start(bf16[256,256]{1,0:T(8,128)(2,1)} %param.21) | copy-start | bytes 393220
  67.0 0.7 copy-start.8
  147.5 9.3 %all-to-all-start = ((bf16[4,4,1024]{2,0,1:T(4,128)(2,1)}), bf16[4,4,1024]{2,0,1:T(4,128)(2,1)S(1)}, u32[]{:S(2)}, u32[]{:S(2)}) async-start(bf16[4,4,1024]{2,0,1:T(4,128)(2,1)} %copy.59), calls=%async_computation | async-start | bytes 65536 | tf_op jit(solution)/shard_map/all_to_all | solution.py:176
  156.9 67.2 %all-to-all-start.1 = ((bf16[4,512,256]{2,0,1:T(4,128)(2,1)}), bf16[4,512,256]{2,0,1:T(4,128)(2,1)S(1)}, u32[]{:S(2)}, u32[]{:S(2)}) async-start(bf16[4,512,256]{2,0,1:T(4,128)(2,1)} %copy.61), calls=%async_computation.1 | async-start | bytes 2097152 | tf_op jit(solution)/shard_map/all_to_all | solution.py:172
where the time goes:
time: 245 us; the launch traced here: 244 us
  local copies, waits for them, and re-layouts  75.3 us (31%)
  blocking collectives  68.3 us (28%)
  matrix products  65.3 us (27%)
  other arithmetic  16.8 us (7%)
  starting transfers between devices  12.7 us (5%)
  waiting for transfers between devices  3.35 us (1%)
    psum x1, blocking collectives, local(): gram, proj = lax.psum((gram, proj), ('mem', 'tok'))  51.7 us
    gather x1, local copies, waits for them, and re-layouts, local(): prior_field.reshape(nearby_ensemble, -1)[:, serial_position]  42.8 us
    sub x4, matrix products, one_block(): expo = jnp.exp(score_matrix - row_top)  29.5 us
    reshape x1, local copies, waits for them, and re-layouts, local(): prior_field.reshape(nearby_ensemble, -1)[:, serial_position]  24.6 us
    all_to_all x1, blocking collectives, local(): lax.all_to_all(mixed_result.astype(jnp.bfloat16), 'mem', split_axis=0, co...  16.7 us
    dot_general x6, matrix products, apply_projection(): jnp.einsum('gsd,de->gse', values, matrix, preferred_element_type=jnp.floa...  15.6 us
    dot_general x4, matrix products, one_block(): jnp.einsum('pol,plj->poj', softmax_weights, value_rows[:, :, lower_column...  15.3 us
    and x1, other arithmetic, one_block(): allowed = (apart <= head_window[head]) & inside[None, :]  5.22 us
  transfers between devices with their start and end apart: 4, of which 1 were waited for; matrix products, arithmetic and copies ran while one was open for 8% of the time, Pallas kernels for 0%

commit v1 on v0

v1 whole, which is shorter than its diff:
```python
import math

import jax
import jax.numpy as jnp
from jax import lax
from jax.experimental import pallas as pl
from jax.experimental.pallas import tpu as pltpu
from jax.sharding import PartitionSpec as P

WIN = 256
NS_STEPS = 8
EPS = 1e-05
Q_ROWS = 128
GROUP = 16
LANES = 128
VMEM_LIMIT = 50 * 1024 * 1024

F32 = jnp.float32
BF16 = jnp.bfloat16


def dot(a, b, contract=((1,), (0,)), precision=None):
    return lax.dot_general(a, b, (contract, ((), ())), precision=precision, preferred_element_type=F32)


def exact_dot(a, b, contract=((1,), (0,))):
    return dot(a, b, contract, lax.Precision.HIGHEST)


def iota(shape, axis):
    return lax.broadcasted_iota(jnp.int32, shape, axis)


def halves(values):
    high = values.astype(BF16)
    return high, (values - high.astype(F32)).astype(BF16)


def rms_scaled(values, gain):
    return values * lax.rsqrt(jnp.mean(values * values, axis=-1, keepdims=True) + EPS) * gain


def vmem_spec():
    return pl.BlockSpec(memory_space=pltpu.VMEM)


def smem_spec():
    return pl.BlockSpec(memory_space=pltpu.SMEM)


def sample_grid_kernel(start_ref, token_ref, channel_ref, value_ref, var_ref, out_ref):
    rows, feat_width = out_ref.shape[1:]
    count = token_ref.shape[1]
    chunk = min(1024, count)
    total = jnp.zeros((4 * rows, feat_width), F32)
    for lower in range(0, count, chunk):
        part = slice(lower, lower + chunk)
        inv_var = 1.0 / var_ref[:, part]
        weighted = value_ref[:, part] * inv_var
        here = iota((rows, chunk), 0) == token_ref[:, part] - start_ref[0]
        pieces = []
        for row in (inv_var, weighted):
            high = row.astype(BF16).astype(F32)
            pieces.append(jnp.where(here, high, 0.0).astype(BF16))
            pieces.append(jnp.where(here, row - high, 0.0).astype(BF16))
        channel_hot = jnp.where(iota((feat_width, chunk), 0) == channel_ref[:, part], 1.0, 0.0).astype(BF16)
        total += dot(jnp.concatenate(pieces, axis=0), channel_hot, ((1,), (1,)))
    out_ref[0] = total[:rows] + total[rows : 2 * rows]
    out_ref[1] = total[2 * rows : 3 * rows] + total[3 * rows :]


def sample_grid(start, obs_token, obs_channel, obs_value, obs_var, rows, feat_width):
    count = obs_token.shape[0]
    return pl.pallas_call(
        sample_grid_kernel,
        out_shape=jax.ShapeDtypeStruct((2, rows, feat_width), F32),
        in_specs=[smem_spec()] + [vmem_spec()] * 4,
        out_specs=vmem_spec(),
        compiler_params=pltpu.CompilerParams(vmem_limit_bytes=VMEM_LIMIT),
        cost_estimate=pl.CostEstimate(flops=8 * rows * count * feat_width, bytes_accessed=16 * count, transcendentals=0),
        name="sample_grid",
    )(start, *(v.reshape(1, count) for v in (obs_token, obs_channel, obs_value, obs_var)))


def forward_kernel(
    place_ref,
    window_ref,
    own_ref,
    left_ref,
    right_ref,
    attn_gain_ref,
    ffn_gain_ref,
    w_query_ref,
    w_key_ref,
    w_value_ref,
    w_out_ref,
    w_gate_ref,
    w_up_ref,
    down_weight_ref,
    out_ref,
    query_buf,
    key_buf,
    value_buf,
    apart_buf,
    mixed_buf,
):
    row_count, feat_width = own_ref.shape[1:]
    reach = left_ref.shape[1]
    head_count = window_ref.shape[0]
    head_size = feat_width // head_count
    blocks = row_count // Q_ROWS
    key_count = Q_ROWS + 2 * reach

    @pl.when(pl.program_id(0) == 0)
    def _():
        rel = jnp.abs(iota((Q_ROWS, key_count), 1) - reach - iota((Q_ROWS, key_count), 0))
        for block in range(blocks):
            k_pos = place_ref[0] - reach + block * Q_ROWS + iota((Q_ROWS, key_count), 1)
            inside = (k_pos >= 0) & (k_pos < place_ref[1])
            apart_buf[block] = jnp.where(inside, rel, 1 << 20)

    attn_gain = attn_gain_ref[...]
    for source, lower, rows in ((left_ref, 0, reach), (own_ref, reach, row_count), (right_ref, reach + row_count, reach)):
        normed = rms_scaled(source[0].astype(F32), attn_gain).astype(BF16)
        key_buf[lower : lower + rows] = dot(normed, w_key_ref[...]).astype(BF16)
        value_buf[lower : lower + rows] = dot(normed, w_value_ref[...]).astype(BF16)
        if source is own_ref:
            queries = dot(normed, w_query_ref[...]).astype(BF16)
            query_buf[...] = queries * jnp.asarray(1.0 / math.sqrt(head_size), BF16)

    column_head = iota((1, feat_width), 1) // head_size

    def one_block(block, carry):
        start = pl.multiple_of(block * Q_ROWS, Q_ROWS)
        queries = query_buf[pl.ds(start, Q_ROWS), :]
        stacked = jnp.concatenate(
            [queries * (column_head == head).astype(F32).astype(BF16) for head in range(head_count)], axis=0
        )
        scores = dot(stacked, key_buf[pl.ds(start, key_count), :], ((1,), (1,)))
        apart = apart_buf[block]
        weights, scales = [], []
        for head in range(head_count):
            score_matrix = scores[head * Q_ROWS : (head + 1) * Q_ROWS]
            score_matrix = jnp.where(apart <= window_ref[head], score_matrix, -1e30)
            expo = jnp.exp(score_matrix - jnp.max(score_matrix, axis=-1, keepdims=True))
            scales.append(1.0 / jnp.sum(expo, axis=-1, keepdims=True))
            weights.append(expo.astype(BF16))
        mixed_all = dot(jnp.concatenate(weights, axis=0), value_buf[pl.ds(start, key_count), :])
        mixed = jnp.zeros((Q_ROWS, feat_width), F32)
        for head in range(head_count):
            mixed = jnp.where(column_head == head, mixed_all[head * Q_ROWS : (head + 1) * Q_ROWS] * scales[head], mixed)
        mixed_buf[pl.ds(start, Q_ROWS), :] = mixed.astype(BF16)
        return carry

    lax.fori_loop(0, blocks, one_block, 0)

    after = (own_ref[0].astype(F32) + dot(mixed_buf[...], w_out_ref[...])).astype(BF16)
    normed_mid = rms_scaled(after.astype(F32), ffn_gain_ref[...]).astype(BF16)
    gate = dot(normed_mid, w_gate_ref[...])
    hidden = (gate * (0.5 + 0.5 * jnp.tanh(0.5 * gate)) * dot(normed_mid, w_up_ref[...])).astype(BF16)
    forecast = (after.astype(F32) + dot(hidden, down_weight_ref[...])).astype(BF16)
    shares, _, share_rows, _ = out_ref.shape
    for share in range(shares):
        out_ref[share, 0] = forecast[share * share_rows : (share + 1) * share_rows]


def forward(place, head_window, own, left, right, gains, weights, shares):
    members, row_count, feat_width = own.shape
    reach = left.shape[1]
    key_count = Q_ROWS + 2 * reach
    hidden_width = weights[4].shape[1]
    macs = members * row_count * feat_width * (6 * feat_width + 3 * hidden_width + 8 * key_count)
    return pl.pallas_call(
        forward_kernel,
        grid=(members,),
        out_shape=jax.ShapeDtypeStruct((shares, members, row_count // shares, feat_width), BF16),
        in_specs=[
            smem_spec(),
            smem_spec(),
            pl.BlockSpec((1, row_count, feat_width), lambda m: (m, 0, 0)),
            pl.BlockSpec((1, reach, feat_width), lambda m: (m, 0, 0)),
            pl.BlockSpec((1, reach, feat_width), lambda m: (m, 0, 0)),
        ]
        + [vmem_spec()] * (len(gains) + len(weights)),
        out_specs=pl.BlockSpec((shares, 1, row_count // shares, feat_width), lambda m: (0, m, 0, 0)),
        scratch_shapes=[
            pltpu.VMEM((row_count, feat_width), BF16),
            pltpu.VMEM((row_count + 2 * reach, feat_width), BF16),
            pltpu.VMEM((row_count + 2 * reach, feat_width), BF16),
            pltpu.VMEM((row_count // Q_ROWS, Q_ROWS, key_count), jnp.int32),
            pltpu.VMEM((row_count, feat_width), BF16),
        ],
        compiler_params=pltpu.CompilerParams(vmem_limit_bytes=VMEM_LIMIT),
        cost_estimate=pl.CostEstimate(flops=2 * macs, bytes_accessed=5 * own.size, transcendentals=0),
        name="forward",
    )(place, head_window, own, left, right, *gains, *weights)


def gram_kernel(share_ref, grid_ref, out_ref):
    members, rows, feat_width = share_ref.shape
    stack = members * GROUP
    total = jnp.zeros((stack, stack), F32)
    proj = jnp.zeros((members, GROUP, feat_width), F32)
    for lower in range(0, rows, GROUP):
        part = slice(lower, lower + GROUP)
        fields = share_ref[:, part, :].astype(F32)
        mean = jnp.sum(fields, axis=0) * (1.0 / members)
        spread = fields - mean[None]
        weight = grid_ref[0, part, :]
        proj += spread * (grid_ref[1, part, :] - weight * mean)[None]
        high, low = halves(spread.reshape(stack, feat_width))
        w_high, w_low = halves((spread * weight[None]).reshape(stack, feat_width))
        last = ((1,), (1,))
        total += dot(w_high, high, last) + dot(w_high, low, last) + dot(w_low, high, last)
    same = iota((stack, stack), 0) % GROUP == iota((stack, stack), 1) % GROUP
    by_row = jnp.sum(jnp.where(same, total, 0.0).reshape(members, GROUP, stack), axis=1)
    folded = (iota((stack, LANES), 0) // GROUP == iota((stack, LANES), 1) % members).astype(F32)
    tiled = exact_dot(by_row, folded)
    per_row = LANES // members
    keep = iota((members, LANES), 0) % per_row == iota((members, LANES), 1) // members
    packed = jnp.sum(jnp.where(keep, tiled, 0.0).reshape(members // per_row, per_row, LANES), axis=1)
    proj_col = jnp.sum(jnp.sum(proj, axis=1), axis=1, keepdims=True)
    proj_row = jnp.sum(
        jnp.where(iota((members, LANES), 0) == iota((members, LANES), 1), proj_col, 0.0), axis=0, keepdims=True
    )
    filled = members // per_row + 1
    blank = jnp.zeros((out_ref.shape[0] - filled, LANES), F32)
    out_ref[...] = jnp.concatenate([packed, proj_row, blank], axis=0)


def gram_partial(share, grid):
    members = share.shape[0]
    filled = members * members // LANES + 1
    return pl.pallas_call(
        gram_kernel,
        out_shape=jax.ShapeDtypeStruct((-(-filled // 8) * 8, LANES), F32),
        in_specs=[vmem_spec()] * 2,
        out_specs=vmem_spec(),
        compiler_params=pltpu.CompilerParams(vmem_limit_bytes=VMEM_LIMIT),
        cost_estimate=pl.CostEstimate(
            flops=6 * GROUP * members * share.size, bytes_accessed=2 * share.size, transcendentals=0
        ),
        name="gram",
    )(share, grid)


def ensemble_transform(gram, proj):
    members = gram.shape[0]
    row, column = iota((members, members), 0), iota((members, members), 1)
    identity = (row == column).astype(F32)
    system = gram + (members - 1.0) * identity
    left, right = system, proj
    for pivot in range(members):
        is_pivot = iota((members, 1), 0) == pivot
        scale = 1.0 / left[pivot : pivot + 1, pivot : pivot + 1]
        pivot_row = left[pivot : pivot + 1, :] * scale
        pivot_right = right[pivot : pivot + 1, :] * scale
        factor = left[:, pivot : pivot + 1]
        left = jnp.where(is_pivot, pivot_row, left - factor * pivot_row)
        right = jnp.where(is_pivot, pivot_right, right - factor * pivot_right)
    mean_weights = right
    mean_level = jnp.sum(jnp.sum(system * identity, axis=1, keepdims=True), axis=0, keepdims=True) / members
    lifted = system + (mean_level - (members - 1.0)) * (1.0 / members)
    frobenius = jnp.sqrt(jnp.sum(jnp.sum(lifted * lifted, axis=1, keepdims=True), axis=0, keepdims=True))
    root_iter = lifted / frobenius
    inv_iter = identity
    for sweep in range(NS_STEPS):
        product = root_iter if sweep == 0 else exact_dot(inv_iter, root_iter)
        correction = 1.5 * identity - 0.5 * product
        inv_iter = correction if sweep == 0 else exact_dot(correction, inv_iter)
        if sweep < NS_STEPS - 1:
            root_iter = exact_dot(root_iter, correction)
    inv_root = inv_iter / jnp.sqrt(frobenius) + (1.0 / math.sqrt(members - 1.0) - 1.0 / jnp.sqrt(mean_level)) * (
        1.0 / members
    )
    moved = mean_weights + math.sqrt(members - 1.0) * inv_root
    return 1.0 / members + moved - jnp.sum(moved, axis=0, keepdims=True) * (1.0 / members)


def combine_kernel(partial_ref, share_ref, out_ref):
    members, rows, feat_width = share_ref.shape
    stack = members * GROUP
    per_row = LANES // members
    sums = jnp.sum(partial_ref[...], axis=0)
    spread_rows = jnp.concatenate(
        [jnp.broadcast_to(sums[r : r + 1], (per_row, LANES)) for r in range(members // per_row)], axis=0
    )
    keep = iota((members, LANES), 0) % per_row == iota((members, LANES), 1) // members
    folded = (iota((LANES, members), 0) % members == iota((LANES, members), 1)).astype(F32)
    gram = exact_dot(jnp.where(keep, spread_rows, 0.0), folded)
    proj_row = jnp.broadcast_to(sums[members // per_row : members // per_row + 1], (members, LANES))
    on_diagonal = iota((members, LANES), 0) == iota((members, LANES), 1)
    proj = jnp.sum(jnp.where(on_diagonal, proj_row, 0.0), axis=1, keepdims=True)
    transform = ensemble_transform(gram, proj)
    pick = (iota((stack, members), 0) // GROUP == iota((stack, members), 1)).astype(F32).astype(BF16)
    same = iota((stack, stack), 0) % GROUP == iota((stack, stack), 1) % GROUP
    mixers = []
    for piece in halves(transform):
        rows_of = dot(pick, piece, ((1,), (1,))).astype(BF16)
        mixers.append(jnp.where(same, dot(rows_of, pick, ((1,), (1,))), 0.0).astype(BF16))
    for lower in range(0, rows, GROUP):
        fields = share_ref[:, lower : lower + GROUP, :].reshape(stack, feat_width)
        mixed = dot(mixers[0], fields) + dot(mixers[1], fields)
        out_ref[:, lower : lower + GROUP, :] = mixed.astype(BF16).reshape(members, GROUP, feat_width)


def combine(partials, share):
    members = share.shape[0]
    return pl.pallas_call(
        combine_kernel,
        out_shape=jax.ShapeDtypeStruct(share.shape, BF16),
        in_specs=[vmem_spec()] * 2,
        out_specs=vmem_spec(),
        compiler_params=pltpu.CompilerParams(vmem_limit_bytes=VMEM_LIMIT),
        cost_estimate=pl.CostEstimate(
            flops=4 * GROUP * members * share.size, bytes_accessed=4 * share.size, transcendentals=0
        ),
        name="combine",
    )(partials, share)


def local(
    ens_state,
    attn_gain,
    ffn_gain,
    w_query,
    w_key,
    w_value,
    w_out,
    w_gate,
    w_up,
    down_weight,
    head_window,
    obs_token,
    obs_channel,
    obs_value,
    obs_var,
):
    own_members, row_count, feat_width = ens_state.shape
    mem_count = lax.axis_size("mem")
    tok_count = lax.axis_size("tok")
    device_count = mem_count * tok_count
    members = own_members * mem_count
    share_rows = row_count // mem_count
    first_pos = lax.axis_index("tok") * row_count
    up = [(i, i + 1) for i in range(tok_count - 1)]
    down = [(i + 1, i) for i in range(tok_count - 1)]
    left = lax.ppermute(ens_state[:, row_count - WIN :], "tok", up)
    right = lax.ppermute(ens_state[:, :WIN], "tok", down)
    share_start = first_pos + lax.axis_index("mem") * share_rows
    grid = sample_grid(
        share_start.astype(jnp.int32).reshape(1), obs_token, obs_channel, obs_value, obs_var, share_rows, feat_width
    )
    place = jnp.stack([first_pos, row_count * tok_count]).astype(jnp.int32)
    forecast = forward(
        place,
        head_window,
        ens_state,
        left,
        right,
        [attn_gain.reshape(1, -1), ffn_gain.reshape(1, -1)],
        [w_query, w_key, w_value, w_out, w_gate, w_up, down_weight],
        mem_count,
    )
    share = lax.all_to_all(forecast, "mem", split_axis=0, concat_axis=0, tiled=True)
    share = share.reshape(members, share_rows, feat_width)
    partial = gram_partial(share, grid)
    partials = lax.all_to_all(
        jnp.broadcast_to(partial[None], (device_count, *partial.shape)),
        ("mem", "tok"),
        split_axis=0,
        concat_axis=0,
        tiled=True,
    )
    mixed = combine(partials, share).reshape(mem_count, own_members, share_rows, feat_width)
    mixed = lax.all_to_all(mixed, "mem", split_axis=0, concat_axis=0, tiled=True)
    return jnp.moveaxis(mixed, 0, 1).reshape(own_members, row_count, feat_width)


def solution(mesh):
    in_specs = (P("mem", "tok", None), *[P()] * 10, *[P("tok")] * 4)
    return jax.shard_map(local, mesh=mesh, in_specs=in_specs, out_specs=P("mem", "tok", None), check_vma=False)
```

time: 245 us -> 99.9 us (0.41)
  local copies, waits for them, and re-layouts: 75.3 us -> 4.8 us
  matrix products: 65.3 us -> 0 us
  Pallas kernels: 0 us -> 35 us
  blocking collectives: 68.3 us -> 39.7 us
  other arithmetic: 16.8 us -> 0.08 us
  waiting for transfers between devices: 3.35 us -> 12.2 us
  starting transfers between devices: 12.7 us -> 7.54 us
    psum x1 -> x0, blocking collectives: 51.7 us -> none  [local(): gram, proj = lax.psum((gram, proj), ('mem', 'tok'))]
    gather x1 -> x0, local copies, waits for them, and re-layouts: 42.8 us -> none  [local(): prior_field.reshape(nearby_ensemble, -1)[:, serial_position]]
    dot_general x37 -> x0, matrix products: 35.5 us -> none  [the longest x6 15.6 us: apply_projection(): jnp.einsum('gsd,de->gse', values, matrix, preferred_element_type=jnp.floa...]
    pallas_call x0 -> x4, Pallas kernels: none -> 35 us  [the longest x1 28.6 us: forward(): pl.pallas_call(forward_kernel, grid=(members,), out_shape=jax.ShapeDtypeS...]
    sub x4 -> x0, matrix products: 29.5 us -> none  [one_block(): expo = jnp.exp(score_matrix - row_top)]
    reshape x1 -> x0, local copies, waits for them, and re-layouts: 24.6 us -> none  [local(): prior_field.reshape(nearby_ensemble, -1)[:, serial_position]]
    all_to_all x1 -> x2, blocking collectives: 16.7 us -> 39.7 us  [the longest x1 22.4 us: local(): lax.all_to_all(jnp.broadcast_to(partial[None], (device_count, *partial.sh...]
    and x2 -> x0, other arithmetic: 5.23 us -> none  [the longest x1 5.22 us: one_block(): allowed = (apart <= head_window[head]) & inside[None, :]]
  transfers between devices with their start and end apart: 4 -> 3, of which waited for: 1 -> 3; matrix products, arithmetic and copies ran while one was open for 8% -> 0% of each run, Pallas kernels for 0% -> 1%
where the time goes in v1:
time: 99.9 us; the launch traced here: 99.5 us
  blocking collectives  39.7 us (40%)
  Pallas kernels  35 us (35%)
  waiting for transfers between devices  12.2 us (12%)
  starting transfers between devices  7.54 us (8%)
  local copies, waits for them, and re-layouts  4.8 us (5%)
    pallas_call x1, Pallas kernels, forward(): pl.pallas_call(forward_kernel, grid=(members,), out_shape=jax.ShapeDtypeS...  28.6 us
    all_to_all x1, blocking collectives, local(): lax.all_to_all(jnp.broadcast_to(partial[None], (device_count, *partial.sh...  22.4 us
    all_to_all x1, blocking collectives, local(): lax.all_to_all(mixed, 'mem', split_axis=0, concat_axis=0, tiled=True)  17.3 us
    all_to_all x1, waiting for transfers between devices, local(): lax.all_to_all(forecast, 'mem', split_axis=0, concat_axis=0, tiled=True)  7.38 us
    ppermute x1, waiting for transfers between devices, local(): right = lax.ppermute(ens_state[:, :WIN], 'tok', down)  4.48 us
    all_to_all x1, starting transfers between devices, local(): lax.all_to_all(forecast, 'mem', split_axis=0, concat_axis=0, tiled=True)  3.86 us
    pallas_call x1, Pallas kernels, combine(): pl.pallas_call(combine_kernel, out_shape=jax.ShapeDtypeStruct(share.shape...  3.64 us
    slice x1, local copies, waits for them, and re-layouts, local(): right = lax.ppermute(ens_state[:, :WIN], 'tok', down)  2.4 us
  transfers between devices with their start and end apart: 3, of which 3 were waited for; matrix products, arithmetic and copies ran while one was open for 0% of the time, Pallas kernels for 1%

profile of v1, /device:TPU:0, one launch (start us, length us, event | category | flops | bytes accessed | tf_op | source)
XLA Modules:
  0.0 99.5 jit_solution(7436960157332235728)
XLA Ops:
  0.0 0.0 copy-start.1
  0.0 0.0 copy-start.2
  0.0 0.0 copy-start.12
  0.0 2.4 %fusion = (bf16[4,256,256]{2,1,0:T(8,128)(2,1)}, bf16[4,256,256]{2,1,0:T(8,128)(2,1)}) fusion(bf16[4,512,256]{2,1,0:T(8,128)(2,1)} %own_ref.1), kind=kLoop, calls=%fused_computation.1 | loop fusion | bytes 2097152 | tf_op jit(solution)/shard_map/slice | solution.py:349
  2.4 2.4 %collective-permute-start = (bf16[4,256,256]{2,1,0:T(8,128)(2,1)}, bf16[4,256,256]{2,1,0:T(8,128)(2,1)S(1)}, u32[]{:S(2)}, u32[]{:S(2)}) collective-permute-start(bf16[4,256,256]{2,1,0:T(8,128)(2,1)} %get-tuple-element.6), channel_id=1, source_target_pairs={{0,1},{1,2},{2,3},{3,4},{4,5},{5,6},{6,7},{8,9},{9,10},{10,11},{11... | collective-permute-start | bytes 1572872 | tf_op jit(solution)/shard_map/ppermute | solution.py:348
  4.8 1.3 %collective-permute-start.1 = (bf16[4,256,256]{2,1,0:T(8,128)(2,1)}, bf16[4,256,256]{2,1,0:T(8,128)(2,1)S(1)}, u32[]{:S(2)}, u32[]{:S(2)}) collective-permute-start(bf16[4,256,256]{2,1,0:T(8,128)(2,1)} %get-tuple-element.5), channel_id=1, source_target_pairs={{1,0},{2,1},{3,2},{4,3},{5,4},{6,5},{7,6},{9,8},{10,9},{11,10},{12... | collective-permute-start | bytes 1572872 | tf_op jit(solution)/shard_map/ppermute | solution.py:349
  6.1 0.1 pad_add_fusion.place_ref
  6.2 0.3 collective-permute-done.left_ref
  6.5 4.5 %collective-permute-done.1.right_ref = bf16[4,256,256]{2,1,0:T(8,128)(2,1)S(1)} collective-permute-done((bf16[4,256,256]{2,1,0:T(8,128)(2,1)}, bf16[4,256,256]{2,1,0:T(8,128)(2,1)S(1)}, u32[]{:S(2)}, u32[]{:S(2)}) %collective-permute-start.1) | collective-permute-done | bytes 524320 | tf_op jit(solution)/shard_map/ppermute | solution.py:349
  11.0 0.0 copy-done.3
  11.0 0.0 copy-done.4
  11.0 0.0 copy-done.5
  11.0 0.0 copy-done.6
  11.0 0.0 copy-done
  11.1 0.0 copy-done.1
  11.1 0.0 copy-done.2
  11.1 0.0 copy-done.12
  11.1 0.6 copy-done.11
  11.7 0.0 copy-done.13
  11.7 28.6 %forward.1 = bf16[4,4,128,256]{3,2,1,0:T(8,128)(2,1)} custom-call(s32[2]{0:T(128)S(1)} %pad_add_fusion.place_ref, s32[4]{0:T(128)S(1)} %copy-done.13, bf16[4,512,256]{2,1,0:T(8,128)(2,1)} %own_ref.1, bf16[4,256,256]{2,1,0:T(8,128)(2,1)S(1)} %collective-permute-done.left_ref, bf16[4,256,256]{2,1,0:T(8,128)(2,1)S(1)} %collective-permute-done.1.right_ref, ...), custom_call_target="tpu_custom_call" | custom-call | flops 10200547328 | bytes 2621440 | tf_op jit(solution)/shard_map/forward/pallas_call | solution.py:173
  40.3 3.9 %all-to-all-start = ((bf16[4,4,128,256]{3,2,1,0:T(8,128)(2,1)}), bf16[4,4,128,256]{3,2,1,0:T(8,128)(2,1)S(1)}, u32[]{:S(2)}, u32[]{:S(2)}) async-start(bf16[4,4,128,256]{3,2,1,0:T(8,128)(2,1)} %forward.1), calls=%async_computation | async-start | bytes 2097152 | tf_op jit(solution)/shard_map/all_to_all | solution.py:365
  44.1 0.0 copy-done.8
  44.1 0.0 copy-done.9
  44.1 0.0 copy-done.10
  44.1 0.7 copy-done.7
  44.8 1.3 %sample_grid.1.grid_ref = f32[2,128,256]{2,1,0:T(8,128)S(1)} custom-call(s32[1]{0:T(128)} %bitcast.4.start_ref, s32[1,4096]{1,0:T(1,128)S(1)} %bitcast.15, s32[1,4096]{1,0:T(1,128)S(1)} %bitcast.16, f32[1,4096]{1,0:T(1,128)S(1)} %bitcast.17, f32[1,4096]{1,0:T(1,128)S(1)} %bitcast.18), custom_call_target="tpu_custom_call" | custom-call | flops 1073741824 | bytes 65536 | tf_op jit(solution)/shard_map/sample_grid/pallas_call | solution.py:74
  46.2 7.4 %all-to-all-done = bf16[4,4,128,256]{3,2,1,0:T(8,128)(2,1)S(1)} async-done(((bf16[4,4,128,256]{3,2,1,0:T(8,128)(2,1)}), bf16[4,4,128,256]{3,2,1,0:T(8,128)(2,1)S(1)}, u32[]{:S(2)}, u32[]{:S(2)}) %all-to-all-start) | async-done | bytes 1048608 | tf_op jit(solution)/shard_map/all_to_all | solution.py:365
  53.5 1.5 %gram.1 = f32[8,128]{1,0:T(8,128)S(1)} custom-call(bf16[16,128,256]{2,1,0:T(8,128)(2,1)S(1)} %bitcast.12, f32[2,128,256]{2,1,0:T(8,128)S(1)} %sample_grid.1.grid_ref), custom_call_target="tpu_custom_call" | custom-call | flops 805306368 | bytes 1048576 | tf_op jit(solution)/shard_map/gram/pallas_call | solution.py:234
  55.1 22.4 %all_to_all.15.partial_ref = f32[32,8,128]{2,1,0:T(8,128)S(1)} all-to-all(f32[32,8,128]{2,1,0:T(8,128)S(1)} %broadcast_in_dim.2), channel_id=1, replica_groups=mesh['mem'=4,'tok'=8] {'mem','tok'}, dimensions={0} | all-to-all | bytes 262144 | tf_op jit(solution)/shard_map/all_to_all | solution.py:368
  77.5 3.6 %combine.1 = bf16[16,128,256]{2,1,0:T(8,128)(2,1)S(1)} custom-call(f32[32,8,128]{2,1,0:T(8,128)S(1)} %all_to_all.15.partial_ref, bf16[16,128,256]{2,1,0:T(8,128)(2,1)S(1)} %bitcast.13), custom_call_target="tpu_custom_call" | custom-call | flops 536870912 | bytes 2097152 | tf_op jit(solution)/shard_map/combine/pallas_call | solution.py:309
  81.2 17.3 %all_to_all.16 = bf16[4,4,128,256]{3,2,1,0:T(8,128)(2,1)S(1)} all-to-all(bf16[4,4,128,256]{3,2,1,0:T(8,128)(2,1)S(1)} %bitcast.14), channel_id=1, replica_groups=mesh['mem'=4,'tok'=8] {'mem'}, dimensions={0} | all-to-all | bytes 2097152 | tf_op jit(solution)/shard_map/all_to_all | solution.py:376
  98.5 1.0 %copy.16 = bf16[4,4,128,256]{3,2,1,0:T(8,128)(2,1)} copy(bf16[4,4,128,256]{3,2,0,1:T(8,128)(2,1)S(1)} %bitcast.21) | data formatting | bytes 2097152 | tf_op jit(solution)/shard_map/transpose | solution.py:377
  (12 shorter events, 0.0 us)
Async XLA Ops:
  0.0 11.0 %copy-start.3 = (bf16[256,256]{1,0:T(8,128)(2,1)S(1)}, bf16[256,256]{1,0:T(8,128)(2,1)}, u32[]{:S(2)}) copy-start(bf16[256,256]{1,0:T(8,128)(2,1)} %w_query_ref.1) | copy-start | bytes 393220
  0.0 11.0 %copy-start.4 = (bf16[256,256]{1,0:T(8,128)(2,1)S(1)}, bf16[256,256]{1,0:T(8,128)(2,1)}, u32[]{:S(2)}) copy-start(bf16[256,256]{1,0:T(8,128)(2,1)} %w_key_ref.1) | copy-start | bytes 393220
  0.0 11.0 %copy-start.5 = (bf16[256,256]{1,0:T(8,128)(2,1)S(1)}, bf16[256,256]{1,0:T(8,128)(2,1)}, u32[]{:S(2)}) copy-start(bf16[256,256]{1,0:T(8,128)(2,1)} %w_value_ref.1) | copy-start | bytes 393220
  0.0 11.0 %copy-start.6 = (bf16[256,256]{1,0:T(8,128)(2,1)S(1)}, bf16[256,256]{1,0:T(8,128)(2,1)}, u32[]{:S(2)}) copy-start(bf16[256,256]{1,0:T(8,128)(2,1)} %w_out_ref.1) | copy-start | bytes 393220
  0.0 11.0 %copy-start = (bf16[256,1024]{1,0:T(8,128)(2,1)S(1)}, bf16[256,1024]{1,0:T(8,128)(2,1)}, u32[]{:S(2)}) copy-start(bf16[256,1024]{1,0:T(8,128)(2,1)} %w_gate_ref.1) | copy-start | bytes 1572868
  0.0 11.0 %copy-start.1 = (bf16[256,1024]{1,0:T(8,128)(2,1)S(1)}, bf16[256,1024]{1,0:T(8,128)(2,1)}, u32[]{:S(2)}) copy-start(bf16[256,1024]{1,0:T(8,128)(2,1)} %w_up_ref.1) | copy-start | bytes 1572868
  0.0 11.0 %copy-start.2 = (bf16[1024,256]{1,0:T(8,128)(2,1)S(1)}, bf16[1024,256]{1,0:T(8,128)(2,1)}, u32[]{:S(2)}) copy-start(bf16[1024,256]{1,0:T(8,128)(2,1)} %down_weight_ref.1) | copy-start | bytes 1572868
  0.0 11.0 %copy-start.12 = (f32[256]{0:T(256)S(1)}, f32[256]{0:T(256)}, u32[]{:S(2)}) copy-start(f32[256]{0:T(256)} %param.17) | copy-start | bytes 3076
  2.4 4.1 %collective-permute-start = (bf16[4,256,256]{2,1,0:T(8,128)(2,1)}, bf16[4,256,256]{2,1,0:T(8,128)(2,1)S(1)}, u32[]{:S(2)}, u32[]{:S(2)}) collective-permute-start(bf16[4,256,256]{2,1,0:T(8,128)(2,1)} %get-tuple-element.6), channel_id=1, source_target_pairs={{0,1},{1,2},{2,3},{3,4},{4,5},{5,6},{6,7},{8,9},{9,10},{10,11},{11... | collective-permute-start | bytes 1572872 | tf_op jit(solution)/shard_map/ppermute | solution.py:348
  4.8 6.2 %collective-permute-start.1 = (bf16[4,256,256]{2,1,0:T(8,128)(2,1)}, bf16[4,256,256]{2,1,0:T(8,128)(2,1)S(1)}, u32[]{:S(2)}, u32[]{:S(2)}) collective-permute-start(bf16[4,256,256]{2,1,0:T(8,128)(2,1)} %get-tuple-element.5), channel_id=1, source_target_pairs={{1,0},{2,1},{3,2},{4,3},{5,4},{6,5},{7,6},{9,8},{10,9},{11,10},{12... | collective-permute-start | bytes 1572872 | tf_op jit(solution)/shard_map/ppermute | solution.py:349
  11.0 0.7 copy-start.11
  11.0 0.7 copy-start.13
  40.3 3.9 %copy-start.8 = (s32[4096]{0:T(1024)S(1)}, s32[4096]{0:T(1024)}, u32[]{:S(2)}) copy-start(s32[4096]{0:T(1024)} %param.27) | copy-start | bytes 49156
  40.3 3.9 %copy-start.9 = (f32[4096]{0:T(1024)S(1)}, f32[4096]{0:T(1024)}, u32[]{:S(2)}) copy-start(f32[4096]{0:T(1024)} %param.28) | copy-start | bytes 49156
  40.3 3.9 %copy-start.10 = (f32[4096]{0:T(1024)S(1)}, f32[4096]{0:T(1024)}, u32[]{:S(2)}) copy-start(f32[4096]{0:T(1024)} %param.29) | copy-start | bytes 49156
  40.3 13.3 %all-to-all-start = ((bf16[4,4,128,256]{3,2,1,0:T(8,128)(2,1)}), bf16[4,4,128,256]{3,2,1,0:T(8,128)(2,1)S(1)}, u32[]{:S(2)}, u32[]{:S(2)}) async-start(bf16[4,4,128,256]{3,2,1,0:T(8,128)(2,1)} %forward.1), calls=%async_computation | async-start | bytes 2097152 | tf_op jit(solution)/shard_map/all_to_all | solution.py:365
  44.1 0.7 copy-start.7

commit v2 on v1

--- a/solution.py
+++ b/solution.py
@@ -164,8 +164,8 @@
         out_ref[share, 0] = forecast[share * share_rows : (share + 1) * share_rows]
 
 
-def forward(place, head_window, own, left, right, gains, weights, shares):
-    members, row_count, feat_width = own.shape
+def forward(place, head_window, own, left, right, gains, weights, shares, first, members):
+    _, row_count, feat_width = own.shape
     reach = left.shape[1]
     key_count = Q_ROWS + 2 * reach
     hidden_width = weights[4].shape[1]
@@ -177,9 +177,9 @@
         in_specs=[
             smem_spec(),
             smem_spec(),
-            pl.BlockSpec((1, row_count, feat_width), lambda m: (m, 0, 0)),
-            pl.BlockSpec((1, reach, feat_width), lambda m: (m, 0, 0)),
-            pl.BlockSpec((1, reach, feat_width), lambda m: (m, 0, 0)),
+            pl.BlockSpec((1, row_count, feat_width), lambda m: (first + m, 0, 0)),
+            pl.BlockSpec((1, reach, feat_width), lambda m: (first + m, 0, 0)),
+            pl.BlockSpec((1, reach, feat_width), lambda m: (first + m, 0, 0)),
         ]
         + [vmem_spec()] * (len(gains) + len(weights)),
         out_specs=pl.BlockSpec((shares, 1, row_count // shares, feat_width), lambda m: (0, m, 0, 0)),
@@ -191,19 +191,23 @@
             pltpu.VMEM((row_count, feat_width), BF16),
         ],
         compiler_params=pltpu.CompilerParams(vmem_limit_bytes=VMEM_LIMIT),
-        cost_estimate=pl.CostEstimate(flops=2 * macs, bytes_accessed=5 * own.size, transcendentals=0),
+        cost_estimate=pl.CostEstimate(flops=2 * macs, bytes_accessed=6 * members * row_count * feat_width, transcendentals=0),
         name="forward",
     )(place, head_window, own, left, right, *gains, *weights)
 
 
-def gram_kernel(share_ref, grid_ref, out_ref):
-    members, rows, feat_width = share_ref.shape
+def gram_kernel(index_ref, *refs):
+    share_refs, grid_ref, out_ref = refs[:-2], refs[-2], refs[-1]
+    rows, feat_width = grid_ref.shape[1:]
+    members = sum(math.prod(ref.shape[:-2]) for ref in share_refs)
     stack = members * GROUP
     total = jnp.zeros((stack, stack), F32)
     proj = jnp.zeros((members, GROUP, feat_width), F32)
     for lower in range(0, rows, GROUP):
         part = slice(lower, lower + GROUP)
-        fields = share_ref[:, part, :].astype(F32)
+        fields = jnp.concatenate(
+            [ref[..., part, :].reshape(-1, GROUP, feat_width).astype(F32) for ref in share_refs], axis=0
+        )
         mean = jnp.sum(fields, axis=0) * (1.0 / members)
         spread = fields - mean[None]
         weight = grid_ref[0, part, :]
@@ -228,20 +232,32 @@
     out_ref[...] = jnp.concatenate([packed, proj_row, blank], axis=0)
 
 
-def gram_partial(share, grid):
-    members = share.shape[0]
+def gram_partial(index, gathered, shares, grid):
+    def here(array):
+        block = (array.shape[0], 1, *array.shape[2:])
+        return pl.BlockSpec(block, lambda i, index: (0, index[0], 0, 0, 0))
+
+    def whole(array):
+        return pl.BlockSpec(array.shape, lambda i, index: (0,) * array.ndim)
+
+    members = sum(v.shape[0] * v.shape[2] for v in gathered) + sum(v.shape[0] * v.shape[1] for v in shares)
     filled = members * members // LANES + 1
+    out_shape = (-(-filled // 8) * 8, LANES)
     return pl.pallas_call(
         gram_kernel,
-        out_shape=jax.ShapeDtypeStruct((-(-filled // 8) * 8, LANES), F32),
-        in_specs=[vmem_spec()] * 2,
-        out_specs=vmem_spec(),
+        grid_spec=pltpu.PrefetchScalarGridSpec(
+            num_scalar_prefetch=1,
+            grid=(1,),
+            in_specs=[here(v) for v in gathered] + [whole(v) for v in (*shares, grid)],
+            out_specs=pl.BlockSpec(out_shape, lambda i, index: (0, 0)),
+        ),
+        out_shape=jax.ShapeDtypeStruct(out_shape, F32),
         compiler_params=pltpu.CompilerParams(vmem_limit_bytes=VMEM_LIMIT),
         cost_estimate=pl.CostEstimate(
-            flops=6 * GROUP * members * share.size, bytes_accessed=2 * share.size, transcendentals=0
+            flops=3 * GROUP * members * members * grid.size, bytes_accessed=members * grid.size, transcendentals=0
         ),
         name="gram",
-    )(share, grid)
+    )(index, *gathered, *shares, grid)
 
 
 def ensemble_transform(gram, proj):
@@ -277,9 +293,8 @@
     return 1.0 / members + moved - jnp.sum(moved, axis=0, keepdims=True) * (1.0 / members)
 
 
-def combine_kernel(partial_ref, share_ref, out_ref):
-    members, rows, feat_width = share_ref.shape
-    stack = members * GROUP
+def solve_kernel(partial_ref, out_ref):
+    members = out_ref.shape[0]
     per_row = LANES // members
     sums = jnp.sum(partial_ref[...], axis=0)
     spread_rows = jnp.concatenate(
@@ -291,32 +306,67 @@
     proj_row = jnp.broadcast_to(sums[members // per_row : members // per_row + 1], (members, LANES))
     on_diagonal = iota((members, LANES), 0) == iota((members, LANES), 1)
     proj = jnp.sum(jnp.where(on_diagonal, proj_row, 0.0), axis=1, keepdims=True)
-    transform = ensemble_transform(gram, proj)
+    out_ref[...] = ensemble_transform(gram, proj)
+
+
+def solve(partials, members):
+    return pl.pallas_call(
+        solve_kernel,
+        out_shape=jax.ShapeDtypeStruct((members, members), F32),
+        in_specs=[vmem_spec()],
+        out_specs=vmem_spec(),
+        compiler_params=pltpu.CompilerParams(vmem_limit_bytes=VMEM_LIMIT),
+        cost_estimate=pl.CostEstimate(flops=10**9, bytes_accessed=partials.size * 4, transcendentals=0),
+        name="solve",
+    )(partials)
+
+
+def combine_kernel(index_ref, transform_ref, *refs):
+    field_refs, out_ref = refs[:-1], refs[-1]
+    own_members, rows, feat_width = out_ref.shape
+    members = transform_ref.shape[0]
+    stack, own_stack = members * GROUP, own_members * GROUP
+    own = iota((own_stack, members), 0) // GROUP
+    place, first, base = jnp.zeros_like(own), 0, 0
+    for ref in field_refs:
+        part = ref.shape[2]
+        inside = (own >= first) & (own < first + part)
+        place = jnp.where(inside, base + index_ref[0] * part + own - first, place)
+        first, base = first + part, base + part * ref.shape[0]
+    pick_own = (place == iota((own_stack, members), 1)).astype(F32).astype(BF16)
     pick = (iota((stack, members), 0) // GROUP == iota((stack, members), 1)).astype(F32).astype(BF16)
-    same = iota((stack, stack), 0) % GROUP == iota((stack, stack), 1) % GROUP
+    same = iota((own_stack, stack), 0) % GROUP == iota((own_stack, stack), 1) % GROUP
     mixers = []
-    for piece in halves(transform):
-        rows_of = dot(pick, piece, ((1,), (1,))).astype(BF16)
+    for piece in halves(transform_ref[...]):
+        rows_of = dot(pick_own, piece, ((1,), (1,))).astype(BF16)
         mixers.append(jnp.where(same, dot(rows_of, pick, ((1,), (1,))), 0.0).astype(BF16))
-    for lower in range(0, rows, GROUP):
-        fields = share_ref[:, lower : lower + GROUP, :].reshape(stack, feat_width)
-        mixed = dot(mixers[0], fields) + dot(mixers[1], fields)
-        out_ref[:, lower : lower + GROUP, :] = mixed.astype(BF16).reshape(members, GROUP, feat_width)
-
-
-def combine(partials, share):
-    members = share.shape[0]
+    mixer = jnp.concatenate(mixers, axis=0)
+    share_rows = field_refs[0].shape[3]
+    for share in range(rows // share_rows):
+        for lower in range(0, share_rows, GROUP):
+            fields = jnp.concatenate(
+                [ref[:, share, :, lower : lower + GROUP, :].reshape(-1, feat_width) for ref in field_refs], axis=0
+            )
+            mixed = dot(mixer, fields)
+            mixed = (mixed[:own_stack] + mixed[own_stack:]).astype(BF16)
+            start = share * share_rows + lower
+            out_ref[:, start : start + GROUP, :] = mixed.reshape(own_members, GROUP, feat_width)
+
+
+def combine(index, transform, gathered):
+    own_members = sum(v.shape[2] for v in gathered)
+    shares, _, share_rows, feat_width = gathered[0].shape[1:]
+    out_shape = (own_members, shares * share_rows, feat_width)
+    size = sum(v.size for v in gathered)
     return pl.pallas_call(
         combine_kernel,
-        out_shape=jax.ShapeDtypeStruct(share.shape, BF16),
-        in_specs=[vmem_spec()] * 2,
+        out_shape=jax.ShapeDtypeStruct(out_shape, BF16),
+        in_specs=[smem_spec()] + [vmem_spec()] * (1 + len(gathered)),
         out_specs=vmem_spec(),
         compiler_params=pltpu.CompilerParams(vmem_limit_bytes=VMEM_LIMIT),
-        cost_estimate=pl.CostEstimate(
-            flops=4 * GROUP * members * share.size, bytes_accessed=4 * share.size, transcendentals=0
-        ),
+        cost_estimate=pl.CostEstimate(flops=4 * GROUP * own_members * size, bytes_accessed=3 * size, transcendentals=0),
         name="combine",
-    )(partials, share)
+    )(index, transform, *gathered)
 
 
 def local(
@@ -352,19 +402,30 @@
         share_start.astype(jnp.int32).reshape(1), obs_token, obs_channel, obs_value, obs_var, share_rows, feat_width
     )
     place = jnp.stack([first_pos, row_count * tok_count]).astype(jnp.int32)
-    forecast = forward(
-        place,
-        head_window,
-        ens_state,
-        left,
-        right,
-        [attn_gain.reshape(1, -1), ffn_gain.reshape(1, -1)],
-        [w_query, w_key, w_value, w_out, w_gate, w_up, down_weight],
-        mem_count,
-    )
-    share = lax.all_to_all(forecast, "mem", split_axis=0, concat_axis=0, tiled=True)
-    share = share.reshape(members, share_rows, feat_width)
-    partial = gram_partial(share, grid)
+    index = lax.axis_index("mem").astype(jnp.int32).reshape(1)
+    half = own_members // 2
+
+    def forecast_of(first, count):
+        return forward(
+            place,
+            head_window,
+            ens_state,
+            left,
+            right,
+            [attn_gain.reshape(1, -1), ffn_gain.reshape(1, -1)],
+            [w_query, w_key, w_value, w_out, w_gate, w_up, down_weight],
+            mem_count,
+            first,
+            count,
+        )
+
+    early = forecast_of(0, half)
+    early_all = lax.all_gather(early, "mem")
+    late = forecast_of(half, own_members - half)
+    late_share = lax.all_to_all(late, "mem", split_axis=0, concat_axis=0, tiled=True)
+    late, late_share = lax.optimization_barrier((late, late_share))
+    late_all = lax.all_gather(late, "mem")
+    partial = gram_partial(index, [early_all], [late_share], grid)
     partials = lax.all_to_all(
         jnp.broadcast_to(partial[None], (device_count, *partial.shape)),
         ("mem", "tok"),
@@ -372,9 +433,7 @@
         concat_axis=0,
         tiled=True,
     )
-    mixed = combine(partials, share).reshape(mem_count, own_members, share_rows, feat_width)
-    mixed = lax.all_to_all(mixed, "mem", split_axis=0, concat_axis=0, tiled=True)
-    return jnp.moveaxis(mixed, 0, 1).reshape(own_members, row_count, feat_width)
+    return combine(index, solve(partials, members), [early_all, late_all])
 
 
 def solution(mesh):

time: 99.9 us -> 125 us (1.25)
  waiting for transfers between devices: 12.2 us -> 37.5 us
  blocking collectives: 39.7 us -> 25.9 us
  between operations: 0.16 us -> 13.6 us
  Pallas kernels: 35 us -> 39.4 us
  starting transfers between devices: 7.54 us -> 4.42 us
    all_gather x0 -> x2, waiting for transfers between devices: none -> 35.8 us  [the longest x1 19 us: local(): late_all = lax.all_gather(late, 'mem')]
    all_to_all x1, blocking collectives: 22.4 us -> 12.6 us  [local(): lax.all_to_all(jnp.broadcast_to(partial[None], (device_count, *partial.sh...]
    all_to_all x1 -> x0, waiting for transfers between devices: 7.38 us -> none  [local(): lax.all_to_all(forecast, 'mem', split_axis=0, concat_axis=0, tiled=True)]
    ppermute x1, waiting for transfers between devices: 4.48 us -> 0.01 us  [local(): right = lax.ppermute(ens_state[:, :WIN], 'tok', down)]
    all_to_all x1, blocking collectives: 17.3 us -> 13.3 us  [local(): lax.all_to_all(late, 'mem', split_axis=0, concat_axis=0, tiled=True)]
    all_to_all x1 -> x0, starting transfers between devices: 3.86 us -> none  [local(): lax.all_to_all(forecast, 'mem', split_axis=0, concat_axis=0, tiled=True)]
    pallas_call x2 -> x3, Pallas kernels: 5.16 us -> 7.72 us  [the longest x1 3.49 us: combine(): pl.pallas_call(combine_kernel, out_shape=jax.ShapeDtypeStruct(out_shape,...]
    pallas_call x1 -> x2, Pallas kernels: 28.6 us -> 30.4 us  [forward(): pl.pallas_call(forward_kernel, grid=(members,), out_shape=jax.ShapeDtypeS...]
  transfers between devices with their start and end apart: 3 -> 4, of which waited for: 3 -> 3; matrix products, arithmetic and copies ran while one was open for 0% -> 0% of each run, Pallas kernels for 1% -> 17%
where the time goes in v2:
time: 125 us
  Pallas kernels  39.4 us (32%)
  waiting for transfers between devices  37.5 us (30%)
  blocking collectives  25.9 us (21%)
  between operations  13.6 us (11%)
  starting transfers between devices  4.42 us (4%)
  local copies, waits for them, and re-layouts  4.06 us (3%)
    pallas_call x2, Pallas kernels, forward(): pl.pallas_call(forward_kernel, grid=(members,), out_shape=jax.ShapeDtypeS...  30.4 us
    all_gather x1, waiting for transfers between devices, local(): late_all = lax.all_gather(late, 'mem')  19 us
    all_gather x1, waiting for transfers between devices, local(): early_all = lax.all_gather(early, 'mem')  16.8 us
    all_to_all x1, blocking collectives, local(): lax.all_to_all(late, 'mem', split_axis=0, concat_axis=0, tiled=True)  13.3 us
    all_to_all x1, blocking collectives, local(): lax.all_to_all(jnp.broadcast_to(partial[None], (device_count, *partial.sh...  12.6 us
    pallas_call x1, Pallas kernels, combine(): pl.pallas_call(combine_kernel, out_shape=jax.ShapeDtypeStruct(out_shape,...  3.49 us
    ppermute x1, starting transfers between devices, local(): left = lax.ppermute(ens_state[:, row_count - WIN:], 'tok', up)  3.06 us
    pallas_call x1, Pallas kernels, solve(): pl.pallas_call(solve_kernel, out_shape=jax.ShapeDtypeStruct((members, mem...  2.68 us
  transfers between devices with their start and end apart: 4, of which 3 were waited for; matrix products, arithmetic and copies ran while one was open for 0% of the time, Pallas kernels for 17%

profile of v2, /device:TPU:0, one launch (start us, length us, event | category | flops | bytes accessed | tf_op | source)
XLA Modules:
  0.0 124.9 jit_solution(11728156782146504386)
XLA Ops:
  6.5 0.0 copy-start.7
  6.6 0.0 copy-start.6
  6.6 0.0 copy-start.5
  6.6 0.0 copy-start.14
  6.6 0.0 copy-start.13
  6.6 0.0 all-gather.5.cloned.1.call-start
  6.6 2.4 %fusion = (bf16[4,256,256]{2,1,0:T(8,128)(2,1)}, bf16[4,256,256]{2,1,0:T(8,128)(2,1)}) fusion(bf16[4,512,256]{2,1,0:T(8,128)(2,1)} %own_ref.3), kind=kLoop, calls=%fused_computation.1 | loop fusion | bytes 2097152 | tf_op jit(solution)/shard_map/slice | solution.py:399
  9.0 1.3 %collective-permute-start.1 = (bf16[4,256,256]{2,1,0:T(8,128)(2,1)}, bf16[4,256,256]{2,1,0:T(8,128)(2,1)S(1)}, u32[]{:S(2)}, u32[]{:S(2)}) collective-permute-start(bf16[4,256,256]{2,1,0:T(8,128)(2,1)} %get-tuple-element.9), channel_id=1, source_target_pairs={{1,0},{2,1},{3,2},{4,3},{5,4},{6,5},{7,6},{9,8},{10,9},{11,10},{12... | collective-permute-start | bytes 1572872 | tf_op jit(solution)/shard_map/ppermute | solution.py:399
  10.3 3.1 %collective-permute-start = (bf16[4,256,256]{2,1,0:T(8,128)(2,1)}, bf16[4,256,256]{2,1,0:T(8,128)(2,1)S(1)}, u32[]{:S(2)}, u32[]{:S(2)}) collective-permute-start(bf16[4,256,256]{2,1,0:T(8,128)(2,1)} %get-tuple-element.10), channel_id=1, source_target_pairs={{0,1},{1,2},{2,3},{3,4},{4,5},{5,6},{6,7},{8,9},{9,10},{10,11},{11... | collective-permute-start | bytes 1572872 | tf_op jit(solution)/shard_map/ppermute | solution.py:398
  13.4 0.1 pad_add_fusion.place_ref
  13.5 0.0 collective-permute-done.1.right_ref
  13.5 1.6 %collective-permute-done.left_ref = bf16[4,256,256]{2,1,0:T(8,128)(2,1)S(1)} collective-permute-done((bf16[4,256,256]{2,1,0:T(8,128)(2,1)}, bf16[4,256,256]{2,1,0:T(8,128)(2,1)S(1)}, u32[]{:S(2)}, u32[]{:S(2)}) %collective-permute-start) | collective-permute-done | bytes 524320 | tf_op jit(solution)/shard_map/ppermute | solution.py:398
  15.1 0.0 copy-done.4
  15.1 0.0 copy-done.2
  15.2 15.2 %forward.2 = bf16[4,2,128,256]{3,2,1,0:T(8,128)(2,1)} custom-call(s32[2]{0:T(128)S(1)} %pad_add_fusion.place_ref, s32[4]{0:T(128)S(1)} %copy-done.15, bf16[4,512,256]{2,1,0:T(8,128)(2,1)} %own_ref.3, bf16[4,256,256]{2,1,0:T(8,128)(2,1)S(1)} %collective-permute-done.left_ref, bf16[4,256,256]{2,1,0:T(8,128)(2,1)S(1)} %collective-permute-done.1.right_ref, ...), custom_call_target="tpu_custom_call" | custom-call | flops 5100273664 | bytes 1572864 | tf_op jit(solution)/shard_map/forward/pallas_call | solution.py:173
  30.3 0.0 all-gather.5.cloned.1.call-update
  30.3 0.0 copy-start.9
  30.4 0.0 copy-start.10
  30.4 0.0 copy-start.11
  30.4 0.0 copy-start.12
  30.4 0.0 all-gather.7.cloned.1.call-start
  30.4 15.2 %forward.3 = bf16[4,2,128,256]{3,2,1,0:T(8,128)(2,1)} custom-call(s32[2]{0:T(128)S(1)} %pad_add_fusion.place_ref, s32[4]{0:T(128)S(1)} %copy-done.15, bf16[4,512,256]{2,1,0:T(8,128)(2,1)} %own_ref.3, bf16[4,256,256]{2,1,0:T(8,128)(2,1)S(1)} %collective-permute-done.left_ref, bf16[4,256,256]{2,1,0:T(8,128)(2,1)S(1)} %collective-permute-done.1.right_ref, ...), custom_call_target="tpu_custom_call" | custom-call | flops 5100273664 | bytes 1572864 | tf_op jit(solution)/shard_map/forward/pallas_call | solution.py:173
  45.6 13.3 %all_to_all.10.refs_1_ = bf16[4,2,128,256]{3,2,1,0:T(8,128)(2,1)S(1)} all-to-all(bf16[4,2,128,256]{3,2,1,0:T(8,128)(2,1)} %forward.3), channel_id=1, replica_groups=mesh['mem'=4,'tok'=8] {'mem'}, dimensions={0} | all-to-all | bytes 1048576 | tf_op jit(solution)/shard_map/all_to_all | solution.py:425
  59.0 0.0 all-gather.7.cloned.1.call-update
  59.0 1.3 %sample_grid.1.refs_2_ = f32[2,128,256]{2,1,0:T(8,128)S(1)} custom-call(s32[1]{0:T(128)} %bitcast.5.start_ref, s32[1,4096]{1,0:T(1,128)S(1)} %bitcast.13, s32[1,4096]{1,0:T(1,128)S(1)} %bitcast.14, f32[1,4096]{1,0:T(1,128)S(1)} %bitcast.15, f32[1,4096]{1,0:T(1,128)S(1)} %bitcast.16), custom_call_target="tpu_custom_call" | custom-call | flops 1073741824 | bytes 65536 | tf_op jit(solution)/shard_map/sample_grid/pallas_call | solution.py:74
  60.4 16.8 %all-gather.5.cloned.1.call-done = bf16[16,2,128,256]{3,2,1,0:T(8,128)(2,1)} async-done(((bf16[4,2,128,256]{3,2,1,0:T(8,128)(2,1)}), bf16[16,2,128,256]{3,2,1,0:T(8,128)(2,1)}) %all-gather.5.cloned.1.call-update) | async-done | bytes 2097168 | tf_op jit(solution)/shard_map/all_gather | solution.py:423
  77.2 1.6 %copy-done = bf16[16,2,128,256]{3,2,1,0:T(8,128)(2,1)S(1)} copy-done((bf16[16,2,128,256]{3,2,1,0:T(8,128)(2,1)S(1)}, bf16[16,2,128,256]{3,2,1,0:T(8,128)(2,1)}, u32[]{:S(2)}) %copy-start) | copy-done | bytes 2097176
  78.8 1.5 %gram.1 = f32[8,128]{1,0:T(8,128)S(1)} custom-call(s32[1]{0:T(128)} %bitcast.index_ref, bf16[4,4,2,128,256]{4,3,2,1,0:T(8,128)(2,1)S(1)} %bitcast.11, bf16[4,2,128,256]{3,2,1,0:T(8,128)(2,1)S(1)} %all_to_all.10.refs_1_, f32[2,128,256]{2,1,0:T(8,128)S(1)} %sample_grid.1.refs_2_), custom_call_target="tpu_custom_call" | custom-call | flops 805306368 | bytes 1048576 | tf_op jit(solution)/shard_map/gram/pallas_call | solution.py:246
  80.4 12.6 %all_to_all.11.partial_ref = f32[32,8,128]{2,1,0:T(8,128)S(1)} all-to-all(f32[32,8,128]{2,1,0:T(8,128)S(1)} %broadcast_in_dim.2), channel_id=1, replica_groups=mesh['mem'=4,'tok'=8] {'mem','tok'}, dimensions={0} | all-to-all | bytes 262144 | tf_op jit(solution)/shard_map/all_to_all | solution.py:429
  92.9 2.7 %solve.1.transform_ref = f32[16,16]{1,0:T(8,128)S(1)} custom-call(f32[32,8,128]{2,1,0:T(8,128)S(1)} %all_to_all.11.partial_ref), custom_call_target="tpu_custom_call" | custom-call | flops 1000000000 | bytes 131072 | tf_op jit(solution)/shard_map/solve/pallas_call | solution.py:313
  95.6 19.0 %all-gather.7.cloned.1.call-done = bf16[16,2,128,256]{3,2,1,0:T(8,128)(2,1)} async-done(((bf16[4,2,128,256]{3,2,1,0:T(8,128)(2,1)}), bf16[16,2,128,256]{3,2,1,0:T(8,128)(2,1)}) %all-gather.7.cloned.1.call-update) | async-done | bytes 2097168 | tf_op jit(solution)/shard_map/all_gather | solution.py:427
  114.6 3.5 %combine.1 = bf16[4,512,256]{2,1,0:T(8,128)(2,1)} custom-call(s32[1]{0:T(128)} %bitcast.index_ref, f32[16,16]{1,0:T(8,128)S(1)} %solve.1.transform_ref, bf16[4,4,2,128,256]{4,3,2,1,0:T(8,128)(2,1)S(1)} %bitcast.12, bf16[4,4,2,128,256]{4,3,2,1,0:T(8,128)(2,1)} %bitcast.21), custom_call_target="tpu_custom_call" | custom-call | flops 536870912 | bytes 6291456 | tf_op jit(solution)/shard_map/combine/pallas_call | solution.py:361
  (21 shorter events, 0.0 us)
Async XLA Ops:
  6.5 8.6 %copy-start.15 = (s32[4]{0:T(128)S(1)}, s32[4]{0:T(128)}, u32[]{:S(2)}) copy-start(s32[4]{0:T(128)} %window_ref.3) | copy-start | bytes 52
  6.5 8.6 %copy-start.4 = (bf16[1024,256]{1,0:T(8,128)(2,1)S(1)}, bf16[1024,256]{1,0:T(8,128)(2,1)}, u32[]{:S(2)}) copy-start(bf16[1024,256]{1,0:T(8,128)(2,1)} %down_weight_ref.3) | copy-start | bytes 1572868
  6.5 8.6 %copy-start.3 = (bf16[256,1024]{1,0:T(8,128)(2,1)S(1)}, bf16[256,1024]{1,0:T(8,128)(2,1)}, u32[]{:S(2)}) copy-start(bf16[256,1024]{1,0:T(8,128)(2,1)} %w_up_ref.3) | copy-start | bytes 1572868
  6.5 8.6 %copy-start.2 = (bf16[256,1024]{1,0:T(8,128)(2,1)S(1)}, bf16[256,1024]{1,0:T(8,128)(2,1)}, u32[]{:S(2)}) copy-start(bf16[256,1024]{1,0:T(8,128)(2,1)} %w_gate_ref.3) | copy-start | bytes 1572868
  6.5 8.6 %copy-start.8 = (bf16[256,256]{1,0:T(8,128)(2,1)S(1)}, bf16[256,256]{1,0:T(8,128)(2,1)}, u32[]{:S(2)}) copy-start(bf16[256,256]{1,0:T(8,128)(2,1)} %w_out_ref.3) | copy-start | bytes 393220
  6.5 8.6 %copy-start.7 = (bf16[256,256]{1,0:T(8,128)(2,1)S(1)}, bf16[256,256]{1,0:T(8,128)(2,1)}, u32[]{:S(2)}) copy-start(bf16[256,256]{1,0:T(8,128)(2,1)} %w_value_ref.3) | copy-start | bytes 393220
  6.6 8.6 %copy-start.6 = (bf16[256,256]{1,0:T(8,128)(2,1)S(1)}, bf16[256,256]{1,0:T(8,128)(2,1)}, u32[]{:S(2)}) copy-start(bf16[256,256]{1,0:T(8,128)(2,1)} %w_key_ref.3) | copy-start | bytes 393220
  6.6 8.6 %copy-start.5 = (bf16[256,256]{1,0:T(8,128)(2,1)S(1)}, bf16[256,256]{1,0:T(8,128)(2,1)}, u32[]{:S(2)}) copy-start(bf16[256,256]{1,0:T(8,128)(2,1)} %w_query_ref.3) | copy-start | bytes 393220
  6.6 8.6 %copy-start.14 = (f32[256]{0:T(256)S(1)}, f32[256]{0:T(256)}, u32[]{:S(2)}) copy-start(f32[256]{0:T(256)} %param.17) | copy-start | bytes 3076
  6.6 8.6 %copy-start.13 = (f32[256]{0:T(256)S(1)}, f32[256]{0:T(256)}, u32[]{:S(2)}) copy-start(f32[256]{0:T(256)} %param.16) | copy-start | bytes 3076
  6.6 70.6 %all-gather.5.cloned.1.call-start = ((), (), s32[]{:S(2)}) async-start(), calls=%async_computation.2 | async-start | bytes 2621440 | tf_op jit(solution)/shard_map/all_gather | solution.py:423
  9.0 4.4 %collective-permute-start.1 = (bf16[4,256,256]{2,1,0:T(8,128)(2,1)}, bf16[4,256,256]{2,1,0:T(8,128)(2,1)S(1)}, u32[]{:S(2)}, u32[]{:S(2)}) collective-permute-start(bf16[4,256,256]{2,1,0:T(8,128)(2,1)} %get-tuple-element.9), channel_id=1, source_target_pairs={{1,0},{2,1},{3,2},{4,3},{5,4},{6,5},{7,6},{9,8},{10,9},{11,10},{12... | collective-permute-start | bytes 1572872 | tf_op jit(solution)/shard_map/ppermute | solution.py:399
  10.3 4.8 %collective-permute-start = (bf16[4,256,256]{2,1,0:T(8,128)(2,1)}, bf16[4,256,256]{2,1,0:T(8,128)(2,1)S(1)}, u32[]{:S(2)}, u32[]{:S(2)}) collective-permute-start(bf16[4,256,256]{2,1,0:T(8,128)(2,1)} %get-tuple-element.10), channel_id=1, source_target_pairs={{0,1},{1,2},{2,3},{3,4},{4,5},{5,6},{6,7},{8,9},{9,10},{10,11},{11... | collective-permute-start | bytes 1572872 | tf_op jit(solution)/shard_map/ppermute | solution.py:398
  30.3 28.7 %copy-start.9 = (s32[4096]{0:T(1024)S(1)}, s32[4096]{0:T(1024)}, u32[]{:S(2)}) copy-start(s32[4096]{0:T(1024)} %param.26) | copy-start | bytes 49156
  30.4 28.6 %copy-start.10 = (s32[4096]{0:T(1024)S(1)}, s32[4096]{0:T(1024)}, u32[]{:S(2)}) copy-start(s32[4096]{0:T(1024)} %param.27) | copy-start | bytes 49156
  30.4 28.6 %copy-start.11 = (f32[4096]{0:T(1024)S(1)}, f32[4096]{0:T(1024)}, u32[]{:S(2)}) copy-start(f32[4096]{0:T(1024)} %param.28) | copy-start | bytes 49156
  30.4 28.6 %copy-start.12 = (f32[4096]{0:T(1024)S(1)}, f32[4096]{0:T(1024)}, u32[]{:S(2)}) copy-start(f32[4096]{0:T(1024)} %param.29) | copy-start | bytes 49156
  30.4 84.2 %all-gather.7.cloned.1.call-start = ((), (), s32[]{:S(2)}) async-start(), calls=%async_computation.3 | async-start | bytes 2621440 | tf_op jit(solution)/shard_map/all_gather | solution.py:427
  77.2 1.6 %copy-start = (bf16[16,2,128,256]{3,2,1,0:T(8,128)(2,1)S(1)}, bf16[16,2,128,256]{3,2,1,0:T(8,128)(2,1)}, u32[]{:S(2)}) copy-start(bf16[16,2,128,256]{3,2,1,0:T(8,128)(2,1)} %all-gather.5.cloned.1.call-done) | copy-start | bytes 6291460
  80.3 34.3 %copy-start.1 = (bf16[16,2,128,256]{3,2,1,0:T(8,128)(2,1)S(1)}, bf16[16,2,128,256]{3,2,1,0:T(8,128)(2,1)}, u32[]{:S(2)}) copy-start(bf16[16,2,128,256]{3,2,1,0:T(8,128)(2,1)} %all-gather.5.cloned.1.call-done) | copy-start | bytes 6291460
Sparse Core Ops, SparseCore 0:
  30.5 46.6 all-gather.4
  79.0 35.5 all-gather.6

commit v3 on v2

--- a/solution.py
+++ b/solution.py
@@ -1,3 +1,4 @@
+import functools
 import math
 
 import jax
@@ -83,6 +84,7 @@
 
 
 def forward_kernel(
+    members,
     place_ref,
     window_ref,
     own_ref,
@@ -97,13 +99,9 @@
     w_gate_ref,
     w_up_ref,
     down_weight_ref,
-    out_ref,
-    query_buf,
-    key_buf,
-    value_buf,
-    apart_buf,
-    mixed_buf,
+    *refs,
 ):
+    out_refs, (query_buf, key_buf, value_buf, apart_buf, mixed_buf) = refs[:-5], refs[-5:]
     row_count, feat_width = own_ref.shape[1:]
     reach = left_ref.shape[1]
     head_count = window_ref.shape[0]
@@ -159,21 +157,35 @@
     gate = dot(normed_mid, w_gate_ref[...])
     hidden = (gate * (0.5 + 0.5 * jnp.tanh(0.5 * gate)) * dot(normed_mid, w_up_ref[...])).astype(BF16)
     forecast = (after.astype(F32) + dot(hidden, down_weight_ref[...])).astype(BF16)
-    shares, _, share_rows, _ = out_ref.shape
-    for share in range(shares):
-        out_ref[share, 0] = forecast[share * share_rows : (share + 1) * share_rows]
-
-
-def forward(place, head_window, own, left, right, gains, weights, shares, first, members):
+    shares, share_rows, _ = out_refs[0].shape
+    for member, out_ref in enumerate(out_refs[:members]):
+
+        @pl.when(pl.program_id(0) == member)
+        def _():
+            for share in range(shares):
+                out_ref[share] = forecast[share * share_rows : (share + 1) * share_rows]
+
+    for out_ref in out_refs[members:]:
+        for share in range(shares):
+            out_ref[share, 0] = forecast[share * share_rows : (share + 1) * share_rows]
+
+
+def forward(place, head_window, own, left, right, gains, weights, shares, first, members, joined):
     _, row_count, feat_width = own.shape
     reach = left.shape[1]
     key_count = Q_ROWS + 2 * reach
     hidden_width = weights[4].shape[1]
     macs = members * row_count * feat_width * (6 * feat_width + 3 * hidden_width + 8 * key_count)
+    share_rows = row_count // shares
+    out_shape = [jax.ShapeDtypeStruct((shares, share_rows, feat_width), BF16)] * members
+    out_specs = [pl.BlockSpec((shares, share_rows, feat_width), lambda m: (0, 0, 0))] * members
+    if joined:
+        out_shape.append(jax.ShapeDtypeStruct((shares, members, share_rows, feat_width), BF16))
+        out_specs.append(pl.BlockSpec((shares, 1, share_rows, feat_width), lambda m: (0, m, 0, 0)))
     return pl.pallas_call(
-        forward_kernel,
+        functools.partial(forward_kernel, members),
         grid=(members,),
-        out_shape=jax.ShapeDtypeStruct((shares, members, row_count // shares, feat_width), BF16),
+        out_shape=out_shape,
         in_specs=[
             smem_spec(),
             smem_spec(),
@@ -182,7 +194,7 @@
             pl.BlockSpec((1, reach, feat_width), lambda m: (first + m, 0, 0)),
         ]
         + [vmem_spec()] * (len(gains) + len(weights)),
-        out_specs=pl.BlockSpec((shares, 1, row_count // shares, feat_width), lambda m: (0, m, 0, 0)),
+        out_specs=out_specs,
         scratch_shapes=[
             pltpu.VMEM((row_count, feat_width), BF16),
             pltpu.VMEM((row_count + 2 * reach, feat_width), BF16),
@@ -196,7 +208,7 @@
     )(place, head_window, own, left, right, *gains, *weights)
 
 
-def gram_kernel(index_ref, *refs):
+def gram_kernel(gathered, index_ref, *refs):
     share_refs, grid_ref, out_ref = refs[:-2], refs[-2], refs[-1]
     rows, feat_width = grid_ref.shape[1:]
     members = sum(math.prod(ref.shape[:-2]) for ref in share_refs)
@@ -205,9 +217,12 @@
     proj = jnp.zeros((members, GROUP, feat_width), F32)
     for lower in range(0, rows, GROUP):
         part = slice(lower, lower + GROUP)
-        fields = jnp.concatenate(
-            [ref[..., part, :].reshape(-1, GROUP, feat_width).astype(F32) for ref in share_refs], axis=0
-        )
+        pieces = []
+        for member, ref in enumerate(share_refs[:gathered]):
+            for source in range(ref.shape[0] * ref.shape[1]):
+                pieces.append(piece_of(ref, member, source)[0, part, :].reshape(1, GROUP, feat_width))
+        pieces += [ref[..., part, :].reshape(-1, GROUP, feat_width) for ref in share_refs[gathered:]]
+        fields = jnp.concatenate(pieces, axis=0).astype(F32)
         mean = jnp.sum(fields, axis=0) * (1.0 / members)
         spread = fields - mean[None]
         weight = grid_ref[0, part, :]
@@ -234,17 +249,17 @@
 
 def gram_partial(index, gathered, shares, grid):
     def here(array):
-        block = (array.shape[0], 1, *array.shape[2:])
-        return pl.BlockSpec(block, lambda i, index: (0, index[0], 0, 0, 0))
+        block = (*array.shape[:2], 1, *array.shape[3:])
+        return pl.BlockSpec(block, lambda i, index: (0, 0, index[0], 0, 0))
 
     def whole(array):
         return pl.BlockSpec(array.shape, lambda i, index: (0,) * array.ndim)
 
-    members = sum(v.shape[0] * v.shape[2] for v in gathered) + sum(v.shape[0] * v.shape[1] for v in shares)
+    members = sum(v.shape[0] * v.shape[1] for v in gathered) + sum(v.shape[0] * v.shape[1] for v in shares)
     filled = members * members // LANES + 1
     out_shape = (-(-filled // 8) * 8, LANES)
     return pl.pallas_call(
-        gram_kernel,
+        functools.partial(gram_kernel, len(gathered)),
         grid_spec=pltpu.PrefetchScalarGridSpec(
             num_scalar_prefetch=1,
             grid=(1,),
@@ -321,18 +336,20 @@
     )(partials)
 
 
-def combine_kernel(index_ref, transform_ref, *refs):
+def combine_kernel(groups, index_ref, transform_ref, *refs):
     field_refs, out_ref = refs[:-1], refs[-1]
     own_members, rows, feat_width = out_ref.shape
     members = transform_ref.shape[0]
     stack, own_stack = members * GROUP, own_members * GROUP
     own = iota((own_stack, members), 0) // GROUP
-    place, first, base = jnp.zeros_like(own), 0, 0
-    for ref in field_refs:
-        part = ref.shape[2]
-        inside = (own >= first) & (own < first + part)
-        place = jnp.where(inside, base + index_ref[0] * part + own - first, place)
-        first, base = first + part, base + part * ref.shape[0]
+    sources = members // own_members
+    place = jnp.zeros_like(own)
+    base = 0
+    for group in groups:
+        first = base // sources
+        inside = (own >= first) & (own < first + group)
+        place = jnp.where(inside, base + index_ref[0] * group + own - first, place)
+        base += group * sources
     pick_own = (place == iota((own_stack, members), 1)).astype(F32).astype(BF16)
     pick = (iota((stack, members), 0) // GROUP == iota((stack, members), 1)).astype(F32).astype(BF16)
     same = iota((own_stack, stack), 0) % GROUP == iota((own_stack, stack), 1) % GROUP
@@ -341,25 +358,29 @@
         rows_of = dot(pick_own, piece, ((1,), (1,))).astype(BF16)
         mixers.append(jnp.where(same, dot(rows_of, pick, ((1,), (1,))), 0.0).astype(BF16))
     mixer = jnp.concatenate(mixers, axis=0)
-    share_rows = field_refs[0].shape[3]
+    share_rows = field_refs[0].shape[-2]
     for share in range(rows // share_rows):
         for lower in range(0, share_rows, GROUP):
-            fields = jnp.concatenate(
-                [ref[:, share, :, lower : lower + GROUP, :].reshape(-1, feat_width) for ref in field_refs], axis=0
-            )
-            mixed = dot(mixer, fields)
+            part = slice(lower, lower + GROUP)
+            pieces, first = [], 0
+            for group in groups:
+                for source in range(sources):
+                    for member in range(first, first + group):
+                        pieces.append(piece_of(field_refs[member], member, source)[share, part, :])
+                first += group
+            mixed = dot(mixer, jnp.concatenate(pieces, axis=0))
             mixed = (mixed[:own_stack] + mixed[own_stack:]).astype(BF16)
             start = share * share_rows + lower
             out_ref[:, start : start + GROUP, :] = mixed.reshape(own_members, GROUP, feat_width)
 
 
-def combine(index, transform, gathered):
-    own_members = sum(v.shape[2] for v in gathered)
-    shares, _, share_rows, feat_width = gathered[0].shape[1:]
+def combine(index, transform, gathered, groups):
+    own_members = len(gathered)
+    shares, share_rows, feat_width = gathered[0].shape[2:]
     out_shape = (own_members, shares * share_rows, feat_width)
     size = sum(v.size for v in gathered)
     return pl.pallas_call(
-        combine_kernel,
+        functools.partial(combine_kernel, groups),
         out_shape=jax.ShapeDtypeStruct(out_shape, BF16),
         in_specs=[smem_spec()] + [vmem_spec()] * (1 + len(gathered)),
         out_specs=vmem_spec(),
@@ -367,6 +388,27 @@
         cost_estimate=pl.CostEstimate(flops=4 * GROUP * own_members * size, bytes_accessed=3 * size, transcendentals=0),
         name="combine",
     )(index, transform, *gathered)
+
+
+def mem_grid(count):
+    fine = max(n for n in range(1, math.isqrt(count) + 1) if count % n == 0)
+    coarse = count // fine
+    along_fine = [[a * fine + b for b in range(fine)] for a in range(coarse)]
+    along_coarse = [[a * fine + b for a in range(coarse)] for b in range(fine)]
+    return along_fine, along_coarse
+
+
+def gathered_over_mem(fields, member):
+    ways = mem_grid(lax.axis_size("mem"))
+    for way in ways if member % 2 == 0 else ways[::-1]:
+        fields = lax.all_gather(fields, "mem", axis_index_groups=way)
+    return fields
+
+
+def piece_of(ref, member, source):
+    if member % 2 == 0:
+        return ref.at[source // ref.shape[1], source % ref.shape[1]]
+    return ref.at[source % ref.shape[0], source // ref.shape[0]]
 
 
 def local(
@@ -405,7 +447,7 @@
     index = lax.axis_index("mem").astype(jnp.int32).reshape(1)
     half = own_members // 2
 
-    def forecast_of(first, count):
+    def forecast_of(first, count, joined):
         return forward(
             place,
             head_window,
@@ -417,15 +459,16 @@
             mem_count,
             first,
             count,
+            joined,
         )
 
-    early = forecast_of(0, half)
-    early_all = lax.all_gather(early, "mem")
-    late = forecast_of(half, own_members - half)
-    late_share = lax.all_to_all(late, "mem", split_axis=0, concat_axis=0, tiled=True)
+    early = forecast_of(0, half, False)
+    early_all = [gathered_over_mem(v, m) for m, v in enumerate(early)]
+    *late, late_joined = forecast_of(half, own_members - half, True)
+    late_share = lax.all_to_all(late_joined, "mem", split_axis=0, concat_axis=0, tiled=True)
     late, late_share = lax.optimization_barrier((late, late_share))
-    late_all = lax.all_gather(late, "mem")
-    partial = gram_partial(index, [early_all], [late_share], grid)
+    late_all = [gathered_over_mem(v, half + m) for m, v in enumerate(late)]
+    partial = gram_partial(index, early_all, [late_share], grid)
     partials = lax.all_to_all(
         jnp.broadcast_to(partial[None], (device_count, *partial.shape)),
         ("mem", "tok"),
@@ -433,7 +476,8 @@
         concat_axis=0,
         tiled=True,
     )
-    return combine(index, solve(partials, members), [early_all, late_all])
+    groups = (1,) * half + (own_members - half,)
+    return combine(index, solve(partials, members), early_all + late_all, groups)
 
 
 def solution(mesh):

time: 125 us -> 159 us (1.27)
  blocking collectives: 25.9 us -> 66.2 us
  waiting for transfers between devices: 37.5 us -> 29.1 us
  local copies, waits for them, and re-layouts: 4.06 us -> 8.27 us
    all_gather x0 -> x4, blocking collectives: none -> 29.7 us  [gathered_over_mem(): fields = lax.all_gather(fields, 'mem', axis_index_groups=way)]
    all_to_all x1, blocking collectives: 12.6 us -> 25.8 us  [local(): lax.all_to_all(jnp.broadcast_to(partial[None], (device_count, *partial.sh...]
    all_gather x2 -> x4, waiting for transfers between devices: 35.8 us -> 24.2 us  [gathered_over_mem(): fields = lax.all_gather(fields, 'mem', axis_index_groups=way)]
    ppermute x1, waiting for transfers between devices: 0.01 us -> 4.48 us  [local(): right = lax.ppermute(ens_state[:, :WIN], 'tok', down)]
    unnamed x32 -> x40, local copies, waits for them, and re-layouts: 1.66 us -> 5.88 us
    all_to_all x1, blocking collectives: 13.3 us -> 10.6 us  [local(): lax.all_to_all(late_joined, 'mem', split_axis=0, concat_axis=0, tiled=True)]
  transfers between devices with their start and end apart: 4 -> 6, of which waited for: 3 -> 4; matrix products, arithmetic and copies ran while one was open for 0% -> 0% of each run, Pallas kernels for 17% -> 13%
where the time goes in v3:
time: 159 us
  blocking collectives  66.2 us (42%)
  Pallas kernels  37.9 us (24%)
  waiting for transfers between devices  29.1 us (18%)
  between operations  13.3 us (8%)
  local copies, waits for them, and re-layouts  8.27 us (5%)
  starting transfers between devices  3.83 us (2%)
    all_gather x4, blocking collectives, gathered_over_mem(): fields = lax.all_gather(fields, 'mem', axis_index_groups=way)  29.7 us
    pallas_call x2, Pallas kernels, forward(): pl.pallas_call(functools.partial(forward_kernel, members), grid=(members,...  29.2 us
    all_to_all x1, blocking collectives, local(): lax.all_to_all(jnp.broadcast_to(partial[None], (device_count, *partial.sh...  25.8 us
    all_gather x4, waiting for transfers between devices, gathered_over_mem(): fields = lax.all_gather(fields, 'mem', axis_index_groups=way)  24.2 us
    all_to_all x1, blocking collectives, local(): lax.all_to_all(late_joined, 'mem', split_axis=0, concat_axis=0, tiled=True)  10.6 us
    unnamed x40, local copies, waits for them, and re-layouts  5.88 us
    ppermute x1, waiting for transfers between devices, local(): right = lax.ppermute(ens_state[:, :WIN], 'tok', down)  4.48 us
  transfers between devices with their start and end apart: 6, of which 4 were waited for; matrix products, arithmetic and copies ran while one was open for 0% of the time, Pallas kernels for 13%

profile of v3, /device:TPU:0, one launch (start us, length us, event | category | flops | bytes accessed | tf_op | source)
XLA Modules:
  0.0 158.6 jit_solution(10458006475502531961)
XLA Ops:
  6.6 0.0 all-gather.13.cloned.1.call-start
  6.6 2.4 %fusion = (bf16[4,256,256]{2,1,0:T(8,128)(2,1)}, bf16[4,256,256]{2,1,0:T(8,128)(2,1)}) fusion(bf16[4,512,256]{2,1,0:T(8,128)(2,1)} %own_ref.3), kind=kLoop, calls=%fused_computation.1 | loop fusion | bytes 2097152 | tf_op jit(solution)/shard_map/slice | solution.py:441
  9.0 2.4 %collective-permute-start = (bf16[4,256,256]{2,1,0:T(8,128)(2,1)}, bf16[4,256,256]{2,1,0:T(8,128)(2,1)S(1)}, u32[]{:S(2)}, u32[]{:S(2)}) collective-permute-start(bf16[4,256,256]{2,1,0:T(8,128)(2,1)} %get-tuple-element.22), channel_id=1, source_target_pairs={{0,1},{1,2},{2,3},{3,4},{4,5},{5,6},{6,7},{8,9},{9,10},{10,11},{11... | collective-permute-start | bytes 1572872 | tf_op jit(solution)/shard_map/ppermute | solution.py:440
  11.4 1.3 collective-permute-start.1
  12.7 0.1 pad_add_fusion.place_ref
  12.8 0.3 collective-permute-done.left_ref
  13.1 4.5 %collective-permute-done.1.right_ref = bf16[4,256,256]{2,1,0:T(8,128)(2,1)S(1)} collective-permute-done((bf16[4,256,256]{2,1,0:T(8,128)(2,1)}, bf16[4,256,256]{2,1,0:T(8,128)(2,1)S(1)}, u32[]{:S(2)}, u32[]{:S(2)}) %collective-permute-start.1) | collective-permute-done | bytes 524320 | tf_op jit(solution)/shard_map/ppermute | solution.py:441
  17.6 0.6 copy-done.17
  18.2 14.5 %forward.2 = (bf16[4,128,256]{2,1,0:T(8,128)(2,1)S(1)}, bf16[4,128,256]{2,1,0:T(8,128)(2,1)S(1)}) custom-call(s32[2]{0:T(128)S(1)} %pad_add_fusion.place_ref, s32[4]{0:T(128)S(1)} %copy-done.19, bf16[4,512,256]{2,1,0:T(8,128)(2,1)} %own_ref.3, bf16[4,256,256]{2,1,0:T(8,128)(2,1)S(1)} %collective-permute-done.left_ref, ...), custom_call_target="tpu_custom_call" | custom-call | flops 5100273664 | bytes 1572864 | tf_op jit(solution)/shard_map/forward/pallas_call | solution.py:185
  32.7 7.2 %all-gather = bf16[8,128,256]{2,1,0:T(8,128)(2,1)} all-gather(bf16[4,128,256]{2,1,0:T(8,128)(2,1)S(1)} %get-tuple-element.13), channel_id=2, replica_groups={{0,8},{16,24},{1,9},{17,25},{2,10},{18,26},{3,11},{19,27},{4,12},{20,28..., dimensions={0}, use_global_device_ids=true | all-gather | bytes 786432 | tf_op jit(solution)/shard_map/all_gather | solution.py:404
  39.9 0.0 all-gather.13.cloned.1.call-update
  39.9 0.0 all-gather.15.cloned.1.call-start
  40.0 7.2 %all-gather.2 = bf16[8,128,256]{2,1,0:T(8,128)(2,1)} all-gather(bf16[4,128,256]{2,1,0:T(8,128)(2,1)S(1)} %get-tuple-element.14), channel_id=4, replica_groups={{0,16},{8,24},{1,17},{9,25},{2,18},{10,26},{3,19},{11,27},{4,20},{12,28..., dimensions={0}, use_global_device_ids=true | all-gather | bytes 786432 | tf_op jit(solution)/shard_map/all_gather | solution.py:404
  47.2 0.0 all-gather.17.cloned.1.call-start
  47.2 0.8 copy-done.12
  48.0 14.7 %forward.3 = (bf16[4,128,256]{2,1,0:T(8,128)(2,1)S(1)}, bf16[4,128,256]{2,1,0:T(8,128)(2,1)S(1)}, bf16[4,2,128,256]{3,2,1,0:T(8,128)(2,1)S(1)}) custom-call(s32[2]{0:T(128)S(1)} %pad_add_fusion.place_ref, s32[4]{0:T(128)S(1)} %copy-done.19, bf16[4,512,256]{2,1,0:T(8,128)(2,1)} %own_ref.3, bf16[4,256,256]{2,1,0:T(8,128)(2,1)S(1)} %collective-permute-done.left_ref, ...), custom_call_target="tpu_custom_call" | custom-call | flops 5100273664 | bytes 1572864 | tf_op jit(solution)/shard_map/forward/pallas_call | solution.py:185
  62.8 10.6 %all_to_all.10.refs_2_ = bf16[4,2,128,256]{3,2,1,0:T(8,128)(2,1)S(1)} all-to-all(bf16[4,2,128,256]{3,2,1,0:T(8,128)(2,1)S(1)} %get-tuple-element.17), channel_id=1, replica_groups=mesh['mem'=4,'tok'=8] {'mem'}, dimensions={0} | all-to-all | bytes 1048576 | tf_op jit(solution)/shard_map/all_to_all | solution.py:468
  73.4 7.1 %all-gather.4 = bf16[8,128,256]{2,1,0:T(8,128)(2,1)} all-gather(bf16[4,128,256]{2,1,0:T(8,128)(2,1)S(1)} %get-tuple-element.19), channel_id=6, replica_groups={{0,8},{16,24},{1,9},{17,25},{2,10},{18,26},{3,11},{19,27},{4,12},{20,28..., dimensions={0}, use_global_device_ids=true | all-gather | bytes 786432 | tf_op jit(solution)/shard_map/all_gather | solution.py:404
  80.6 0.0 all-gather.19.cloned.1.call-start
  80.7 8.2 %all-gather.6 = bf16[8,128,256]{2,1,0:T(8,128)(2,1)} all-gather(bf16[4,128,256]{2,1,0:T(8,128)(2,1)S(1)} %get-tuple-element.20), channel_id=8, replica_groups={{0,16},{8,24},{1,17},{9,25},{2,18},{10,26},{3,19},{11,27},{4,20},{12,28..., dimensions={0}, use_global_device_ids=true | all-gather | bytes 786432 | tf_op jit(solution)/shard_map/all_gather | solution.py:404
  88.9 0.7 copy-done.14
  89.7 1.3 sample_grid.1.refs_3_
  91.0 0.0 all-gather.13.cloned.1.call-done
  91.0 4.0 %all-gather.15.cloned.1.call-done = bf16[4,4,128,256]{3,2,1,0:T(8,128)(2,1)} async-done(((bf16[2,4,128,256]{3,2,1,0:T(8,128)(2,1)}), bf16[4,4,128,256]{3,2,1,0:T(8,128)(2,1)}) %all-gather.15.cloned.1.call-update) | async-done | bytes 1048592 | tf_op jit(solution)/shard_map/all_gather | solution.py:404
  95.0 1.2 copy-done
  96.3 1.2 copy-done.2
  97.5 1.5 gram.1
  99.1 25.8 %all_to_all.11.partial_ref = f32[32,8,128]{2,1,0:T(8,128)S(1)} all-to-all(f32[32,8,128]{2,1,0:T(8,128)S(1)} %broadcast_in_dim.2), channel_id=1, replica_groups=mesh['mem'=4,'tok'=8] {'mem','tok'}, dimensions={0} | all-to-all | bytes 262144 | tf_op jit(solution)/shard_map/all_to_all | solution.py:472
  124.9 2.7 %solve.1.transform_ref = f32[16,16]{1,0:T(8,128)S(1)} custom-call(f32[32,8,128]{2,1,0:T(8,128)S(1)} %all_to_all.11.partial_ref), custom_call_target="tpu_custom_call" | custom-call | flops 1000000000 | bytes 131072 | tf_op jit(solution)/shard_map/solve/pallas_call | solution.py:328
  127.6 20.1 %all-gather.19.cloned.1.call-done = bf16[4,4,128,256]{3,2,1,0:T(8,128)(2,1)} async-done(((bf16[2,4,128,256]{3,2,1,0:T(8,128)(2,1)}), bf16[4,4,128,256]{3,2,1,0:T(8,128)(2,1)}) %all-gather.19.cloned.1.call-update) | async-done | bytes 1048592 | tf_op jit(solution)/shard_map/all_gather | solution.py:404
  147.7 1.2 copy-done.4
  149.0 3.1 %combine.1 = bf16[4,512,256]{2,1,0:T(8,128)(2,1)} custom-call(s32[1]{0:T(128)} %bitcast.index_ref, f32[16,16]{1,0:T(8,128)S(1)} %solve.1.transform_ref, bf16[2,2,4,128,256]{4,3,2,1,0:T(8,128)(2,1)S(1)} %bitcast.18, bf16[2,2,4,128,256]{4,3,2,1,0:T(8,128)(2,1)S(1)} %bitcast.20, bf16[2,2,4,128,256]{4,3,2,1,0:T(8,128)(2,1)S(1)} %bitcast.21, ...), custom_call_target="tpu_custom_call" | custom-call | flops 536870912 | bytes 6291456 | tf_op jit(solution)/shard_map/combine/pallas_call | solution.py:382
  (39 shorter events, 0.2 us)
Async XLA Ops:
  6.5 11.0 %copy-start.8 = (bf16[256,256]{1,0:T(8,128)(2,1)S(1)}, bf16[256,256]{1,0:T(8,128)(2,1)}, u32[]{:S(2)}) copy-start(bf16[256,256]{1,0:T(8,128)(2,1)} %w_query_ref.3) | copy-start | bytes 393220
  6.5 11.0 %copy-start.9 = (bf16[256,256]{1,0:T(8,128)(2,1)S(1)}, bf16[256,256]{1,0:T(8,128)(2,1)}, u32[]{:S(2)}) copy-start(bf16[256,256]{1,0:T(8,128)(2,1)} %w_key_ref.3) | copy-start | bytes 393220
  6.5 11.0 %copy-start.10 = (bf16[256,256]{1,0:T(8,128)(2,1)S(1)}, bf16[256,256]{1,0:T(8,128)(2,1)}, u32[]{:S(2)}) copy-start(bf16[256,256]{1,0:T(8,128)(2,1)} %w_value_ref.3) | copy-start | bytes 393220
  6.5 11.1 %copy-start.11 = (bf16[256,256]{1,0:T(8,128)(2,1)S(1)}, bf16[256,256]{1,0:T(8,128)(2,1)}, u32[]{:S(2)}) copy-start(bf16[256,256]{1,0:T(8,128)(2,1)} %w_out_ref.3) | copy-start | bytes 393220
  6.5 11.1 %copy-start.5 = (bf16[256,1024]{1,0:T(8,128)(2,1)S(1)}, bf16[256,1024]{1,0:T(8,128)(2,1)}, u32[]{:S(2)}) copy-start(bf16[256,1024]{1,0:T(8,128)(2,1)} %w_gate_ref.3) | copy-start | bytes 1572868
  6.5 11.1 %copy-start.6 = (bf16[256,1024]{1,0:T(8,128)(2,1)S(1)}, bf16[256,1024]{1,0:T(8,128)(2,1)}, u32[]{:S(2)}) copy-start(bf16[256,1024]{1,0:T(8,128)(2,1)} %w_up_ref.3) | copy-start | bytes 1572868
  6.6 11.1 %copy-start.7 = (bf16[1024,256]{1,0:T(8,128)(2,1)S(1)}, bf16[1024,256]{1,0:T(8,128)(2,1)}, u32[]{:S(2)}) copy-start(bf16[1024,256]{1,0:T(8,128)(2,1)} %down_weight_ref.3) | copy-start | bytes 1572868
  6.6 84.4 %all-gather.13.cloned.1.call-start = ((), (), s32[]{:S(2)}) async-start(), calls=%async_computation.2 | async-start | bytes 1572864 | tf_op jit(solution)/shard_map/all_gather | solution.py:404
  6.6 11.0 %copy-start.18 = (f32[256]{0:T(256)S(1)}, f32[256]{0:T(256)}, u32[]{:S(2)}) copy-start(f32[256]{0:T(256)} %param.17) | copy-start | bytes 3076
  9.0 4.1 %collective-permute-start = (bf16[4,256,256]{2,1,0:T(8,128)(2,1)}, bf16[4,256,256]{2,1,0:T(8,128)(2,1)S(1)}, u32[]{:S(2)}, u32[]{:S(2)}) collective-permute-start(bf16[4,256,256]{2,1,0:T(8,128)(2,1)} %get-tuple-element.22), channel_id=1, source_target_pairs={{0,1},{1,2},{2,3},{3,4},{4,5},{5,6},{6,7},{8,9},{9,10},{10,11},{11... | collective-permute-start | bytes 1572872 | tf_op jit(solution)/shard_map/ppermute | solution.py:440
  11.4 6.2 %collective-permute-start.1 = (bf16[4,256,256]{2,1,0:T(8,128)(2,1)}, bf16[4,256,256]{2,1,0:T(8,128)(2,1)S(1)}, u32[]{:S(2)}, u32[]{:S(2)}) collective-permute-start(bf16[4,256,256]{2,1,0:T(8,128)(2,1)} %get-tuple-element.21), channel_id=1, source_target_pairs={{1,0},{2,1},{3,2},{4,3},{5,4},{6,5},{7,6},{9,8},{10,9},{11,10},{12... | collective-permute-start | bytes 1572872 | tf_op jit(solution)/shard_map/ppermute | solution.py:441
  17.6 0.7 copy-start.17
  17.6 0.7 copy-start.19
  39.9 55.1 %all-gather.15.cloned.1.call-start = ((), (), s32[]{:S(2)}) async-start(), calls=%async_computation.3 | async-start | bytes 1572864 | tf_op jit(solution)/shard_map/all_gather | solution.py:404
  47.1 0.9 copy-start.12
  47.2 80.4 %all-gather.17.cloned.1.call-start = ((), (), s32[]{:S(2)}) async-start(), calls=%async_computation.4 | async-start | bytes 1572864 | tf_op jit(solution)/shard_map/all_gather | solution.py:404
  80.6 67.1 %all-gather.19.cloned.1.call-start = ((), (), s32[]{:S(2)}) async-start(), calls=%async_computation.5 | async-start | bytes 1572864 | tf_op jit(solution)/shard_map/all_gather | solution.py:404
  88.9 0.7 copy-start.14
  88.9 0.7 copy-start.15
  88.9 0.7 copy-start.16
  88.9 0.7 copy-start.13
  95.0 1.2 copy-start
  96.3 1.2 copy-start.2
  124.9 22.8 %copy-start.1 = (bf16[4,4,128,256]{3,2,1,0:T(8,128)(2,1)S(1)}, bf16[4,4,128,256]{3,2,1,0:T(8,128)(2,1)}, u32[]{:S(2)}) copy-start(bf16[4,4,128,256]{3,2,1,0:T(8,128)(2,1)} %all-gather.13.cloned.1.call-done) | copy-start | bytes 3145732
  124.9 22.8 %copy-start.3 = (bf16[4,4,128,256]{3,2,1,0:T(8,128)(2,1)S(1)}, bf16[4,4,128,256]{3,2,1,0:T(8,128)(2,1)}, u32[]{:S(2)}) copy-start(bf16[4,4,128,256]{3,2,1,0:T(8,128)(2,1)} %all-gather.15.cloned.1.call-done) | copy-start | bytes 3145732
  147.7 1.2 copy-start.4
Sparse Core Ops, SparseCore 0:
  40.0 29.2 all-gather.12
  70.9 24.1 all-gather.14
  96.6 28.0 all-gather.16
  126.1 21.6 all-gather.18

commit v4 on v1

v4 whole, which is shorter than its diff:
```python
import functools
import math

import jax
import jax.numpy as jnp
from jax import lax
from jax.experimental import pallas as pl
from jax.experimental.pallas import tpu as pltpu
from jax.sharding import PartitionSpec as P

WIN = 256
NS_STEPS = 8
EPS = 1e-05
Q_ROWS = 128
GROUP = 16
LANES = 128
VMEM_LIMIT = 50 * 1024 * 1024

F32 = jnp.float32
BF16 = jnp.bfloat16


def dot(a, b, contract=((1,), (0,)), precision=None):
    return lax.dot_general(a, b, (contract, ((), ())), precision=precision, preferred_element_type=F32)


def exact_dot(a, b, contract=((1,), (0,))):
    return dot(a, b, contract, lax.Precision.HIGHEST)


def iota(shape, axis):
    return lax.broadcasted_iota(jnp.int32, shape, axis)


def halves(values):
    high = values.astype(BF16)
    return high, (values - high.astype(F32)).astype(BF16)


def rms_scaled(values, gain):
    return values * lax.rsqrt(jnp.mean(values * values, axis=-1, keepdims=True) + EPS) * gain


def vmem_spec():
    return pl.BlockSpec(memory_space=pltpu.VMEM)


def smem_spec():
    return pl.BlockSpec(memory_space=pltpu.SMEM)


def edges_kernel(own_ref, head_ref, tail_ref, sems):
    members, reach, _ = head_ref.shape
    rows = own_ref.shape[1]
    copies = []
    for member in range(members):
        for which, (lower, out_ref) in enumerate(((rows - reach, tail_ref), (0, head_ref))):
            copies.append(
                pltpu.make_async_copy(
                    own_ref.at[member, pl.ds(lower, reach)], out_ref.at[member], sems.at[which, member]
                )
            )
    for copy in copies:
        copy.start()
    for copy in copies:
        copy.wait()


def edges(own, reach):
    members, _, feat_width = own.shape
    return pl.pallas_call(
        edges_kernel,
        out_shape=[jax.ShapeDtypeStruct((members, reach, feat_width), own.dtype)] * 2,
        in_specs=[pl.BlockSpec(memory_space=pl.ANY)],
        out_specs=[pl.BlockSpec(memory_space=pl.ANY)] * 2,
        scratch_shapes=[pltpu.SemaphoreType.DMA((2, members))],
        cost_estimate=pl.CostEstimate(flops=0, bytes_accessed=8 * members * reach * feat_width, transcendentals=0),
        name="edges",
    )(own)


def sample_grid_kernel(stride, start_ref, token_ref, channel_ref, value_ref, var_ref, out_ref):
    rows, feat_width = out_ref.shape[1:]
    share_rows = rows // 2
    count = token_ref.shape[1]
    chunk = min(1024, count)
    total = jnp.zeros((4 * rows, feat_width), F32)
    for lower in range(0, count, chunk):
        part = slice(lower, lower + chunk)
        inv_var = 1.0 / var_ref[:, part]
        weighted = value_ref[:, part] * inv_var
        row = iota((rows, chunk), 0)
        row = jnp.where(row < share_rows, row, row + (stride - share_rows))
        here = row == token_ref[:, part] - start_ref[0]
        pieces = []
        for values in (inv_var, weighted):
            high = values.astype(BF16).astype(F32)
            pieces.append(jnp.where(here, high, 0.0).astype(BF16))
            pieces.append(jnp.where(here, values - high, 0.0).astype(BF16))
        channel_hot = jnp.where(iota((feat_width, chunk), 0) == channel_ref[:, part], 1.0, 0.0).astype(BF16)
        total += dot(jnp.concatenate(pieces, axis=0), channel_hot, ((1,), (1,)))
    out_ref[0] = total[:rows] + total[rows : 2 * rows]
    out_ref[1] = total[2 * rows : 3 * rows] + total[3 * rows :]


def sample_grid(start, obs_token, obs_channel, obs_value, obs_var, share_rows, stride, feat_width):
    count = obs_token.shape[0]
    rows = 2 * share_rows
    return pl.pallas_call(
        functools.partial(sample_grid_kernel, stride),
        out_shape=jax.ShapeDtypeStruct((2, rows, feat_width), F32),
        in_specs=[smem_spec()] + [vmem_spec()] * 4,
        out_specs=vmem_spec(),
        compiler_params=pltpu.CompilerParams(vmem_limit_bytes=VMEM_LIMIT),
        cost_estimate=pl.CostEstimate(flops=8 * rows * count * feat_width, bytes_accessed=16 * count, transcendentals=0),
        name="sample_grid",
    )(start, *(v.reshape(1, count) for v in (obs_token, obs_channel, obs_value, obs_var)))


def project_kernel(
    heads, own_ref, gain_ref, w_query_ref, w_key_ref, w_value_ref, query_ref, key_ref, value_ref, turned_ref
):
    @pl.when(pl.program_id(0) == 0)
    def _():
        turned_ref[...] = w_value_ref[...].astype(F32).T.astype(BF16)

    scale = math.log2(math.e) / math.sqrt(own_ref.shape[2] // heads)
    normed = rms_scaled(own_ref[0].astype(F32), gain_ref[...]).astype(BF16)
    query_ref[0] = (dot(normed, w_query_ref[...]) * scale).astype(BF16)
    key_ref[0] = dot(normed, w_key_ref[...]).astype(BF16)
    value_ref[0] = dot(turned_ref[...], normed, ((1,), (1,))).astype(BF16)


def project(own, heads, gain, w_query, w_key, w_value):
    members, rows, feat_width = own.shape
    block = pl.BlockSpec((1, rows, feat_width), lambda m: (m, 0, 0))
    return pl.pallas_call(
        functools.partial(project_kernel, heads),
        grid=(members,),
        out_shape=[
            jax.ShapeDtypeStruct((members, rows, feat_width), BF16),
            jax.ShapeDtypeStruct((members, rows, feat_width), BF16),
            jax.ShapeDtypeStruct((members, feat_width, rows), BF16),
        ],
        in_specs=[block] + [vmem_spec()] * 4,
        out_specs=[block, block, pl.BlockSpec((1, feat_width, rows), lambda m: (m, 0, 0))],
        scratch_shapes=[pltpu.VMEM((feat_width, feat_width), BF16)],
        compiler_params=pltpu.CompilerParams(vmem_limit_bytes=VMEM_LIMIT),
        cost_estimate=pl.CostEstimate(
            flops=6 * own.size * feat_width, bytes_accessed=8 * own.size, transcendentals=0
        ),
        name="project",
    )(own, gain, w_query, w_key, w_value)


def forward_kernel(
    halo_first,
    place_ref,
    window_ref,
    state_ref,
    query_ref,
    key_ref,
    value_ref,
    halo_ref,
    attn_gain_ref,
    ffn_gain_ref,
    w_key_ref,
    w_value_ref,
    w_out_ref,
    w_gate_ref,
    w_up_ref,
    down_weight_ref,
    out_ref,
    key_buf,
    value_buf,
    turned_buf,
    bias_buf,
    mixed_buf,
):
    rows, feat_width = state_ref.shape[1:]
    reach = halo_ref.shape[1]
    own_rows = key_ref.shape[1]
    head_count = window_ref.shape[0]
    head_size = feat_width // head_count
    blocks = rows // Q_ROWS
    key_count = Q_ROWS + 2 * reach

    @pl.when(pl.program_id(0) == 0)
    def _():
        turned_buf[...] = w_value_ref[...].astype(F32).T.astype(BF16)
        value_buf[feat_width:, :] = jnp.ones((value_buf.shape[0] - feat_width, value_buf.shape[1]), BF16)
        apart = jnp.abs(iota((key_count, Q_ROWS), 0) - reach - iota((key_count, Q_ROWS), 1))
        for block in range(blocks):
            k_pos = place_ref[0] + block * Q_ROWS + iota((key_count, Q_ROWS), 0)
            inside = (k_pos >= 0) & (k_pos < place_ref[1])
            for head in range(head_count):
                bias_buf[block, head] = jnp.where(inside & (apart <= window_ref[head]), 0.0, -1e30)

    own_at, halo_at = (reach, 0) if halo_first else (0, own_rows)
    normed = rms_scaled(halo_ref[0].astype(F32), attn_gain_ref[...]).astype(BF16)
    key_buf[own_at : own_at + own_rows] = key_ref[0]
    value_buf[:feat_width, own_at : own_at + own_rows] = value_ref[0]
    key_buf[halo_at : halo_at + reach] = dot(normed, w_key_ref[...]).astype(BF16)
    value_buf[:feat_width, halo_at : halo_at + reach] = dot(turned_buf[...], normed, ((1,), (1,))).astype(BF16)

    column_head = iota((1, feat_width), 1) // head_size
    for block in range(blocks):
        start = block * Q_ROWS
        queries = query_ref[0, start : start + Q_ROWS, :]
        stacked = jnp.concatenate(
            [queries * (column_head == head).astype(F32).astype(BF16) for head in range(head_count)], axis=0
        )
        scores = dot(key_buf[start : start + key_count, :], stacked, ((1,), (1,)))
        weights = []
        for head in range(head_count):
            score_matrix = scores[:, head * Q_ROWS : (head + 1) * Q_ROWS] + bias_buf[block, head]
            row_top = jnp.max(score_matrix, axis=0, keepdims=True)
            weights.append(jnp.exp2((score_matrix - row_top).astype(BF16)))
        mixed_all = dot(value_buf[:, start : start + key_count], jnp.concatenate(weights, axis=1))
        mixed = []
        for head in range(head_count):
            columns = slice(head * Q_ROWS, (head + 1) * Q_ROWS)
            total = mixed_all[feat_width : feat_width + 1, columns]
            mixed.append(mixed_all[head * head_size : (head + 1) * head_size, columns] * (1.0 / total))
        mixed_buf[start : start + Q_ROWS, :] = jnp.concatenate(mixed, axis=0).T.astype(BF16)

    after = (state_ref[0].astype(F32) + dot(mixed_buf[...], w_out_ref[...])).astype(BF16)
    normed_mid = rms_scaled(after.astype(F32), ffn_gain_ref[...]).astype(BF16)
    gate = dot(normed_mid, w_gate_ref[...])
    hidden = (gate * (0.5 + 0.5 * jnp.tanh(0.5 * gate)) * dot(normed_mid, w_up_ref[...])).astype(BF16)
    forecast = (after.astype(F32) + dot(hidden, down_weight_ref[...])).astype(BF16)
    targets, _, out_rows, _ = out_ref.shape
    for target in range(targets):
        lower = target * out_rows if targets * out_rows == rows else 0
        out_ref[target, 0] = forecast[lower : lower + out_rows]


def forward(place, head_window, own, projected, halo, gains, weights, half, targets, out_rows):
    members, row_count, feat_width = own.shape
    rows, reach = row_count // 2, halo.shape[1]
    key_count = Q_ROWS + 2 * reach
    hidden_width = weights[3].shape[1]
    macs = members * rows * feat_width * (2 * feat_width + 3 * hidden_width + 8 * key_count)
    here = pl.BlockSpec((1, rows, feat_width), lambda m: (m, half, 0))
    ones_rows = 16
    return pl.pallas_call(
        functools.partial(forward_kernel, half == 0),
        grid=(members,),
        out_shape=jax.ShapeDtypeStruct((targets, members, out_rows, feat_width), BF16),
        in_specs=[
            smem_spec(),
            smem_spec(),
            here,
            here,
            pl.BlockSpec((1, row_count, feat_width), lambda m: (m, 0, 0)),
            pl.BlockSpec((1, feat_width, row_count), lambda m: (m, 0, 0)),
            pl.BlockSpec((1, reach, feat_width), lambda m: (m, 0, 0)),
        ]
        + [vmem_spec()] * (len(gains) + len(weights)),
        out_specs=pl.BlockSpec((targets, 1, out_rows, feat_width), lambda m: (0, m, 0, 0)),
        scratch_shapes=[
            pltpu.VMEM((row_count + reach, feat_width), BF16),
            pltpu.VMEM((feat_width + ones_rows, row_count + reach), BF16),
            pltpu.VMEM((feat_width, feat_width), BF16),
            pltpu.VMEM((rows // Q_ROWS, head_window.shape[0], key_count, Q_ROWS), F32),
            pltpu.VMEM((rows, feat_width), BF16),
        ],
        compiler_params=pltpu.CompilerParams(vmem_limit_bytes=VMEM_LIMIT),
        cost_estimate=pl.CostEstimate(flops=2 * macs, bytes_accessed=6 * own.size, transcendentals=0),
        name="forward",
    )(place, head_window, own, *projected, halo, *gains, *weights)


def gram_kernel(index_ref, early_ref, late_ref, grid_ref, out_ref):
    share_rows, feat_width = late_ref.shape[2:]
    members = late_ref.shape[0] * late_ref.shape[1]
    stack = members * GROUP
    total = jnp.zeros((stack, stack), F32)
    proj = jnp.zeros((members, GROUP, feat_width), F32)
    for half, ref in enumerate((early_ref, late_ref)):
        for lower in range(0, share_rows, GROUP):
            fields = ref[:, :, lower : lower + GROUP, :].reshape(members, GROUP, feat_width).astype(F32)
            mean = jnp.sum(fields, axis=0) * (1.0 / members)
            spread = fields - mean[None]
            part = slice(half * share_rows + lower, half * share_rows + lower + GROUP)
            weight = grid_ref[0, part, :]
            proj += spread * (grid_ref[1, part, :] - weight * mean)[None]
            high, low = halves(spread.reshape(stack, feat_width))
            w_high, w_low = halves((spread * weight[None]).reshape(stack, feat_width))
            last = ((1,), (1,))
            total += dot(w_high, high, last) + dot(w_high, low, last) + dot(w_low, high, last)
    same = iota((stack, stack), 0) % GROUP == iota((stack, stack), 1) % GROUP
    by_row = jnp.sum(jnp.where(same, total, 0.0).reshape(members, GROUP, stack), axis=1)
    folded = (iota((stack, LANES), 0) // GROUP == iota((stack, LANES), 1) % members).astype(F32)
    tiled = exact_dot(by_row, folded)
    per_row = LANES // members
    keep = iota((members, LANES), 0) % per_row == iota((members, LANES), 1) // members
    packed = jnp.sum(jnp.where(keep, tiled, 0.0).reshape(members // per_row, per_row, LANES), axis=1)
    proj_col = jnp.sum(jnp.sum(proj, axis=1), axis=1, keepdims=True)
    proj_row = jnp.sum(
        jnp.where(iota((members, LANES), 0) == iota((members, LANES), 1), proj_col, 0.0), axis=0, keepdims=True
    )
    filled = members // per_row + 1
    blank = jnp.zeros((out_ref.shape[0] - filled, LANES), F32)
    out_ref[...] = jnp.concatenate([packed, proj_row, blank], axis=0)


def gram_partial(index, early_all, late_share, grid):
    members = late_share.shape[0] * late_share.shape[1]
    filled = members * members // LANES + 1
    out_shape = (-(-filled // 8) * 8, LANES)
    return pl.pallas_call(
        gram_kernel,
        grid_spec=pltpu.PrefetchScalarGridSpec(
            num_scalar_prefetch=1,
            grid=(1,),
            in_specs=[
                pl.BlockSpec(late_share.shape, lambda i, index: (0, 0, index[0], 0)),
                pl.BlockSpec(late_share.shape, lambda i, index: (0, 0, 0, 0)),
                pl.BlockSpec(grid.shape, lambda i, index: (0, 0, 0)),
            ],
            out_specs=pl.BlockSpec(out_shape, lambda i, index: (0, 0)),
        ),
        out_shape=jax.ShapeDtypeStruct(out_shape, F32),
        compiler_params=pltpu.CompilerParams(vmem_limit_bytes=VMEM_LIMIT),
        cost_estimate=pl.CostEstimate(
            flops=3 * GROUP * members * members * grid.size, bytes_accessed=members * grid.size, transcendentals=0
        ),
        name="gram",
    )(index, early_all, late_share, grid)


def ensemble_transform(gram, proj):
    members = gram.shape[0]
    row, column = iota((members, members), 0), iota((members, members), 1)
    identity = (row == column).astype(F32)
    system = gram + (members - 1.0) * identity
    left, right = system, proj
    for pivot in range(members):
        is_pivot = iota((members, 1), 0) == pivot
        scale = 1.0 / left[pivot : pivot + 1, pivot : pivot + 1]
        pivot_row = left[pivot : pivot + 1, :] * scale
        pivot_right = right[pivot : pivot + 1, :] * scale
        factor = left[:, pivot : pivot + 1]
        left = jnp.where(is_pivot, pivot_row, left - factor * pivot_row)
        right = jnp.where(is_pivot, pivot_right, right - factor * pivot_right)
    mean_weights = right
    mean_level = jnp.sum(jnp.sum(system * identity, axis=1, keepdims=True), axis=0, keepdims=True) / members
    lifted = system + (mean_level - (members - 1.0)) * (1.0 / members)
    frobenius = jnp.sqrt(jnp.sum(jnp.sum(lifted * lifted, axis=1, keepdims=True), axis=0, keepdims=True))
    root_iter = lifted / frobenius
    inv_iter = identity
    for sweep in range(NS_STEPS):
        product = root_iter if sweep == 0 else exact_dot(inv_iter, root_iter)
        correction = 1.5 * identity - 0.5 * product
        inv_iter = correction if sweep == 0 else exact_dot(correction, inv_iter)
        if sweep < NS_STEPS - 1:
            root_iter = exact_dot(root_iter, correction)
    inv_root = inv_iter / jnp.sqrt(frobenius) + (1.0 / math.sqrt(members - 1.0) - 1.0 / jnp.sqrt(mean_level)) * (
        1.0 / members
    )
    moved = mean_weights + math.sqrt(members - 1.0) * inv_root
    return 1.0 / members + moved - jnp.sum(moved, axis=0, keepdims=True) * (1.0 / members)


def mixers(transform, first, count):
    members = transform.shape[0]
    shape = (count * GROUP, members * GROUP)
    pick_out = (iota((shape[0], members), 0) // GROUP + first == iota((shape[0], members), 1)).astype(F32).astype(BF16)
    pick_in = (iota((shape[1], members), 0) // GROUP == iota((shape[1], members), 1)).astype(F32).astype(BF16)
    same = iota(shape, 0) % GROUP == iota(shape, 1) % GROUP
    pieces = []
    for piece in halves(transform):
        rows_of = dot(pick_out, piece, ((1,), (1,))).astype(BF16)
        pieces.append(jnp.where(same, dot(rows_of, pick_in, ((1,), (1,))), 0.0).astype(BF16))
    return jnp.concatenate(pieces, axis=0)


def mix(mixer, fields):
    mixed = dot(mixer, fields)
    count = mixed.shape[0] // 2
    return (mixed[:count] + mixed[count:]).astype(BF16)


def solve_kernel(partial_ref, share_ref, transform_ref, out_ref):
    members = transform_ref.shape[0]
    share_rows, feat_width = share_ref.shape[2:]
    per_row = LANES // members
    sums = jnp.sum(partial_ref[...], axis=0)
    spread_rows = jnp.concatenate(
        [jnp.broadcast_to(sums[r : r + 1], (per_row, LANES)) for r in range(members // per_row)], axis=0
    )
    keep = iota((members, LANES), 0) % per_row == iota((members, LANES), 1) // members
    folded = (iota((LANES, members), 0) % members == iota((LANES, members), 1)).astype(F32)
    gram = exact_dot(jnp.where(keep, spread_rows, 0.0), folded)
    proj_row = jnp.broadcast_to(sums[members // per_row : members // per_row + 1], (members, LANES))
    on_diagonal = iota((members, LANES), 0) == iota((members, LANES), 1)
    proj = jnp.sum(jnp.where(on_diagonal, proj_row, 0.0), axis=1, keepdims=True)
    transform = ensemble_transform(gram, proj)
    transform_ref[...] = transform
    mixer = mixers(transform, 0, members)
    for lower in range(0, share_rows, GROUP):
        fields = share_ref[:, :, lower : lower + GROUP, :].reshape(members * GROUP, feat_width)
        out_ref[:, :, lower : lower + GROUP, :] = mix(mixer, fields).reshape(*share_ref.shape[:2], GROUP, feat_width)


def solve(partials, share):
    members = share.shape[0] * share.shape[1]
    return pl.pallas_call(
        solve_kernel,
        out_shape=[jax.ShapeDtypeStruct((members, members), F32), jax.ShapeDtypeStruct(share.shape, BF16)],
        in_specs=[vmem_spec()] * 2,
        out_specs=[vmem_spec()] * 2,
        compiler_params=pltpu.CompilerParams(vmem_limit_bytes=VMEM_LIMIT),
        cost_estimate=pl.CostEstimate(flops=10**9, bytes_accessed=partials.size * 4, transcendentals=0),
        name="solve",
    )(partials, share)


def combine_kernel(index_ref, transform_ref, fields_ref, out_ref, mixer_buf):
    sources, own_members, rows, feat_width = fields_ref.shape

    @pl.when(pl.program_id(0) == 0)
    def _():
        mixer_buf[...] = mixers(transform_ref[...], index_ref[0] * own_members, own_members)

    mixer = mixer_buf[...]
    for lower in range(0, rows, GROUP):
        fields = fields_ref[:, :, lower : lower + GROUP, :].reshape(sources * own_members * GROUP, feat_width)
        out_ref[:, lower : lower + GROUP, :] = mix(mixer, fields).reshape(own_members, GROUP, feat_width)


def combine(index, transform, fields):
    sources, own_members, rows, feat_width = fields.shape
    block = min(64, rows)
    return pl.pallas_call(
        combine_kernel,
        grid=(rows // block,),
        out_shape=jax.ShapeDtypeStruct((own_members, 2 * rows, feat_width), BF16),
        in_specs=[
            smem_spec(),
            vmem_spec(),
            pl.BlockSpec((sources, own_members, block, feat_width), lambda i: (0, 0, i, 0)),
        ],
        out_specs=pl.BlockSpec((own_members, block, feat_width), lambda i: (0, i, 0)),
        scratch_shapes=[pltpu.VMEM((2 * own_members * GROUP, transform.shape[0] * GROUP), BF16)],
        compiler_params=pltpu.CompilerParams(vmem_limit_bytes=VMEM_LIMIT),
        cost_estimate=pl.CostEstimate(
            flops=4 * GROUP * own_members * fields.size, bytes_accessed=3 * fields.size, transcendentals=0
        ),
        name="combine",
    )(index, transform, fields)


def local(
    ens_state,
    attn_gain,
    ffn_gain,
    w_query,
    w_key,
    w_value,
    w_out,
    w_gate,
    w_up,
    down_weight,
    head_window,
    obs_token,
    obs_channel,
    obs_value,
    obs_var,
):
    own_members, row_count, feat_width = ens_state.shape
    mem_count = lax.axis_size("mem")
    tok_count = lax.axis_size("tok")
    device_count = mem_count * tok_count
    half_rows = row_count // 2
    share_rows = half_rows // mem_count
    first_pos = lax.axis_index("tok") * row_count
    index = lax.axis_index("mem").astype(jnp.int32).reshape(1)
    head, tail = edges(ens_state, WIN)
    left = lax.ppermute(tail, "tok", [(i, i + 1) for i in range(tok_count - 1)])
    right = lax.ppermute(head, "tok", [(i + 1, i) for i in range(tok_count - 1)])
    gains = [attn_gain.reshape(1, -1), ffn_gain.reshape(1, -1)]
    projected = project(ens_state, head_window.shape[0], gains[0], w_query, w_key, w_value)
    share_start = (first_pos + index * share_rows).astype(jnp.int32)
    grid = sample_grid(share_start, obs_token, obs_channel, obs_value, obs_var, share_rows, half_rows, feat_width)

    def forecast_of(half, halo, out_rows):
        ext_start = first_pos + half * half_rows - WIN
        place = jnp.stack([ext_start, row_count * tok_count]).astype(jnp.int32)
        weights = [w_key, w_value, w_out, w_gate, w_up, down_weight]
        return forward(place, head_window, ens_state, projected, halo, gains, weights, half, mem_count, out_rows)

    def exchanged(fields, axes="mem"):
        return lax.all_to_all(fields, axes, split_axis=0, concat_axis=0, tiled=True)

    early_all = exchanged(forecast_of(0, left, half_rows))
    late_share = exchanged(forecast_of(1, right, share_rows))
    partial = gram_partial(index, early_all, late_share, grid)
    partials = exchanged(jnp.broadcast_to(partial[None], (device_count, *partial.shape)), ("mem", "tok"))
    transform, late_mixed = solve(partials, late_share)
    late_back = exchanged(late_mixed)
    analysis = combine(index, transform, early_all)
    late_back = jnp.moveaxis(late_back, 0, 1).reshape(own_members, half_rows, feat_width)
    return lax.dynamic_update_slice(analysis, late_back, (0, half_rows, 0))


def solution(mesh):
    in_specs = (P("mem", "tok", None), *[P()] * 10, *[P("tok")] * 4)
    return jax.shard_map(local, mesh=mesh, in_specs=in_specs, out_specs=P("mem", "tok", None), check_vma=False)
```

time: 99.9 us -> 140 us (1.40)
  Pallas kernels: 35 us -> 71.9 us
  blocking collectives: 39.7 us -> 11.8 us
  waiting for transfers between devices: 12.2 us -> 29.8 us
  starting transfers between devices: 7.54 us -> 18.2 us
  local copies, waits for them, and re-layouts: 4.8 us -> 7.25 us
    pallas_call x4 -> x8, Pallas kernels: 35 us -> 71.9 us  [the longest x1 32.9 us: edges(): pl.pallas_call(edges_kernel, out_shape=[jax.ShapeDtypeStruct((members, re...]
    all_to_all x2 -> x1, blocking collectives: 39.7 us -> 11.8 us  [exchanged(): return lax.all_to_all(fields, axes, split_axis=0, concat_axis=0, tiled=True)]
    all_to_all x1 -> x3, waiting for transfers between devices: 7.38 us -> 29.8 us  [exchanged(): return lax.all_to_all(fields, axes, split_axis=0, concat_axis=0, tiled=True)]
    all_to_all x1 -> x3, starting transfers between devices: 3.86 us -> 13 us  [exchanged(): return lax.all_to_all(fields, axes, split_axis=0, concat_axis=0, tiled=True)]
    unnamed x28 -> x42, local copies, waits for them, and re-layouts: 1.35 us -> 6.37 us
    ppermute x2, waiting for transfers between devices: 4.79 us -> 0.01 us  [the longest x1 0.01 us: local(): left = lax.ppermute(tail, 'tok', [(i, i + 1) for i in range(tok_count - 1)])]
    slice x1 -> x0, local copies, waits for them, and re-layouts: 2.4 us -> none  [local(): right = lax.ppermute(ens_state[:, :WIN], 'tok', down)]
    ppermute x2, starting transfers between devices: 3.68 us -> 5.15 us  [the longest x1 3.86 us: local(): left = lax.ppermute(tail, 'tok', [(i, i + 1) for i in range(tok_count - 1)])]
  transfers between devices with their start and end apart: 3 -> 5, of which waited for: 3 -> 2; matrix products, arithmetic and copies ran while one was open for 0% -> 0% of each run, Pallas kernels for 1% -> 24%
where the time goes in v4:
time: 140 us; the launch traced here: 139 us
  Pallas kernels  71.9 us (51%)
  waiting for transfers between devices  29.8 us (21%)
  starting transfers between devices  18.2 us (13%)
  blocking collectives  11.8 us (8%)
  local copies, waits for them, and re-layouts  7.25 us (5%)
    pallas_call x1, Pallas kernels, edges(): pl.pallas_call(edges_kernel, out_shape=[jax.ShapeDtypeStruct((members, re...  32.9 us
    all_to_all x3, waiting for transfers between devices, exchanged(): return lax.all_to_all(fields, axes, split_axis=0, concat_axis=0, tiled=True)  29.8 us
    pallas_call x2, Pallas kernels, forward(): pl.pallas_call(functools.partial(forward_kernel, half == 0), grid=(member...  26.1 us
    all_to_all x3, starting transfers between devices, exchanged(): return lax.all_to_all(fields, axes, split_axis=0, concat_axis=0, tiled=True)  13 us
    all_to_all x1, blocking collectives, exchanged(): return lax.all_to_all(fields, axes, split_axis=0, concat_axis=0, tiled=True)  11.8 us
    unnamed x42, local copies, waits for them, and re-layouts  6.37 us
    pallas_call x1, Pallas kernels, solve(): pl.pallas_call(solve_kernel, out_shape=[jax.ShapeDtypeStruct((members, me...  4.15 us
    ppermute x1, starting transfers between devices, local(): left = lax.ppermute(tail, 'tok', [(i, i + 1) for i in range(tok_count - 1)])  3.86 us
  transfers between devices with their start and end apart: 5, of which 2 were waited for; matrix products, arithmetic and copies ran while one was open for 0% of the time, Pallas kernels for 24%

profile of v4, /device:TPU:0, one launch (start us, length us, event | category | flops | bytes accessed | tf_op | source)
XLA Modules:
  0.0 139.3 jit_solution(1424920269100807678)
XLA Ops:
  0.0 32.9 %edges.1 = (bf16[4,256,256]{2,1,0:T(8,128)(2,1)}, bf16[4,256,256]{2,1,0:T(8,128)(2,1)}) custom-call(bf16[4,512,256]{2,1,0:T(8,128)(2,1)} %state_ref.3), custom_call_target="tpu_custom_call" | custom-call | bytes 2097152 | tf_op jit(solution)/shard_map/edges/pallas_call | solution.py:71
  33.0 1.3 collective-permute-start.1
  34.3 3.9 %collective-permute-start = (bf16[4,256,256]{2,1,0:T(8,128)(2,1)}, bf16[4,256,256]{2,1,0:T(8,128)(2,1)}, u32[]{:S(2)}, u32[]{:S(2)}) collective-permute-start(bf16[4,256,256]{2,1,0:T(8,128)(2,1)} %get-tuple-element.15), channel_id=1, source_target_pairs={{0,1},{1,2},{2,3},{3,4},{4,5},{5,6},{6,7},{8,9},{9,10},{10,11},{11... | collective-permute-start | bytes 1572872 | tf_op jit(solution)/shard_map/ppermute | solution.py:481
  38.1 0.9 copy-done.4
  39.0 0.9 copy-done.5
  39.9 0.9 copy-done.7
  40.8 0.7 copy-done.14
  41.5 3.4 %project.1 = (bf16[4,512,256]{2,1,0:T(8,128)(2,1)S(1)}, bf16[4,512,256]{2,1,0:T(8,128)(2,1)S(1)}, bf16[4,256,512]{2,1,0:T(8,128)(2,1)S(1)}) custom-call(bf16[4,512,256]{2,1,0:T(8,128)(2,1)} %state_ref.3, f32[1,256]{1,0:T(1,128)S(1)} %bitcast.15, bf16[256,256]{1,0:T(8,128)(2,1)S(1)} %copy-done.4, bf16[256,256]{1,0:T(8,128)(2,1)S(1)} %copy-done.5, ...), custom_call_target="tpu_custom_call" | custom-call | flops 805306368 | bytes 4194304 | tf_op jit(solution)/shard_map/project/pallas_call | solution.py:137
  44.9 0.0 copy-start.18
  45.0 1.0 copy-done.18
  45.9 1.0 copy-done.19
  46.9 1.0 copy-done.20
  47.9 0.1 pad_add_fusion.place_ref
  47.9 0.1 pad_add_fusion.1.place_ref
  48.1 0.0 copy-start.6
  48.1 0.0 copy-start.8
  48.1 0.0 copy-start.15
  48.1 12.8 %forward.3 = bf16[4,4,64,256]{3,2,1,0:T(8,128)(2,1)} custom-call(s32[2]{0:T(128)S(1)} %pad_add_fusion.place_ref, s32[4]{0:T(128)S(1)} %copy-done.17, bf16[4,512,256]{2,1,0:T(8,128)(2,1)S(1)} %copy-done, bf16[4,512,256]{2,1,0:T(8,128)(2,1)} %copy-done.18, bf16[4,512,256]{2,1,0:T(8,128)(2,1)} %copy-done.19, bf16[4,256,512]{2,1,0:T(8,128)(2,1)} %copy-done.20, ...), custom_call_target="tpu_custom_call" | custom-call | flops 4563402752 | bytes 3145728 | tf_op jit(solution)/shard_map/forward/pallas_call | solution.py:246
  60.9 5.2 %all-to-all-start.1 = ((bf16[4,4,64,256]{3,2,1,0:T(8,128)(2,1)}), bf16[4,4,64,256]{3,2,1,0:T(8,128)(2,1)S(1)}, u32[]{:S(2)}, u32[]{:S(2)}) async-start(bf16[4,4,64,256]{3,2,1,0:T(8,128)(2,1)} %forward.3), calls=%async_computation.1 | async-start | bytes 1048576 | tf_op jit(solution)/shard_map/all_to_all | solution.py:495
  66.2 13.3 %forward.2 = bf16[4,4,256,256]{3,2,1,0:T(8,128)(2,1)} custom-call(s32[2]{0:T(128)S(1)} %pad_add_fusion.1.place_ref, s32[4]{0:T(128)S(1)} %copy-done.17, bf16[4,512,256]{2,1,0:T(8,128)(2,1)S(1)} %copy-done, bf16[4,512,256]{2,1,0:T(8,128)(2,1)} %copy-done.18, bf16[4,512,256]{2,1,0:T(8,128)(2,1)} %copy-done.19, bf16[4,256,512]{2,1,0:T(8,128)(2,1)} %copy-done.20, ...), custom_call_target="tpu_custom_call" | custom-call | flops 4563402752 | bytes 3145728 | tf_op jit(solution)/shard_map/forward/pallas_call | solution.py:246
  79.4 0.0 copy-start.12
  79.5 0.0 copy-start.13
  79.5 4.3 %all-to-all-start = ((bf16[4,4,256,256]{3,2,1,0:T(8,128)(2,1)}), bf16[4,4,256,256]{3,2,1,0:T(8,128)(2,1)S(1)}, u32[]{:S(2)}, u32[]{:S(2)}) async-start(bf16[4,4,256,256]{3,2,1,0:T(8,128)(2,1)} %forward.2), calls=%async_computation | async-start | bytes 4194304 | tf_op jit(solution)/shard_map/all_to_all | solution.py:495
  83.8 1.3 sample_grid.1.grid_ref
  85.2 23.5 %all-to-all-done.early_ref.fields_ref = bf16[4,4,256,256]{3,2,1,0:T(8,128)(2,1)S(1)} async-done(((bf16[4,4,256,256]{3,2,1,0:T(8,128)(2,1)}), bf16[4,4,256,256]{3,2,1,0:T(8,128)(2,1)S(1)}, u32[]{:S(2)}, u32[]{:S(2)}) %all-to-all-start) | async-done | bytes 2097184 | tf_op jit(solution)/shard_map/all_to_all | solution.py:495
  108.7 1.5 %gram.1 = f32[8,128]{1,0:T(8,128)S(1)} custom-call(s32[1]{0:T(128)} %bitcast.index_ref, bf16[4,4,256,256]{3,2,1,0:T(8,128)(2,1)S(1)} %all-to-all-done.early_ref.fields_ref, bf16[4,4,64,256]{3,2,1,0:T(8,128)(2,1)S(1)} %all-to-all-done.1.late_ref.share_ref, f32[2,128,256]{2,1,0:T(8,128)S(1)} %sample_grid.1.grid_ref), custom_call_target="tpu_custom_call" | custom-call | flops 805306368 | bytes 1048576 | tf_op jit(solution)/shard_map/gram/pallas_call | solution.py:312
  110.2 11.8 %all_to_all.20.partial_ref = f32[32,8,128]{2,1,0:T(8,128)S(1)} all-to-all(f32[32,8,128]{2,1,0:T(8,128)S(1)} %broadcast_in_dim.2), channel_id=1, replica_groups=mesh['mem'=4,'tok'=8] {'mem','tok'}, dimensions={0} | all-to-all | bytes 262144 | tf_op jit(solution)/shard_map/all_to_all | solution.py:495
  122.0 4.2 %solve.1 = (f32[16,16]{1,0:T(8,128)S(1)}, bf16[4,4,64,256]{3,2,1,0:T(8,128)(2,1)}) custom-call(f32[32,8,128]{2,1,0:T(8,128)S(1)} %all_to_all.20.partial_ref, bf16[4,4,64,256]{3,2,1,0:T(8,128)(2,1)S(1)} %all-to-all-done.1.late_ref.share_ref), custom_call_target="tpu_custom_call" | custom-call | flops 1000000000 | bytes 131072 | tf_op jit(solution)/shard_map/solve/pallas_call | solution.py:409
  126.2 3.5 %all-to-all-start.3 = ((bf16[4,4,64,256]{3,2,1,0:T(8,128)(2,1)}), bf16[4,4,64,256]{3,2,1,0:T(8,128)(2,1)S(1)}, u32[]{:S(2)}, u32[]{:S(2)}) async-start(bf16[4,4,64,256]{3,2,1,0:T(8,128)(2,1)} %get-tuple-element.18), calls=%async_computation.3 | async-start | bytes 1048576 | tf_op jit(solution)/shard_map/all_to_all | solution.py:495
  129.7 2.4 %combine.1 = bf16[4,512,256]{2,1,0:T(8,128)(2,1)} custom-call(s32[1]{0:T(128)} %bitcast.index_ref, f32[16,16]{1,0:T(8,128)S(1)} %get-tuple-element.17.transform_ref, bf16[4,4,256,256]{3,2,1,0:T(8,128)(2,1)S(1)} %all-to-all-done.early_ref.fields_ref), custom_call_target="tpu_custom_call" | custom-call | flops 268435456 | bytes 3145728 | tf_op jit(solution)/shard_map/combine/pallas_call | solution.py:436
  132.1 6.3 %all-to-all-done.3 = bf16[4,4,64,256]{3,2,1,0:T(8,128)(2,1)S(1)} async-done(((bf16[4,4,64,256]{3,2,1,0:T(8,128)(2,1)}), bf16[4,4,64,256]{3,2,1,0:T(8,128)(2,1)S(1)}, u32[]{:S(2)}, u32[]{:S(2)}) %all-to-all-start.3) | async-done | bytes 524320 | tf_op jit(solution)/shard_map/all_to_all | solution.py:495
  138.5 0.8 constant_dynamic-update-slice_fusion
  (34 shorter events, 0.1 us)
Async XLA Ops:
  0.0 48.0 %copy-start = (bf16[4,512,256]{2,1,0:T(8,128)(2,1)S(1)}, bf16[4,512,256]{2,1,0:T(8,128)(2,1)}, u32[]{:S(2)}) copy-start(bf16[4,512,256]{2,1,0:T(8,128)(2,1)} %state_ref.3) | copy-start | bytes 3145732
  0.0 48.0 %copy-start.1 = (bf16[256,1024]{1,0:T(8,128)(2,1)S(1)}, bf16[256,1024]{1,0:T(8,128)(2,1)}, u32[]{:S(2)}) copy-start(bf16[256,1024]{1,0:T(8,128)(2,1)} %w_gate_ref.3) | copy-start | bytes 1572868
  0.0 48.0 %copy-start.2 = (bf16[256,1024]{1,0:T(8,128)(2,1)S(1)}, bf16[256,1024]{1,0:T(8,128)(2,1)}, u32[]{:S(2)}) copy-start(bf16[256,1024]{1,0:T(8,128)(2,1)} %w_up_ref.3) | copy-start | bytes 1572868
  0.0 48.0 %copy-start.3 = (bf16[1024,256]{1,0:T(8,128)(2,1)S(1)}, bf16[1024,256]{1,0:T(8,128)(2,1)}, u32[]{:S(2)}) copy-start(bf16[1024,256]{1,0:T(8,128)(2,1)} %down_weight_ref.3) | copy-start | bytes 1572868
  33.0 15.1 %collective-permute-start.1 = (bf16[4,256,256]{2,1,0:T(8,128)(2,1)}, bf16[4,256,256]{2,1,0:T(8,128)(2,1)S(1)}, u32[]{:S(2)}, u32[]{:S(2)}) collective-permute-start(bf16[4,256,256]{2,1,0:T(8,128)(2,1)} %get-tuple-element.16), channel_id=1, source_target_pairs={{1,0},{2,1},{3,2},{4,3},{5,4},{6,5},{7,6},{9,8},{10,9},{11,10},{12... | collective-permute-start | bytes 1572872 | tf_op jit(solution)/shard_map/ppermute | solution.py:482
  34.3 31.9 %collective-permute-start = (bf16[4,256,256]{2,1,0:T(8,128)(2,1)}, bf16[4,256,256]{2,1,0:T(8,128)(2,1)}, u32[]{:S(2)}, u32[]{:S(2)}) collective-permute-start(bf16[4,256,256]{2,1,0:T(8,128)(2,1)} %get-tuple-element.15), channel_id=1, source_target_pairs={{0,1},{1,2},{2,3},{3,4},{4,5},{5,6},{6,7},{8,9},{9,10},{10,11},{11... | collective-permute-start | bytes 1572872 | tf_op jit(solution)/shard_map/ppermute | solution.py:481
  38.1 0.9 copy-start.4
  39.0 0.9 copy-start.5
  39.9 0.9 copy-start.7
  40.8 0.7 copy-start.14
  41.5 6.6 %copy-start.9 = (bf16[256,256]{1,0:T(8,128)(2,1)S(1)}, bf16[256,256]{1,0:T(8,128)(2,1)}, u32[]{:S(2)}) copy-start(bf16[256,256]{1,0:T(8,128)(2,1)} %w_out_ref.3) | copy-start | bytes 393220
  41.5 6.6 %copy-start.16 = (f32[256]{0:T(256)S(1)}, f32[256]{0:T(256)}, u32[]{:S(2)}) copy-start(f32[256]{0:T(256)} %param.17) | copy-start | bytes 3076
  41.5 6.6 %copy-start.17 = (s32[4]{0:T(128)S(1)}, s32[4]{0:T(128)}, u32[]{:S(2)}) copy-start(s32[4]{0:T(128)} %window_ref.3) | copy-start | bytes 52
  44.9 1.0 copy-start.18
  45.9 1.0 copy-start.19
  46.9 1.0 copy-start.20
  48.1 18.1 %copy-start.6 = (bf16[256,256]{1,0:T(8,128)(2,1)S(1)}, bf16[256,256]{1,0:T(8,128)(2,1)}, u32[]{:S(2)}) copy-start(bf16[256,256]{1,0:T(8,128)(2,1)} %w_key_ref.5) | copy-start | bytes 393220
  48.1 18.1 %copy-start.8 = (bf16[256,256]{1,0:T(8,128)(2,1)S(1)}, bf16[256,256]{1,0:T(8,128)(2,1)}, u32[]{:S(2)}) copy-start(bf16[256,256]{1,0:T(8,128)(2,1)} %w_value_ref.5) | copy-start | bytes 393220
  48.1 18.1 %copy-start.15 = (f32[256]{0:T(256)S(1)}, f32[256]{0:T(256)}, u32[]{:S(2)}) copy-start(f32[256]{0:T(256)} %param.16) | copy-start | bytes 3076
  60.9 18.5 %all-to-all-start.1 = ((bf16[4,4,64,256]{3,2,1,0:T(8,128)(2,1)}), bf16[4,4,64,256]{3,2,1,0:T(8,128)(2,1)S(1)}, u32[]{:S(2)}, u32[]{:S(2)}) async-start(bf16[4,4,64,256]{3,2,1,0:T(8,128)(2,1)} %forward.3), calls=%async_computation.1 | async-start | bytes 1048576 | tf_op jit(solution)/shard_map/all_to_all | solution.py:495
  79.4 4.4 %copy-start.10 = (s32[4096]{0:T(1024)S(1)}, s32[4096]{0:T(1024)}, u32[]{:S(2)}) copy-start(s32[4096]{0:T(1024)} %param.26) | copy-start | bytes 49156
  79.4 4.4 %copy-start.11 = (s32[4096]{0:T(1024)S(1)}, s32[4096]{0:T(1024)}, u32[]{:S(2)}) copy-start(s32[4096]{0:T(1024)} %param.27) | copy-start | bytes 49156
  79.4 4.4 %copy-start.12 = (f32[4096]{0:T(1024)S(1)}, f32[4096]{0:T(1024)}, u32[]{:S(2)}) copy-start(f32[4096]{0:T(1024)} %param.28) | copy-start | bytes 49156
  79.5 4.4 %copy-start.13 = (f32[4096]{0:T(1024)S(1)}, f32[4096]{0:T(1024)}, u32[]{:S(2)}) copy-start(f32[4096]{0:T(1024)} %param.29) | copy-start | bytes 49156
  79.5 29.2 %all-to-all-start = ((bf16[4,4,256,256]{3,2,1,0:T(8,128)(2,1)}), bf16[4,4,256,256]{3,2,1,0:T(8,128)(2,1)S(1)}, u32[]{:S(2)}, u32[]{:S(2)}) async-start(bf16[4,4,256,256]{3,2,1,0:T(8,128)(2,1)} %forward.2), calls=%async_computation | async-start | bytes 4194304 | tf_op jit(solution)/shard_map/all_to_all | solution.py:495
  126.2 12.2 %all-to-all-start.3 = ((bf16[4,4,64,256]{3,2,1,0:T(8,128)(2,1)}), bf16[4,4,64,256]{3,2,1,0:T(8,128)(2,1)S(1)}, u32[]{:S(2)}, u32[]{:S(2)}) async-start(bf16[4,4,64,256]{3,2,1,0:T(8,128)(2,1)} %get-tuple-element.18), calls=%async_computation.3 | async-start | bytes 1048576 | tf_op jit(solution)/shard_map/all_to_all | solution.py:495

commit v5 on v4

--- a/solution.py
+++ b/solution.py
@@ -14,7 +14,7 @@
 Q_ROWS = 128
 GROUP = 16
 LANES = 128
-VMEM_LIMIT = 50 * 1024 * 1024
+VMEM_LIMIT = 60 * 1024 * 1024
 
 F32 = jnp.float32
 BF16 = jnp.bfloat16
@@ -49,31 +49,22 @@
     return pl.BlockSpec(memory_space=pltpu.SMEM)
 
 
-def edges_kernel(own_ref, head_ref, tail_ref, sems):
-    members, reach, _ = head_ref.shape
-    rows = own_ref.shape[1]
-    copies = []
-    for member in range(members):
-        for which, (lower, out_ref) in enumerate(((rows - reach, tail_ref), (0, head_ref))):
-            copies.append(
-                pltpu.make_async_copy(
-                    own_ref.at[member, pl.ds(lower, reach)], out_ref.at[member], sems.at[which, member]
-                )
-            )
-    for copy in copies:
-        copy.start()
-    for copy in copies:
-        copy.wait()
+def edges_kernel(own_ref, head_ref, tail_ref):
+    reach = head_ref.shape[1]
+    head_ref[...] = own_ref[:, :reach, :]
+    tail_ref[...] = own_ref[:, own_ref.shape[1] - reach :, :]
 
 
 def edges(own, reach):
-    members, _, feat_width = own.shape
+    members, rows, feat_width = own.shape
+    edge = pl.BlockSpec((1, reach, feat_width), lambda m: (m, 0, 0))
     return pl.pallas_call(
         edges_kernel,
+        grid=(members,),
         out_shape=[jax.ShapeDtypeStruct((members, reach, feat_width), own.dtype)] * 2,
-        in_specs=[pl.BlockSpec(memory_space=pl.ANY)],
-        out_specs=[pl.BlockSpec(memory_space=pl.ANY)] * 2,
-        scratch_shapes=[pltpu.SemaphoreType.DMA((2, members))],
+        in_specs=[pl.BlockSpec((1, rows, feat_width), lambda m: (m, 0, 0))],
+        out_specs=[edge] * 2,
+        compiler_params=pltpu.CompilerParams(vmem_limit_bytes=VMEM_LIMIT),
         cost_estimate=pl.CostEstimate(flops=0, bytes_accessed=8 * members * reach * feat_width, transcendentals=0),
         name="edges",
     )(own)
@@ -170,13 +161,9 @@
     w_gate_ref,
     w_up_ref,
     down_weight_ref,
-    out_ref,
-    key_buf,
-    value_buf,
-    turned_buf,
-    bias_buf,
-    mixed_buf,
+    *refs,
 ):
+    out_ref, key_buf, value_buf, turned_buf, bias_buf, mixed_buf = refs[-6:]
     rows, feat_width = state_ref.shape[1:]
     reach = halo_ref.shape[1]
     own_rows = key_ref.shape[1]
@@ -235,7 +222,7 @@
         out_ref[target, 0] = forecast[lower : lower + out_rows]
 
 
-def forward(place, head_window, own, projected, halo, gains, weights, half, targets, out_rows):
+def forward(place, head_window, own, projected, halo, gains, weights, half, targets, out_rows, earlier):
     members, row_count, feat_width = own.shape
     rows, reach = row_count // 2, halo.shape[1]
     key_count = Q_ROWS + 2 * reach
@@ -256,7 +243,8 @@
             pl.BlockSpec((1, feat_width, row_count), lambda m: (m, 0, 0)),
             pl.BlockSpec((1, reach, feat_width), lambda m: (m, 0, 0)),
         ]
-        + [vmem_spec()] * (len(gains) + len(weights)),
+        + [vmem_spec()] * (len(gains) + len(weights))
+        + [pl.BlockSpec(memory_space=pl.ANY)] * len(earlier),
         out_specs=pl.BlockSpec((targets, 1, out_rows, feat_width), lambda m: (0, m, 0, 0)),
         scratch_shapes=[
             pltpu.VMEM((row_count + reach, feat_width), BF16),
@@ -268,7 +256,7 @@
         compiler_params=pltpu.CompilerParams(vmem_limit_bytes=VMEM_LIMIT),
         cost_estimate=pl.CostEstimate(flops=2 * macs, bytes_accessed=6 * own.size, transcendentals=0),
         name="forward",
-    )(place, head_window, own, *projected, halo, *gains, *weights)
+    )(place, head_window, own, *projected, halo, *gains, *weights, *earlier)
 
 
 def gram_kernel(index_ref, early_ref, late_ref, grid_ref, out_ref):
@@ -485,17 +473,20 @@
     share_start = (first_pos + index * share_rows).astype(jnp.int32)
     grid = sample_grid(share_start, obs_token, obs_channel, obs_value, obs_var, share_rows, half_rows, feat_width)
 
-    def forecast_of(half, halo, out_rows):
+    def forecast_of(half, halo, out_rows, earlier=()):
         ext_start = first_pos + half * half_rows - WIN
         place = jnp.stack([ext_start, row_count * tok_count]).astype(jnp.int32)
         weights = [w_key, w_value, w_out, w_gate, w_up, down_weight]
-        return forward(place, head_window, ens_state, projected, halo, gains, weights, half, mem_count, out_rows)
+        return forward(
+            place, head_window, ens_state, projected, halo, gains, weights, half, mem_count, out_rows, earlier
+        )
 
     def exchanged(fields, axes="mem"):
         return lax.all_to_all(fields, axes, split_axis=0, concat_axis=0, tiled=True)
 
-    early_all = exchanged(forecast_of(0, left, half_rows))
-    late_share = exchanged(forecast_of(1, right, share_rows))
+    early = forecast_of(0, left, half_rows)
+    early_all = exchanged(early)
+    late_share = exchanged(forecast_of(1, right, share_rows, (early,)))
     partial = gram_partial(index, early_all, late_share, grid)
     partials = exchanged(jnp.broadcast_to(partial[None], (device_count, *partial.shape)), ("mem", "tok"))
     transform, late_mixed = solve(partials, late_share)

time: 140 us -> 122 us (0.87)
  Pallas kernels: 71.9 us -> 51.5 us
  blocking collectives: 11.8 us -> 27.2 us
  starting transfers between devices: 18.2 us -> 10.7 us
  waiting for transfers between devices: 29.8 us -> 27 us
  local copies, waits for them, and re-layouts: 7.25 us -> 4.47 us
    pallas_call x1, Pallas kernels: 32.9 us -> 3.33 us  [edges(): pl.pallas_call(edges_kernel, grid=(members,), out_shape=[jax.ShapeDtypeSt...]
    all_to_all x1 -> x2, blocking collectives: 11.8 us -> 27.2 us  [exchanged(): return lax.all_to_all(fields, axes, split_axis=0, concat_axis=0, tiled=True)]
    all_to_all x3 -> x2, starting transfers between devices: 13 us -> 7.08 us  [exchanged(): return lax.all_to_all(fields, axes, split_axis=0, concat_axis=0, tiled=True)]
    unnamed x42 -> x6, local copies, waits for them, and re-layouts: 6.37 us -> 2.91 us
    all_to_all x3 -> x2, waiting for transfers between devices: 29.8 us -> 26.9 us  [exchanged(): return lax.all_to_all(fields, axes, split_axis=0, concat_axis=0, tiled=True)]
    pallas_call x1, Pallas kernels: 1.52 us -> 3.37 us  [gram_partial(): pl.pallas_call(gram_kernel, grid_spec=pltpu.PrefetchScalarGridSpec(num_sc...]
    pallas_call x2, Pallas kernels: 26.1 us -> 27.8 us  [forward(): pl.pallas_call(functools.partial(forward_kernel, half == 0), grid=(member...]
    pallas_call x1, Pallas kernels: 2.43 us -> 4.18 us  [combine(): pl.pallas_call(combine_kernel, grid=(rows // block,), out_shape=jax.Shape...]
  transfers between devices with their start and end apart: 5 -> 4, of which waited for: 2 -> 2; matrix products, arithmetic and copies ran while one was open for 0% -> 1% of each run, Pallas kernels for 24% -> 21%
where the time goes in v5:
time: 122 us
  Pallas kernels  51.5 us (42%)
  blocking collectives  27.2 us (22%)
  waiting for transfers between devices  27 us (22%)
  starting transfers between devices  10.7 us (9%)
  local copies, waits for them, and re-layouts  4.47 us (4%)
    pallas_call x2, Pallas kernels, forward(): pl.pallas_call(functools.partial(forward_kernel, half == 0), grid=(member...  27.8 us
    all_to_all x2, blocking collectives, exchanged(): return lax.all_to_all(fields, axes, split_axis=0, concat_axis=0, tiled=True)  27.2 us
    all_to_all x2, waiting for transfers between devices, exchanged(): return lax.all_to_all(fields, axes, split_axis=0, concat_axis=0, tiled=True)  26.9 us
    all_to_all x2, starting transfers between devices, exchanged(): return lax.all_to_all(fields, axes, split_axis=0, concat_axis=0, tiled=True)  7.08 us
    pallas_call x1, Pallas kernels, solve(): pl.pallas_call(solve_kernel, out_shape=[jax.ShapeDtypeStruct((members, me...  5.27 us
    pallas_call x1, Pallas kernels, project(): pl.pallas_call(functools.partial(project_kernel, heads), grid=(members,),...  4.7 us
    pallas_call x1, Pallas kernels, combine(): pl.pallas_call(combine_kernel, grid=(rows // block,), out_shape=jax.Shape...  4.18 us
    pallas_call x1, Pallas kernels, gram_partial(): pl.pallas_call(gram_kernel, grid_spec=pltpu.PrefetchScalarGridSpec(num_sc...  3.37 us
  transfers between devices with their start and end apart: 4, of which 2 were waited for; matrix products, arithmetic and copies ran while one was open for 1% of the time, Pallas kernels for 21%

profile of v5, /device:TPU:0, one launch (start us, length us, event | category | flops | bytes accessed | tf_op | source)
XLA Modules:
  0.0 121.6 jit_solution(7763554998944922871)
XLA Ops:
  0.0 3.3 %edges.1 = (bf16[4,256,256]{2,1,0:T(8,128)(2,1)}, bf16[4,256,256]{2,1,0:T(8,128)(2,1)}) custom-call(bf16[4,512,256]{2,1,0:T(8,128)(2,1)} %state_ref.3), custom_call_target="tpu_custom_call" | custom-call | bytes 2097152 | tf_op jit(solution)/shard_map/edges/pallas_call | solution.py:61
  3.3 2.4 %collective-permute-start = (bf16[4,256,256]{2,1,0:T(8,128)(2,1)}, bf16[4,256,256]{2,1,0:T(8,128)(2,1)S(1)}, u32[]{:S(2)}, u32[]{:S(2)}) collective-permute-start(bf16[4,256,256]{2,1,0:T(8,128)(2,1)} %get-tuple-element.15), channel_id=1, source_target_pairs={{0,1},{1,2},{2,3},{3,4},{4,5},{5,6},{6,7},{8,9},{9,10},{10,11},{11... | collective-permute-start | bytes 1572872 | tf_op jit(solution)/shard_map/ppermute | solution.py:469
  5.7 1.3 %collective-permute-start.1 = (bf16[4,256,256]{2,1,0:T(8,128)(2,1)}, bf16[4,256,256]{2,1,0:T(8,128)(2,1)S(1)}, u32[]{:S(2)}, u32[]{:S(2)}) collective-permute-start(bf16[4,256,256]{2,1,0:T(8,128)(2,1)} %get-tuple-element.16), channel_id=1, source_target_pairs={{1,0},{2,1},{3,2},{4,3},{5,4},{6,5},{7,6},{9,8},{10,9},{11,10},{12... | collective-permute-start | bytes 1572872 | tf_op jit(solution)/shard_map/ppermute | solution.py:470
  7.0 4.7 %project.1 = (bf16[4,512,256]{2,1,0:T(8,128)(2,1)}, bf16[4,512,256]{2,1,0:T(8,128)(2,1)}, bf16[4,256,512]{2,1,0:T(8,128)(2,1)}) custom-call(bf16[4,512,256]{2,1,0:T(8,128)(2,1)} %state_ref.3, f32[1,256]{1,0:T(1,128)} %bitcast.17, bf16[256,256]{1,0:T(8,128)(2,1)} %w_query_ref.1, bf16[256,256]{1,0:T(8,128)(2,1)} %w_key_ref.5, bf16[256,256]{1,0:T(8,128)(2,1)} %w_value_ref.5), custom_call_target="tpu_custom_call" | custom-call | flops 805306368 | bytes 4194304 | tf_op jit(solution)/shard_map/project/pallas_call | solution.py:128
  11.7 0.6 pad_add_fusion
  12.3 0.0 collective-permute-done.halo_ref
  12.3 0.0 copy-start.2
  12.3 0.8 copy-done.2
  13.1 14.1 %forward.2.refs_0_ = bf16[4,4,256,256]{3,2,1,0:T(8,128)(2,1)} custom-call(s32[2]{0:T(128)} %get-tuple-element.20.place_ref, s32[4]{0:T(128)} %window_ref.3, bf16[4,512,256]{2,1,0:T(8,128)(2,1)} %state_ref.3, bf16[4,512,256]{2,1,0:T(8,128)(2,1)} %get-tuple-element.12.query_ref, bf16[4,512,256]{2,1,0:T(8,128)(2,1)} %get-tuple-element.13.key_ref, ...), custom_call_target="tpu_custom_call" | custom-call | flops 4563402752 | bytes 3145728 | tf_op jit(solution)/shard_map/forward/pallas_call | solution.py:233
  27.3 0.0 collective-permute-done.1.halo_ref
  27.3 0.0 copy-start.1
  27.3 0.8 copy-done.1
  28.1 13.7 %forward.3 = bf16[4,4,64,256]{3,2,1,0:T(8,128)(2,1)} custom-call(s32[2]{0:T(128)} %get-tuple-element.19.place_ref, s32[4]{0:T(128)} %window_ref.3, bf16[4,512,256]{2,1,0:T(8,128)(2,1)} %state_ref.3, bf16[4,512,256]{2,1,0:T(8,128)(2,1)} %get-tuple-element.12.query_ref, bf16[4,512,256]{2,1,0:T(8,128)(2,1)} %get-tuple-element.13.key_ref, ...), custom_call_target="tpu_custom_call" | custom-call | flops 4563402752 | bytes 3145728 | tf_op jit(solution)/shard_map/forward/pallas_call | solution.py:233
  41.8 12.3 %all_to_all.20.late_ref.share_ref = bf16[4,4,64,256]{3,2,1,0:T(8,128)(2,1)} all-to-all(bf16[4,4,64,256]{3,2,1,0:T(8,128)(2,1)} %forward.3), channel_id=1, replica_groups=mesh['mem'=4,'tok'=8] {'mem'}, dimensions={0} | all-to-all | bytes 1048576 | tf_op jit(solution)/shard_map/all_to_all | solution.py:485
  54.1 3.6 %all-to-all-start = ((bf16[4,4,256,256]{3,2,1,0:T(8,128)(2,1)}), bf16[4,4,256,256]{3,2,1,0:T(8,128)(2,1)S(1)}, u32[]{:S(2)}, u32[]{:S(2)}) async-start(bf16[4,4,256,256]{3,2,1,0:T(8,128)(2,1)} %forward.2.refs_0_), calls=%async_computation | async-start | bytes 4194304 | tf_op jit(solution)/shard_map/all_to_all | solution.py:485
  57.7 2.8 %sample_grid.1.grid_ref = f32[2,128,256]{2,1,0:T(8,128)} custom-call(s32[1]{0:T(128)S(6)} %add.9.start_ref, s32[1,4096]{1,0:T(1,128)} %bitcast.13, s32[1,4096]{1,0:T(1,128)} %bitcast.14, f32[1,4096]{1,0:T(1,128)} %bitcast.15, f32[1,4096]{1,0:T(1,128)} %bitcast.16), custom_call_target="tpu_custom_call" | custom-call | flops 1073741824 | bytes 65536 | tf_op jit(solution)/shard_map/sample_grid/pallas_call | solution.py:100
  60.5 22.4 %all-to-all-done.early_ref.fields_ref = bf16[4,4,256,256]{3,2,1,0:T(8,128)(2,1)S(1)} async-done(((bf16[4,4,256,256]{3,2,1,0:T(8,128)(2,1)}), bf16[4,4,256,256]{3,2,1,0:T(8,128)(2,1)S(1)}, u32[]{:S(2)}, u32[]{:S(2)}) %all-to-all-start) | async-done | bytes 2097184 | tf_op jit(solution)/shard_map/all_to_all | solution.py:485
  82.9 0.0 copy-start
  82.9 1.3 %copy-done = bf16[4,4,256,256]{3,2,1,0:T(8,128)(2,1)} copy-done((bf16[4,4,256,256]{3,2,1,0:T(8,128)(2,1)}, bf16[4,4,256,256]{3,2,1,0:T(8,128)(2,1)S(1)}, u32[]{:S(2)}) %copy-start) | copy-done | bytes 2097176
  84.2 3.4 %gram.1 = f32[8,128]{1,0:T(8,128)} custom-call(s32[1]{0:T(128)} %bitcast.index_ref, bf16[4,4,256,256]{3,2,1,0:T(8,128)(2,1)} %copy-done, bf16[4,4,64,256]{3,2,1,0:T(8,128)(2,1)} %all_to_all.20.late_ref.share_ref, f32[2,128,256]{2,1,0:T(8,128)} %sample_grid.1.grid_ref), custom_call_target="tpu_custom_call" | custom-call | flops 805306368 | bytes 1048576 | tf_op jit(solution)/shard_map/gram/pallas_call | solution.py:300
  87.6 0.7 broadcast_in_dim.2
  88.3 14.9 %all_to_all.21.partial_ref = f32[32,8,128]{2,1,0:T(8,128)} all-to-all(f32[32,8,128]{2,1,0:T(8,128)S(1)} %broadcast_in_dim.2), channel_id=1, replica_groups=mesh['mem'=4,'tok'=8] {'mem','tok'}, dimensions={0} | all-to-all | bytes 262144 | tf_op jit(solution)/shard_map/all_to_all | solution.py:485
  103.2 5.3 %solve.1 = (f32[16,16]{1,0:T(8,128)}, bf16[4,4,64,256]{3,2,1,0:T(8,128)(2,1)}) custom-call(f32[32,8,128]{2,1,0:T(8,128)} %all_to_all.21.partial_ref, bf16[4,4,64,256]{3,2,1,0:T(8,128)(2,1)} %all_to_all.20.late_ref.share_ref), custom_call_target="tpu_custom_call" | custom-call | flops 1000000000 | bytes 131072 | tf_op jit(solution)/shard_map/solve/pallas_call | solution.py:397
  108.5 3.5 %all-to-all-start.3 = ((bf16[4,4,64,256]{3,2,1,0:T(8,128)(2,1)}), bf16[4,4,64,256]{3,2,1,0:T(8,128)(2,1)S(1)}, u32[]{:S(2)}, u32[]{:S(2)}) async-start(bf16[4,4,64,256]{3,2,1,0:T(8,128)(2,1)} %get-tuple-element.18), calls=%async_computation.3 | async-start | bytes 1048576 | tf_op jit(solution)/shard_map/all_to_all | solution.py:485
  112.0 4.2 %combine.1 = bf16[4,512,256]{2,1,0:T(8,128)(2,1)} custom-call(s32[1]{0:T(128)} %bitcast.index_ref, f32[16,16]{1,0:T(8,128)} %get-tuple-element.17.transform_ref, bf16[4,4,256,256]{3,2,1,0:T(8,128)(2,1)} %copy-done), custom_call_target="tpu_custom_call" | custom-call | flops 268435456 | bytes 3145728 | tf_op jit(solution)/shard_map/combine/pallas_call | solution.py:424
  116.1 4.6 %all-to-all-done.3 = bf16[4,4,64,256]{3,2,1,0:T(8,128)(2,1)S(1)} async-done(((bf16[4,4,64,256]{3,2,1,0:T(8,128)(2,1)}), bf16[4,4,64,256]{3,2,1,0:T(8,128)(2,1)S(1)}, u32[]{:S(2)}, u32[]{:S(2)}) %all-to-all-start.3) | async-done | bytes 524320 | tf_op jit(solution)/shard_map/all_to_all | solution.py:485
  120.7 0.8 constant_dynamic-update-slice_fusion
  (1 shorter events, 0.0 us)
Async XLA Ops:
  3.3 9.0 %collective-permute-start = (bf16[4,256,256]{2,1,0:T(8,128)(2,1)}, bf16[4,256,256]{2,1,0:T(8,128)(2,1)S(1)}, u32[]{:S(2)}, u32[]{:S(2)}) collective-permute-start(bf16[4,256,256]{2,1,0:T(8,128)(2,1)} %get-tuple-element.15), channel_id=1, source_target_pairs={{0,1},{1,2},{2,3},{3,4},{4,5},{5,6},{6,7},{8,9},{9,10},{10,11},{11... | collective-permute-start | bytes 1572872 | tf_op jit(solution)/shard_map/ppermute | solution.py:469
  5.7 21.5 %collective-permute-start.1 = (bf16[4,256,256]{2,1,0:T(8,128)(2,1)}, bf16[4,256,256]{2,1,0:T(8,128)(2,1)S(1)}, u32[]{:S(2)}, u32[]{:S(2)}) collective-permute-start(bf16[4,256,256]{2,1,0:T(8,128)(2,1)} %get-tuple-element.16), channel_id=1, source_target_pairs={{1,0},{2,1},{3,2},{4,3},{5,4},{6,5},{7,6},{9,8},{10,9},{11,10},{12... | collective-permute-start | bytes 1572872 | tf_op jit(solution)/shard_map/ppermute | solution.py:470
  12.3 0.8 copy-start.2
  27.3 0.8 copy-start.1
  54.1 28.8 %all-to-all-start = ((bf16[4,4,256,256]{3,2,1,0:T(8,128)(2,1)}), bf16[4,4,256,256]{3,2,1,0:T(8,128)(2,1)S(1)}, u32[]{:S(2)}, u32[]{:S(2)}) async-start(bf16[4,4,256,256]{3,2,1,0:T(8,128)(2,1)} %forward.2.refs_0_), calls=%async_computation | async-start | bytes 4194304 | tf_op jit(solution)/shard_map/all_to_all | solution.py:485
  82.9 1.3 %copy-start = (bf16[4,4,256,256]{3,2,1,0:T(8,128)(2,1)}, bf16[4,4,256,256]{3,2,1,0:T(8,128)(2,1)S(1)}, u32[]{:S(2)}) copy-start(bf16[4,4,256,256]{3,2,1,0:T(8,128)(2,1)S(1)} %all-to-all-done.early_ref.fields_ref) | copy-start | bytes 6291460
  108.5 12.2 %all-to-all-start.3 = ((bf16[4,4,64,256]{3,2,1,0:T(8,128)(2,1)}), bf16[4,4,64,256]{3,2,1,0:T(8,128)(2,1)S(1)}, u32[]{:S(2)}, u32[]{:S(2)}) async-start(bf16[4,4,64,256]{3,2,1,0:T(8,128)(2,1)} %get-tuple-element.18), calls=%async_computation.3 | async-start | bytes 1048576 | tf_op jit(solution)/shard_map/all_to_all | solution.py:485

commit v6 on v1

--- a/solution.py
+++ b/solution.py
@@ -1,3 +1,4 @@
+import functools
 import math
 
 import jax
@@ -13,7 +14,9 @@
 Q_ROWS = 128
 GROUP = 16
 LANES = 128
-VMEM_LIMIT = 50 * 1024 * 1024
+VMEM_LIMIT = 32 * 1024 * 1024
+SAFE_SCORE = 56.0
+HIDDEN_CHUNK = 256
 
 F32 = jnp.float32
 BF16 = jnp.bfloat16
@@ -82,15 +85,42 @@
     )(start, *(v.reshape(1, count) for v in (obs_token, obs_channel, obs_value, obs_var)))
 
 
+def project_kernel(heads, own_ref, gain_ref, w_query_ref, w_key_ref, w_value_ref, query_ref, key_ref, value_ref):
+    scale = math.log2(math.e) / math.sqrt(own_ref.shape[2] // heads)
+    normed = rms_scaled(own_ref[0].astype(F32), gain_ref[...]).astype(BF16)
+    query_ref[0] = (dot(normed, w_query_ref[...]) * scale).astype(BF16)
+    key_ref[0] = dot(normed, w_key_ref[...]).astype(BF16)
+    value_ref[0] = dot(normed, w_value_ref[...]).astype(BF16)
+
+
+def project(own, heads, gain, w_query, w_key, w_value):
+    members, rows, feat_width = own.shape
+    block = pl.BlockSpec((1, rows, feat_width), lambda m: (m, 0, 0))
+    return pl.pallas_call(
+        functools.partial(project_kernel, heads),
+        grid=(members,),
+        out_shape=[jax.ShapeDtypeStruct((members, rows, feat_width), BF16)] * 3,
+        in_specs=[block] + [vmem_spec()] * 4,
+        out_specs=[block] * 3,
+        compiler_params=pltpu.CompilerParams(vmem_limit_bytes=VMEM_LIMIT),
+        cost_estimate=pl.CostEstimate(
+            flops=6 * own.size * feat_width, bytes_accessed=8 * own.size, transcendentals=0
+        ),
+        name="project",
+    )(own, gain, w_query, w_key, w_value)
+
+
 def forward_kernel(
     place_ref,
     window_ref,
-    own_ref,
+    state_ref,
+    query_ref,
+    key_ref,
+    value_ref,
     left_ref,
     right_ref,
     attn_gain_ref,
     ffn_gain_ref,
-    w_query_ref,
     w_key_ref,
     w_value_ref,
     w_out_ref,
@@ -98,102 +128,135 @@
     w_up_ref,
     down_weight_ref,
     out_ref,
-    query_buf,
     key_buf,
     value_buf,
-    apart_buf,
+    bias_buf,
     mixed_buf,
 ):
-    row_count, feat_width = own_ref.shape[1:]
+    rows, feat_width = state_ref.shape[1:]
     reach = left_ref.shape[1]
     head_count = window_ref.shape[0]
     head_size = feat_width // head_count
-    blocks = row_count // Q_ROWS
+    blocks = rows // Q_ROWS
     key_count = Q_ROWS + 2 * reach
 
     @pl.when(pl.program_id(0) == 0)
     def _():
-        rel = jnp.abs(iota((Q_ROWS, key_count), 1) - reach - iota((Q_ROWS, key_count), 0))
+        apart = jnp.abs(iota((Q_ROWS, key_count), 1) - reach - iota((Q_ROWS, key_count), 0))
         for block in range(blocks):
             k_pos = place_ref[0] - reach + block * Q_ROWS + iota((Q_ROWS, key_count), 1)
             inside = (k_pos >= 0) & (k_pos < place_ref[1])
-            apart_buf[block] = jnp.where(inside, rel, 1 << 20)
-
-    attn_gain = attn_gain_ref[...]
-    for source, lower, rows in ((left_ref, 0, reach), (own_ref, reach, row_count), (right_ref, reach + row_count, reach)):
-        normed = rms_scaled(source[0].astype(F32), attn_gain).astype(BF16)
-        key_buf[lower : lower + rows] = dot(normed, w_key_ref[...]).astype(BF16)
-        value_buf[lower : lower + rows] = dot(normed, w_value_ref[...]).astype(BF16)
-        if source is own_ref:
-            queries = dot(normed, w_query_ref[...]).astype(BF16)
-            query_buf[...] = queries * jnp.asarray(1.0 / math.sqrt(head_size), BF16)
+            for head in range(head_count):
+                bias_buf[block, head] = jnp.where(inside & (apart <= window_ref[head]), 0.0, -1e30)
+
+    key_buf[reach : reach + rows] = key_ref[0]
+    value_buf[reach : reach + rows] = value_ref[0]
+    for ref, lower in ((left_ref, 0), (right_ref, reach + rows)):
+        normed = rms_scaled(ref[0].astype(F32), attn_gain_ref[...]).astype(BF16)
+        key_buf[lower : lower + reach] = dot(normed, w_key_ref[...]).astype(BF16)
+        value_buf[lower : lower + reach] = dot(normed, w_value_ref[...]).astype(BF16)
 
     column_head = iota((1, feat_width), 1) // head_size
-
-    def one_block(block, carry):
-        start = pl.multiple_of(block * Q_ROWS, Q_ROWS)
-        queries = query_buf[pl.ds(start, Q_ROWS), :]
-        stacked = jnp.concatenate(
-            [queries * (column_head == head).astype(F32).astype(BF16) for head in range(head_count)], axis=0
-        )
-        scores = dot(stacked, key_buf[pl.ds(start, key_count), :], ((1,), (1,)))
-        apart = apart_buf[block]
-        weights, scales = [], []
-        for head in range(head_count):
-            score_matrix = scores[head * Q_ROWS : (head + 1) * Q_ROWS]
-            score_matrix = jnp.where(apart <= window_ref[head], score_matrix, -1e30)
-            expo = jnp.exp(score_matrix - jnp.max(score_matrix, axis=-1, keepdims=True))
-            scales.append(1.0 / jnp.sum(expo, axis=-1, keepdims=True))
-            weights.append(expo.astype(BF16))
-        mixed_all = dot(jnp.concatenate(weights, axis=0), value_buf[pl.ds(start, key_count), :])
-        mixed = jnp.zeros((Q_ROWS, feat_width), F32)
-        for head in range(head_count):
-            mixed = jnp.where(column_head == head, mixed_all[head * Q_ROWS : (head + 1) * Q_ROWS] * scales[head], mixed)
-        mixed_buf[pl.ds(start, Q_ROWS), :] = mixed.astype(BF16)
-        return carry
-
-    lax.fori_loop(0, blocks, one_block, 0)
-
-    after = (own_ref[0].astype(F32) + dot(mixed_buf[...], w_out_ref[...])).astype(BF16)
+    head_masks = [(column_head == head).astype(F32).astype(BF16) for head in range(head_count)]
+    by_head = (iota((feat_width, LANES), 0) // head_size == iota((feat_width, LANES), 1)).astype(F32).astype(BF16)
+
+    def largest_norm(values):
+        squares = values.astype(F32)
+        return jnp.max(dot((squares * squares).astype(BF16), by_head), axis=0, keepdims=True)
+
+    bound = jnp.max(largest_norm(query_ref[0]) * largest_norm(key_buf[...])) * 1.02
+    safe = bound <= SAFE_SCORE * SAFE_SCORE
+
+    def joined_heads(mixed_all, totals, count):
+        mixed = mixed_all[:count] * (1.0 / totals[0])
+        for head in range(1, head_count):
+            part = mixed_all[head * count : (head + 1) * count] * (1.0 / totals[head])
+            mixed = jnp.where(column_head == head, part, mixed)
+        return mixed.astype(BF16)
+
+    @pl.when(safe)
+    def _():
+        pair = 2 * Q_ROWS
+        span = pair + 2 * reach
+        corner = jnp.zeros((Q_ROWS, Q_ROWS), BF16)
+        for start in range(0, rows, pair):
+            queries = query_ref[0, start : start + pair, :]
+            stacked = jnp.concatenate([queries * mask for mask in head_masks], axis=0)
+            scores = dot(stacked, key_buf[start : start + span, :], ((1,), (1,)))
+            weights, totals = [], []
+            for head in range(head_count):
+                top = head * pair
+                bias = [bias_buf[start // Q_ROWS + part, head] for part in range(2)]
+                upper = jnp.exp2(scores[top : top + Q_ROWS, :key_count] + bias[0])
+                lower = jnp.exp2(scores[top + Q_ROWS : top + pair, Q_ROWS:] + bias[1])
+                totals.append(
+                    jnp.concatenate([jnp.sum(v, axis=-1, keepdims=True) for v in (upper, lower)], axis=0)
+                )
+                weights.append(jnp.concatenate([upper.astype(BF16), corner], axis=1))
+                weights.append(jnp.concatenate([corner, lower.astype(BF16)], axis=1))
+            mixed_all = dot(jnp.concatenate(weights, axis=0), value_buf[start : start + span, :])
+            mixed_buf[start : start + pair, :] = joined_heads(mixed_all, totals, pair)
+
+    @pl.when(jnp.logical_not(safe))
+    def _():
+        def one_block(block, carry):
+            start = pl.multiple_of(block * Q_ROWS, Q_ROWS)
+            queries = query_ref[0, pl.ds(start, Q_ROWS), :]
+            stacked = jnp.concatenate([queries * mask for mask in head_masks], axis=0)
+            scores = dot(stacked, key_buf[pl.ds(start, key_count), :], ((1,), (1,)))
+            weights, totals = [], []
+            for head in range(head_count):
+                score_matrix = scores[head * Q_ROWS : (head + 1) * Q_ROWS] + bias_buf[block, head]
+                expo = jnp.exp2(score_matrix - jnp.max(score_matrix, axis=-1, keepdims=True))
+                totals.append(jnp.sum(expo, axis=-1, keepdims=True))
+                weights.append(expo.astype(BF16))
+            mixed_all = dot(jnp.concatenate(weights, axis=0), value_buf[pl.ds(start, key_count), :])
+            mixed_buf[pl.ds(start, Q_ROWS), :] = joined_heads(mixed_all, totals, Q_ROWS)
+            return carry
+
+        lax.fori_loop(0, blocks, one_block, 0)
+
+    after = (state_ref[0].astype(F32) + dot(mixed_buf[...], w_out_ref[...])).astype(BF16)
     normed_mid = rms_scaled(after.astype(F32), ffn_gain_ref[...]).astype(BF16)
-    gate = dot(normed_mid, w_gate_ref[...])
-    hidden = (gate * (0.5 + 0.5 * jnp.tanh(0.5 * gate)) * dot(normed_mid, w_up_ref[...])).astype(BF16)
-    forecast = (after.astype(F32) + dot(hidden, down_weight_ref[...])).astype(BF16)
+    forecast = after.astype(F32)
+    for lower in range(0, w_gate_ref.shape[1], HIDDEN_CHUNK):
+        part = slice(lower, lower + HIDDEN_CHUNK)
+        gate = dot(normed_mid, w_gate_ref[:, part])
+        hidden = (gate * (0.5 + 0.5 * jnp.tanh(0.5 * gate)) * dot(normed_mid, w_up_ref[:, part])).astype(BF16)
+        forecast += dot(hidden, down_weight_ref[part, :])
+    forecast = forecast.astype(BF16)
     shares, _, share_rows, _ = out_ref.shape
     for share in range(shares):
         out_ref[share, 0] = forecast[share * share_rows : (share + 1) * share_rows]
 
 
-def forward(place, head_window, own, left, right, gains, weights, shares):
+def forward(place, head_window, own, projected, left, right, gains, weights, shares):
     members, row_count, feat_width = own.shape
     reach = left.shape[1]
     key_count = Q_ROWS + 2 * reach
-    hidden_width = weights[4].shape[1]
-    macs = members * row_count * feat_width * (6 * feat_width + 3 * hidden_width + 8 * key_count)
+    hidden_width = weights[3].shape[1]
+    macs = members * row_count * feat_width * (3 * feat_width + 3 * hidden_width + 8 * key_count)
+    member_block = pl.BlockSpec((1, row_count, feat_width), lambda m: (m, 0, 0))
+    edge_block = pl.BlockSpec((1, reach, feat_width), lambda m: (m, 0, 0))
     return pl.pallas_call(
         forward_kernel,
         grid=(members,),
         out_shape=jax.ShapeDtypeStruct((shares, members, row_count // shares, feat_width), BF16),
-        in_specs=[
-            smem_spec(),
-            smem_spec(),
-            pl.BlockSpec((1, row_count, feat_width), lambda m: (m, 0, 0)),
-            pl.BlockSpec((1, reach, feat_width), lambda m: (m, 0, 0)),
-            pl.BlockSpec((1, reach, feat_width), lambda m: (m, 0, 0)),
-        ]
+        in_specs=[smem_spec()] * 2
+        + [member_block] * (1 + len(projected))
+        + [edge_block] * 2
         + [vmem_spec()] * (len(gains) + len(weights)),
         out_specs=pl.BlockSpec((shares, 1, row_count // shares, feat_width), lambda m: (0, m, 0, 0)),
         scratch_shapes=[
-            pltpu.VMEM((row_count, feat_width), BF16),
             pltpu.VMEM((row_count + 2 * reach, feat_width), BF16),
             pltpu.VMEM((row_count + 2 * reach, feat_width), BF16),
-            pltpu.VMEM((row_count // Q_ROWS, Q_ROWS, key_count), jnp.int32),
+            pltpu.VMEM((row_count // Q_ROWS, head_window.shape[0], Q_ROWS, key_count), F32),
             pltpu.VMEM((row_count, feat_width), BF16),
         ],
         compiler_params=pltpu.CompilerParams(vmem_limit_bytes=VMEM_LIMIT),
-        cost_estimate=pl.CostEstimate(flops=2 * macs, bytes_accessed=5 * own.size, transcendentals=0),
+        cost_estimate=pl.CostEstimate(flops=2 * macs, bytes_accessed=10 * own.size, transcendentals=0),
         name="forward",
-    )(place, head_window, own, left, right, *gains, *weights)
+    )(place, head_window, own, *projected, left, right, *gains, *weights)
 
 
 def gram_kernel(share_ref, grid_ref, out_ref):
@@ -352,16 +415,10 @@
         share_start.astype(jnp.int32).reshape(1), obs_token, obs_channel, obs_value, obs_var, share_rows, feat_width
     )
     place = jnp.stack([first_pos, row_count * tok_count]).astype(jnp.int32)
-    forecast = forward(
-        place,
-        head_window,
-        ens_state,
-        left,
-        right,
-        [attn_gain.reshape(1, -1), ffn_gain.reshape(1, -1)],
-        [w_query, w_key, w_value, w_out, w_gate, w_up, down_weight],
-        mem_count,
-    )
+    gains = [attn_gain.reshape(1, -1), ffn_gain.reshape(1, -1)]
+    projected = project(ens_state, head_window.shape[0], gains[0], w_query, w_key, w_value)
+    weights = [w_key, w_value, w_out, w_gate, w_up, down_weight]
+    forecast = forward(place, head_window, ens_state, projected, left, right, gains, weights, mem_count)
     share = lax.all_to_all(forecast, "mem", split_axis=0, concat_axis=0, tiled=True)
     share = share.reshape(members, share_rows, feat_width)
     partial = gram_partial(share, grid)

time: 99.9 us -> 98.5 us (0.986)
  waiting for transfers between devices: 12.2 us -> 9.48 us
  Pallas kernels: 35 us -> 36.8 us
    ppermute x1, waiting for transfers between devices: 4.48 us -> 2.1 us  [local(): right = lax.ppermute(ens_state[:, :WIN], 'tok', down)]
    pallas_call x0 -> x1, Pallas kernels: none -> 1.78 us  [project(): pl.pallas_call(functools.partial(project_kernel, heads), grid=(members,),...]
    slice x1, local copies, waits for them, and re-layouts: 2.4 us -> 1.38 us  [local(): right = lax.ppermute(ens_state[:, :WIN], 'tok', down)]
    unnamed x28 -> x30, local copies, waits for them, and re-layouts: 1.35 us -> 2.03 us
  transfers between devices with their start and end apart: 3 -> 3, of which waited for: 3 -> 2; matrix products, arithmetic and copies ran while one was open for 0% -> 0% of each run, Pallas kernels for 1% -> 3%
where the time goes in v6:
time: 98.5 us; the launch traced here: 98 us
  blocking collectives  39.6 us (40%)
  Pallas kernels  36.8 us (37%)
  waiting for transfers between devices  9.48 us (10%)
  starting transfers between devices  7.55 us (8%)
  local copies, waits for them, and re-layouts  4.46 us (5%)
    pallas_call x1, Pallas kernels, forward(): pl.pallas_call(forward_kernel, grid=(members,), out_shape=jax.ShapeDtypeS...  28.5 us
    all_to_all x1, blocking collectives, local(): lax.all_to_all(jnp.broadcast_to(partial[None], (device_count, *partial.sh...  22.2 us
    all_to_all x1, blocking collectives, local(): lax.all_to_all(mixed, 'mem', split_axis=0, concat_axis=0, tiled=True)  17.3 us
    all_to_all x1, waiting for transfers between devices, local(): lax.all_to_all(forecast, 'mem', split_axis=0, concat_axis=0, tiled=True)  7.38 us
    all_to_all x1, starting transfers between devices, local(): lax.all_to_all(forecast, 'mem', split_axis=0, concat_axis=0, tiled=True)  3.86 us
    pallas_call x1, Pallas kernels, combine(): pl.pallas_call(combine_kernel, out_shape=jax.ShapeDtypeStruct(share.shape...  3.64 us
    ppermute x1, starting transfers between devices, local(): left = lax.ppermute(ens_state[:, row_count - WIN:], 'tok', up)  2.4 us
    ppermute x1, waiting for transfers between devices, local(): right = lax.ppermute(ens_state[:, :WIN], 'tok', down)  2.1 us
  transfers between devices with their start and end apart: 3, of which 2 were waited for; matrix products, arithmetic and copies ran while one was open for 0% of the time, Pallas kernels for 3%

profile of v6, /device:TPU:0, one launch (start us, length us, event | category | flops | bytes accessed | tf_op | source)
XLA Modules:
  0.0 98.0 jit_solution(3127239472902958144)
XLA Ops:
  0.0 1.4 %fusion = (bf16[4,256,256]{2,1,0:T(8,128)(2,1)S(1)}, bf16[4,256,256]{2,1,0:T(8,128)(2,1)S(1)}) fusion(bf16[4,512,256]{2,1,0:T(8,128)(2,1)} %state_ref.1), kind=kLoop, calls=%fused_computation.1 | loop fusion | bytes 2097152 | tf_op jit(solution)/shard_map/slice | solution.py:412
  1.4 2.4 %collective-permute-start = (bf16[4,256,256]{2,1,0:T(8,128)(2,1)S(1)}, bf16[4,256,256]{2,1,0:T(8,128)(2,1)S(1)}, u32[]{:S(2)}, u32[]{:S(2)}) collective-permute-start(bf16[4,256,256]{2,1,0:T(8,128)(2,1)S(1)} %get-tuple-element.12), channel_id=1, source_target_pairs={{0,1},{1,2},{2,3},{3,4},{4,5},{5,6},{6,7},{8,9},{9,10},{10,11},{11... | collective-permute-start | bytes 1572872 | tf_op jit(solution)/shard_map/ppermute | solution.py:411
  3.8 1.3 %collective-permute-start.1 = (bf16[4,256,256]{2,1,0:T(8,128)(2,1)S(1)}, bf16[4,256,256]{2,1,0:T(8,128)(2,1)S(1)}, u32[]{:S(2)}, u32[]{:S(2)}) collective-permute-start(bf16[4,256,256]{2,1,0:T(8,128)(2,1)S(1)} %get-tuple-element.11), channel_id=1, source_target_pairs={{1,0},{2,1},{3,2},{4,3},{5,4},{6,5},{7,6},{9,8},{10,9},{11,10},{12... | collective-permute-start | bytes 1572872 | tf_op jit(solution)/shard_map/ppermute | solution.py:412
  5.1 0.0 copy-start.12
  5.1 0.0 copy-done
  5.1 0.0 copy-done.4
  5.1 0.0 copy-done.5
  5.1 0.0 copy-done.6
  5.2 0.6 copy-done.12
  5.8 1.8 %project.1 = (bf16[4,512,256]{2,1,0:T(8,128)(2,1)S(1)}, bf16[4,512,256]{2,1,0:T(8,128)(2,1)S(1)}, bf16[4,512,256]{2,1,0:T(8,128)(2,1)S(1)}) custom-call(bf16[4,512,256]{2,1,0:T(8,128)(2,1)S(1)} %copy-done, f32[1,256]{1,0:T(1,128)S(1)} %bitcast.19, bf16[256,256]{1,0:T(8,128)(2,1)S(1)} %copy-done.4, bf16[256,256]{1,0:T(8,128)(2,1)S(1)} %copy-done.5, ...), custom_call_target="tpu_custom_call" | custom-call | flops 805306368 | bytes 4194304 | tf_op jit(solution)/shard_map/project/pallas_call | solution.py:99
  7.6 0.1 pad_add_fusion.place_ref
  7.7 0.0 collective-permute-done.left_ref
  7.7 2.1 %collective-permute-done.1.right_ref = bf16[4,256,256]{2,1,0:T(8,128)(2,1)S(1)} collective-permute-done((bf16[4,256,256]{2,1,0:T(8,128)(2,1)S(1)}, bf16[4,256,256]{2,1,0:T(8,128)(2,1)S(1)}, u32[]{:S(2)}, u32[]{:S(2)}) %collective-permute-start.1) | collective-permute-done | bytes 524320 | tf_op jit(solution)/shard_map/ppermute | solution.py:412
  9.8 0.0 copy-done.1
  9.8 0.0 copy-done.2
  9.8 0.0 copy-done.3
  9.8 0.0 copy-done.7
  9.8 0.6 copy-done.13
  10.4 0.0 copy-done.14
  10.4 28.5 %forward.1 = bf16[4,4,128,256]{3,2,1,0:T(8,128)(2,1)} custom-call(s32[2]{0:T(128)S(1)} %pad_add_fusion.place_ref, s32[4]{0:T(128)S(1)} %copy-done.14, bf16[4,512,256]{2,1,0:T(8,128)(2,1)S(1)} %copy-done, bf16[4,512,256]{2,1,0:T(8,128)(2,1)S(1)} %get-tuple-element.8.query_ref, bf16[4,512,256]{2,1,0:T(8,128)(2,1)S(1)} %get-tuple-element.9.key_ref, ...), custom_call_target="tpu_custom_call" | custom-call | flops 9395240960 | bytes 5242880 | tf_op jit(solution)/shard_map/forward/pallas_call | solution.py:241
  38.9 3.9 %all-to-all-start = ((bf16[4,4,128,256]{3,2,1,0:T(8,128)(2,1)}), bf16[4,4,128,256]{3,2,1,0:T(8,128)(2,1)S(1)}, u32[]{:S(2)}, u32[]{:S(2)}) async-start(bf16[4,4,128,256]{3,2,1,0:T(8,128)(2,1)} %forward.1), calls=%async_computation | async-start | bytes 2097152 | tf_op jit(solution)/shard_map/all_to_all | solution.py:422
  42.8 0.0 copy-done.9
  42.8 0.0 copy-done.10
  42.8 0.0 copy-done.11
  42.8 0.7 copy-done.8
  43.5 1.3 %sample_grid.1.grid_ref = f32[2,128,256]{2,1,0:T(8,128)S(1)} custom-call(s32[1]{0:T(128)} %bitcast.4.start_ref, s32[1,4096]{1,0:T(1,128)S(1)} %bitcast.15, s32[1,4096]{1,0:T(1,128)S(1)} %bitcast.16, f32[1,4096]{1,0:T(1,128)S(1)} %bitcast.17, f32[1,4096]{1,0:T(1,128)S(1)} %bitcast.18), custom_call_target="tpu_custom_call" | custom-call | flops 1073741824 | bytes 65536 | tf_op jit(solution)/shard_map/sample_grid/pallas_call | solution.py:77
  44.9 7.4 %all-to-all-done = bf16[4,4,128,256]{3,2,1,0:T(8,128)(2,1)S(1)} async-done(((bf16[4,4,128,256]{3,2,1,0:T(8,128)(2,1)}), bf16[4,4,128,256]{3,2,1,0:T(8,128)(2,1)S(1)}, u32[]{:S(2)}, u32[]{:S(2)}) %all-to-all-start) | async-done | bytes 1048608 | tf_op jit(solution)/shard_map/all_to_all | solution.py:422
  52.2 1.5 %gram.1 = f32[8,128]{1,0:T(8,128)S(1)} custom-call(bf16[16,128,256]{2,1,0:T(8,128)(2,1)S(1)} %bitcast.12, f32[2,128,256]{2,1,0:T(8,128)S(1)} %sample_grid.1.grid_ref), custom_call_target="tpu_custom_call" | custom-call | flops 805306368 | bytes 1048576 | tf_op jit(solution)/shard_map/gram/pallas_call | solution.py:297
  53.8 22.2 %all_to_all.15.partial_ref = f32[32,8,128]{2,1,0:T(8,128)S(1)} all-to-all(f32[32,8,128]{2,1,0:T(8,128)S(1)} %broadcast_in_dim.2), channel_id=1, replica_groups=mesh['mem'=4,'tok'=8] {'mem','tok'}, dimensions={0} | all-to-all | bytes 262144 | tf_op jit(solution)/shard_map/all_to_all | solution.py:425
  76.0 3.6 %combine.1 = bf16[16,128,256]{2,1,0:T(8,128)(2,1)S(1)} custom-call(f32[32,8,128]{2,1,0:T(8,128)S(1)} %all_to_all.15.partial_ref, bf16[16,128,256]{2,1,0:T(8,128)(2,1)S(1)} %bitcast.13), custom_call_target="tpu_custom_call" | custom-call | flops 536870912 | bytes 2097152 | tf_op jit(solution)/shard_map/combine/pallas_call | solution.py:372
  79.7 17.3 %all_to_all.16 = bf16[4,4,128,256]{3,2,1,0:T(8,128)(2,1)S(1)} all-to-all(bf16[4,4,128,256]{3,2,1,0:T(8,128)(2,1)S(1)} %bitcast.14), channel_id=1, replica_groups=mesh['mem'=4,'tok'=8] {'mem'}, dimensions={0} | all-to-all | bytes 2097152 | tf_op jit(solution)/shard_map/all_to_all | solution.py:433
  97.0 1.0 %copy.16 = bf16[4,4,128,256]{3,2,1,0:T(8,128)(2,1)} copy(bf16[4,4,128,256]{3,2,0,1:T(8,128)(2,1)S(1)} %bitcast.22) | data formatting | bytes 2097152 | tf_op jit(solution)/shard_map/transpose | solution.py:434
  (15 shorter events, 0.0 us)
Async XLA Ops:
  0.0 5.1 %copy-start = (bf16[4,512,256]{2,1,0:T(8,128)(2,1)S(1)}, bf16[4,512,256]{2,1,0:T(8,128)(2,1)}, u32[]{:S(2)}) copy-start(bf16[4,512,256]{2,1,0:T(8,128)(2,1)} %state_ref.1) | copy-start | bytes 3145732
  0.0 5.1 %copy-start.4 = (bf16[256,256]{1,0:T(8,128)(2,1)S(1)}, bf16[256,256]{1,0:T(8,128)(2,1)}, u32[]{:S(2)}) copy-start(bf16[256,256]{1,0:T(8,128)(2,1)} %w_query_ref.1) | copy-start | bytes 393220
  0.0 5.1 %copy-start.5 = (bf16[256,256]{1,0:T(8,128)(2,1)S(1)}, bf16[256,256]{1,0:T(8,128)(2,1)}, u32[]{:S(2)}) copy-start(bf16[256,256]{1,0:T(8,128)(2,1)} %w_key_ref.3) | copy-start | bytes 393220
  0.0 5.1 %copy-start.6 = (bf16[256,256]{1,0:T(8,128)(2,1)S(1)}, bf16[256,256]{1,0:T(8,128)(2,1)}, u32[]{:S(2)}) copy-start(bf16[256,256]{1,0:T(8,128)(2,1)} %w_value_ref.3) | copy-start | bytes 393220
  1.4 6.3 %collective-permute-start = (bf16[4,256,256]{2,1,0:T(8,128)(2,1)S(1)}, bf16[4,256,256]{2,1,0:T(8,128)(2,1)S(1)}, u32[]{:S(2)}, u32[]{:S(2)}) collective-permute-start(bf16[4,256,256]{2,1,0:T(8,128)(2,1)S(1)} %get-tuple-element.12), channel_id=1, source_target_pairs={{0,1},{1,2},{2,3},{3,4},{4,5},{5,6},{6,7},{8,9},{9,10},{10,11},{11... | collective-permute-start | bytes 1572872 | tf_op jit(solution)/shard_map/ppermute | solution.py:411
  3.8 6.0 %collective-permute-start.1 = (bf16[4,256,256]{2,1,0:T(8,128)(2,1)S(1)}, bf16[4,256,256]{2,1,0:T(8,128)(2,1)S(1)}, u32[]{:S(2)}, u32[]{:S(2)}) collective-permute-start(bf16[4,256,256]{2,1,0:T(8,128)(2,1)S(1)} %get-tuple-element.11), channel_id=1, source_target_pairs={{1,0},{2,1},{3,2},{4,3},{5,4},{6,5},{7,6},{9,8},{10,9},{11,10},{12... | collective-permute-start | bytes 1572872 | tf_op jit(solution)/shard_map/ppermute | solution.py:412
  5.1 0.7 copy-start.12
  5.8 4.0 %copy-start.1 = (bf16[256,1024]{1,0:T(8,128)(2,1)S(1)}, bf16[256,1024]{1,0:T(8,128)(2,1)}, u32[]{:S(2)}) copy-start(bf16[256,1024]{1,0:T(8,128)(2,1)} %w_gate_ref.1) | copy-start | bytes 1572868
  5.8 4.0 %copy-start.2 = (bf16[256,1024]{1,0:T(8,128)(2,1)S(1)}, bf16[256,1024]{1,0:T(8,128)(2,1)}, u32[]{:S(2)}) copy-start(bf16[256,1024]{1,0:T(8,128)(2,1)} %w_up_ref.1) | copy-start | bytes 1572868
  5.8 4.0 %copy-start.3 = (bf16[1024,256]{1,0:T(8,128)(2,1)S(1)}, bf16[1024,256]{1,0:T(8,128)(2,1)}, u32[]{:S(2)}) copy-start(bf16[1024,256]{1,0:T(8,128)(2,1)} %down_weight_ref.1) | copy-start | bytes 1572868
  5.8 4.0 %copy-start.7 = (bf16[256,256]{1,0:T(8,128)(2,1)S(1)}, bf16[256,256]{1,0:T(8,128)(2,1)}, u32[]{:S(2)}) copy-start(bf16[256,256]{1,0:T(8,128)(2,1)} %w_out_ref.1) | copy-start | bytes 393220
  9.8 0.7 copy-start.13
  9.8 0.7 copy-start.14
  38.9 3.9 %copy-start.9 = (s32[4096]{0:T(1024)S(1)}, s32[4096]{0:T(1024)}, u32[]{:S(2)}) copy-start(s32[4096]{0:T(1024)} %param.27) | copy-start | bytes 49156
  38.9 3.9 %copy-start.10 = (f32[4096]{0:T(1024)S(1)}, f32[4096]{0:T(1024)}, u32[]{:S(2)}) copy-start(f32[4096]{0:T(1024)} %param.28) | copy-start | bytes 49156
  38.9 3.9 %copy-start.11 = (f32[4096]{0:T(1024)S(1)}, f32[4096]{0:T(1024)}, u32[]{:S(2)}) copy-start(f32[4096]{0:T(1024)} %param.29) | copy-start | bytes 49156
  38.9 13.3 %all-to-all-start = ((bf16[4,4,128,256]{3,2,1,0:T(8,128)(2,1)}), bf16[4,4,128,256]{3,2,1,0:T(8,128)(2,1)S(1)}, u32[]{:S(2)}, u32[]{:S(2)}) async-start(bf16[4,4,128,256]{3,2,1,0:T(8,128)(2,1)} %forward.1), calls=%async_computation | async-start | bytes 2097152 | tf_op jit(solution)/shard_map/all_to_all | solution.py:422
  42.8 0.7 copy-start.8

commit v7 on v6

--- a/solution.py
+++ b/solution.py
@@ -85,23 +85,45 @@
     )(start, *(v.reshape(1, count) for v in (obs_token, obs_channel, obs_value, obs_var)))
 
 
-def project_kernel(heads, own_ref, gain_ref, w_query_ref, w_key_ref, w_value_ref, query_ref, key_ref, value_ref):
+def head_lanes(feat_width, heads):
+    lane_head = iota((feat_width, LANES), 0) // (feat_width // heads)
+    return (lane_head == iota((feat_width, LANES), 1)).astype(F32).astype(BF16)
+
+
+def largest_norms(values, heads):
+    squares = dot((values * values).astype(BF16), head_lanes(values.shape[1], heads))
+    return jnp.max(squares, axis=0, keepdims=True)
+
+
+def project_kernel(
+    heads, own_ref, gain_ref, w_query_ref, w_key_ref, w_value_ref, query_ref, key_ref, value_ref, norm_ref
+):
     scale = math.log2(math.e) / math.sqrt(own_ref.shape[2] // heads)
     normed = rms_scaled(own_ref[0].astype(F32), gain_ref[...]).astype(BF16)
-    query_ref[0] = (dot(normed, w_query_ref[...]) * scale).astype(BF16)
-    key_ref[0] = dot(normed, w_key_ref[...]).astype(BF16)
+    queries = dot(normed, w_query_ref[...]) * scale
+    keys = dot(normed, w_key_ref[...])
+    query_ref[0] = queries.astype(BF16)
+    key_ref[0] = keys.T.astype(BF16)
     value_ref[0] = dot(normed, w_value_ref[...]).astype(BF16)
+    blank = jnp.zeros((norm_ref.shape[1] - 2, LANES), F32)
+    norm_ref[0] = jnp.concatenate([largest_norms(queries, heads), largest_norms(keys, heads), blank], axis=0)
 
 
 def project(own, heads, gain, w_query, w_key, w_value):
     members, rows, feat_width = own.shape
-    block = pl.BlockSpec((1, rows, feat_width), lambda m: (m, 0, 0))
+    upright = (members, rows, feat_width)
+    shapes = [upright, (members, feat_width, rows), upright]
+    norm_shape = (members, 8, LANES)
+
+    def spec(shape):
+        return pl.BlockSpec((1, *shape[1:]), lambda m: (m, 0, 0))
+
     return pl.pallas_call(
         functools.partial(project_kernel, heads),
         grid=(members,),
-        out_shape=[jax.ShapeDtypeStruct((members, rows, feat_width), BF16)] * 3,
-        in_specs=[block] + [vmem_spec()] * 4,
-        out_specs=[block] * 3,
+        out_shape=[jax.ShapeDtypeStruct(v, BF16) for v in shapes] + [jax.ShapeDtypeStruct(norm_shape, F32)],
+        in_specs=[spec(upright)] + [vmem_spec()] * 4,
+        out_specs=[spec(v) for v in (*shapes, norm_shape)],
         compiler_params=pltpu.CompilerParams(vmem_limit_bytes=VMEM_LIMIT),
         cost_estimate=pl.CostEstimate(
             flops=6 * own.size * feat_width, bytes_accessed=8 * own.size, transcendentals=0
@@ -117,6 +139,7 @@
     query_ref,
     key_ref,
     value_ref,
+    norm_ref,
     left_ref,
     right_ref,
     attn_gain_ref,
@@ -137,6 +160,7 @@
     reach = left_ref.shape[1]
     head_count = window_ref.shape[0]
     head_size = feat_width // head_count
+    group_heads = LANES // head_size
     blocks = rows // Q_ROWS
     key_count = Q_ROWS + 2 * reach
 
@@ -149,44 +173,51 @@
             for head in range(head_count):
                 bias_buf[block, head] = jnp.where(inside & (apart <= window_ref[head]), 0.0, -1e30)
 
-    key_buf[reach : reach + rows] = key_ref[0]
+    key_buf[:, reach : reach + rows] = key_ref[0]
     value_buf[reach : reach + rows] = value_ref[0]
+    key_norms = norm_ref[0, 1:2, :]
     for ref, lower in ((left_ref, 0), (right_ref, reach + rows)):
         normed = rms_scaled(ref[0].astype(F32), attn_gain_ref[...]).astype(BF16)
-        key_buf[lower : lower + reach] = dot(normed, w_key_ref[...]).astype(BF16)
+        keys = dot(normed, w_key_ref[...])
+        key_norms = jnp.maximum(key_norms, largest_norms(keys, head_count))
+        key_buf[:, lower : lower + reach] = keys.T.astype(BF16)
         value_buf[lower : lower + reach] = dot(normed, w_value_ref[...]).astype(BF16)
 
-    column_head = iota((1, feat_width), 1) // head_size
-    head_masks = [(column_head == head).astype(F32).astype(BF16) for head in range(head_count)]
-    by_head = (iota((feat_width, LANES), 0) // head_size == iota((feat_width, LANES), 1)).astype(F32).astype(BF16)
-
-    def largest_norm(values):
-        squares = values.astype(F32)
-        return jnp.max(dot((squares * squares).astype(BF16), by_head), axis=0, keepdims=True)
-
-    bound = jnp.max(largest_norm(query_ref[0]) * largest_norm(key_buf[...])) * 1.02
+    bound = jnp.max(norm_ref[0, 0:1, :] * key_norms) * 1.05
     safe = bound <= SAFE_SCORE * SAFE_SCORE
 
-    def joined_heads(mixed_all, totals, count):
+    lane_head = iota((1, LANES), 1) // head_size
+    head_masks = [(lane_head == head).astype(F32).astype(BF16) for head in range(group_heads)]
+
+    def scores_of(start, count, group):
+        lanes = slice(group * LANES, (group + 1) * LANES)
+        queries = query_ref[0, pl.ds(start, count), lanes]
+        stacked = jnp.concatenate([queries * mask for mask in head_masks], axis=0)
+        return dot(stacked, key_buf[lanes, pl.ds(start, count + 2 * reach)])
+
+    def mix_values(start, count, group, weights, totals):
+        lanes = slice(group * LANES, (group + 1) * LANES)
+        mixed_all = dot(jnp.concatenate(weights, axis=0), value_buf[pl.ds(start, count + 2 * reach), lanes])
         mixed = mixed_all[:count] * (1.0 / totals[0])
-        for head in range(1, head_count):
+        for head in range(1, group_heads):
             part = mixed_all[head * count : (head + 1) * count] * (1.0 / totals[head])
-            mixed = jnp.where(column_head == head, part, mixed)
-        return mixed.astype(BF16)
+            mixed = jnp.where(lane_head == head, part, mixed)
+        mixed_buf[pl.ds(start, count), lanes] = mixed.astype(BF16)
+
+    groups = head_count // group_heads
 
     @pl.when(safe)
     def _():
         pair = 2 * Q_ROWS
-        span = pair + 2 * reach
         corner = jnp.zeros((Q_ROWS, Q_ROWS), BF16)
-        for start in range(0, rows, pair):
-            queries = query_ref[0, start : start + pair, :]
-            stacked = jnp.concatenate([queries * mask for mask in head_masks], axis=0)
-            scores = dot(stacked, key_buf[start : start + span, :], ((1,), (1,)))
+        units = [(start, group) for start in range(0, rows, pair) for group in range(groups)]
+        scores = scores_of(units[0][0], pair, units[0][1])
+        for at, (start, group) in enumerate(units):
+            following = scores_of(units[at + 1][0], pair, units[at + 1][1]) if at + 1 < len(units) else None
             weights, totals = [], []
-            for head in range(head_count):
+            for head in range(group_heads):
                 top = head * pair
-                bias = [bias_buf[start // Q_ROWS + part, head] for part in range(2)]
+                bias = [bias_buf[start // Q_ROWS + part, group * group_heads + head] for part in range(2)]
                 upper = jnp.exp2(scores[top : top + Q_ROWS, :key_count] + bias[0])
                 lower = jnp.exp2(scores[top + Q_ROWS : top + pair, Q_ROWS:] + bias[1])
                 totals.append(
@@ -194,35 +225,31 @@
                 )
                 weights.append(jnp.concatenate([upper.astype(BF16), corner], axis=1))
                 weights.append(jnp.concatenate([corner, lower.astype(BF16)], axis=1))
-            mixed_all = dot(jnp.concatenate(weights, axis=0), value_buf[start : start + span, :])
-            mixed_buf[start : start + pair, :] = joined_heads(mixed_all, totals, pair)
+            mix_values(start, pair, group, weights, totals)
+            scores = following
 
     @pl.when(jnp.logical_not(safe))
     def _():
-        def one_block(block, carry):
-            start = pl.multiple_of(block * Q_ROWS, Q_ROWS)
-            queries = query_ref[0, pl.ds(start, Q_ROWS), :]
-            stacked = jnp.concatenate([queries * mask for mask in head_masks], axis=0)
-            scores = dot(stacked, key_buf[pl.ds(start, key_count), :], ((1,), (1,)))
-            weights, totals = [], []
-            for head in range(head_count):
-                score_matrix = scores[head * Q_ROWS : (head + 1) * Q_ROWS] + bias_buf[block, head]
-                expo = jnp.exp2(score_matrix - jnp.max(score_matrix, axis=-1, keepdims=True))
-                totals.append(jnp.sum(expo, axis=-1, keepdims=True))
-                weights.append(expo.astype(BF16))
-            mixed_all = dot(jnp.concatenate(weights, axis=0), value_buf[pl.ds(start, key_count), :])
-            mixed_buf[pl.ds(start, Q_ROWS), :] = joined_heads(mixed_all, totals, Q_ROWS)
-            return carry
-
-        lax.fori_loop(0, blocks, one_block, 0)
+        for block in range(blocks):
+            start = block * Q_ROWS
+            for group in range(groups):
+                scores = scores_of(start, Q_ROWS, group)
+                weights, totals = [], []
+                for head in range(group_heads):
+                    score_matrix = scores[head * Q_ROWS : (head + 1) * Q_ROWS]
+                    score_matrix = score_matrix + bias_buf[block, group * group_heads + head]
+                    expo = jnp.exp2(score_matrix - jnp.max(score_matrix, axis=-1, keepdims=True))
+                    totals.append(jnp.sum(expo, axis=-1, keepdims=True))
+                    weights.append(expo.astype(BF16))
+                mix_values(start, Q_ROWS, group, weights, totals)
 
     after = (state_ref[0].astype(F32) + dot(mixed_buf[...], w_out_ref[...])).astype(BF16)
     normed_mid = rms_scaled(after.astype(F32), ffn_gain_ref[...]).astype(BF16)
     forecast = after.astype(F32)
     for lower in range(0, w_gate_ref.shape[1], HIDDEN_CHUNK):
         part = slice(lower, lower + HIDDEN_CHUNK)
-        gate = dot(normed_mid, w_gate_ref[:, part])
-        hidden = (gate * (0.5 + 0.5 * jnp.tanh(0.5 * gate)) * dot(normed_mid, w_up_ref[:, part])).astype(BF16)
+        gate = 0.5 * dot(normed_mid, w_gate_ref[:, part])
+        hidden = (gate * (1.0 + jnp.tanh(gate)) * dot(normed_mid, w_up_ref[:, part])).astype(BF16)
         forecast += dot(hidden, down_weight_ref[part, :])
     forecast = forecast.astype(BF16)
     shares, _, share_rows, _ = out_ref.shape
@@ -236,19 +263,18 @@
     key_count = Q_ROWS + 2 * reach
     hidden_width = weights[3].shape[1]
     macs = members * row_count * feat_width * (3 * feat_width + 3 * hidden_width + 8 * key_count)
-    member_block = pl.BlockSpec((1, row_count, feat_width), lambda m: (m, 0, 0))
     edge_block = pl.BlockSpec((1, reach, feat_width), lambda m: (m, 0, 0))
     return pl.pallas_call(
         forward_kernel,
         grid=(members,),
         out_shape=jax.ShapeDtypeStruct((shares, members, row_count // shares, feat_width), BF16),
         in_specs=[smem_spec()] * 2
-        + [member_block] * (1 + len(projected))
+        + [pl.BlockSpec((1, *v.shape[1:]), lambda m: (m, 0, 0)) for v in (own, *projected)]
         + [edge_block] * 2
         + [vmem_spec()] * (len(gains) + len(weights)),
         out_specs=pl.BlockSpec((shares, 1, row_count // shares, feat_width), lambda m: (0, m, 0, 0)),
         scratch_shapes=[
-            pltpu.VMEM((row_count + 2 * reach, feat_width), BF16),
+            pltpu.VMEM((feat_width, row_count + 2 * reach), BF16),
             pltpu.VMEM((row_count + 2 * reach, feat_width), BF16),
             pltpu.VMEM((row_count // Q_ROWS, head_window.shape[0], Q_ROWS, key_count), F32),
             pltpu.VMEM((row_count, feat_width), BF16),

time: 98.5 us -> 93.2 us (0.946)
  Pallas kernels: 36.8 us -> 32 us
    pallas_call x1, Pallas kernels: 28.5 us -> 23.2 us  [forward(): pl.pallas_call(forward_kernel, grid=(members,), out_shape=jax.ShapeDtypeS...]
  transfers between devices with their start and end apart: 3 -> 3, of which waited for: 2 -> 2; matrix products, arithmetic and copies ran while one was open for 0% -> 0% of each run, Pallas kernels for 3% -> 4%
where the time goes in v7:
time: 93.2 us; the launch traced here: 92.8 us
  blocking collectives  39.6 us (42%)
  Pallas kernels  32 us (34%)
  waiting for transfers between devices  8.91 us (10%)
  starting transfers between devices  7.58 us (8%)
  local copies, waits for them, and re-layouts  4.46 us (5%)
    pallas_call x1, Pallas kernels, forward(): pl.pallas_call(forward_kernel, grid=(members,), out_shape=jax.ShapeDtypeS...  23.2 us
    all_to_all x1, blocking collectives, local(): lax.all_to_all(jnp.broadcast_to(partial[None], (device_count, *partial.sh...  22.2 us
    all_to_all x1, blocking collectives, local(): lax.all_to_all(mixed, 'mem', split_axis=0, concat_axis=0, tiled=True)  17.3 us
    all_to_all x1, waiting for transfers between devices, local(): lax.all_to_all(forecast, 'mem', split_axis=0, concat_axis=0, tiled=True)  7.38 us
    all_to_all x1, starting transfers between devices, local(): lax.all_to_all(forecast, 'mem', split_axis=0, concat_axis=0, tiled=True)  3.89 us
    pallas_call x1, Pallas kernels, combine(): pl.pallas_call(combine_kernel, out_shape=jax.ShapeDtypeStruct(share.shape...  3.64 us
    ppermute x1, starting transfers between devices, local(): left = lax.ppermute(ens_state[:, row_count - WIN:], 'tok', up)  2.4 us
    pallas_call x1, Pallas kernels, project(): pl.pallas_call(functools.partial(project_kernel, heads), grid=(members,),...  2.35 us
  transfers between devices with their start and end apart: 3, of which 2 were waited for; matrix products, arithmetic and copies ran while one was open for 0% of the time, Pallas kernels for 4%

profile of v7, /device:TPU:0, one launch (start us, length us, event | category | flops | bytes accessed | tf_op | source)
XLA Modules:
  0.0 92.8 jit_solution(11524450493801291440)
XLA Ops:
  0.0 1.4 %fusion = (bf16[4,256,256]{2,1,0:T(8,128)(2,1)S(1)}, bf16[4,256,256]{2,1,0:T(8,128)(2,1)S(1)}) fusion(bf16[4,512,256]{2,1,0:T(8,128)(2,1)} %state_ref.1), kind=kLoop, calls=%fused_computation.1 | loop fusion | bytes 2097152 | tf_op jit(solution)/shard_map/slice | solution.py:438
  1.4 2.4 %collective-permute-start = (bf16[4,256,256]{2,1,0:T(8,128)(2,1)S(1)}, bf16[4,256,256]{2,1,0:T(8,128)(2,1)S(1)}, u32[]{:S(2)}, u32[]{:S(2)}) collective-permute-start(bf16[4,256,256]{2,1,0:T(8,128)(2,1)S(1)} %get-tuple-element.14), channel_id=1, source_target_pairs={{0,1},{1,2},{2,3},{3,4},{4,5},{5,6},{6,7},{8,9},{9,10},{10,11},{11... | collective-permute-start | bytes 1572872 | tf_op jit(solution)/shard_map/ppermute | solution.py:437
  3.8 1.3 %collective-permute-start.1 = (bf16[4,256,256]{2,1,0:T(8,128)(2,1)S(1)}, bf16[4,256,256]{2,1,0:T(8,128)(2,1)S(1)}, u32[]{:S(2)}, u32[]{:S(2)}) collective-permute-start(bf16[4,256,256]{2,1,0:T(8,128)(2,1)S(1)} %get-tuple-element.13), channel_id=1, source_target_pairs={{1,0},{2,1},{3,2},{4,3},{5,4},{6,5},{7,6},{9,8},{10,9},{11,10},{12... | collective-permute-start | bytes 1572872 | tf_op jit(solution)/shard_map/ppermute | solution.py:438
  5.1 0.0 copy-start.12
  5.1 0.0 copy-done
  5.1 0.0 copy-done.4
  5.1 0.0 copy-done.5
  5.1 0.0 copy-done.6
  5.2 0.6 copy-done.12
  5.8 2.3 %project.1 = (bf16[4,512,256]{2,1,0:T(8,128)(2,1)S(1)}, bf16[4,256,512]{2,1,0:T(8,128)(2,1)S(1)}, bf16[4,512,256]{2,1,0:T(8,128)(2,1)S(1)}, f32[4,8,128]{2,1,0:T(8,128)S(1)}) custom-call(bf16[4,512,256]{2,1,0:T(8,128)(2,1)S(1)} %copy-done, f32[1,256]{1,0:T(1,128)S(1)} %bitcast.19, bf16[256,256]{1,0:T(8,128)(2,1)S(1)} %copy-done.4, ...), custom_call_target="tpu_custom_call" | custom-call | flops 805306368 | bytes 4194304 | tf_op jit(solution)/shard_map/project/pallas_call | solution.py:121
  8.2 0.1 pad_add_fusion.place_ref
  8.2 0.0 collective-permute-done.left_ref
  8.2 1.5 %collective-permute-done.1.right_ref = bf16[4,256,256]{2,1,0:T(8,128)(2,1)S(1)} collective-permute-done((bf16[4,256,256]{2,1,0:T(8,128)(2,1)S(1)}, bf16[4,256,256]{2,1,0:T(8,128)(2,1)S(1)}, u32[]{:S(2)}, u32[]{:S(2)}) %collective-permute-start.1) | collective-permute-done | bytes 524320 | tf_op jit(solution)/shard_map/ppermute | solution.py:438
  9.8 0.0 copy-done.1
  9.8 0.0 copy-done.2
  9.8 0.0 copy-done.3
  9.8 0.0 copy-done.7
  9.8 0.6 copy-done.13
  10.4 0.0 copy-done.14
  10.4 23.2 %forward.1 = bf16[4,4,128,256]{3,2,1,0:T(8,128)(2,1)} custom-call(s32[2]{0:T(128)S(1)} %pad_add_fusion.place_ref, s32[4]{0:T(128)S(1)} %copy-done.14, bf16[4,512,256]{2,1,0:T(8,128)(2,1)S(1)} %copy-done, bf16[4,512,256]{2,1,0:T(8,128)(2,1)S(1)} %get-tuple-element.9.query_ref, bf16[4,256,512]{2,1,0:T(8,128)(2,1)S(1)} %get-tuple-element.10.key_ref, ...), custom_call_target="tpu_custom_call" | custom-call | flops 9395240960 | bytes 5242880 | tf_op jit(solution)/shard_map/forward/pallas_call | solution.py:267
  33.7 3.9 %all-to-all-start = ((bf16[4,4,128,256]{3,2,1,0:T(8,128)(2,1)}), bf16[4,4,128,256]{3,2,1,0:T(8,128)(2,1)S(1)}, u32[]{:S(2)}, u32[]{:S(2)}) async-start(bf16[4,4,128,256]{3,2,1,0:T(8,128)(2,1)} %forward.1), calls=%async_computation | async-start | bytes 2097152 | tf_op jit(solution)/shard_map/all_to_all | solution.py:448
  37.6 0.0 copy-done.9
  37.6 0.0 copy-done.10
  37.6 0.0 copy-done.11
  37.6 0.7 copy-done.8
  38.3 1.3 %sample_grid.1.grid_ref = f32[2,128,256]{2,1,0:T(8,128)S(1)} custom-call(s32[1]{0:T(128)} %bitcast.4.start_ref, s32[1,4096]{1,0:T(1,128)S(1)} %bitcast.15, s32[1,4096]{1,0:T(1,128)S(1)} %bitcast.16, f32[1,4096]{1,0:T(1,128)S(1)} %bitcast.17, f32[1,4096]{1,0:T(1,128)S(1)} %bitcast.18), custom_call_target="tpu_custom_call" | custom-call | flops 1073741824 | bytes 65536 | tf_op jit(solution)/shard_map/sample_grid/pallas_call | solution.py:77
  39.6 7.4 %all-to-all-done = bf16[4,4,128,256]{3,2,1,0:T(8,128)(2,1)S(1)} async-done(((bf16[4,4,128,256]{3,2,1,0:T(8,128)(2,1)}), bf16[4,4,128,256]{3,2,1,0:T(8,128)(2,1)S(1)}, u32[]{:S(2)}, u32[]{:S(2)}) %all-to-all-start) | async-done | bytes 1048608 | tf_op jit(solution)/shard_map/all_to_all | solution.py:448
  47.0 1.5 %gram.1 = f32[8,128]{1,0:T(8,128)S(1)} custom-call(bf16[16,128,256]{2,1,0:T(8,128)(2,1)S(1)} %bitcast.12, f32[2,128,256]{2,1,0:T(8,128)S(1)} %sample_grid.1.grid_ref), custom_call_target="tpu_custom_call" | custom-call | flops 805306368 | bytes 1048576 | tf_op jit(solution)/shard_map/gram/pallas_call | solution.py:323
  48.5 22.2 %all_to_all.15.partial_ref = f32[32,8,128]{2,1,0:T(8,128)S(1)} all-to-all(f32[32,8,128]{2,1,0:T(8,128)S(1)} %broadcast_in_dim.2), channel_id=1, replica_groups=mesh['mem'=4,'tok'=8] {'mem','tok'}, dimensions={0} | all-to-all | bytes 262144 | tf_op jit(solution)/shard_map/all_to_all | solution.py:451
  70.8 3.6 %combine.1 = bf16[16,128,256]{2,1,0:T(8,128)(2,1)S(1)} custom-call(f32[32,8,128]{2,1,0:T(8,128)S(1)} %all_to_all.15.partial_ref, bf16[16,128,256]{2,1,0:T(8,128)(2,1)S(1)} %bitcast.13), custom_call_target="tpu_custom_call" | custom-call | flops 536870912 | bytes 2097152 | tf_op jit(solution)/shard_map/combine/pallas_call | solution.py:398
  74.4 17.3 %all_to_all.16 = bf16[4,4,128,256]{3,2,1,0:T(8,128)(2,1)S(1)} all-to-all(bf16[4,4,128,256]{3,2,1,0:T(8,128)(2,1)S(1)} %bitcast.14), channel_id=1, replica_groups=mesh['mem'=4,'tok'=8] {'mem'}, dimensions={0} | all-to-all | bytes 2097152 | tf_op jit(solution)/shard_map/all_to_all | solution.py:459
  91.7 1.0 %copy.16 = bf16[4,4,128,256]{3,2,1,0:T(8,128)(2,1)} copy(bf16[4,4,128,256]{3,2,0,1:T(8,128)(2,1)S(1)} %bitcast.22) | data formatting | bytes 2097152 | tf_op jit(solution)/shard_map/transpose | solution.py:460
  (15 shorter events, 0.0 us)
Async XLA Ops:
  0.0 5.1 %copy-start = (bf16[4,512,256]{2,1,0:T(8,128)(2,1)S(1)}, bf16[4,512,256]{2,1,0:T(8,128)(2,1)}, u32[]{:S(2)}) copy-start(bf16[4,512,256]{2,1,0:T(8,128)(2,1)} %state_ref.1) | copy-start | bytes 3145732
  0.0 5.1 %copy-start.4 = (bf16[256,256]{1,0:T(8,128)(2,1)S(1)}, bf16[256,256]{1,0:T(8,128)(2,1)}, u32[]{:S(2)}) copy-start(bf16[256,256]{1,0:T(8,128)(2,1)} %w_query_ref.1) | copy-start | bytes 393220
  0.0 5.1 %copy-start.5 = (bf16[256,256]{1,0:T(8,128)(2,1)S(1)}, bf16[256,256]{1,0:T(8,128)(2,1)}, u32[]{:S(2)}) copy-start(bf16[256,256]{1,0:T(8,128)(2,1)} %w_key_ref.3) | copy-start | bytes 393220
  0.0 5.1 %copy-start.6 = (bf16[256,256]{1,0:T(8,128)(2,1)S(1)}, bf16[256,256]{1,0:T(8,128)(2,1)}, u32[]{:S(2)}) copy-start(bf16[256,256]{1,0:T(8,128)(2,1)} %w_value_ref.3) | copy-start | bytes 393220
  1.4 6.8 %collective-permute-start = (bf16[4,256,256]{2,1,0:T(8,128)(2,1)S(1)}, bf16[4,256,256]{2,1,0:T(8,128)(2,1)S(1)}, u32[]{:S(2)}, u32[]{:S(2)}) collective-permute-start(bf16[4,256,256]{2,1,0:T(8,128)(2,1)S(1)} %get-tuple-element.14), channel_id=1, source_target_pairs={{0,1},{1,2},{2,3},{3,4},{4,5},{5,6},{6,7},{8,9},{9,10},{10,11},{11... | collective-permute-start | bytes 1572872 | tf_op jit(solution)/shard_map/ppermute | solution.py:437
  3.8 6.0 %collective-permute-start.1 = (bf16[4,256,256]{2,1,0:T(8,128)(2,1)S(1)}, bf16[4,256,256]{2,1,0:T(8,128)(2,1)S(1)}, u32[]{:S(2)}, u32[]{:S(2)}) collective-permute-start(bf16[4,256,256]{2,1,0:T(8,128)(2,1)S(1)} %get-tuple-element.13), channel_id=1, source_target_pairs={{1,0},{2,1},{3,2},{4,3},{5,4},{6,5},{7,6},{9,8},{10,9},{11,10},{12... | collective-permute-start | bytes 1572872 | tf_op jit(solution)/shard_map/ppermute | solution.py:438
  5.1 0.7 copy-start.12
  5.8 4.0 %copy-start.1 = (bf16[256,1024]{1,0:T(8,128)(2,1)S(1)}, bf16[256,1024]{1,0:T(8,128)(2,1)}, u32[]{:S(2)}) copy-start(bf16[256,1024]{1,0:T(8,128)(2,1)} %w_gate_ref.1) | copy-start | bytes 1572868
  5.8 4.0 %copy-start.2 = (bf16[256,1024]{1,0:T(8,128)(2,1)S(1)}, bf16[256,1024]{1,0:T(8,128)(2,1)}, u32[]{:S(2)}) copy-start(bf16[256,1024]{1,0:T(8,128)(2,1)} %w_up_ref.1) | copy-start | bytes 1572868
  5.8 4.0 %copy-start.3 = (bf16[1024,256]{1,0:T(8,128)(2,1)S(1)}, bf16[1024,256]{1,0:T(8,128)(2,1)}, u32[]{:S(2)}) copy-start(bf16[1024,256]{1,0:T(8,128)(2,1)} %down_weight_ref.1) | copy-start | bytes 1572868
  5.8 4.0 %copy-start.7 = (bf16[256,256]{1,0:T(8,128)(2,1)S(1)}, bf16[256,256]{1,0:T(8,128)(2,1)}, u32[]{:S(2)}) copy-start(bf16[256,256]{1,0:T(8,128)(2,1)} %w_out_ref.1) | copy-start | bytes 393220
  9.8 0.7 copy-start.13
  9.8 0.7 copy-start.14
  33.7 3.9 %copy-start.9 = (s32[4096]{0:T(1024)S(1)}, s32[4096]{0:T(1024)}, u32[]{:S(2)}) copy-start(s32[4096]{0:T(1024)} %param.27) | copy-start | bytes 49156
  33.7 3.9 %copy-start.10 = (f32[4096]{0:T(1024)S(1)}, f32[4096]{0:T(1024)}, u32[]{:S(2)}) copy-start(f32[4096]{0:T(1024)} %param.28) | copy-start | bytes 49156
  33.7 3.9 %copy-start.11 = (f32[4096]{0:T(1024)S(1)}, f32[4096]{0:T(1024)}, u32[]{:S(2)}) copy-start(f32[4096]{0:T(1024)} %param.29) | copy-start | bytes 49156
  33.7 13.3 %all-to-all-start = ((bf16[4,4,128,256]{3,2,1,0:T(8,128)(2,1)}), bf16[4,4,128,256]{3,2,1,0:T(8,128)(2,1)S(1)}, u32[]{:S(2)}, u32[]{:S(2)}) async-start(bf16[4,4,128,256]{3,2,1,0:T(8,128)(2,1)} %forward.1), calls=%async_computation | async-start | bytes 2097152 | tf_op jit(solution)/shard_map/all_to_all | solution.py:448
  37.6 0.7 copy-start.8

commit v8 on v7

--- a/solution.py
+++ b/solution.py
@@ -95,41 +95,160 @@
     return jnp.max(squares, axis=0, keepdims=True)
 
 
-def project_kernel(
-    heads, own_ref, gain_ref, w_query_ref, w_key_ref, w_value_ref, query_ref, key_ref, value_ref, norm_ref
+def band_bias(window, lower, upper, reach):
+    apart = jnp.abs(iota((Q_ROWS, upper - lower), 1) + (lower - reach) - iota((Q_ROWS, upper - lower), 0))
+    return jnp.where(apart <= window, 0.0, -1e30)
+
+
+def head_masks(head_size):
+    lane_head = iota((1, LANES), 1) // head_size
+    return [(lane_head == head).astype(F32).astype(BF16) for head in range(LANES // head_size)]
+
+
+def stacked_heads(queries, head_size):
+    return jnp.concatenate([queries * mask for mask in head_masks(head_size)], axis=0)
+
+
+def by_lane_head(parts, head_size):
+    lane_head = iota((1, LANES), 1) // head_size
+    joined = parts[0]
+    for head in range(1, len(parts)):
+        joined = jnp.where(lane_head == head, parts[head], joined)
+    return joined
+
+
+def row_sums(values):
+    return jnp.sum(values, axis=-1, keepdims=True)
+
+
+def padded_lanes(values, before, after):
+    pieces = [jnp.zeros((values.shape[0], before), BF16)] if before else []
+    pieces.append(values.astype(BF16))
+    if after:
+        pieces.append(jnp.zeros((values.shape[0], after), BF16))
+    return jnp.concatenate(pieces, axis=1) if len(pieces) > 1 else pieces[0]
+
+
+def unit_weights(scores, count, spans, bias_of):
+    width = scores.shape[1]
+    weights, totals = [], []
+    for head in range(scores.shape[0] // count):
+        sums = []
+        for block, (lower, upper) in enumerate(spans):
+            top = head * count + block * Q_ROWS
+            expo = jnp.exp2(scores[top : top + Q_ROWS, lower:upper] + bias_of(head, block))
+            sums.append(row_sums(expo))
+            weights.append(padded_lanes(expo, lower, width - upper))
+        totals.append(jnp.concatenate(sums, axis=0))
+    return jnp.concatenate(weights, axis=0), totals
+
+
+def inner_kernel(
+    window_ref,
+    own_ref,
+    gain_ref,
+    w_query_ref,
+    w_key_ref,
+    w_value_ref,
+    query_ref,
+    key_ref,
+    value_ref,
+    norm_ref,
+    mixed_ref,
+    total_ref,
+    bias_buf,
 ):
-    scale = math.log2(math.e) / math.sqrt(own_ref.shape[2] // heads)
+    rows, feat_width = own_ref.shape[1:]
+    heads = window_ref.shape[0]
+    head_size = feat_width // heads
+    group_heads = LANES // head_size
+    reach = (bias_buf.shape[2] - Q_ROWS) // 2
+    reach_blocks = reach // Q_ROWS
+    blocks = rows // Q_ROWS
+
+    @pl.when(pl.program_id(0) == 0)
+    def _():
+        for head in range(heads):
+            bias_buf[head] = band_bias(window_ref[head], 0, Q_ROWS + 2 * reach, reach)
+
     normed = rms_scaled(own_ref[0].astype(F32), gain_ref[...]).astype(BF16)
-    queries = dot(normed, w_query_ref[...]) * scale
-    keys = dot(normed, w_key_ref[...])
-    query_ref[0] = queries.astype(BF16)
-    key_ref[0] = keys.T.astype(BF16)
+    query_rows = dot(normed, w_query_ref[...]) * (math.log2(math.e) / math.sqrt(head_size))
+    key_rows = dot(normed, w_key_ref[...])
+    query_ref[0] = query_rows.astype(BF16)
+    key_ref[0] = key_rows.T.astype(BF16)
     value_ref[0] = dot(normed, w_value_ref[...]).astype(BF16)
+    query_norms, key_norms = largest_norms(query_rows, heads), largest_norms(key_rows, heads)
     blank = jnp.zeros((norm_ref.shape[1] - 2, LANES), F32)
-    norm_ref[0] = jnp.concatenate([largest_norms(queries, heads), largest_norms(keys, heads), blank], axis=0)
-
-
-def project(own, heads, gain, w_query, w_key, w_value):
+    norm_ref[0] = jnp.concatenate([query_norms, key_norms, blank], axis=0)
+
+    @pl.when(is_safe(query_norms, key_norms))
+    def _():
+        count = 2 * Q_ROWS
+        units = [(first, group) for first in range(0, blocks, 2) for group in range(heads // group_heads)]
+
+        def scores_of(first, group):
+            lanes = slice(group * LANES, (group + 1) * LANES)
+            queries = query_ref[0, first * Q_ROWS : first * Q_ROWS + count, lanes]
+            return dot(stacked_heads(queries, head_size), key_ref[0, lanes, :])
+
+        scores = scores_of(*units[0])
+        totals_by_lane = jnp.zeros((count, LANES), F32)
+        for at, (first, group) in enumerate(units):
+            following = scores_of(*units[at + 1]) if at + 1 < len(units) else None
+            ranges = [(max(0, b - reach_blocks), min(blocks, b + reach_blocks + 1)) for b in (first, first + 1)]
+            spans = [(lower * Q_ROWS, upper * Q_ROWS) for lower, upper in ranges]
+
+            def bias_of(head, block):
+                shift = (reach_blocks - first - block) * Q_ROWS
+                lower, upper = spans[block]
+                return bias_buf[group * group_heads + head, :, lower + shift : upper + shift]
+
+            weights, totals = unit_weights(scores, count, spans, bias_of)
+            lanes = slice(group * LANES, (group + 1) * LANES)
+            mixed = dot(weights, value_ref[0, :, lanes])
+            start = first * Q_ROWS
+            parts = [mixed[head * count : (head + 1) * count] for head in range(group_heads)]
+            mixed_ref[0, start : start + count, lanes] = by_lane_head(parts, head_size)
+            for head, total in enumerate(totals):
+                here = iota((1, LANES), 1) == group * group_heads + head
+                totals_by_lane = jnp.where(here, total, totals_by_lane)
+            total_ref[0, start : start + count, :] = totals_by_lane
+            scores = following
+
+
+def is_safe(query_norms, key_norms):
+    return jnp.max(query_norms * key_norms) * 1.05 <= SAFE_SCORE * SAFE_SCORE
+
+
+def inner(head_window, own, gain, w_query, w_key, w_value, reach):
     members, rows, feat_width = own.shape
+    heads = head_window.shape[0]
     upright = (members, rows, feat_width)
-    shapes = [upright, (members, feat_width, rows), upright]
-    norm_shape = (members, 8, LANES)
+    shapes = [
+        (upright, BF16),
+        ((members, feat_width, rows), BF16),
+        (upright, BF16),
+        ((members, 8, LANES), F32),
+        (upright, F32),
+        ((members, rows, LANES), F32),
+    ]
 
     def spec(shape):
         return pl.BlockSpec((1, *shape[1:]), lambda m: (m, 0, 0))
 
     return pl.pallas_call(
-        functools.partial(project_kernel, heads),
+        inner_kernel,
         grid=(members,),
-        out_shape=[jax.ShapeDtypeStruct(v, BF16) for v in shapes] + [jax.ShapeDtypeStruct(norm_shape, F32)],
-        in_specs=[spec(upright)] + [vmem_spec()] * 4,
-        out_specs=[spec(v) for v in (*shapes, norm_shape)],
+        out_shape=[jax.ShapeDtypeStruct(*v) for v in shapes],
+        in_specs=[smem_spec(), spec(upright)] + [vmem_spec()] * 4,
+        out_specs=[spec(shape) for shape, _ in shapes],
+        scratch_shapes=[pltpu.VMEM((heads, Q_ROWS, Q_ROWS + 2 * reach), F32)],
         compiler_params=pltpu.CompilerParams(vmem_limit_bytes=VMEM_LIMIT),
         cost_estimate=pl.CostEstimate(
-            flops=6 * own.size * feat_width, bytes_accessed=8 * own.size, transcendentals=0
+            flops=own.size * (6 * feat_width + 16 * rows), bytes_accessed=14 * own.size, transcendentals=0
         ),
-        name="project",
-    )(own, gain, w_query, w_key, w_value)
+        name="inner",
+    )(head_window, own, gain, w_query, w_key, w_value)
 
 
 def forward_kernel(
@@ -140,6 +259,8 @@
     key_ref,
     value_ref,
     norm_ref,
+    inner_mixed_ref,
+    inner_total_ref,
     left_ref,
     right_ref,
     attn_gain_ref,
@@ -151,97 +272,100 @@
     w_up_ref,
     down_weight_ref,
     out_ref,
+    halo_key_buf,
+    halo_value_buf,
+    bias_buf,
+    mixed_buf,
     key_buf,
     value_buf,
-    bias_buf,
-    mixed_buf,
 ):
     rows, feat_width = state_ref.shape[1:]
     reach = left_ref.shape[1]
-    head_count = window_ref.shape[0]
-    head_size = feat_width // head_count
+    heads = window_ref.shape[0]
+    head_size = feat_width // heads
     group_heads = LANES // head_size
     blocks = rows // Q_ROWS
     key_count = Q_ROWS + 2 * reach
+    count = 2 * Q_ROWS
+    first_valid = place_ref[0] - reach >= 0
+    last_valid = place_ref[0] + rows + reach <= place_ref[1]
 
     @pl.when(pl.program_id(0) == 0)
     def _():
-        apart = jnp.abs(iota((Q_ROWS, key_count), 1) - reach - iota((Q_ROWS, key_count), 0))
-        for block in range(blocks):
-            k_pos = place_ref[0] - reach + block * Q_ROWS + iota((Q_ROWS, key_count), 1)
-            inside = (k_pos >= 0) & (k_pos < place_ref[1])
-            for head in range(head_count):
-                bias_buf[block, head] = jnp.where(inside & (apart <= window_ref[head]), 0.0, -1e30)
-
-    key_buf[:, reach : reach + rows] = key_ref[0]
-    value_buf[reach : reach + rows] = value_ref[0]
+        for head in range(heads):
+            left_bias = band_bias(window_ref[head], 0, reach, reach)
+            right_bias = band_bias(window_ref[head], key_count - reach, key_count, reach)
+            bias_buf[0, head] = jnp.where(first_valid, left_bias, -1e30)
+            bias_buf[1, head] = jnp.where(last_valid, right_bias, -1e30)
+
     key_norms = norm_ref[0, 1:2, :]
-    for ref, lower in ((left_ref, 0), (right_ref, reach + rows)):
+    for side, ref in enumerate((left_ref, right_ref)):
         normed = rms_scaled(ref[0].astype(F32), attn_gain_ref[...]).astype(BF16)
         keys = dot(normed, w_key_ref[...])
-        key_norms = jnp.maximum(key_norms, largest_norms(keys, head_count))
-        key_buf[:, lower : lower + reach] = keys.T.astype(BF16)
-        value_buf[lower : lower + reach] = dot(normed, w_value_ref[...]).astype(BF16)
-
-    bound = jnp.max(norm_ref[0, 0:1, :] * key_norms) * 1.05
-    safe = bound <= SAFE_SCORE * SAFE_SCORE
-
-    lane_head = iota((1, LANES), 1) // head_size
-    head_masks = [(lane_head == head).astype(F32).astype(BF16) for head in range(group_heads)]
-
-    def scores_of(start, count, group):
-        lanes = slice(group * LANES, (group + 1) * LANES)
-        queries = query_ref[0, pl.ds(start, count), lanes]
-        stacked = jnp.concatenate([queries * mask for mask in head_masks], axis=0)
-        return dot(stacked, key_buf[lanes, pl.ds(start, count + 2 * reach)])
-
-    def mix_values(start, count, group, weights, totals):
-        lanes = slice(group * LANES, (group + 1) * LANES)
-        mixed_all = dot(jnp.concatenate(weights, axis=0), value_buf[pl.ds(start, count + 2 * reach), lanes])
-        mixed = mixed_all[:count] * (1.0 / totals[0])
-        for head in range(1, group_heads):
-            part = mixed_all[head * count : (head + 1) * count] * (1.0 / totals[head])
-            mixed = jnp.where(lane_head == head, part, mixed)
-        mixed_buf[pl.ds(start, count), lanes] = mixed.astype(BF16)
-
-    groups = head_count // group_heads
+        key_norms = jnp.maximum(key_norms, largest_norms(keys, heads))
+        halo_key_buf[side] = keys.T.astype(BF16)
+        halo_value_buf[side] = dot(normed, w_value_ref[...]).astype(BF16)
+    safe = is_safe(norm_ref[0, 0:1, :], key_norms)
 
     @pl.when(safe)
     def _():
-        pair = 2 * Q_ROWS
-        corner = jnp.zeros((Q_ROWS, Q_ROWS), BF16)
-        units = [(start, group) for start in range(0, rows, pair) for group in range(groups)]
-        scores = scores_of(units[0][0], pair, units[0][1])
-        for at, (start, group) in enumerate(units):
-            following = scores_of(units[at + 1][0], pair, units[at + 1][1]) if at + 1 < len(units) else None
-            weights, totals = [], []
-            for head in range(group_heads):
-                top = head * pair
-                bias = [bias_buf[start // Q_ROWS + part, group * group_heads + head] for part in range(2)]
-                upper = jnp.exp2(scores[top : top + Q_ROWS, :key_count] + bias[0])
-                lower = jnp.exp2(scores[top + Q_ROWS : top + pair, Q_ROWS:] + bias[1])
-                totals.append(
-                    jnp.concatenate([jnp.sum(v, axis=-1, keepdims=True) for v in (upper, lower)], axis=0)
-                )
-                weights.append(jnp.concatenate([upper.astype(BF16), corner], axis=1))
-                weights.append(jnp.concatenate([corner, lower.astype(BF16)], axis=1))
-            mix_values(start, pair, group, weights, totals)
+        units = [(side, group) for side in range(2) for group in range(heads // group_heads)]
+
+        def scores_of(side, group):
+            lanes = slice(group * LANES, (group + 1) * LANES)
+            start = side * (rows - count)
+            queries = query_ref[0, start : start + count, lanes]
+            return dot(stacked_heads(queries, head_size), halo_key_buf[side, lanes, :])
+
+        scores = scores_of(*units[0])
+        for at, (side, group) in enumerate(units):
+            following = scores_of(*units[at + 1]) if at + 1 < len(units) else None
+            spans = [(0, reach), (Q_ROWS, reach)] if side == 0 else [(0, reach - Q_ROWS), (0, reach)]
+
+            def bias_of(head, block):
+                lower, upper = spans[block]
+                shift = -block * Q_ROWS if side == 0 else (1 - block) * Q_ROWS
+                return bias_buf[side, group * group_heads + head, :, lower + shift : upper + shift]
+
+            weights, totals = unit_weights(scores, count, spans, bias_of)
+            lanes = slice(group * LANES, (group + 1) * LANES)
+            mixed = dot(weights, halo_value_buf[side, :, lanes])
+            start = side * (rows - count)
+            parts = []
+            for head, total in enumerate(totals):
+                at_lane = group * group_heads + head
+                total = total + inner_total_ref[0, start : start + count, at_lane : at_lane + 1]
+                part = mixed[head * count : (head + 1) * count] + inner_mixed_ref[0, start : start + count, lanes]
+                parts.append(part * (1.0 / total))
+            mixed_buf[start : start + count, lanes] = by_lane_head(parts, head_size).astype(BF16)
             scores = following
 
     @pl.when(jnp.logical_not(safe))
     def _():
+        key_buf[:, :reach] = halo_key_buf[0]
+        key_buf[:, reach : reach + rows] = key_ref[0]
+        key_buf[:, reach + rows :] = halo_key_buf[1]
+        value_buf[:reach] = halo_value_buf[0]
+        value_buf[reach : reach + rows] = value_ref[0]
+        value_buf[reach + rows :] = halo_value_buf[1]
         for block in range(blocks):
             start = block * Q_ROWS
-            for group in range(groups):
-                scores = scores_of(start, Q_ROWS, group)
+            k_pos = place_ref[0] - reach + start + iota((Q_ROWS, key_count), 1)
+            inside = (k_pos >= 0) & (k_pos < place_ref[1])
+            for group in range(heads // group_heads):
+                lanes = slice(group * LANES, (group + 1) * LANES)
+                queries = query_ref[0, start : start + Q_ROWS, lanes]
+                scores = dot(stacked_heads(queries, head_size), key_buf[lanes, start : start + key_count])
                 weights, totals = [], []
                 for head in range(group_heads):
-                    score_matrix = scores[head * Q_ROWS : (head + 1) * Q_ROWS]
-                    score_matrix = score_matrix + bias_buf[block, group * group_heads + head]
+                    bias = band_bias(window_ref[group * group_heads + head], 0, key_count, reach)
+                    score_matrix = scores[head * Q_ROWS : (head + 1) * Q_ROWS] + jnp.where(inside, bias, -1e30)
                     expo = jnp.exp2(score_matrix - jnp.max(score_matrix, axis=-1, keepdims=True))
-                    totals.append(jnp.sum(expo, axis=-1, keepdims=True))
+                    totals.append(row_sums(expo))
                     weights.append(expo.astype(BF16))
-                mix_values(start, Q_ROWS, group, weights, totals)
+                mixed = dot(jnp.concatenate(weights, axis=0), value_buf[start : start + key_count, lanes])
+                parts = [mixed[head * Q_ROWS : (head + 1) * Q_ROWS] * (1.0 / v) for head, v in enumerate(totals)]
+                mixed_buf[start : start + Q_ROWS, lanes] = by_lane_head(parts, head_size).astype(BF16)
 
     after = (state_ref[0].astype(F32) + dot(mixed_buf[...], w_out_ref[...])).astype(BF16)
     normed_mid = rms_scaled(after.astype(F32), ffn_gain_ref[...]).astype(BF16)
@@ -257,32 +381,36 @@
         out_ref[share, 0] = forecast[share * share_rows : (share + 1) * share_rows]
 
 
-def forward(place, head_window, own, projected, left, right, gains, weights, shares):
+def forward(place, head_window, own, inner_parts, left, right, gains, weights, shares):
     members, row_count, feat_width = own.shape
     reach = left.shape[1]
-    key_count = Q_ROWS + 2 * reach
+    heads = head_window.shape[0]
     hidden_width = weights[3].shape[1]
-    macs = members * row_count * feat_width * (3 * feat_width + 3 * hidden_width + 8 * key_count)
-    edge_block = pl.BlockSpec((1, reach, feat_width), lambda m: (m, 0, 0))
+    macs = members * row_count * feat_width * (3 * feat_width + 3 * hidden_width + 4 * reach)
+
+    def spec(array):
+        return pl.BlockSpec((1, *array.shape[1:]), lambda m: (m, 0, 0))
+
     return pl.pallas_call(
         forward_kernel,
         grid=(members,),
         out_shape=jax.ShapeDtypeStruct((shares, members, row_count // shares, feat_width), BF16),
         in_specs=[smem_spec()] * 2
-        + [pl.BlockSpec((1, *v.shape[1:]), lambda m: (m, 0, 0)) for v in (own, *projected)]
-        + [edge_block] * 2
+        + [spec(v) for v in (own, *inner_parts, left, right)]
         + [vmem_spec()] * (len(gains) + len(weights)),
         out_specs=pl.BlockSpec((shares, 1, row_count // shares, feat_width), lambda m: (0, m, 0, 0)),
         scratch_shapes=[
+            pltpu.VMEM((2, feat_width, reach), BF16),
+            pltpu.VMEM((2, reach, feat_width), BF16),
+            pltpu.VMEM((2, heads, Q_ROWS, reach), F32),
+            pltpu.VMEM((row_count, feat_width), BF16),
             pltpu.VMEM((feat_width, row_count + 2 * reach), BF16),
             pltpu.VMEM((row_count + 2 * reach, feat_width), BF16),
-            pltpu.VMEM((row_count // Q_ROWS, head_window.shape[0], Q_ROWS, key_count), F32),
-            pltpu.VMEM((row_count, feat_width), BF16),
         ],
         compiler_params=pltpu.CompilerParams(vmem_limit_bytes=VMEM_LIMIT),
         cost_estimate=pl.CostEstimate(flops=2 * macs, bytes_accessed=10 * own.size, transcendentals=0),
         name="forward",
-    )(place, head_window, own, *projected, left, right, *gains, *weights)
+    )(place, head_window, own, *inner_parts, left, right, *gains, *weights)
 
 
 def gram_kernel(share_ref, grid_ref, out_ref):
@@ -442,9 +570,9 @@
     )
     place = jnp.stack([first_pos, row_count * tok_count]).astype(jnp.int32)
     gains = [attn_gain.reshape(1, -1), ffn_gain.reshape(1, -1)]
-    projected = project(ens_state, head_window.shape[0], gains[0], w_query, w_key, w_value)
+    inner_parts = inner(head_window, ens_state, gains[0], w_query, w_key, w_value, WIN)
     weights = [w_key, w_value, w_out, w_gate, w_up, down_weight]
-    forecast = forward(place, head_window, ens_state, projected, left, right, gains, weights, mem_count)
+    forecast = forward(place, head_window, ens_state, inner_parts, left, right, gains, weights, mem_count)
     share = lax.all_to_all(forecast, "mem", split_axis=0, concat_axis=0, tiled=True)
     share = share.reshape(members, share_rows, feat_width)
     partial = gram_partial(share, grid)

time: 93.2 us -> 92.9 us (level)
  local copies, waits for them, and re-layouts: 4.46 us -> 2.5 us
  Pallas kernels: 32 us -> 33.7 us
    unnamed x30, local copies, waits for them, and re-layouts: 2.03 us -> 0.07 us
    pallas_call x1, Pallas kernels: 2.35 us -> 3.6 us  [inner(): pl.pallas_call(inner_kernel, grid=(members,), out_shape=[jax.ShapeDtypeSt...]
  transfers between devices with their start and end apart: 3 -> 3, of which waited for: 2 -> 2; matrix products, arithmetic and copies ran while one was open for 0% -> 0% of each run, Pallas kernels for 4% -> 5%
where the time goes in v8:
time: 92.9 us; the launch traced here: 92.5 us
  blocking collectives  39.5 us (43%)
  Pallas kernels  33.7 us (36%)
  waiting for transfers between devices  8.92 us (10%)
  starting transfers between devices  7.55 us (8%)
  local copies, waits for them, and re-layouts  2.5 us (3%)
    pallas_call x1, Pallas kernels, forward(): pl.pallas_call(forward_kernel, grid=(members,), out_shape=jax.ShapeDtypeS...  23.6 us
    all_to_all x1, blocking collectives, local(): lax.all_to_all(jnp.broadcast_to(partial[None], (device_count, *partial.sh...  22.2 us
    all_to_all x1, blocking collectives, local(): lax.all_to_all(mixed, 'mem', split_axis=0, concat_axis=0, tiled=True)  17.3 us
    all_to_all x1, waiting for transfers between devices, local(): lax.all_to_all(forecast, 'mem', split_axis=0, concat_axis=0, tiled=True)  8.05 us
    all_to_all x1, starting transfers between devices, local(): lax.all_to_all(forecast, 'mem', split_axis=0, concat_axis=0, tiled=True)  3.86 us
    pallas_call x1, Pallas kernels, combine(): pl.pallas_call(combine_kernel, out_shape=jax.ShapeDtypeStruct(share.shape...  3.64 us
    pallas_call x1, Pallas kernels, inner(): pl.pallas_call(inner_kernel, grid=(members,), out_shape=[jax.ShapeDtypeSt...  3.6 us
    ppermute x1, starting transfers between devices, local(): left = lax.ppermute(ens_state[:, row_count - WIN:], 'tok', up)  2.4 us
  transfers between devices with their start and end apart: 3, of which 2 were waited for; matrix products, arithmetic and copies ran while one was open for 0% of the time, Pallas kernels for 5%

profile of v8, /device:TPU:0, one launch (start us, length us, event | category | flops | bytes accessed | tf_op | source)
XLA Modules:
  0.0 92.5 jit_solution(15008399542423655304)
XLA Ops:
  0.0 0.0 copy-start.14
  0.0 1.4 %fusion = (bf16[4,256,256]{2,1,0:T(8,128)(2,1)S(1)}, bf16[4,256,256]{2,1,0:T(8,128)(2,1)S(1)}) fusion(bf16[4,512,256]{2,1,0:T(8,128)(2,1)} %state_ref.1), kind=kLoop, calls=%fused_computation.1 | loop fusion | bytes 2097152 | tf_op jit(solution)/shard_map/slice | solution.py:566
  1.4 2.4 %collective-permute-start = (bf16[4,256,256]{2,1,0:T(8,128)(2,1)S(1)}, bf16[4,256,256]{2,1,0:T(8,128)(2,1)S(1)}, u32[]{:S(2)}, u32[]{:S(2)}) collective-permute-start(bf16[4,256,256]{2,1,0:T(8,128)(2,1)S(1)} %get-tuple-element.18), channel_id=1, source_target_pairs={{0,1},{1,2},{2,3},{3,4},{4,5},{5,6},{6,7},{8,9},{9,10},{10,11},{11... | collective-permute-start | bytes 1572872 | tf_op jit(solution)/shard_map/ppermute | solution.py:565
  3.8 1.3 %collective-permute-start.1 = (bf16[4,256,256]{2,1,0:T(8,128)(2,1)S(1)}, bf16[4,256,256]{2,1,0:T(8,128)(2,1)S(1)}, u32[]{:S(2)}, u32[]{:S(2)}) collective-permute-start(bf16[4,256,256]{2,1,0:T(8,128)(2,1)S(1)} %get-tuple-element.17), channel_id=1, source_target_pairs={{1,0},{2,1},{3,2},{4,3},{5,4},{6,5},{7,6},{9,8},{10,9},{11,10},{12... | collective-permute-start | bytes 1572872 | tf_op jit(solution)/shard_map/ppermute | solution.py:566
  5.1 0.1 pad_add_fusion.place_ref
  5.2 0.0 copy-done
  5.2 0.0 copy-done.12
  5.2 0.0 copy-done.4
  5.2 0.0 copy-done.5
  5.2 0.0 copy-done.6
  5.2 0.0 copy-done.14
  5.2 0.0 copy-start.1
  5.2 0.0 copy-start.2
  5.3 0.0 copy-start.3
  5.3 0.0 copy-start.7
  5.3 0.0 copy-start.13
  5.3 3.6 %inner.1 = (bf16[4,512,256]{2,1,0:T(8,128)(2,1)S(1)}, bf16[4,256,512]{2,1,0:T(8,128)(2,1)S(1)}, bf16[4,512,256]{2,1,0:T(8,128)(2,1)S(1)}, f32[4,8,128]{2,1,0:T(8...) custom-call(s32[4]{0:T(128)S(1)} %copy-done.14, bf16[4,512,256]{2,1,0:T(8,128)(2,1)S(1)} %copy-done, ...), custom_call_target="tpu_custom_call" | custom-call | flops 5100273664 | bytes 7340032 | tf_op jit(solution)/shard_map/inner/pallas_call | solution.py:239
  8.9 0.0 collective-permute-done.left_ref
  8.9 0.9 collective-permute-done.1.right_ref
  9.8 0.0 copy-done.1
  9.8 0.0 copy-done.2
  9.8 0.0 copy-done.3
  9.8 0.0 copy-done.7
  9.8 23.6 %forward.1 = bf16[4,4,128,256]{3,2,1,0:T(8,128)(2,1)} custom-call(s32[2]{0:T(128)S(1)} %pad_add_fusion.place_ref, s32[4]{0:T(128)S(1)} %copy-done.14, bf16[4,512,256]{2,1,0:T(8,128)(2,1)S(1)} %copy-done, bf16[4,512,256]{2,1,0:T(8,128)(2,1)S(1)} %get-tuple-element.11.query_ref, bf16[4,256,512]{2,1,0:T(8,128)(2,1)S(1)} %get-tuple-element.12.key_ref, ...), custom_call_target="tpu_custom_call" | custom-call | flops 5100273664 | bytes 5242880 | tf_op jit(solution)/shard_map/forward/pallas_call | solution.py:394
  33.5 3.9 %all-to-all-start = ((bf16[4,4,128,256]{3,2,1,0:T(8,128)(2,1)}), bf16[4,4,128,256]{3,2,1,0:T(8,128)(2,1)S(1)}, u32[]{:S(2)}, u32[]{:S(2)}) async-start(bf16[4,4,128,256]{3,2,1,0:T(8,128)(2,1)} %forward.1), calls=%async_computation | async-start | bytes 2097152 | tf_op jit(solution)/shard_map/all_to_all | solution.py:576
  37.4 1.3 %sample_grid.1.grid_ref = f32[2,128,256]{2,1,0:T(8,128)S(1)} custom-call(s32[1]{0:T(128)} %bitcast.4.start_ref, s32[1,4096]{1,0:T(1,128)S(1)} %bitcast.15, s32[1,4096]{1,0:T(1,128)S(1)} %bitcast.16, f32[1,4096]{1,0:T(1,128)S(1)} %bitcast.17, f32[1,4096]{1,0:T(1,128)S(1)} %bitcast.18), custom_call_target="tpu_custom_call" | custom-call | flops 1073741824 | bytes 65536 | tf_op jit(solution)/shard_map/sample_grid/pallas_call | solution.py:77
  38.7 8.1 %all-to-all-done = bf16[4,4,128,256]{3,2,1,0:T(8,128)(2,1)S(1)} async-done(((bf16[4,4,128,256]{3,2,1,0:T(8,128)(2,1)}), bf16[4,4,128,256]{3,2,1,0:T(8,128)(2,1)S(1)}, u32[]{:S(2)}, u32[]{:S(2)}) %all-to-all-start) | async-done | bytes 1048608 | tf_op jit(solution)/shard_map/all_to_all | solution.py:576
  46.8 1.5 %gram.1 = f32[8,128]{1,0:T(8,128)S(1)} custom-call(bf16[16,128,256]{2,1,0:T(8,128)(2,1)S(1)} %bitcast.12, f32[2,128,256]{2,1,0:T(8,128)S(1)} %sample_grid.1.grid_ref), custom_call_target="tpu_custom_call" | custom-call | flops 805306368 | bytes 1048576 | tf_op jit(solution)/shard_map/gram/pallas_call | solution.py:451
  48.3 22.2 %all_to_all.15.partial_ref = f32[32,8,128]{2,1,0:T(8,128)S(1)} all-to-all(f32[32,8,128]{2,1,0:T(8,128)S(1)} %broadcast_in_dim.2), channel_id=1, replica_groups=mesh['mem'=4,'tok'=8] {'mem','tok'}, dimensions={0} | all-to-all | bytes 262144 | tf_op jit(solution)/shard_map/all_to_all | solution.py:579
  70.5 3.6 %combine.1 = bf16[16,128,256]{2,1,0:T(8,128)(2,1)S(1)} custom-call(f32[32,8,128]{2,1,0:T(8,128)S(1)} %all_to_all.15.partial_ref, bf16[16,128,256]{2,1,0:T(8,128)(2,1)S(1)} %bitcast.13), custom_call_target="tpu_custom_call" | custom-call | flops 536870912 | bytes 2097152 | tf_op jit(solution)/shard_map/combine/pallas_call | solution.py:526
  74.2 17.3 %all_to_all.16 = bf16[4,4,128,256]{3,2,1,0:T(8,128)(2,1)S(1)} all-to-all(bf16[4,4,128,256]{3,2,1,0:T(8,128)(2,1)S(1)} %bitcast.14), channel_id=1, replica_groups=mesh['mem'=4,'tok'=8] {'mem'}, dimensions={0} | all-to-all | bytes 2097152 | tf_op jit(solution)/shard_map/all_to_all | solution.py:587
  91.5 1.0 %copy.16 = bf16[4,4,128,256]{3,2,1,0:T(8,128)(2,1)} copy(bf16[4,4,128,256]{3,2,0,1:T(8,128)(2,1)S(1)} %bitcast.22) | data formatting | bytes 2097152 | tf_op jit(solution)/shard_map/transpose | solution.py:588
  (15 shorter events, 0.0 us)
Async XLA Ops:
  0.0 5.2 %copy-start = (bf16[4,512,256]{2,1,0:T(8,128)(2,1)S(1)}, bf16[4,512,256]{2,1,0:T(8,128)(2,1)}, u32[]{:S(2)}) copy-start(bf16[4,512,256]{2,1,0:T(8,128)(2,1)} %state_ref.1) | copy-start | bytes 3145732
  0.0 5.2 %copy-start.12 = (f32[256]{0:T(256)S(1)}, f32[256]{0:T(256)}, u32[]{:S(2)}) copy-start(f32[256]{0:T(256)} %param.16) | copy-start | bytes 3076
  0.0 5.2 %copy-start.4 = (bf16[256,256]{1,0:T(8,128)(2,1)S(1)}, bf16[256,256]{1,0:T(8,128)(2,1)}, u32[]{:S(2)}) copy-start(bf16[256,256]{1,0:T(8,128)(2,1)} %w_query_ref.1) | copy-start | bytes 393220
  0.0 5.2 %copy-start.5 = (bf16[256,256]{1,0:T(8,128)(2,1)S(1)}, bf16[256,256]{1,0:T(8,128)(2,1)}, u32[]{:S(2)}) copy-start(bf16[256,256]{1,0:T(8,128)(2,1)} %w_key_ref.3) | copy-start | bytes 393220
  0.0 5.2 %copy-start.6 = (bf16[256,256]{1,0:T(8,128)(2,1)S(1)}, bf16[256,256]{1,0:T(8,128)(2,1)}, u32[]{:S(2)}) copy-start(bf16[256,256]{1,0:T(8,128)(2,1)} %w_value_ref.3) | copy-start | bytes 393220
  0.0 5.2 %copy-start.14 = (s32[4]{0:T(128)S(1)}, s32[4]{0:T(128)}, u32[]{:S(2)}) copy-start(s32[4]{0:T(128)} %window_ref.3) | copy-start | bytes 52
  1.4 7.5 %collective-permute-start = (bf16[4,256,256]{2,1,0:T(8,128)(2,1)S(1)}, bf16[4,256,256]{2,1,0:T(8,128)(2,1)S(1)}, u32[]{:S(2)}, u32[]{:S(2)}) collective-permute-start(bf16[4,256,256]{2,1,0:T(8,128)(2,1)S(1)} %get-tuple-element.18), channel_id=1, source_target_pairs={{0,1},{1,2},{2,3},{3,4},{4,5},{5,6},{6,7},{8,9},{9,10},{10,11},{11... | collective-permute-start | bytes 1572872 | tf_op jit(solution)/shard_map/ppermute | solution.py:565
  3.8 6.0 %collective-permute-start.1 = (bf16[4,256,256]{2,1,0:T(8,128)(2,1)S(1)}, bf16[4,256,256]{2,1,0:T(8,128)(2,1)S(1)}, u32[]{:S(2)}, u32[]{:S(2)}) collective-permute-start(bf16[4,256,256]{2,1,0:T(8,128)(2,1)S(1)} %get-tuple-element.17), channel_id=1, source_target_pairs={{1,0},{2,1},{3,2},{4,3},{5,4},{6,5},{7,6},{9,8},{10,9},{11,10},{12... | collective-permute-start | bytes 1572872 | tf_op jit(solution)/shard_map/ppermute | solution.py:566
  5.2 4.6 %copy-start.1 = (bf16[256,1024]{1,0:T(8,128)(2,1)S(1)}, bf16[256,1024]{1,0:T(8,128)(2,1)}, u32[]{:S(2)}) copy-start(bf16[256,1024]{1,0:T(8,128)(2,1)} %w_gate_ref.1) | copy-start | bytes 1572868
  5.2 4.5 %copy-start.2 = (bf16[256,1024]{1,0:T(8,128)(2,1)S(1)}, bf16[256,1024]{1,0:T(8,128)(2,1)}, u32[]{:S(2)}) copy-start(bf16[256,1024]{1,0:T(8,128)(2,1)} %w_up_ref.1) | copy-start | bytes 1572868
  5.3 4.5 %copy-start.3 = (bf16[1024,256]{1,0:T(8,128)(2,1)S(1)}, bf16[1024,256]{1,0:T(8,128)(2,1)}, u32[]{:S(2)}) copy-start(bf16[1024,256]{1,0:T(8,128)(2,1)} %down_weight_ref.1) | copy-start | bytes 1572868
  5.3 4.5 %copy-start.7 = (bf16[256,256]{1,0:T(8,128)(2,1)S(1)}, bf16[256,256]{1,0:T(8,128)(2,1)}, u32[]{:S(2)}) copy-start(bf16[256,256]{1,0:T(8,128)(2,1)} %w_out_ref.1) | copy-start | bytes 393220
  5.3 4.5 %copy-start.13 = (f32[256]{0:T(256)S(1)}, f32[256]{0:T(256)}, u32[]{:S(2)}) copy-start(f32[256]{0:T(256)} %param.17) | copy-start | bytes 3076
  33.5 3.9 %copy-start.8 = (s32[4096]{0:T(1024)S(1)}, s32[4096]{0:T(1024)}, u32[]{:S(2)}) copy-start(s32[4096]{0:T(1024)} %param.26) | copy-start | bytes 49156
  33.5 3.9 %copy-start.9 = (s32[4096]{0:T(1024)S(1)}, s32[4096]{0:T(1024)}, u32[]{:S(2)}) copy-start(s32[4096]{0:T(1024)} %param.27) | copy-start | bytes 49156
  33.5 3.9 %copy-start.10 = (f32[4096]{0:T(1024)S(1)}, f32[4096]{0:T(1024)}, u32[]{:S(2)}) copy-start(f32[4096]{0:T(1024)} %param.28) | copy-start | bytes 49156
  33.5 3.9 %copy-start.11 = (f32[4096]{0:T(1024)S(1)}, f32[4096]{0:T(1024)}, u32[]{:S(2)}) copy-start(f32[4096]{0:T(1024)} %param.29) | copy-start | bytes 49156
  33.5 13.3 %all-to-all-start = ((bf16[4,4,128,256]{3,2,1,0:T(8,128)(2,1)}), bf16[4,4,128,256]{3,2,1,0:T(8,128)(2,1)S(1)}, u32[]{:S(2)}, u32[]{:S(2)}) async-start(bf16[4,4,128,256]{3,2,1,0:T(8,128)(2,1)} %forward.1), calls=%async_computation | async-start | bytes 2097152 | tf_op jit(solution)/shard_map/all_to_all | solution.py:576

commit v9 on v7

--- a/solution.py
+++ b/solution.py
@@ -40,7 +40,11 @@
 
 
 def rms_scaled(values, gain):
-    return values * lax.rsqrt(jnp.mean(values * values, axis=-1, keepdims=True) + EPS) * gain
+    rows, width = values.shape
+    ones = jnp.ones((width, LANES), BF16)
+    means = dot((values * values).astype(BF16), ones) * (1.0 / width)
+    scale = lax.rsqrt(means + EPS)
+    return values * jnp.concatenate([scale] * (width // LANES), axis=1) * gain
 
 
 def vmem_spec():
@@ -172,16 +176,24 @@
             inside = (k_pos >= 0) & (k_pos < place_ref[1])
             for head in range(head_count):
                 bias_buf[block, head] = jnp.where(inside & (apart <= window_ref[head]), 0.0, -1e30)
+        value_buf[...] = jnp.ones(value_buf.shape, BF16)
 
     key_buf[:, reach : reach + rows] = key_ref[0]
-    value_buf[reach : reach + rows] = value_ref[0]
+    groups = head_count // group_heads
+
+    def put_values(lower, values):
+        for group in range(groups):
+            lanes = slice(2 * group * LANES, (2 * group + 1) * LANES)
+            value_buf[lower : lower + values.shape[0], lanes] = values[:, group * LANES : (group + 1) * LANES]
+
+    put_values(reach, value_ref[0])
     key_norms = norm_ref[0, 1:2, :]
     for ref, lower in ((left_ref, 0), (right_ref, reach + rows)):
         normed = rms_scaled(ref[0].astype(F32), attn_gain_ref[...]).astype(BF16)
         keys = dot(normed, w_key_ref[...])
         key_norms = jnp.maximum(key_norms, largest_norms(keys, head_count))
         key_buf[:, lower : lower + reach] = keys.T.astype(BF16)
-        value_buf[lower : lower + reach] = dot(normed, w_value_ref[...]).astype(BF16)
+        put_values(lower, dot(normed, w_value_ref[...]).astype(BF16))
 
     bound = jnp.max(norm_ref[0, 0:1, :] * key_norms) * 1.05
     safe = bound <= SAFE_SCORE * SAFE_SCORE
@@ -195,16 +207,15 @@
         stacked = jnp.concatenate([queries * mask for mask in head_masks], axis=0)
         return dot(stacked, key_buf[lanes, pl.ds(start, count + 2 * reach)])
 
-    def mix_values(start, count, group, weights, totals):
-        lanes = slice(group * LANES, (group + 1) * LANES)
+    def mix_values(start, count, group, weights):
+        lanes = slice(2 * group * LANES, 2 * (group + 1) * LANES)
         mixed_all = dot(jnp.concatenate(weights, axis=0), value_buf[pl.ds(start, count + 2 * reach), lanes])
-        mixed = mixed_all[:count] * (1.0 / totals[0])
+        mixed, totals = mixed_all[:count, :LANES], mixed_all[:count, LANES:]
         for head in range(1, group_heads):
-            part = mixed_all[head * count : (head + 1) * count] * (1.0 / totals[head])
-            mixed = jnp.where(lane_head == head, part, mixed)
-        mixed_buf[pl.ds(start, count), lanes] = mixed.astype(BF16)
-
-    groups = head_count // group_heads
+            part = mixed_all[head * count : (head + 1) * count]
+            mixed = jnp.where(lane_head == head, part[:, :LANES], mixed)
+            totals = jnp.where(lane_head == head, part[:, LANES:], totals)
+        mixed_buf[pl.ds(start, count), group * LANES : (group + 1) * LANES] = (mixed / totals).astype(BF16)
 
     @pl.when(safe)
     def _():
@@ -214,18 +225,15 @@
         scores = scores_of(units[0][0], pair, units[0][1])
         for at, (start, group) in enumerate(units):
             following = scores_of(units[at + 1][0], pair, units[at + 1][1]) if at + 1 < len(units) else None
-            weights, totals = [], []
+            weights = []
             for head in range(group_heads):
                 top = head * pair
                 bias = [bias_buf[start // Q_ROWS + part, group * group_heads + head] for part in range(2)]
                 upper = jnp.exp2(scores[top : top + Q_ROWS, :key_count] + bias[0])
                 lower = jnp.exp2(scores[top + Q_ROWS : top + pair, Q_ROWS:] + bias[1])
-                totals.append(
-                    jnp.concatenate([jnp.sum(v, axis=-1, keepdims=True) for v in (upper, lower)], axis=0)
-                )
                 weights.append(jnp.concatenate([upper.astype(BF16), corner], axis=1))
                 weights.append(jnp.concatenate([corner, lower.astype(BF16)], axis=1))
-            mix_values(start, pair, group, weights, totals)
+            mix_values(start, pair, group, weights)
             scores = following
 
     @pl.when(jnp.logical_not(safe))
@@ -234,14 +242,13 @@
             start = block * Q_ROWS
             for group in range(groups):
                 scores = scores_of(start, Q_ROWS, group)
-                weights, totals = [], []
+                weights = []
                 for head in range(group_heads):
                     score_matrix = scores[head * Q_ROWS : (head + 1) * Q_ROWS]
                     score_matrix = score_matrix + bias_buf[block, group * group_heads + head]
                     expo = jnp.exp2(score_matrix - jnp.max(score_matrix, axis=-1, keepdims=True))
-                    totals.append(jnp.sum(expo, axis=-1, keepdims=True))
                     weights.append(expo.astype(BF16))
-                mix_values(start, Q_ROWS, group, weights, totals)
+                mix_values(start, Q_ROWS, group, weights)
 
     after = (state_ref[0].astype(F32) + dot(mixed_buf[...], w_out_ref[...])).astype(BF16)
     normed_mid = rms_scaled(after.astype(F32), ffn_gain_ref[...]).astype(BF16)
@@ -275,7 +282,7 @@
         out_specs=pl.BlockSpec((shares, 1, row_count // shares, feat_width), lambda m: (0, m, 0, 0)),
         scratch_shapes=[
             pltpu.VMEM((feat_width, row_count + 2 * reach), BF16),
-            pltpu.VMEM((row_count + 2 * reach, feat_width), BF16),
+            pltpu.VMEM((row_count + 2 * reach, 2 * feat_width), BF16),
             pltpu.VMEM((row_count // Q_ROWS, head_window.shape[0], Q_ROWS, key_count), F32),
             pltpu.VMEM((row_count, feat_width), BF16),
         ],

time: 93.2 us -> 92.4 us (level)
  no operation moved by 1% of the time
where the time goes in v9:
time: 92.4 us; the launch traced here: 92 us
  blocking collectives  39.5 us (43%)
  Pallas kernels  31.7 us (34%)
  waiting for transfers between devices  8.46 us (9%)
  starting transfers between devices  7.55 us (8%)
  local copies, waits for them, and re-layouts  4.46 us (5%)
    pallas_call x1, Pallas kernels, forward(): pl.pallas_call(forward_kernel, grid=(members,), out_shape=jax.ShapeDtypeS...  22.5 us
    all_to_all x1, blocking collectives, local(): lax.all_to_all(jnp.broadcast_to(partial[None], (device_count, *partial.sh...  22.2 us
    all_to_all x1, blocking collectives, local(): lax.all_to_all(mixed, 'mem', split_axis=0, concat_axis=0, tiled=True)  17.3 us
    all_to_all x1, waiting for transfers between devices, local(): lax.all_to_all(forecast, 'mem', split_axis=0, concat_axis=0, tiled=True)  7.38 us
    all_to_all x1, starting transfers between devices, local(): lax.all_to_all(forecast, 'mem', split_axis=0, concat_axis=0, tiled=True)  3.85 us
    pallas_call x1, Pallas kernels, combine(): pl.pallas_call(combine_kernel, out_shape=jax.ShapeDtypeStruct(share.shape...  3.64 us
    pallas_call x1, Pallas kernels, project(): pl.pallas_call(functools.partial(project_kernel, heads), grid=(members,),...  2.8 us
    ppermute x1, starting transfers between devices, local(): left = lax.ppermute(ens_state[:, row_count - WIN:], 'tok', up)  2.4 us
  transfers between devices with their start and end apart: 3, of which 2 were waited for; matrix products, arithmetic and copies ran while one was open for 0% of the time, Pallas kernels for 4%

profile of v9, /device:TPU:0, one launch (start us, length us, event | category | flops | bytes accessed | tf_op | source)
XLA Modules:
  0.0 92.0 jit_solution(5937533167796561827)
XLA Ops:
  0.0 1.4 %fusion = (bf16[4,256,256]{2,1,0:T(8,128)(2,1)S(1)}, bf16[4,256,256]{2,1,0:T(8,128)(2,1)S(1)}) fusion(bf16[4,512,256]{2,1,0:T(8,128)(2,1)} %state_ref.1), kind=kLoop, calls=%fused_computation.1 | loop fusion | bytes 2097152 | tf_op jit(solution)/shard_map/slice | solution.py:445
  1.4 2.4 %collective-permute-start = (bf16[4,256,256]{2,1,0:T(8,128)(2,1)S(1)}, bf16[4,256,256]{2,1,0:T(8,128)(2,1)S(1)}, u32[]{:S(2)}, u32[]{:S(2)}) collective-permute-start(bf16[4,256,256]{2,1,0:T(8,128)(2,1)S(1)} %get-tuple-element.14), channel_id=1, source_target_pairs={{0,1},{1,2},{2,3},{3,4},{4,5},{5,6},{6,7},{8,9},{9,10},{10,11},{11... | collective-permute-start | bytes 1572872 | tf_op jit(solution)/shard_map/ppermute | solution.py:444
  3.8 1.3 %collective-permute-start.1 = (bf16[4,256,256]{2,1,0:T(8,128)(2,1)S(1)}, bf16[4,256,256]{2,1,0:T(8,128)(2,1)S(1)}, u32[]{:S(2)}, u32[]{:S(2)}) collective-permute-start(bf16[4,256,256]{2,1,0:T(8,128)(2,1)S(1)} %get-tuple-element.13), channel_id=1, source_target_pairs={{1,0},{2,1},{3,2},{4,3},{5,4},{6,5},{7,6},{9,8},{10,9},{11,10},{12... | collective-permute-start | bytes 1572872 | tf_op jit(solution)/shard_map/ppermute | solution.py:445
  5.1 0.0 copy-start.12
  5.1 0.0 copy-done
  5.1 0.0 copy-done.4
  5.1 0.0 copy-done.5
  5.1 0.0 copy-done.6
  5.2 0.6 copy-done.12
  5.8 2.8 %project.1 = (bf16[4,512,256]{2,1,0:T(8,128)(2,1)S(1)}, bf16[4,256,512]{2,1,0:T(8,128)(2,1)S(1)}, bf16[4,512,256]{2,1,0:T(8,128)(2,1)S(1)}, f32[4,8,128]{2,1,0:T(8,128)S(1)}) custom-call(bf16[4,512,256]{2,1,0:T(8,128)(2,1)S(1)} %copy-done, f32[1,256]{1,0:T(1,128)S(1)} %bitcast.19, bf16[256,256]{1,0:T(8,128)(2,1)S(1)} %copy-done.4, ...), custom_call_target="tpu_custom_call" | custom-call | flops 805306368 | bytes 4194304 | tf_op jit(solution)/shard_map/project/pallas_call | solution.py:125
  8.6 0.1 pad_add_fusion.place_ref
  8.7 0.0 collective-permute-done.left_ref
  8.7 1.1 %collective-permute-done.1.right_ref = bf16[4,256,256]{2,1,0:T(8,128)(2,1)S(1)} collective-permute-done((bf16[4,256,256]{2,1,0:T(8,128)(2,1)S(1)}, bf16[4,256,256]{2,1,0:T(8,128)(2,1)S(1)}, u32[]{:S(2)}, u32[]{:S(2)}) %collective-permute-start.1) | collective-permute-done | bytes 524320 | tf_op jit(solution)/shard_map/ppermute | solution.py:445
  9.8 0.0 copy-done.1
  9.8 0.0 copy-done.2
  9.8 0.0 copy-done.3
  9.8 0.0 copy-done.7
  9.8 0.6 copy-done.13
  10.4 0.0 copy-done.14
  10.4 22.5 %forward.1 = bf16[4,4,128,256]{3,2,1,0:T(8,128)(2,1)} custom-call(s32[2]{0:T(128)S(1)} %pad_add_fusion.place_ref, s32[4]{0:T(128)S(1)} %copy-done.14, bf16[4,512,256]{2,1,0:T(8,128)(2,1)S(1)} %copy-done, bf16[4,512,256]{2,1,0:T(8,128)(2,1)S(1)} %get-tuple-element.9.query_ref, bf16[4,256,512]{2,1,0:T(8,128)(2,1)S(1)} %get-tuple-element.10.key_ref, ...), custom_call_target="tpu_custom_call" | custom-call | flops 9395240960 | bytes 5242880 | tf_op jit(solution)/shard_map/forward/pallas_call | solution.py:274
  32.9 3.9 %all-to-all-start = ((bf16[4,4,128,256]{3,2,1,0:T(8,128)(2,1)}), bf16[4,4,128,256]{3,2,1,0:T(8,128)(2,1)S(1)}, u32[]{:S(2)}, u32[]{:S(2)}) async-start(bf16[4,4,128,256]{3,2,1,0:T(8,128)(2,1)} %forward.1), calls=%async_computation | async-start | bytes 2097152 | tf_op jit(solution)/shard_map/all_to_all | solution.py:455
  36.8 0.0 copy-done.9
  36.8 0.0 copy-done.10
  36.8 0.0 copy-done.11
  36.8 0.7 copy-done.8
  37.5 1.3 %sample_grid.1.grid_ref = f32[2,128,256]{2,1,0:T(8,128)S(1)} custom-call(s32[1]{0:T(128)} %bitcast.4.start_ref, s32[1,4096]{1,0:T(1,128)S(1)} %bitcast.15, s32[1,4096]{1,0:T(1,128)S(1)} %bitcast.16, f32[1,4096]{1,0:T(1,128)S(1)} %bitcast.17, f32[1,4096]{1,0:T(1,128)S(1)} %bitcast.18), custom_call_target="tpu_custom_call" | custom-call | flops 1073741824 | bytes 65536 | tf_op jit(solution)/shard_map/sample_grid/pallas_call | solution.py:81
  38.8 7.4 %all-to-all-done = bf16[4,4,128,256]{3,2,1,0:T(8,128)(2,1)S(1)} async-done(((bf16[4,4,128,256]{3,2,1,0:T(8,128)(2,1)}), bf16[4,4,128,256]{3,2,1,0:T(8,128)(2,1)S(1)}, u32[]{:S(2)}, u32[]{:S(2)}) %all-to-all-start) | async-done | bytes 1048608 | tf_op jit(solution)/shard_map/all_to_all | solution.py:455
  46.2 1.5 %gram.1 = f32[8,128]{1,0:T(8,128)S(1)} custom-call(bf16[16,128,256]{2,1,0:T(8,128)(2,1)S(1)} %bitcast.12, f32[2,128,256]{2,1,0:T(8,128)S(1)} %sample_grid.1.grid_ref), custom_call_target="tpu_custom_call" | custom-call | flops 805306368 | bytes 1048576 | tf_op jit(solution)/shard_map/gram/pallas_call | solution.py:330
  47.7 22.2 %all_to_all.15.partial_ref = f32[32,8,128]{2,1,0:T(8,128)S(1)} all-to-all(f32[32,8,128]{2,1,0:T(8,128)S(1)} %broadcast_in_dim.2), channel_id=1, replica_groups=mesh['mem'=4,'tok'=8] {'mem','tok'}, dimensions={0} | all-to-all | bytes 262144 | tf_op jit(solution)/shard_map/all_to_all | solution.py:458
  70.0 3.6 %combine.1 = bf16[16,128,256]{2,1,0:T(8,128)(2,1)S(1)} custom-call(f32[32,8,128]{2,1,0:T(8,128)S(1)} %all_to_all.15.partial_ref, bf16[16,128,256]{2,1,0:T(8,128)(2,1)S(1)} %bitcast.13), custom_call_target="tpu_custom_call" | custom-call | flops 536870912 | bytes 2097152 | tf_op jit(solution)/shard_map/combine/pallas_call | solution.py:405
  73.6 17.3 %all_to_all.16 = bf16[4,4,128,256]{3,2,1,0:T(8,128)(2,1)S(1)} all-to-all(bf16[4,4,128,256]{3,2,1,0:T(8,128)(2,1)S(1)} %bitcast.14), channel_id=1, replica_groups=mesh['mem'=4,'tok'=8] {'mem'}, dimensions={0} | all-to-all | bytes 2097152 | tf_op jit(solution)/shard_map/all_to_all | solution.py:466
  90.9 1.0 %copy.16 = bf16[4,4,128,256]{3,2,1,0:T(8,128)(2,1)} copy(bf16[4,4,128,256]{3,2,0,1:T(8,128)(2,1)S(1)} %bitcast.22) | data formatting | bytes 2097152 | tf_op jit(solution)/shard_map/transpose | solution.py:467
  (15 shorter events, 0.0 us)
Async XLA Ops:
  0.0 5.1 %copy-start = (bf16[4,512,256]{2,1,0:T(8,128)(2,1)S(1)}, bf16[4,512,256]{2,1,0:T(8,128)(2,1)}, u32[]{:S(2)}) copy-start(bf16[4,512,256]{2,1,0:T(8,128)(2,1)} %state_ref.1) | copy-start | bytes 3145732
  0.0 5.1 %copy-start.4 = (bf16[256,256]{1,0:T(8,128)(2,1)S(1)}, bf16[256,256]{1,0:T(8,128)(2,1)}, u32[]{:S(2)}) copy-start(bf16[256,256]{1,0:T(8,128)(2,1)} %w_query_ref.1) | copy-start | bytes 393220
  0.0 5.1 %copy-start.5 = (bf16[256,256]{1,0:T(8,128)(2,1)S(1)}, bf16[256,256]{1,0:T(8,128)(2,1)}, u32[]{:S(2)}) copy-start(bf16[256,256]{1,0:T(8,128)(2,1)} %w_key_ref.3) | copy-start | bytes 393220
  0.0 5.1 %copy-start.6 = (bf16[256,256]{1,0:T(8,128)(2,1)S(1)}, bf16[256,256]{1,0:T(8,128)(2,1)}, u32[]{:S(2)}) copy-start(bf16[256,256]{1,0:T(8,128)(2,1)} %w_value_ref.3) | copy-start | bytes 393220
  1.4 7.3 %collective-permute-start = (bf16[4,256,256]{2,1,0:T(8,128)(2,1)S(1)}, bf16[4,256,256]{2,1,0:T(8,128)(2,1)S(1)}, u32[]{:S(2)}, u32[]{:S(2)}) collective-permute-start(bf16[4,256,256]{2,1,0:T(8,128)(2,1)S(1)} %get-tuple-element.14), channel_id=1, source_target_pairs={{0,1},{1,2},{2,3},{3,4},{4,5},{5,6},{6,7},{8,9},{9,10},{10,11},{11... | collective-permute-start | bytes 1572872 | tf_op jit(solution)/shard_map/ppermute | solution.py:444
  3.8 6.0 %collective-permute-start.1 = (bf16[4,256,256]{2,1,0:T(8,128)(2,1)S(1)}, bf16[4,256,256]{2,1,0:T(8,128)(2,1)S(1)}, u32[]{:S(2)}, u32[]{:S(2)}) collective-permute-start(bf16[4,256,256]{2,1,0:T(8,128)(2,1)S(1)} %get-tuple-element.13), channel_id=1, source_target_pairs={{1,0},{2,1},{3,2},{4,3},{5,4},{6,5},{7,6},{9,8},{10,9},{11,10},{12... | collective-permute-start | bytes 1572872 | tf_op jit(solution)/shard_map/ppermute | solution.py:445
  5.1 0.7 copy-start.12
  5.8 4.0 %copy-start.1 = (bf16[256,1024]{1,0:T(8,128)(2,1)S(1)}, bf16[256,1024]{1,0:T(8,128)(2,1)}, u32[]{:S(2)}) copy-start(bf16[256,1024]{1,0:T(8,128)(2,1)} %w_gate_ref.1) | copy-start | bytes 1572868
  5.8 4.0 %copy-start.2 = (bf16[256,1024]{1,0:T(8,128)(2,1)S(1)}, bf16[256,1024]{1,0:T(8,128)(2,1)}, u32[]{:S(2)}) copy-start(bf16[256,1024]{1,0:T(8,128)(2,1)} %w_up_ref.1) | copy-start | bytes 1572868
  5.8 4.0 %copy-start.3 = (bf16[1024,256]{1,0:T(8,128)(2,1)S(1)}, bf16[1024,256]{1,0:T(8,128)(2,1)}, u32[]{:S(2)}) copy-start(bf16[1024,256]{1,0:T(8,128)(2,1)} %down_weight_ref.1) | copy-start | bytes 1572868
  5.8 4.0 %copy-start.7 = (bf16[256,256]{1,0:T(8,128)(2,1)S(1)}, bf16[256,256]{1,0:T(8,128)(2,1)}, u32[]{:S(2)}) copy-start(bf16[256,256]{1,0:T(8,128)(2,1)} %w_out_ref.1) | copy-start | bytes 393220
  9.8 0.7 copy-start.13
  9.8 0.7 copy-start.14
  32.9 3.9 %copy-start.9 = (s32[4096]{0:T(1024)S(1)}, s32[4096]{0:T(1024)}, u32[]{:S(2)}) copy-start(s32[4096]{0:T(1024)} %param.27) | copy-start | bytes 49156
  32.9 3.9 %copy-start.10 = (f32[4096]{0:T(1024)S(1)}, f32[4096]{0:T(1024)}, u32[]{:S(2)}) copy-start(f32[4096]{0:T(1024)} %param.28) | copy-start | bytes 49156
  32.9 3.9 %copy-start.11 = (f32[4096]{0:T(1024)S(1)}, f32[4096]{0:T(1024)}, u32[]{:S(2)}) copy-start(f32[4096]{0:T(1024)} %param.29) | copy-start | bytes 49156
  32.9 13.3 %all-to-all-start = ((bf16[4,4,128,256]{3,2,1,0:T(8,128)(2,1)}), bf16[4,4,128,256]{3,2,1,0:T(8,128)(2,1)S(1)}, u32[]{:S(2)}, u32[]{:S(2)}) async-start(bf16[4,4,128,256]{3,2,1,0:T(8,128)(2,1)} %forward.1), calls=%async_computation | async-start | bytes 2097152 | tf_op jit(solution)/shard_map/all_to_all | solution.py:455
  36.8 0.7 copy-start.8

commit v10 on v9

--- a/solution.py
+++ b/solution.py
@@ -154,12 +154,9 @@
     w_gate_ref,
     w_up_ref,
     down_weight_ref,
-    out_ref,
-    key_buf,
-    value_buf,
-    bias_buf,
-    mixed_buf,
+    *refs,
 ):
+    out_refs, (key_buf, value_buf, bias_buf, mixed_buf, forecast_buf) = refs[:-5], refs[-5:]
     rows, feat_width = state_ref.shape[1:]
     reach = left_ref.shape[1]
     head_count = window_ref.shape[0]
@@ -258,10 +255,11 @@
         gate = 0.5 * dot(normed_mid, w_gate_ref[:, part])
         hidden = (gate * (1.0 + jnp.tanh(gate)) * dot(normed_mid, w_up_ref[:, part])).astype(BF16)
         forecast += dot(hidden, down_weight_ref[part, :])
-    forecast = forecast.astype(BF16)
-    shares, _, share_rows, _ = out_ref.shape
-    for share in range(shares):
-        out_ref[share, 0] = forecast[share * share_rows : (share + 1) * share_rows]
+    forecast_buf[...] = forecast.astype(BF16)
+    share_rows = out_refs[0].shape[1]
+    for part, out_ref in enumerate(out_refs):
+        lower = pl.multiple_of((place_ref[2] ^ part) * share_rows, share_rows)
+        out_ref[0] = forecast_buf[pl.ds(lower, share_rows), :]
 
 
 def forward(place, head_window, own, projected, left, right, gains, weights, shares):
@@ -274,16 +272,17 @@
     return pl.pallas_call(
         forward_kernel,
         grid=(members,),
-        out_shape=jax.ShapeDtypeStruct((shares, members, row_count // shares, feat_width), BF16),
+        out_shape=[jax.ShapeDtypeStruct((members, row_count // shares, feat_width), BF16)] * shares,
         in_specs=[smem_spec()] * 2
         + [pl.BlockSpec((1, *v.shape[1:]), lambda m: (m, 0, 0)) for v in (own, *projected)]
         + [edge_block] * 2
         + [vmem_spec()] * (len(gains) + len(weights)),
-        out_specs=pl.BlockSpec((shares, 1, row_count // shares, feat_width), lambda m: (0, m, 0, 0)),
+        out_specs=[pl.BlockSpec((1, row_count // shares, feat_width), lambda m: (m, 0, 0))] * shares,
         scratch_shapes=[
             pltpu.VMEM((feat_width, row_count + 2 * reach), BF16),
             pltpu.VMEM((row_count + 2 * reach, 2 * feat_width), BF16),
             pltpu.VMEM((row_count // Q_ROWS, head_window.shape[0], Q_ROWS, key_count), F32),
+            pltpu.VMEM((row_count, feat_width), BF16),
             pltpu.VMEM((row_count, feat_width), BF16),
         ],
         compiler_params=pltpu.CompilerParams(vmem_limit_bytes=VMEM_LIMIT),
@@ -292,14 +291,21 @@
     )(place, head_window, own, *projected, left, right, *gains, *weights)
 
 
-def gram_kernel(share_ref, grid_ref, out_ref):
-    members, rows, feat_width = share_ref.shape
+def global_member(held, index, own_members):
+    return ((held // own_members) ^ index) * own_members + held % own_members
+
+
+def gram_kernel(index_ref, *refs):
+    share_refs, grid_ref, out_ref = refs[:-2], refs[-2], refs[-1]
+    own_members, rows, feat_width = share_refs[0].shape
+    members = own_members * len(share_refs)
+    index = index_ref[0]
     stack = members * GROUP
     total = jnp.zeros((stack, stack), F32)
     proj = jnp.zeros((members, GROUP, feat_width), F32)
     for lower in range(0, rows, GROUP):
         part = slice(lower, lower + GROUP)
-        fields = share_ref[:, part, :].astype(F32)
+        fields = jnp.concatenate([ref[:, part, :] for ref in share_refs], axis=0).astype(F32)
         mean = jnp.sum(fields, axis=0) * (1.0 / members)
         spread = fields - mean[None]
         weight = grid_ref[0, part, :]
@@ -310,34 +316,36 @@
         total += dot(w_high, high, last) + dot(w_high, low, last) + dot(w_low, high, last)
     same = iota((stack, stack), 0) % GROUP == iota((stack, stack), 1) % GROUP
     by_row = jnp.sum(jnp.where(same, total, 0.0).reshape(members, GROUP, stack), axis=1)
-    folded = (iota((stack, LANES), 0) // GROUP == iota((stack, LANES), 1) % members).astype(F32)
-    tiled = exact_dot(by_row, folded)
+    column = global_member(iota((stack, LANES), 0) // GROUP, index, own_members)
+    folded = (column == iota((stack, LANES), 1) % members).astype(F32)
+    held = global_member(iota((members, members), 1), index, own_members)
+    in_order = (held == iota((members, members), 0)).astype(F32)
+    tiled = exact_dot(in_order, exact_dot(by_row, folded))
     per_row = LANES // members
     keep = iota((members, LANES), 0) % per_row == iota((members, LANES), 1) // members
     packed = jnp.sum(jnp.where(keep, tiled, 0.0).reshape(members // per_row, per_row, LANES), axis=1)
     proj_col = jnp.sum(jnp.sum(proj, axis=1), axis=1, keepdims=True)
-    proj_row = jnp.sum(
-        jnp.where(iota((members, LANES), 0) == iota((members, LANES), 1), proj_col, 0.0), axis=0, keepdims=True
-    )
+    at_lane = global_member(iota((members, LANES), 0), index, own_members) == iota((members, LANES), 1)
+    proj_row = jnp.sum(jnp.where(at_lane, proj_col, 0.0), axis=0, keepdims=True)
     filled = members // per_row + 1
     blank = jnp.zeros((out_ref.shape[0] - filled, LANES), F32)
     out_ref[...] = jnp.concatenate([packed, proj_row, blank], axis=0)
 
 
-def gram_partial(share, grid):
-    members = share.shape[0]
+def gram_partial(index, shares, grid):
+    members = shares[0].shape[0] * len(shares)
     filled = members * members // LANES + 1
     return pl.pallas_call(
         gram_kernel,
         out_shape=jax.ShapeDtypeStruct((-(-filled // 8) * 8, LANES), F32),
-        in_specs=[vmem_spec()] * 2,
+        in_specs=[smem_spec()] + [vmem_spec()] * (len(shares) + 1),
         out_specs=vmem_spec(),
         compiler_params=pltpu.CompilerParams(vmem_limit_bytes=VMEM_LIMIT),
         cost_estimate=pl.CostEstimate(
-            flops=6 * GROUP * members * share.size, bytes_accessed=2 * share.size, transcendentals=0
+            flops=3 * GROUP * members * members * grid.size, bytes_accessed=members * grid.size, transcendentals=0
         ),
         name="gram",
-    )(share, grid)
+    )(index, *shares, grid)
 
 
 def ensemble_transform(gram, proj):
@@ -373,8 +381,10 @@
     return 1.0 / members + moved - jnp.sum(moved, axis=0, keepdims=True) * (1.0 / members)
 
 
-def combine_kernel(partial_ref, share_ref, out_ref):
-    members, rows, feat_width = share_ref.shape
+def combine_kernel(index_ref, partial_ref, *refs):
+    share_refs, out_refs = refs[: len(refs) // 2], refs[len(refs) // 2 :]
+    own_members, rows, feat_width = share_refs[0].shape
+    members = own_members * len(share_refs)
     stack = members * GROUP
     per_row = LANES // members
     sums = jnp.sum(partial_ref[...], axis=0)
@@ -388,31 +398,64 @@
     on_diagonal = iota((members, LANES), 0) == iota((members, LANES), 1)
     proj = jnp.sum(jnp.where(on_diagonal, proj_row, 0.0), axis=1, keepdims=True)
     transform = ensemble_transform(gram, proj)
-    pick = (iota((stack, members), 0) // GROUP == iota((stack, members), 1)).astype(F32).astype(BF16)
+    held = global_member(iota((stack, members), 0) // GROUP, index_ref[0], own_members)
+    pick = (held == iota((stack, members), 1)).astype(F32).astype(BF16)
     same = iota((stack, stack), 0) % GROUP == iota((stack, stack), 1) % GROUP
     mixers = []
     for piece in halves(transform):
         rows_of = dot(pick, piece, ((1,), (1,))).astype(BF16)
         mixers.append(jnp.where(same, dot(rows_of, pick, ((1,), (1,))), 0.0).astype(BF16))
     for lower in range(0, rows, GROUP):
-        fields = share_ref[:, lower : lower + GROUP, :].reshape(stack, feat_width)
-        mixed = dot(mixers[0], fields) + dot(mixers[1], fields)
-        out_ref[:, lower : lower + GROUP, :] = mixed.astype(BF16).reshape(members, GROUP, feat_width)
-
-
-def combine(partials, share):
-    members = share.shape[0]
+        part = slice(lower, lower + GROUP)
+        fields = jnp.concatenate([ref[:, part, :].reshape(-1, feat_width) for ref in share_refs], axis=0)
+        mixed = (dot(mixers[0], fields) + dot(mixers[1], fields)).astype(BF16)
+        own_stack = own_members * GROUP
+        for at, out_ref in enumerate(out_refs):
+            piece = mixed[at * own_stack : (at + 1) * own_stack]
+            out_ref[:, part, :] = piece.reshape(own_members, GROUP, feat_width)
+
+
+def combine(index, partials, shares):
+    size = shares[0].size * len(shares)
+    members = shares[0].shape[0] * len(shares)
     return pl.pallas_call(
         combine_kernel,
-        out_shape=jax.ShapeDtypeStruct(share.shape, BF16),
-        in_specs=[vmem_spec()] * 2,
-        out_specs=vmem_spec(),
+        out_shape=[jax.ShapeDtypeStruct(v.shape, BF16) for v in shares],
+        in_specs=[smem_spec()] + [vmem_spec()] * (1 + len(shares)),
+        out_specs=[vmem_spec()] * len(shares),
         compiler_params=pltpu.CompilerParams(vmem_limit_bytes=VMEM_LIMIT),
-        cost_estimate=pl.CostEstimate(
-            flops=4 * GROUP * members * share.size, bytes_accessed=4 * share.size, transcendentals=0
-        ),
+        cost_estimate=pl.CostEstimate(flops=4 * GROUP * members * size, bytes_accessed=4 * size, transcendentals=0),
         name="combine",
-    )(partials, share)
+    )(index, partials, *shares)
+
+
+def assemble_kernel(index_ref, *refs):
+    part_refs, out_ref = refs[:-1], refs[-1]
+    rows = part_refs[0].shape[1]
+    for part, ref in enumerate(part_refs):
+        lower = pl.multiple_of((index_ref[0] ^ part) * rows, rows)
+        out_ref[0, pl.ds(lower, rows), :] = ref[0]
+
+
+def assemble(index, parts):
+    members, rows, feat_width = parts[0].shape
+    return pl.pallas_call(
+        assemble_kernel,
+        grid=(members,),
+        out_shape=jax.ShapeDtypeStruct((members, len(parts) * rows, feat_width), BF16),
+        in_specs=[smem_spec()] + [pl.BlockSpec((1, rows, feat_width), lambda m: (m, 0, 0))] * len(parts),
+        out_specs=pl.BlockSpec((1, len(parts) * rows, feat_width), lambda m: (m, 0, 0)),
+        compiler_params=pltpu.CompilerParams(vmem_limit_bytes=VMEM_LIMIT),
+        cost_estimate=pl.CostEstimate(flops=0, bytes_accessed=4 * len(parts) * parts[0].size, transcendentals=0),
+        name="assemble",
+    )(index, *parts)
+
+
+def exchanged(parts):
+    count = lax.axis_size("mem")
+    return [
+        lax.ppermute(v, "mem", [(i, i ^ part) for i in range(count)]) if part else v for part, v in enumerate(parts)
+    ]
 
 
 def local(
@@ -436,7 +479,6 @@
     mem_count = lax.axis_size("mem")
     tok_count = lax.axis_size("tok")
     device_count = mem_count * tok_count
-    members = own_members * mem_count
     share_rows = row_count // mem_count
     first_pos = lax.axis_index("tok") * row_count
     up = [(i, i + 1) for i in range(tok_count - 1)]
@@ -447,14 +489,15 @@
     grid = sample_grid(
         share_start.astype(jnp.int32).reshape(1), obs_token, obs_channel, obs_value, obs_var, share_rows, feat_width
     )
-    place = jnp.stack([first_pos, row_count * tok_count]).astype(jnp.int32)
+    index = lax.axis_index("mem")
+    place = jnp.stack([first_pos, row_count * tok_count, index]).astype(jnp.int32)
+    index = index.astype(jnp.int32).reshape(1)
     gains = [attn_gain.reshape(1, -1), ffn_gain.reshape(1, -1)]
     projected = project(ens_state, head_window.shape[0], gains[0], w_query, w_key, w_value)
     weights = [w_key, w_value, w_out, w_gate, w_up, down_weight]
     forecast = forward(place, head_window, ens_state, projected, left, right, gains, weights, mem_count)
-    share = lax.all_to_all(forecast, "mem", split_axis=0, concat_axis=0, tiled=True)
-    share = share.reshape(members, share_rows, feat_width)
-    partial = gram_partial(share, grid)
+    shares = exchanged(forecast)
+    partial = gram_partial(index, shares, grid)
     partials = lax.all_to_all(
         jnp.broadcast_to(partial[None], (device_count, *partial.shape)),
         ("mem", "tok"),
@@ -462,9 +505,7 @@
         concat_axis=0,
         tiled=True,
     )
-    mixed = combine(partials, share).reshape(mem_count, own_members, share_rows, feat_width)
-    mixed = lax.all_to_all(mixed, "mem", split_axis=0, concat_axis=0, tiled=True)
-    return jnp.moveaxis(mixed, 0, 1).reshape(own_members, row_count, feat_width)
+    return assemble(index, exchanged(combine(index, partials, shares)))
 
 
 def solution(mesh):

time: 92.4 us -> 87.6 us (0.948)
  blocking collectives: 39.5 us -> 22.3 us
  waiting for transfers between devices: 8.46 us -> 17.6 us
  starting transfers between devices: 7.55 us -> 10.8 us
  Pallas kernels: 31.7 us -> 32.8 us
  local copies, waits for them, and re-layouts: 4.46 us -> 3.52 us
    all_to_all x1 -> x0, blocking collectives: 17.3 us -> none  [local(): lax.all_to_all(mixed, 'mem', split_axis=0, concat_axis=0, tiled=True)]
    ppermute x0 -> x6, waiting for transfers between devices: none -> 16.6 us  [exchanged(): lax.ppermute(v, 'mem', [(i, i ^ part) for i in range(count)])]
    all_to_all x1 -> x0, waiting for transfers between devices: 7.38 us -> none  [local(): lax.all_to_all(forecast, 'mem', split_axis=0, concat_axis=0, tiled=True)]
    ppermute x0 -> x6, starting transfers between devices: none -> 7.11 us  [exchanged(): lax.ppermute(v, 'mem', [(i, i ^ part) for i in range(count)])]
    all_to_all x1 -> x0, starting transfers between devices: 3.85 us -> none  [local(): lax.all_to_all(forecast, 'mem', split_axis=0, concat_axis=0, tiled=True)]
    transpose x1 -> x0, local copies, waits for them, and re-layouts: 1.04 us -> none  [local(): return jnp.moveaxis(mixed, 0, 1).reshape(own_members, row_count, feat_width)]
    pallas_call x2 -> x3, Pallas kernels: 26.1 us -> 27 us  [the longest x1 21.9 us: forward(): pl.pallas_call(forward_kernel, grid=(members,), out_shape=[jax.ShapeDtype...]
  transfers between devices with their start and end apart: 3 -> 8, of which waited for: 2 -> 5; matrix products, arithmetic and copies ran while one was open for 0% -> 0% of each run, Pallas kernels for 4% -> 5%
where the time goes in v10:
time: 87.6 us; the launch traced here: 87.3 us
  Pallas kernels  32.8 us (37%)
  blocking collectives  22.3 us (25%)
  waiting for transfers between devices  17.6 us (20%)
  starting transfers between devices  10.8 us (12%)
  local copies, waits for them, and re-layouts  3.52 us (4%)
    all_to_all x1, blocking collectives, local(): lax.all_to_all(jnp.broadcast_to(partial[None], (device_count, *partial.sh...  22.3 us
    pallas_call x1, Pallas kernels, forward(): pl.pallas_call(forward_kernel, grid=(members,), out_shape=[jax.ShapeDtype...  21.9 us
    ppermute x6, waiting for transfers between devices, exchanged(): lax.ppermute(v, 'mem', [(i, i ^ part) for i in range(count)])  16.6 us
    ppermute x6, starting transfers between devices, exchanged(): lax.ppermute(v, 'mem', [(i, i ^ part) for i in range(count)])  7.11 us
    pallas_call x1, Pallas kernels, combine(): pl.pallas_call(combine_kernel, out_shape=[jax.ShapeDtypeStruct(v.shape, B...  3.64 us
    pallas_call x1, Pallas kernels, project(): pl.pallas_call(functools.partial(project_kernel, heads), grid=(members,),...  2.8 us
    ppermute x1, starting transfers between devices, local(): left = lax.ppermute(ens_state[:, row_count - WIN:], 'tok', up)  2.39 us
    slice x1, local copies, waits for them, and re-layouts, local(): right = lax.ppermute(ens_state[:, :WIN], 'tok', down)  2.17 us
  transfers between devices with their start and end apart: 8, of which 5 were waited for; matrix products, arithmetic and copies ran while one was open for 0% of the time, Pallas kernels for 5%

profile of v10, /device:TPU:0, one launch (start us, length us, event | category | flops | bytes accessed | tf_op | source)
XLA Modules:
  0.0 87.3 jit_solution(1867936595580110172)
XLA Ops:
  0.0 2.2 %fusion = (bf16[4,256,256]{2,1,0:T(8,128)(2,1)S(1)}, bf16[4,256,256]{2,1,0:T(8,128)(2,1)}) fusion(bf16[4,512,256]{2,1,0:T(8,128)(2,1)} %state_ref.1), kind=kLoop, calls=%fused_computation.1 | loop fusion | bytes 2097152 | tf_op jit(solution)/shard_map/slice | solution.py:487
  2.2 2.4 %collective-permute-start = (bf16[4,256,256]{2,1,0:T(8,128)(2,1)}, bf16[4,256,256]{2,1,0:T(8,128)(2,1)S(1)}, u32[]{:S(2)}, u32[]{:S(2)}) collective-permute-start(bf16[4,256,256]{2,1,0:T(8,128)(2,1)} %get-tuple-element.30), channel_id=1, source_target_pairs={{0,1},{1,2},{2,3},{3,4},{4,5},{5,6},{6,7},{8,9},{9,10},{10,11},{11... | collective-permute-start | bytes 1572872 | tf_op jit(solution)/shard_map/ppermute | solution.py:486
  4.6 1.3 %collective-permute-start.1 = (bf16[4,256,256]{2,1,0:T(8,128)(2,1)S(1)}, bf16[4,256,256]{2,1,0:T(8,128)(2,1)S(1)}, u32[]{:S(2)}, u32[]{:S(2)}) collective-permute-start(bf16[4,256,256]{2,1,0:T(8,128)(2,1)S(1)} %get-tuple-element.29), channel_id=1, source_target_pairs={{1,0},{2,1},{3,2},{4,3},{5,4},{6,5},{7,6},{9,8},{10,9},{11,10},{12... | collective-permute-start | bytes 1572872 | tf_op jit(solution)/shard_map/ppermute | solution.py:487
  5.9 0.0 copy-start.12
  5.9 0.0 copy-done
  5.9 0.6 copy-done.12
  6.6 2.8 %project.1 = (bf16[4,512,256]{2,1,0:T(8,128)(2,1)S(1)}, bf16[4,256,512]{2,1,0:T(8,128)(2,1)S(1)}, bf16[4,512,256]{2,1,0:T(8,128)(2,1)S(1)}, f32[4,8,128]{2,1,0:T(8,128)S(1)}) custom-call(bf16[4,512,256]{2,1,0:T(8,128)(2,1)S(1)} %copy-done, f32[1,256]{1,0:T(1,128)S(1)} %bitcast.13, bf16[256,256]{1,0:T(8,128)(2,1)S(1)} %copy-done.4, ...), custom_call_target="tpu_custom_call" | custom-call | flops 805306368 | bytes 4194304 | tf_op jit(solution)/shard_map/project/pallas_call | solution.py:125
  9.4 0.1 pad_add_fusion.place_ref
  9.5 0.0 collective-permute-done.left_ref
  9.5 1.1 %collective-permute-done.1.right_ref = bf16[4,256,256]{2,1,0:T(8,128)(2,1)S(1)} collective-permute-done((bf16[4,256,256]{2,1,0:T(8,128)(2,1)S(1)}, bf16[4,256,256]{2,1,0:T(8,128)(2,1)S(1)}, u32[]{:S(2)}, u32[]{:S(2)}) %collective-permute-start.1) | collective-permute-done | bytes 524320 | tf_op jit(solution)/shard_map/ppermute | solution.py:487
  10.6 0.6 copy-done.13
  11.2 21.9 %forward.1 = (bf16[4,128,256]{2,1,0:T(8,128)(2,1)S(1)}, bf16[4,128,256]{2,1,0:T(8,128)(2,1)S(1)}, bf16[4,128,256]{2,1,0:T(8,128)(2,1)S(1)}, bf16[4,128,256]{2,1,0:T(8,128)(2,1)S(1)}) custom-call(s32[3]{0:T(128)S(1)} %pad_add_fusion.place_ref, s32[4]{0:T(128)S(1)} %copy-done.14, bf16[4,512,256]{2,1,0:T(8,128)(2,1)S(1)} %copy-done, ...), custom_call_target="tpu_custom_call" | custom-call | flops 9395240960 | bytes 5242880 | tf_op jit(solution)/shard_map/forward/pallas_call | solution.py:272
  33.1 0.0 copy-start.8
  33.1 1.6 %collective-permute-start.2 = (bf16[4,128,256]{2,1,0:T(8,128)(2,1)S(1)}, bf16[4,128,256]{2,1,0:T(8,128)(2,1)S(1)}, u32[]{:S(2)}, u32[]{:S(2)}) collective-permute-start(bf16[4,128,256]{2,1,0:T(8,128)(2,1)S(1)} %get-tuple-element.22), channel_id=1, source_target_pairs={{0,8},{8,0},{16,24},{24,16},{1,9},{9,1},{17,25},{25,17},{2,10},{10... | collective-permute-start | bytes 786440 | tf_op jit(solution)/shard_map/ppermute | solution.py:457
  34.7 1.5 %collective-permute-start.3 = (bf16[4,128,256]{2,1,0:T(8,128)(2,1)S(1)}, bf16[4,128,256]{2,1,0:T(8,128)(2,1)S(1)}, u32[]{:S(2)}, u32[]{:S(2)}) collective-permute-start(bf16[4,128,256]{2,1,0:T(8,128)(2,1)S(1)} %get-tuple-element.23), channel_id=1, source_target_pairs={{0,16},{8,24},{16,0},{24,8},{1,17},{9,25},{17,1},{25,9},{2,18},{10... | collective-permute-start | bytes 786440 | tf_op jit(solution)/shard_map/ppermute | solution.py:457
  36.2 0.5 collective-permute-start.4
  36.7 0.0 copy-done.9
  36.7 0.0 copy-done.11
  36.7 1.3 %sample_grid.1.refs_4_ = f32[2,128,256]{2,1,0:T(8,128)S(1)} custom-call(s32[1]{0:T(128)} %bitcast.4.start_ref, s32[1,4096]{1,0:T(1,128)S(1)} %bitcast.9, s32[1,4096]{1,0:T(1,128)S(1)} %bitcast.10, f32[1,4096]{1,0:T(1,128)S(1)} %bitcast.11, f32[1,4096]{1,0:T(1,128)S(1)} %bitcast.12), custom_call_target="tpu_custom_call" | custom-call | flops 1073741824 | bytes 65536 | tf_op jit(solution)/shard_map/sample_grid/pallas_call | solution.py:81
  38.0 1.5 %collective-permute-done.2.refs_1_ = bf16[4,128,256]{2,1,0:T(8,128)(2,1)S(1)} collective-permute-done((bf16[4,128,256]{2,1,0:T(8,128)(2,1)S(1)}, bf16[4,128,256]{2,1,0:T(8,128)(2,1)S(1)}, u32[]{:S(2)}, u32[]{:S(2)}) %collective-permute-start.2) | collective-permute-done | bytes 262176 | tf_op jit(solution)/shard_map/ppermute | solution.py:457
  39.6 4.3 %collective-permute-done.3.refs_2_ = bf16[4,128,256]{2,1,0:T(8,128)(2,1)S(1)} collective-permute-done((bf16[4,128,256]{2,1,0:T(8,128)(2,1)S(1)}, bf16[4,128,256]{2,1,0:T(8,128)(2,1)S(1)}, u32[]{:S(2)}, u32[]{:S(2)}) %collective-permute-start.3) | collective-permute-done | bytes 262176 | tf_op jit(solution)/shard_map/ppermute | solution.py:457
  43.9 0.0 collective-permute-done.4.refs_3_
  43.9 1.7 %gram.1 = f32[8,128]{1,0:T(8,128)S(1)} custom-call(s32[1]{0:T(128)} %bitcast.index_ref, bf16[4,128,256]{2,1,0:T(8,128)(2,1)S(1)} %get-tuple-element.21.refs_0_, bf16[4,128,256]{2,1,0:T(8,128)(2,1)S(1)} %collective-permute-done.2.refs_1_, bf16[4,128,256]{2,1,0:T(8,128)(2,1)S(1)} %collective-permute-done.3.refs_2_, ...), custom_call_target="tpu_custom_call" | custom-call | flops 805306368 | bytes 1048576 | tf_op jit(solution)/shard_map/gram/pallas_call | solution.py:338
  45.5 22.3 %all_to_all.5.partial_ref = f32[32,8,128]{2,1,0:T(8,128)S(1)} all-to-all(f32[32,8,128]{2,1,0:T(8,128)S(1)} %broadcast_in_dim.2), channel_id=1, replica_groups=mesh['mem'=4,'tok'=8] {'mem','tok'}, dimensions={0} | all-to-all | bytes 262144 | tf_op jit(solution)/shard_map/all_to_all | solution.py:501
  67.9 3.6 %combine.1 = (bf16[4,128,256]{2,1,0:T(8,128)(2,1)S(1)}, bf16[4,128,256]{2,1,0:T(8,128)(2,1)S(1)}, bf16[4,128,256]{2,1,0:T(8,128)(2,1)S(1)}, bf16[4,128,256]{2,1,0:T(8,128)(2,1)S(1)}) custom-call(s32[1]{0:T(128)} %bitcast.index_ref, f32[32,8,128]{2,1,0:T(8,128)S(1)} %all_to_all.5.partial_ref, bf16[4,128,256]{2,1,0:T(8,128)(2,1)S(1)} %get-tuple-element.21.refs_0_, ...), custom_call_target="tpu_custom_call" | custom-call | flops 536870912 | bytes 2097152 | tf_op jit(solution)/shard_map/combine/pallas_call | solution.py:421
  71.5 0.9 %collective-permute-start.5 = (bf16[4,128,256]{2,1,0:T(8,128)(2,1)S(1)}, bf16[4,128,256]{2,1,0:T(8,128)(2,1)S(1)}, u32[]{:S(2)}, u32[]{:S(2)}) collective-permute-start(bf16[4,128,256]{2,1,0:T(8,128)(2,1)S(1)} %get-tuple-element.26), channel_id=1, source_target_pairs={{0,8},{8,0},{16,24},{24,16},{1,9},{9,1},{17,25},{25,17},{2,10},{10... | collective-permute-start | bytes 786440 | tf_op jit(solution)/shard_map/ppermute | solution.py:457
  72.4 0.7 collective-permute-start.6
  73.1 2.0 %collective-permute-start.7 = (bf16[4,128,256]{2,1,0:T(8,128)(2,1)S(1)}, bf16[4,128,256]{2,1,0:T(8,128)(2,1)S(1)}, u32[]{:S(2)}, u32[]{:S(2)}) collective-permute-start(bf16[4,128,256]{2,1,0:T(8,128)(2,1)S(1)} %get-tuple-element.28), channel_id=1, source_target_pairs={{0,24},{8,16},{16,8},{24,0},{1,25},{9,17},{17,9},{25,1},{2,26},{10... | collective-permute-start | bytes 786440 | tf_op jit(solution)/shard_map/ppermute | solution.py:457
  75.1 5.6 %collective-permute-done.5.refs_1_ = bf16[4,128,256]{2,1,0:T(8,128)(2,1)S(1)} collective-permute-done((bf16[4,128,256]{2,1,0:T(8,128)(2,1)S(1)}, bf16[4,128,256]{2,1,0:T(8,128)(2,1)S(1)}, u32[]{:S(2)}, u32[]{:S(2)}) %collective-permute-start.5) | collective-permute-done | bytes 262176 | tf_op jit(solution)/shard_map/ppermute | solution.py:457
  80.7 5.1 %collective-permute-done.6.refs_2_ = bf16[4,128,256]{2,1,0:T(8,128)(2,1)S(1)} collective-permute-done((bf16[4,128,256]{2,1,0:T(8,128)(2,1)S(1)}, bf16[4,128,256]{2,1,0:T(8,128)(2,1)S(1)}, u32[]{:S(2)}, u32[]{:S(2)}) %collective-permute-start.6) | collective-permute-done | bytes 262176 | tf_op jit(solution)/shard_map/ppermute | solution.py:457
  85.8 0.0 collective-permute-done.7.refs_3_
  85.8 1.5 %assemble.1 = bf16[4,512,256]{2,1,0:T(8,128)(2,1)} custom-call(s32[1]{0:T(128)} %bitcast.index_ref, bf16[4,128,256]{2,1,0:T(8,128)(2,1)S(1)} %get-tuple-element.25.refs_0_, bf16[4,128,256]{2,1,0:T(8,128)(2,1)S(1)} %collective-permute-done.5.refs_1_, bf16[4,128,256]{2,1,0:T(8,128)(2,1)S(1)} %collective-permute-done.6.refs_2_, ...), custom_call_target="tpu_custom_call" | custom-call | bytes 2097152 | tf_op jit(solution)/shard_map/assemble/pallas_call | solution.py:442
  (24 shorter events, 0.1 us)
Async XLA Ops:
  0.0 5.9 %copy-start = (bf16[4,512,256]{2,1,0:T(8,128)(2,1)S(1)}, bf16[4,512,256]{2,1,0:T(8,128)(2,1)}, u32[]{:S(2)}) copy-start(bf16[4,512,256]{2,1,0:T(8,128)(2,1)} %state_ref.1) | copy-start | bytes 3145732
  0.0 5.9 %copy-start.4 = (bf16[256,256]{1,0:T(8,128)(2,1)S(1)}, bf16[256,256]{1,0:T(8,128)(2,1)}, u32[]{:S(2)}) copy-start(bf16[256,256]{1,0:T(8,128)(2,1)} %w_query_ref.1) | copy-start | bytes 393220
  0.0 5.9 %copy-start.5 = (bf16[256,256]{1,0:T(8,128)(2,1)S(1)}, bf16[256,256]{1,0:T(8,128)(2,1)}, u32[]{:S(2)}) copy-start(bf16[256,256]{1,0:T(8,128)(2,1)} %w_key_ref.3) | copy-start | bytes 393220
  0.0 5.9 %copy-start.6 = (bf16[256,256]{1,0:T(8,128)(2,1)S(1)}, bf16[256,256]{1,0:T(8,128)(2,1)}, u32[]{:S(2)}) copy-start(bf16[256,256]{1,0:T(8,128)(2,1)} %w_value_ref.3) | copy-start | bytes 393220
  2.2 7.3 %collective-permute-start = (bf16[4,256,256]{2,1,0:T(8,128)(2,1)}, bf16[4,256,256]{2,1,0:T(8,128)(2,1)S(1)}, u32[]{:S(2)}, u32[]{:S(2)}) collective-permute-start(bf16[4,256,256]{2,1,0:T(8,128)(2,1)} %get-tuple-element.30), channel_id=1, source_target_pairs={{0,1},{1,2},{2,3},{3,4},{4,5},{5,6},{6,7},{8,9},{9,10},{10,11},{11... | collective-permute-start | bytes 1572872 | tf_op jit(solution)/shard_map/ppermute | solution.py:486
  4.6 6.0 %collective-permute-start.1 = (bf16[4,256,256]{2,1,0:T(8,128)(2,1)S(1)}, bf16[4,256,256]{2,1,0:T(8,128)(2,1)S(1)}, u32[]{:S(2)}, u32[]{:S(2)}) collective-permute-start(bf16[4,256,256]{2,1,0:T(8,128)(2,1)S(1)} %get-tuple-element.29), channel_id=1, source_target_pairs={{1,0},{2,1},{3,2},{4,3},{5,4},{6,5},{7,6},{9,8},{10,9},{11,10},{12... | collective-permute-start | bytes 1572872 | tf_op jit(solution)/shard_map/ppermute | solution.py:487
  5.9 0.7 copy-start.12
  6.6 4.0 %copy-start.1 = (bf16[256,1024]{1,0:T(8,128)(2,1)S(1)}, bf16[256,1024]{1,0:T(8,128)(2,1)}, u32[]{:S(2)}) copy-start(bf16[256,1024]{1,0:T(8,128)(2,1)} %w_gate_ref.1) | copy-start | bytes 1572868
  6.6 4.0 %copy-start.2 = (bf16[256,1024]{1,0:T(8,128)(2,1)S(1)}, bf16[256,1024]{1,0:T(8,128)(2,1)}, u32[]{:S(2)}) copy-start(bf16[256,1024]{1,0:T(8,128)(2,1)} %w_up_ref.1) | copy-start | bytes 1572868
  6.6 4.0 %copy-start.3 = (bf16[1024,256]{1,0:T(8,128)(2,1)S(1)}, bf16[1024,256]{1,0:T(8,128)(2,1)}, u32[]{:S(2)}) copy-start(bf16[1024,256]{1,0:T(8,128)(2,1)} %down_weight_ref.1) | copy-start | bytes 1572868
  6.6 4.0 %copy-start.7 = (bf16[256,256]{1,0:T(8,128)(2,1)S(1)}, bf16[256,256]{1,0:T(8,128)(2,1)}, u32[]{:S(2)}) copy-start(bf16[256,256]{1,0:T(8,128)(2,1)} %w_out_ref.1) | copy-start | bytes 393220
  10.5 0.7 copy-start.13
  10.5 0.7 copy-start.14
  11.2 25.5 %copy-start.9 = (s32[4096]{0:T(1024)S(1)}, s32[4096]{0:T(1024)}, u32[]{:S(2)}) copy-start(s32[4096]{0:T(1024)} %param.27) | copy-start | bytes 49156
  11.2 25.5 %copy-start.10 = (f32[4096]{0:T(1024)S(1)}, f32[4096]{0:T(1024)}, u32[]{:S(2)}) copy-start(f32[4096]{0:T(1024)} %param.28) | copy-start | bytes 49156
  11.2 25.5 %copy-start.11 = (f32[4096]{0:T(1024)S(1)}, f32[4096]{0:T(1024)}, u32[]{:S(2)}) copy-start(f32[4096]{0:T(1024)} %param.29) | copy-start | bytes 49156
  33.1 3.6 %copy-start.8 = (s32[4096]{0:T(1024)S(1)}, s32[4096]{0:T(1024)}, u32[]{:S(2)}) copy-start(s32[4096]{0:T(1024)} %param.26) | copy-start | bytes 49156
  33.1 6.4 %collective-permute-start.2 = (bf16[4,128,256]{2,1,0:T(8,128)(2,1)S(1)}, bf16[4,128,256]{2,1,0:T(8,128)(2,1)S(1)}, u32[]{:S(2)}, u32[]{:S(2)}) collective-permute-start(bf16[4,128,256]{2,1,0:T(8,128)(2,1)S(1)} %get-tuple-element.22), channel_id=1, source_target_pairs={{0,8},{8,0},{16,24},{24,16},{1,9},{9,1},{17,25},{25,17},{2,10},{10... | collective-permute-start | bytes 786440 | tf_op jit(solution)/shard_map/ppermute | solution.py:457
  34.7 9.2 %collective-permute-start.3 = (bf16[4,128,256]{2,1,0:T(8,128)(2,1)S(1)}, bf16[4,128,256]{2,1,0:T(8,128)(2,1)S(1)}, u32[]{:S(2)}, u32[]{:S(2)}) collective-permute-start(bf16[4,128,256]{2,1,0:T(8,128)(2,1)S(1)} %get-tuple-element.23), channel_id=1, source_target_pairs={{0,16},{8,24},{16,0},{24,8},{1,17},{9,25},{17,1},{25,9},{2,18},{10... | collective-permute-start | bytes 786440 | tf_op jit(solution)/shard_map/ppermute | solution.py:457
  36.2 7.7 %collective-permute-start.4 = (bf16[4,128,256]{2,1,0:T(8,128)(2,1)S(1)}, bf16[4,128,256]{2,1,0:T(8,128)(2,1)S(1)}, u32[]{:S(2)}, u32[]{:S(2)}) collective-permute-start(bf16[4,128,256]{2,1,0:T(8,128)(2,1)S(1)} %get-tuple-element.24), channel_id=1, source_target_pairs={{0,24},{8,16},{16,8},{24,0},{1,25},{9,17},{17,9},{25,1},{2,26},{10... | collective-permute-start | bytes 786440 | tf_op jit(solution)/shard_map/ppermute | solution.py:457
  71.5 9.2 %collective-permute-start.5 = (bf16[4,128,256]{2,1,0:T(8,128)(2,1)S(1)}, bf16[4,128,256]{2,1,0:T(8,128)(2,1)S(1)}, u32[]{:S(2)}, u32[]{:S(2)}) collective-permute-start(bf16[4,128,256]{2,1,0:T(8,128)(2,1)S(1)} %get-tuple-element.26), channel_id=1, source_target_pairs={{0,8},{8,0},{16,24},{24,16},{1,9},{9,1},{17,25},{25,17},{2,10},{10... | collective-permute-start | bytes 786440 | tf_op jit(solution)/shard_map/ppermute | solution.py:457
  72.4 13.4 %collective-permute-start.6 = (bf16[4,128,256]{2,1,0:T(8,128)(2,1)S(1)}, bf16[4,128,256]{2,1,0:T(8,128)(2,1)S(1)}, u32[]{:S(2)}, u32[]{:S(2)}) collective-permute-start(bf16[4,128,256]{2,1,0:T(8,128)(2,1)S(1)} %get-tuple-element.27), channel_id=1, source_target_pairs={{0,16},{8,24},{16,0},{24,8},{1,17},{9,25},{17,1},{25,9},{2,18},{10... | collective-permute-start | bytes 786440 | tf_op jit(solution)/shard_map/ppermute | solution.py:457
  73.1 12.7 %collective-permute-start.7 = (bf16[4,128,256]{2,1,0:T(8,128)(2,1)S(1)}, bf16[4,128,256]{2,1,0:T(8,128)(2,1)S(1)}, u32[]{:S(2)}, u32[]{:S(2)}) collective-permute-start(bf16[4,128,256]{2,1,0:T(8,128)(2,1)S(1)} %get-tuple-element.28), channel_id=1, source_target_pairs={{0,24},{8,16},{16,8},{24,0},{1,25},{9,17},{17,9},{25,1},{2,26},{10... | collective-permute-start | bytes 786440 | tf_op jit(solution)/shard_map/ppermute | solution.py:457

commit v11 on v10

--- a/solution.py
+++ b/solution.py
@@ -137,6 +137,7 @@
 
 
 def forward_kernel(
+    earlier,
     place_ref,
     window_ref,
     state_ref,
@@ -156,6 +157,7 @@
     down_weight_ref,
     *refs,
 ):
+    refs = refs[earlier:]
     out_refs, (key_buf, value_buf, bias_buf, mixed_buf, forecast_buf) = refs[:-5], refs[-5:]
     rows, feat_width = state_ref.shape[1:]
     reach = left_ref.shape[1]
@@ -262,21 +264,25 @@
         out_ref[0] = forecast_buf[pl.ds(lower, share_rows), :]
 
 
-def forward(place, head_window, own, projected, left, right, gains, weights, shares):
-    members, row_count, feat_width = own.shape
-    reach = left.shape[1]
+def forward(place, head_window, own, projected, left, right, gains, weights, shares, first, earlier):
+    _, row_count, feat_width = own.shape
+    members, reach, _ = left.shape
     key_count = Q_ROWS + 2 * reach
     hidden_width = weights[3].shape[1]
     macs = members * row_count * feat_width * (3 * feat_width + 3 * hidden_width + 8 * key_count)
-    edge_block = pl.BlockSpec((1, reach, feat_width), lambda m: (m, 0, 0))
+
+    def spec(array, offset):
+        return pl.BlockSpec((1, *array.shape[1:]), lambda m: (m + offset, 0, 0))
+
     return pl.pallas_call(
-        forward_kernel,
+        functools.partial(forward_kernel, len(earlier)),
         grid=(members,),
         out_shape=[jax.ShapeDtypeStruct((members, row_count // shares, feat_width), BF16)] * shares,
         in_specs=[smem_spec()] * 2
-        + [pl.BlockSpec((1, *v.shape[1:]), lambda m: (m, 0, 0)) for v in (own, *projected)]
-        + [edge_block] * 2
-        + [vmem_spec()] * (len(gains) + len(weights)),
+        + [spec(v, first) for v in (own, *projected)]
+        + [spec(v, 0) for v in (left, right)]
+        + [vmem_spec()] * (len(gains) + len(weights))
+        + [pl.BlockSpec(memory_space=pl.ANY)] * len(earlier),
         out_specs=[pl.BlockSpec((1, row_count // shares, feat_width), lambda m: (m, 0, 0))] * shares,
         scratch_shapes=[
             pltpu.VMEM((feat_width, row_count + 2 * reach), BF16),
@@ -286,19 +292,22 @@
             pltpu.VMEM((row_count, feat_width), BF16),
         ],
         compiler_params=pltpu.CompilerParams(vmem_limit_bytes=VMEM_LIMIT),
-        cost_estimate=pl.CostEstimate(flops=2 * macs, bytes_accessed=10 * own.size, transcendentals=0),
+        cost_estimate=pl.CostEstimate(
+            flops=2 * macs, bytes_accessed=10 * members * row_count * feat_width, transcendentals=0
+        ),
         name="forward",
-    )(place, head_window, own, *projected, left, right, *gains, *weights)
+    )(place, head_window, own, *projected, left, right, *gains, *weights, *earlier)
 
 
 def global_member(held, index, own_members):
     return ((held // own_members) ^ index) * own_members + held % own_members
 
 
-def gram_kernel(index_ref, *refs):
+def gram_kernel(parts, index_ref, *refs):
     share_refs, grid_ref, out_ref = refs[:-2], refs[-2], refs[-1]
-    own_members, rows, feat_width = share_refs[0].shape
-    members = own_members * len(share_refs)
+    rows, feat_width = share_refs[0].shape[1:]
+    members = sum(ref.shape[0] for ref in share_refs)
+    own_members = members // parts
     index = index_ref[0]
     stack = members * GROUP
     total = jnp.zeros((stack, stack), F32)
@@ -333,19 +342,20 @@
 
 
 def gram_partial(index, shares, grid):
-    members = shares[0].shape[0] * len(shares)
+    flat = [v for part in shares for v in part]
+    members = sum(v.shape[0] for v in flat)
     filled = members * members // LANES + 1
     return pl.pallas_call(
-        gram_kernel,
+        functools.partial(gram_kernel, len(shares)),
         out_shape=jax.ShapeDtypeStruct((-(-filled // 8) * 8, LANES), F32),
-        in_specs=[smem_spec()] + [vmem_spec()] * (len(shares) + 1),
+        in_specs=[smem_spec()] + [vmem_spec()] * (len(flat) + 1),
         out_specs=vmem_spec(),
         compiler_params=pltpu.CompilerParams(vmem_limit_bytes=VMEM_LIMIT),
         cost_estimate=pl.CostEstimate(
             flops=3 * GROUP * members * members * grid.size, bytes_accessed=members * grid.size, transcendentals=0
         ),
         name="gram",
-    )(index, *shares, grid)
+    )(index, *flat, grid)
 
 
 def ensemble_transform(gram, proj):
@@ -381,10 +391,10 @@
     return 1.0 / members + moved - jnp.sum(moved, axis=0, keepdims=True) * (1.0 / members)
 
 
-def combine_kernel(index_ref, partial_ref, *refs):
-    share_refs, out_refs = refs[: len(refs) // 2], refs[len(refs) // 2 :]
-    own_members, rows, feat_width = share_refs[0].shape
-    members = own_members * len(share_refs)
+def combine_kernel(parts, index_ref, partial_ref, *refs):
+    share_refs, out_refs = refs[:-parts], refs[-parts:]
+    own_members, rows, feat_width = out_refs[0].shape
+    members = own_members * parts
     stack = members * GROUP
     per_row = LANES // members
     sums = jnp.sum(partial_ref[...], axis=0)
@@ -416,17 +426,21 @@
 
 
 def combine(index, partials, shares):
-    size = shares[0].size * len(shares)
-    members = shares[0].shape[0] * len(shares)
+    flat = [v for part in shares for v in part]
+    own_members = sum(v.shape[0] for v in shares[0])
+    shape = (own_members, *flat[0].shape[1:])
+    size = len(shares) * math.prod(shape)
     return pl.pallas_call(
-        combine_kernel,
-        out_shape=[jax.ShapeDtypeStruct(v.shape, BF16) for v in shares],
-        in_specs=[smem_spec()] + [vmem_spec()] * (1 + len(shares)),
+        functools.partial(combine_kernel, len(shares)),
+        out_shape=[jax.ShapeDtypeStruct(shape, BF16)] * len(shares),
+        in_specs=[smem_spec()] + [vmem_spec()] * (1 + len(flat)),
         out_specs=[vmem_spec()] * len(shares),
         compiler_params=pltpu.CompilerParams(vmem_limit_bytes=VMEM_LIMIT),
-        cost_estimate=pl.CostEstimate(flops=4 * GROUP * members * size, bytes_accessed=4 * size, transcendentals=0),
+        cost_estimate=pl.CostEstimate(
+            flops=4 * GROUP * own_members * len(shares) * size, bytes_accessed=4 * size, transcendentals=0
+        ),
         name="combine",
-    )(index, partials, *shares)
+    )(index, partials, *flat)
 
 
 def assemble_kernel(index_ref, *refs):
@@ -483,8 +497,15 @@
     first_pos = lax.axis_index("tok") * row_count
     up = [(i, i + 1) for i in range(tok_count - 1)]
     down = [(i + 1, i) for i in range(tok_count - 1)]
-    left = lax.ppermute(ens_state[:, row_count - WIN :], "tok", up)
-    right = lax.ppermute(ens_state[:, :WIN], "tok", down)
+    half = own_members // 2
+    bounds = [(0, half), (half, own_members)]
+    halos = [
+        (
+            lax.ppermute(ens_state[lower:upper, row_count - WIN :], "tok", up),
+            lax.ppermute(ens_state[lower:upper, :WIN], "tok", down),
+        )
+        for lower, upper in bounds
+    ]
     share_start = first_pos + lax.axis_index("mem") * share_rows
     grid = sample_grid(
         share_start.astype(jnp.int32).reshape(1), obs_token, obs_channel, obs_value, obs_var, share_rows, feat_width
@@ -495,8 +516,14 @@
     gains = [attn_gain.reshape(1, -1), ffn_gain.reshape(1, -1)]
     projected = project(ens_state, head_window.shape[0], gains[0], w_query, w_key, w_value)
     weights = [w_key, w_value, w_out, w_gate, w_up, down_weight]
-    forecast = forward(place, head_window, ens_state, projected, left, right, gains, weights, mem_count)
-    shares = exchanged(forecast)
+    by_half, earlier = [], []
+    for (lower, _), (left, right) in zip(bounds, halos):
+        forecast = forward(
+            place, head_window, ens_state, projected, left, right, gains, weights, mem_count, lower, earlier
+        )
+        earlier = forecast[:1]
+        by_half.append(exchanged(forecast))
+    shares = list(zip(*by_half))
     partial = gram_partial(index, shares, grid)
     partials = lax.all_to_all(
         jnp.broadcast_to(partial[None], (device_count, *partial.shape)),

time: 87.6 us -> 90.9 us (1.038)
  starting transfers between devices: 10.8 us -> 21.2 us
  blocking collectives: 22.3 us -> 13.5 us
  Pallas kernels: 32.8 us -> 34.2 us
    all_to_all x1, blocking collectives: 22.3 us -> 13.5 us  [local(): lax.all_to_all(jnp.broadcast_to(partial[None], (device_count, *partial.sh...]
    ppermute x2 -> x4, starting transfers between devices: 3.68 us -> 10.2 us  [the longest x2 7.6 us: local(): lax.ppermute(ens_state[lower:upper, row_count - WIN:], 'tok', up)]
    ppermute x6 -> x9, starting transfers between devices: 7.11 us -> 11 us  [exchanged(): lax.ppermute(v, 'mem', [(i, i ^ part) for i in range(count)])]
    ppermute x6 -> x9, waiting for transfers between devices: 16.6 us -> 18 us  [exchanged(): lax.ppermute(v, 'mem', [(i, i ^ part) for i in range(count)])]
    pallas_call x3 -> x4, Pallas kernels: 27.2 us -> 28.5 us  [the longest x2 23.2 us: forward(): pl.pallas_call(functools.partial(forward_kernel, len(earlier)), grid=(mem...]
    ppermute x2 -> x4, waiting for transfers between devices: 1.08 us -> 0.01 us  [the longest x2 0.01 us: local(): lax.ppermute(ens_state[lower:upper, :WIN], 'tok', down)]
  transfers between devices with their start and end apart: 8 -> 13, of which waited for: 5 -> 5; matrix products, arithmetic and copies ran while one was open for 0% -> 0% of each run, Pallas kernels for 5% -> 17%
where the time goes in v11:
time: 90.9 us; the launch traced here: 90.6 us
  Pallas kernels  34.2 us (38%)
  starting transfers between devices  21.2 us (23%)
  waiting for transfers between devices  18 us (20%)
  blocking collectives  13.5 us (15%)
  local copies, waits for them, and re-layouts  3.4 us (4%)
    pallas_call x2, Pallas kernels, forward(): pl.pallas_call(functools.partial(forward_kernel, len(earlier)), grid=(mem...  23.2 us
    ppermute x9, waiting for transfers between devices, exchanged(): lax.ppermute(v, 'mem', [(i, i ^ part) for i in range(count)])  18 us
    all_to_all x1, blocking collectives, local(): lax.all_to_all(jnp.broadcast_to(partial[None], (device_count, *partial.sh...  13.5 us
    ppermute x9, starting transfers between devices, exchanged(): lax.ppermute(v, 'mem', [(i, i ^ part) for i in range(count)])  11 us
    ppermute x2, starting transfers between devices, local(): lax.ppermute(ens_state[lower:upper, row_count - WIN:], 'tok', up)  7.6 us
    pallas_call x1, Pallas kernels, combine(): pl.pallas_call(functools.partial(combine_kernel, len(shares)), out_shape=...  3.64 us
    pallas_call x1, Pallas kernels, project(): pl.pallas_call(functools.partial(project_kernel, heads), grid=(members,),...  2.8 us
    ppermute x2, starting transfers between devices, local(): lax.ppermute(ens_state[lower:upper, :WIN], 'tok', down)  2.58 us
  transfers between devices with their start and end apart: 13, of which 5 were waited for; matrix products, arithmetic and copies ran while one was open for 0% of the time, Pallas kernels for 17%

profile of v11, /device:TPU:0, one launch (start us, length us, event | category | flops | bytes accessed | tf_op | source)
XLA Modules:
  0.0 90.6 jit_solution(12776208909287774671)
XLA Ops:
  0.0 2.1 %fusion = (bf16[2,256,256]{2,1,0:T(8,128)(2,1)S(1)}, bf16[2,256,256]{2,1,0:T(8,128)(2,1)S(1)}, bf16[2,256,256]{2,1,0:T(8,128)(2,1)S(1)}, bf16[2,256,256]{2,1,0:T(8,128)(2,1)}) fusion(bf16[4,512,256]{2,1,0:T(8,128)(2,1)} %state_ref.3), kind=kLoop, calls=%fused_computation.1 | loop fusion | bytes 2097152 | tf_op jit(solution)/shard_map/slice | solution.py:505
  2.1 2.4 %collective-permute-start = (bf16[2,256,256]{2,1,0:T(8,128)(2,1)}, bf16[2,256,256]{2,1,0:T(8,128)(2,1)S(1)}, u32[]{:S(2)}, u32[]{:S(2)}) collective-permute-start(bf16[2,256,256]{2,1,0:T(8,128)(2,1)} %get-tuple-element.40), channel_id=1, source_target_pairs={{0,1},{1,2},{2,3},{3,4},{4,5},{5,6},{6,7},{8,9},{9,10},{10,11},{11... | collective-permute-start | bytes 786440 | tf_op jit(solution)/shard_map/ppermute | solution.py:504
  4.5 1.3 %collective-permute-start.1 = (bf16[2,256,256]{2,1,0:T(8,128)(2,1)S(1)}, bf16[2,256,256]{2,1,0:T(8,128)(2,1)S(1)}, u32[]{:S(2)}, u32[]{:S(2)}) collective-permute-start(bf16[2,256,256]{2,1,0:T(8,128)(2,1)S(1)} %get-tuple-element.39), channel_id=1, source_target_pairs={{1,0},{2,1},{3,2},{4,3},{5,4},{6,5},{7,6},{9,8},{10,9},{11,10},{12... | collective-permute-start | bytes 786440 | tf_op jit(solution)/shard_map/ppermute | solution.py:505
  5.8 5.2 %collective-permute-start.2 = (bf16[2,256,256]{2,1,0:T(8,128)(2,1)S(1)}, bf16[2,256,256]{2,1,0:T(8,128)(2,1)S(1)}, u32[]{:S(2)}, u32[]{:S(2)}) collective-permute-start(bf16[2,256,256]{2,1,0:T(8,128)(2,1)S(1)} %get-tuple-element.38), channel_id=1, source_target_pairs={{0,1},{1,2},{2,3},{3,4},{4,5},{5,6},{6,7},{8,9},{9,10},{10,11},{11... | collective-permute-start | bytes 786440 | tf_op jit(solution)/shard_map/ppermute | solution.py:504
  11.0 1.3 %collective-permute-start.3 = (bf16[2,256,256]{2,1,0:T(8,128)(2,1)S(1)}, bf16[2,256,256]{2,1,0:T(8,128)(2,1)S(1)}, u32[]{:S(2)}, u32[]{:S(2)}) collective-permute-start(bf16[2,256,256]{2,1,0:T(8,128)(2,1)S(1)} %get-tuple-element.37), channel_id=1, source_target_pairs={{1,0},{2,1},{3,2},{4,3},{5,4},{6,5},{7,6},{9,8},{10,9},{11,10},{12... | collective-permute-start | bytes 786440 | tf_op jit(solution)/shard_map/ppermute | solution.py:505
  12.3 0.0 copy-start.12
  12.3 0.6 copy-done.12
  13.0 2.8 %project.1 = (bf16[4,512,256]{2,1,0:T(8,128)(2,1)S(1)}, bf16[4,256,512]{2,1,0:T(8,128)(2,1)S(1)}, bf16[4,512,256]{2,1,0:T(8,128)(2,1)S(1)}, f32[4,8,128]{2,1,0:T(8,128)S(1)}) custom-call(bf16[4,512,256]{2,1,0:T(8,128)(2,1)S(1)} %copy-done, f32[1,256]{1,0:T(1,128)S(1)} %bitcast.13, bf16[256,256]{1,0:T(8,128)(2,1)S(1)} %copy-done.4, ...), custom_call_target="tpu_custom_call" | custom-call | flops 805306368 | bytes 4194304 | tf_op jit(solution)/shard_map/project/pallas_call | solution.py:125
  15.8 0.1 pad_add_fusion.place_ref
  15.9 0.0 copy-start.14
  15.9 0.6 copy-done.13
  16.6 11.5 %forward.2 = (bf16[2,128,256]{2,1,0:T(8,128)(2,1)S(1)}, bf16[2,128,256]{2,1,0:T(8,128)(2,1)S(1)}, bf16[2,128,256]{2,1,0:T(8,128)(2,1)S(1)}, bf16[2,128,256]{2,1,0:T(8,128)(2,1)S(1)}) custom-call(s32[3]{0:T(128)S(1)} %pad_add_fusion.place_ref, s32[4]{0:T(128)S(1)} %copy-done.14, bf16[4,512,256]{2,1,0:T(8,128)(2,1)S(1)} %copy-done, ...), custom_call_target="tpu_custom_call" | custom-call | flops 4697620480 | bytes 2621440 | tf_op jit(solution)/shard_map/forward/pallas_call | solution.py:277
  28.1 11.7 %forward.3 = (bf16[2,128,256]{2,1,0:T(8,128)(2,1)S(1)}, bf16[2,128,256]{2,1,0:T(8,128)(2,1)S(1)}, bf16[2,128,256]{2,1,0:T(8,128)(2,1)S(1)}, bf16[2,128,256]{2,1,0:T(8,128)(2,1)S(1)}) custom-call(s32[3]{0:T(128)S(1)} %pad_add_fusion.place_ref, s32[4]{0:T(128)S(1)} %copy-done.14, bf16[4,512,256]{2,1,0:T(8,128)(2,1)S(1)} %copy-done, ...), custom_call_target="tpu_custom_call" | custom-call | flops 4697620480 | bytes 2621440 | tf_op jit(solution)/shard_map/forward/pallas_call | solution.py:277
  39.9 1.6 %collective-permute-start.5 = (bf16[2,128,256]{2,1,0:T(8,128)(2,1)S(1)}, bf16[2,128,256]{2,1,0:T(8,128)(2,1)S(1)}, u32[]{:S(2)}, u32[]{:S(2)}) collective-permute-start(bf16[2,128,256]{2,1,0:T(8,128)(2,1)S(1)} %get-tuple-element.28), channel_id=1, source_target_pairs={{0,8},{8,0},{16,24},{24,16},{1,9},{9,1},{17,25},{25,17},{2,10},{10... | collective-permute-start | bytes 393224 | tf_op jit(solution)/shard_map/ppermute | solution.py:471
  41.4 1.5 %collective-permute-start.7 = (bf16[2,128,256]{2,1,0:T(8,128)(2,1)S(1)}, bf16[2,128,256]{2,1,0:T(8,128)(2,1)S(1)}, u32[]{:S(2)}, u32[]{:S(2)}) collective-permute-start(bf16[2,128,256]{2,1,0:T(8,128)(2,1)S(1)} %get-tuple-element.30), channel_id=1, source_target_pairs={{0,16},{8,24},{16,0},{24,8},{1,17},{9,25},{17,1},{25,9},{2,18},{10... | collective-permute-start | bytes 393224 | tf_op jit(solution)/shard_map/ppermute | solution.py:471
  43.0 0.5 collective-permute-start.9
  43.4 1.5 %collective-permute-start.4 = (bf16[2,128,256]{2,1,0:T(8,128)(2,1)S(1)}, bf16[2,128,256]{2,1,0:T(8,128)(2,1)S(1)}, u32[]{:S(2)}, u32[]{:S(2)}) collective-permute-start(bf16[2,128,256]{2,1,0:T(8,128)(2,1)S(1)} %get-tuple-element.27), channel_id=1, source_target_pairs={{0,8},{8,0},{16,24},{24,16},{1,9},{9,1},{17,25},{25,17},{2,10},{10... | collective-permute-start | bytes 393224 | tf_op jit(solution)/shard_map/ppermute | solution.py:471
  44.9 1.5 %collective-permute-start.6 = (bf16[2,128,256]{2,1,0:T(8,128)(2,1)S(1)}, bf16[2,128,256]{2,1,0:T(8,128)(2,1)S(1)}, u32[]{:S(2)}, u32[]{:S(2)}) collective-permute-start(bf16[2,128,256]{2,1,0:T(8,128)(2,1)S(1)} %get-tuple-element.29), channel_id=1, source_target_pairs={{0,16},{8,24},{16,0},{24,8},{1,17},{9,25},{17,1},{25,9},{2,18},{10... | collective-permute-start | bytes 393224 | tf_op jit(solution)/shard_map/ppermute | solution.py:471
  46.5 0.9 %collective-permute-start.8 = (bf16[2,128,256]{2,1,0:T(8,128)(2,1)S(1)}, bf16[2,128,256]{2,1,0:T(8,128)(2,1)S(1)}, u32[]{:S(2)}, u32[]{:S(2)}) collective-permute-start(bf16[2,128,256]{2,1,0:T(8,128)(2,1)S(1)} %get-tuple-element.31), channel_id=1, source_target_pairs={{0,24},{8,16},{16,8},{24,0},{1,25},{9,17},{17,9},{25,1},{2,26},{10... | collective-permute-start | bytes 393224 | tf_op jit(solution)/shard_map/ppermute | solution.py:471
  47.4 1.3 %sample_grid.1.refs_8_ = f32[2,128,256]{2,1,0:T(8,128)S(1)} custom-call(s32[1]{0:T(128)} %bitcast.4.start_ref, s32[1,4096]{1,0:T(1,128)S(1)} %bitcast.9, s32[1,4096]{1,0:T(1,128)S(1)} %bitcast.10, f32[1,4096]{1,0:T(1,128)S(1)} %bitcast.11, f32[1,4096]{1,0:T(1,128)S(1)} %bitcast.12), custom_call_target="tpu_custom_call" | custom-call | flops 1073741824 | bytes 65536 | tf_op jit(solution)/shard_map/sample_grid/pallas_call | solution.py:81
  48.7 0.8 collective-permute-done.9.refs_7_
  49.5 1.8 %collective-permute-done.4.refs_2_ = bf16[2,128,256]{2,1,0:T(8,128)(2,1)S(1)} collective-permute-done((bf16[2,128,256]{2,1,0:T(8,128)(2,1)S(1)}, bf16[2,128,256]{2,1,0:T(8,128)(2,1)S(1)}, u32[]{:S(2)}, u32[]{:S(2)}) %collective-permute-start.4) | collective-permute-done | bytes 131104 | tf_op jit(solution)/shard_map/ppermute | solution.py:471
  51.3 4.7 %collective-permute-done.6.refs_4_ = bf16[2,128,256]{2,1,0:T(8,128)(2,1)S(1)} collective-permute-done((bf16[2,128,256]{2,1,0:T(8,128)(2,1)S(1)}, bf16[2,128,256]{2,1,0:T(8,128)(2,1)S(1)}, u32[]{:S(2)}, u32[]{:S(2)}) %collective-permute-start.6) | collective-permute-done | bytes 131104 | tf_op jit(solution)/shard_map/ppermute | solution.py:471
  56.0 1.7 %gram.1 = f32[8,128]{1,0:T(8,128)S(1)} custom-call(s32[1]{0:T(128)} %bitcast.index_ref, bf16[2,128,256]{2,1,0:T(8,128)(2,1)S(1)} %get-tuple-element.25.refs_0_, bf16[2,128,256]{2,1,0:T(8,128)(2,1)S(1)} %get-tuple-element.26.refs_1_, bf16[2,128,256]{2,1,0:T(8,128)(2,1)S(1)} %collective-permute-done.4.refs_2_, ...), custom_call_target="tpu_custom_call" | custom-call | flops 805306368 | bytes 1048576 | tf_op jit(solution)/shard_map/gram/pallas_call | solution.py:348
  57.7 13.5 %all_to_all.5.partial_ref = f32[32,8,128]{2,1,0:T(8,128)S(1)} all-to-all(f32[32,8,128]{2,1,0:T(8,128)S(1)} %broadcast_in_dim.2), channel_id=1, replica_groups=mesh['mem'=4,'tok'=8] {'mem','tok'}, dimensions={0} | all-to-all | bytes 262144 | tf_op jit(solution)/shard_map/all_to_all | solution.py:528
  71.2 3.6 %combine.1 = (bf16[4,128,256]{2,1,0:T(8,128)(2,1)S(1)}, bf16[4,128,256]{2,1,0:T(8,128)(2,1)S(1)}, bf16[4,128,256]{2,1,0:T(8,128)(2,1)S(1)}, bf16[4,128,256]{2,1,0:T(8,128)(2,1)S(1)}) custom-call(s32[1]{0:T(128)} %bitcast.index_ref, f32[32,8,128]{2,1,0:T(8,128)S(1)} %all_to_all.5.partial_ref, bf16[2,128,256]{2,1,0:T(8,128)(2,1)S(1)} %get-tuple-element.25.refs_0_, ...), custom_call_target="tpu_custom_call" | custom-call | flops 536870912 | bytes 2097152 | tf_op jit(solution)/shard_map/combine/pallas_call | solution.py:433
  74.8 0.9 collective-permute-start.10
  75.7 0.7 collective-permute-start.11
  76.4 2.0 %collective-permute-start.12 = (bf16[4,128,256]{2,1,0:T(8,128)(2,1)S(1)}, bf16[4,128,256]{2,1,0:T(8,128)(2,1)S(1)}, u32[]{:S(2)}, u32[]{:S(2)}) collective-permute-start(bf16[4,128,256]{2,1,0:T(8,128)(2,1)S(1)} %get-tuple-element.36), channel_id=1, source_target_pairs={{0,24},{8,16},{16,8},{24,0},{1,25},{9,17},{17,9},{25,1},{2,26},{10... | collective-permute-start | bytes 786440 | tf_op jit(solution)/shard_map/ppermute | solution.py:471
  78.4 5.6 %collective-permute-done.10.refs_1_ = bf16[4,128,256]{2,1,0:T(8,128)(2,1)S(1)} collective-permute-done((bf16[4,128,256]{2,1,0:T(8,128)(2,1)S(1)}, bf16[4,128,256]{2,1,0:T(8,128)(2,1)S(1)}, u32[]{:S(2)}, u32[]{:S(2)}) %collective-permute-start.10) | collective-permute-done | bytes 262176 | tf_op jit(solution)/shard_map/ppermute | solution.py:471
  84.0 5.1 %collective-permute-done.11.refs_2_ = bf16[4,128,256]{2,1,0:T(8,128)(2,1)S(1)} collective-permute-done((bf16[4,128,256]{2,1,0:T(8,128)(2,1)S(1)}, bf16[4,128,256]{2,1,0:T(8,128)(2,1)S(1)}, u32[]{:S(2)}, u32[]{:S(2)}) %collective-permute-start.11) | collective-permute-done | bytes 262176 | tf_op jit(solution)/shard_map/ppermute | solution.py:471
  89.1 1.5 %assemble.1 = bf16[4,512,256]{2,1,0:T(8,128)(2,1)} custom-call(s32[1]{0:T(128)} %bitcast.index_ref, bf16[4,128,256]{2,1,0:T(8,128)(2,1)S(1)} %get-tuple-element.33.refs_0_, bf16[4,128,256]{2,1,0:T(8,128)(2,1)S(1)} %collective-permute-done.10.refs_1_, bf16[4,128,256]{2,1,0:T(8,128)(2,1)S(1)} %collective-permute-done.11.refs_2_, ...), custom_call_target="tpu_custom_call" | custom-call | bytes 2097152 | tf_op jit(solution)/shard_map/assemble/pallas_call | solution.py:456
  (35 shorter events, 0.1 us)
Async XLA Ops:
  0.0 12.3 %copy-start = (bf16[4,512,256]{2,1,0:T(8,128)(2,1)S(1)}, bf16[4,512,256]{2,1,0:T(8,128)(2,1)}, u32[]{:S(2)}) copy-start(bf16[4,512,256]{2,1,0:T(8,128)(2,1)} %state_ref.3) | copy-start | bytes 3145732
  0.0 12.3 %copy-start.4 = (bf16[256,256]{1,0:T(8,128)(2,1)S(1)}, bf16[256,256]{1,0:T(8,128)(2,1)}, u32[]{:S(2)}) copy-start(bf16[256,256]{1,0:T(8,128)(2,1)} %w_query_ref.1) | copy-start | bytes 393220
  0.0 12.3 %copy-start.5 = (bf16[256,256]{1,0:T(8,128)(2,1)S(1)}, bf16[256,256]{1,0:T(8,128)(2,1)}, u32[]{:S(2)}) copy-start(bf16[256,256]{1,0:T(8,128)(2,1)} %w_key_ref.5) | copy-start | bytes 393220
  0.0 12.3 %copy-start.6 = (bf16[256,256]{1,0:T(8,128)(2,1)S(1)}, bf16[256,256]{1,0:T(8,128)(2,1)}, u32[]{:S(2)}) copy-start(bf16[256,256]{1,0:T(8,128)(2,1)} %w_value_ref.5) | copy-start | bytes 393220
  2.1 13.8 %collective-permute-start = (bf16[2,256,256]{2,1,0:T(8,128)(2,1)}, bf16[2,256,256]{2,1,0:T(8,128)(2,1)S(1)}, u32[]{:S(2)}, u32[]{:S(2)}) collective-permute-start(bf16[2,256,256]{2,1,0:T(8,128)(2,1)} %get-tuple-element.40), channel_id=1, source_target_pairs={{0,1},{1,2},{2,3},{3,4},{4,5},{5,6},{6,7},{8,9},{9,10},{10,11},{11... | collective-permute-start | bytes 786440 | tf_op jit(solution)/shard_map/ppermute | solution.py:504
  4.5 11.4 %collective-permute-start.1 = (bf16[2,256,256]{2,1,0:T(8,128)(2,1)S(1)}, bf16[2,256,256]{2,1,0:T(8,128)(2,1)S(1)}, u32[]{:S(2)}, u32[]{:S(2)}) collective-permute-start(bf16[2,256,256]{2,1,0:T(8,128)(2,1)S(1)} %get-tuple-element.39), channel_id=1, source_target_pairs={{1,0},{2,1},{3,2},{4,3},{5,4},{6,5},{7,6},{9,8},{10,9},{11,10},{12... | collective-permute-start | bytes 786440 | tf_op jit(solution)/shard_map/ppermute | solution.py:505
  5.8 22.3 %collective-permute-start.2 = (bf16[2,256,256]{2,1,0:T(8,128)(2,1)S(1)}, bf16[2,256,256]{2,1,0:T(8,128)(2,1)S(1)}, u32[]{:S(2)}, u32[]{:S(2)}) collective-permute-start(bf16[2,256,256]{2,1,0:T(8,128)(2,1)S(1)} %get-tuple-element.38), channel_id=1, source_target_pairs={{0,1},{1,2},{2,3},{3,4},{4,5},{5,6},{6,7},{8,9},{9,10},{10,11},{11... | collective-permute-start | bytes 786440 | tf_op jit(solution)/shard_map/ppermute | solution.py:504
  11.0 17.1 %collective-permute-start.3 = (bf16[2,256,256]{2,1,0:T(8,128)(2,1)S(1)}, bf16[2,256,256]{2,1,0:T(8,128)(2,1)S(1)}, u32[]{:S(2)}, u32[]{:S(2)}) collective-permute-start(bf16[2,256,256]{2,1,0:T(8,128)(2,1)S(1)} %get-tuple-element.37), channel_id=1, source_target_pairs={{1,0},{2,1},{3,2},{4,3},{5,4},{6,5},{7,6},{9,8},{10,9},{11,10},{12... | collective-permute-start | bytes 786440 | tf_op jit(solution)/shard_map/ppermute | solution.py:505
  12.3 0.7 copy-start.12
  13.0 2.9 %copy-start.1 = (bf16[256,1024]{1,0:T(8,128)(2,1)S(1)}, bf16[256,1024]{1,0:T(8,128)(2,1)}, u32[]{:S(2)}) copy-start(bf16[256,1024]{1,0:T(8,128)(2,1)} %w_gate_ref.3) | copy-start | bytes 1572868
  13.0 2.9 %copy-start.2 = (bf16[256,1024]{1,0:T(8,128)(2,1)S(1)}, bf16[256,1024]{1,0:T(8,128)(2,1)}, u32[]{:S(2)}) copy-start(bf16[256,1024]{1,0:T(8,128)(2,1)} %w_up_ref.3) | copy-start | bytes 1572868
  13.0 2.9 %copy-start.3 = (bf16[1024,256]{1,0:T(8,128)(2,1)S(1)}, bf16[1024,256]{1,0:T(8,128)(2,1)}, u32[]{:S(2)}) copy-start(bf16[1024,256]{1,0:T(8,128)(2,1)} %down_weight_ref.3) | copy-start | bytes 1572868
  13.0 2.9 %copy-start.7 = (bf16[256,256]{1,0:T(8,128)(2,1)S(1)}, bf16[256,256]{1,0:T(8,128)(2,1)}, u32[]{:S(2)}) copy-start(bf16[256,256]{1,0:T(8,128)(2,1)} %w_out_ref.3) | copy-start | bytes 393220
  15.9 0.7 copy-start.13
  15.9 0.7 copy-start.14
  28.1 19.3 %copy-start.9 = (s32[4096]{0:T(1024)S(1)}, s32[4096]{0:T(1024)}, u32[]{:S(2)}) copy-start(s32[4096]{0:T(1024)} %param.27) | copy-start | bytes 49156
  28.1 19.3 %copy-start.10 = (f32[4096]{0:T(1024)S(1)}, f32[4096]{0:T(1024)}, u32[]{:S(2)}) copy-start(f32[4096]{0:T(1024)} %param.28) | copy-start | bytes 49156
  28.1 19.2 %copy-start.11 = (f32[4096]{0:T(1024)S(1)}, f32[4096]{0:T(1024)}, u32[]{:S(2)}) copy-start(f32[4096]{0:T(1024)} %param.29) | copy-start | bytes 49156
  39.9 7.5 %copy-start.8 = (s32[4096]{0:T(1024)S(1)}, s32[4096]{0:T(1024)}, u32[]{:S(2)}) copy-start(s32[4096]{0:T(1024)} %param.26) | copy-start | bytes 49156
  39.9 6.6 %collective-permute-start.5 = (bf16[2,128,256]{2,1,0:T(8,128)(2,1)S(1)}, bf16[2,128,256]{2,1,0:T(8,128)(2,1)S(1)}, u32[]{:S(2)}, u32[]{:S(2)}) collective-permute-start(bf16[2,128,256]{2,1,0:T(8,128)(2,1)S(1)} %get-tuple-element.28), channel_id=1, source_target_pairs={{0,8},{8,0},{16,24},{24,16},{1,9},{9,1},{17,25},{25,17},{2,10},{10... | collective-permute-start | bytes 393224 | tf_op jit(solution)/shard_map/ppermute | solution.py:471
  41.4 7.3 %collective-permute-start.7 = (bf16[2,128,256]{2,1,0:T(8,128)(2,1)S(1)}, bf16[2,128,256]{2,1,0:T(8,128)(2,1)S(1)}, u32[]{:S(2)}, u32[]{:S(2)}) collective-permute-start(bf16[2,128,256]{2,1,0:T(8,128)(2,1)S(1)} %get-tuple-element.30), channel_id=1, source_target_pairs={{0,16},{8,24},{16,0},{24,8},{1,17},{9,25},{17,1},{25,9},{2,18},{10... | collective-permute-start | bytes 393224 | tf_op jit(solution)/shard_map/ppermute | solution.py:471
  43.0 6.6 %collective-permute-start.9 = (bf16[2,128,256]{2,1,0:T(8,128)(2,1)S(1)}, bf16[2,128,256]{2,1,0:T(8,128)(2,1)S(1)}, u32[]{:S(2)}, u32[]{:S(2)}) collective-permute-start(bf16[2,128,256]{2,1,0:T(8,128)(2,1)S(1)} %get-tuple-element.32), channel_id=1, source_target_pairs={{0,24},{8,16},{16,8},{24,0},{1,25},{9,17},{17,9},{25,1},{2,26},{10... | collective-permute-start | bytes 393224 | tf_op jit(solution)/shard_map/ppermute | solution.py:471
  43.4 7.9 %collective-permute-start.4 = (bf16[2,128,256]{2,1,0:T(8,128)(2,1)S(1)}, bf16[2,128,256]{2,1,0:T(8,128)(2,1)S(1)}, u32[]{:S(2)}, u32[]{:S(2)}) collective-permute-start(bf16[2,128,256]{2,1,0:T(8,128)(2,1)S(1)} %get-tuple-element.27), channel_id=1, source_target_pairs={{0,8},{8,0},{16,24},{24,16},{1,9},{9,1},{17,25},{25,17},{2,10},{10... | collective-permute-start | bytes 393224 | tf_op jit(solution)/shard_map/ppermute | solution.py:471
  44.9 11.1 %collective-permute-start.6 = (bf16[2,128,256]{2,1,0:T(8,128)(2,1)S(1)}, bf16[2,128,256]{2,1,0:T(8,128)(2,1)S(1)}, u32[]{:S(2)}, u32[]{:S(2)}) collective-permute-start(bf16[2,128,256]{2,1,0:T(8,128)(2,1)S(1)} %get-tuple-element.29), channel_id=1, source_target_pairs={{0,16},{8,24},{16,0},{24,8},{1,17},{9,25},{17,1},{25,9},{2,18},{10... | collective-permute-start | bytes 393224 | tf_op jit(solution)/shard_map/ppermute | solution.py:471
  46.5 9.6 %collective-permute-start.8 = (bf16[2,128,256]{2,1,0:T(8,128)(2,1)S(1)}, bf16[2,128,256]{2,1,0:T(8,128)(2,1)S(1)}, u32[]{:S(2)}, u32[]{:S(2)}) collective-permute-start(bf16[2,128,256]{2,1,0:T(8,128)(2,1)S(1)} %get-tuple-element.31), channel_id=1, source_target_pairs={{0,24},{8,16},{16,8},{24,0},{1,25},{9,17},{17,9},{25,1},{2,26},{10... | collective-permute-start | bytes 393224 | tf_op jit(solution)/shard_map/ppermute | solution.py:471
  74.8 9.2 %collective-permute-start.10 = (bf16[4,128,256]{2,1,0:T(8,128)(2,1)S(1)}, bf16[4,128,256]{2,1,0:T(8,128)(2,1)S(1)}, u32[]{:S(2)}, u32[]{:S(2)}) collective-permute-start(bf16[4,128,256]{2,1,0:T(8,128)(2,1)S(1)} %get-tuple-element.34), channel_id=1, source_target_pairs={{0,8},{8,0},{16,24},{24,16},{1,9},{9,1},{17,25},{25,17},{2,10},{10... | collective-permute-start | bytes 786440 | tf_op jit(solution)/shard_map/ppermute | solution.py:471
  75.7 13.4 %collective-permute-start.11 = (bf16[4,128,256]{2,1,0:T(8,128)(2,1)S(1)}, bf16[4,128,256]{2,1,0:T(8,128)(2,1)S(1)}, u32[]{:S(2)}, u32[]{:S(2)}) collective-permute-start(bf16[4,128,256]{2,1,0:T(8,128)(2,1)S(1)} %get-tuple-element.35), channel_id=1, source_target_pairs={{0,16},{8,24},{16,0},{24,8},{1,17},{9,25},{17,1},{25,9},{2,18},{10... | collective-permute-start | bytes 786440 | tf_op jit(solution)/shard_map/ppermute | solution.py:471
  76.4 12.7 %collective-permute-start.12 = (bf16[4,128,256]{2,1,0:T(8,128)(2,1)S(1)}, bf16[4,128,256]{2,1,0:T(8,128)(2,1)S(1)}, u32[]{:S(2)}, u32[]{:S(2)}) collective-permute-start(bf16[4,128,256]{2,1,0:T(8,128)(2,1)S(1)} %get-tuple-element.36), channel_id=1, source_target_pairs={{0,24},{8,16},{16,8},{24,0},{1,25},{9,17},{17,9},{25,1},{2,26},{10... | collective-permute-start | bytes 786440 | tf_op jit(solution)/shard_map/ppermute | solution.py:471

commit v12 on v10

--- a/solution.py
+++ b/solution.py
@@ -99,41 +99,161 @@
     return jnp.max(squares, axis=0, keepdims=True)
 
 
-def project_kernel(
-    heads, own_ref, gain_ref, w_query_ref, w_key_ref, w_value_ref, query_ref, key_ref, value_ref, norm_ref
+def is_safe(query_norms, key_norms):
+    return jnp.max(query_norms * key_norms) * 1.05 <= SAFE_SCORE * SAFE_SCORE
+
+
+def query_scale(head_size):
+    return math.log2(math.e) / math.sqrt(head_size)
+
+
+def band_bias(window, lower, upper, reach):
+    apart = jnp.abs(iota((Q_ROWS, upper - lower), 1) + (lower - reach) - iota((Q_ROWS, upper - lower), 0))
+    return jnp.where(apart <= window, 0.0, -1e30)
+
+
+def group_lanes(group):
+    return slice(group * LANES, (group + 1) * LANES)
+
+
+def stacked_heads(queries, head_size):
+    lane_head = iota((1, LANES), 1) // head_size
+    masks = [(lane_head == head).astype(F32).astype(BF16) for head in range(LANES // head_size)]
+    return jnp.concatenate([queries * mask for mask in masks], axis=0)
+
+
+def put_values(buf, lower, values):
+    for group in range(values.shape[1] // LANES):
+        lanes = slice(2 * group * LANES, (2 * group + 1) * LANES)
+        buf[lower : lower + values.shape[0], lanes] = values[:, group_lanes(group)]
+
+
+def weighted_sums(weights, values, head_size):
+    mixed_all = dot(weights, values)
+    heads = LANES // head_size
+    count = mixed_all.shape[0] // heads
+    lane_head = iota((1, LANES), 1) // head_size
+    mixed, totals = mixed_all[:count, :LANES], mixed_all[:count, LANES:]
+    for head in range(1, heads):
+        part = mixed_all[head * count : (head + 1) * count]
+        mixed = jnp.where(lane_head == head, part[:, :LANES], mixed)
+        totals = jnp.where(lane_head == head, part[:, LANES:], totals)
+    return mixed, totals
+
+
+def padded_lanes(values, before, after):
+    pieces = [jnp.zeros((values.shape[0], before), BF16)] if before else []
+    pieces.append(values.astype(BF16))
+    if after:
+        pieces.append(jnp.zeros((values.shape[0], after), BF16))
+    return jnp.concatenate(pieces, axis=1) if len(pieces) > 1 else pieces[0]
+
+
+def unit_weights(scores, spans, bias_of):
+    width = scores.shape[1]
+    count = len(spans) * Q_ROWS
+    weights = []
+    for head in range(scores.shape[0] // count):
+        for block, (lower, upper) in enumerate(spans):
+            top = head * count + block * Q_ROWS
+            expo = jnp.exp2(scores[top : top + Q_ROWS, lower:upper] + bias_of(head, block))
+            weights.append(padded_lanes(expo, lower, width - upper))
+    return jnp.concatenate(weights, axis=0)
+
+
+def inner_kernel(
+    window_ref,
+    own_ref,
+    gain_ref,
+    w_query_ref,
+    w_key_ref,
+    w_value_ref,
+    query_ref,
+    norm_ref,
+    mixed_ref,
+    total_ref,
+    key_buf,
+    value_buf,
+    bias_buf,
 ):
-    scale = math.log2(math.e) / math.sqrt(own_ref.shape[2] // heads)
+    rows, feat_width = own_ref.shape[1:]
+    heads = window_ref.shape[0]
+    head_size = feat_width // heads
+    group_heads = LANES // head_size
+    key_count = bias_buf.shape[2]
+    reach = (key_count - Q_ROWS) // 2
+    reach_blocks = reach // Q_ROWS
+    blocks = rows // Q_ROWS
+
+    @pl.when(pl.program_id(0) == 0)
+    def _():
+        for head in range(heads):
+            bias_buf[head] = band_bias(window_ref[head], 0, key_count, reach)
+        value_buf[...] = jnp.ones(value_buf.shape, BF16)
+
     normed = rms_scaled(own_ref[0].astype(F32), gain_ref[...]).astype(BF16)
-    queries = dot(normed, w_query_ref[...]) * scale
-    keys = dot(normed, w_key_ref[...])
-    query_ref[0] = queries.astype(BF16)
-    key_ref[0] = keys.T.astype(BF16)
-    value_ref[0] = dot(normed, w_value_ref[...]).astype(BF16)
+    query_rows = dot(normed, w_query_ref[...]) * query_scale(head_size)
+    key_rows = dot(normed, w_key_ref[...])
+    query_ref[0] = query_rows.astype(BF16)
+    key_buf[...] = key_rows.T.astype(BF16)
+    put_values(value_buf, 0, dot(normed, w_value_ref[...]).astype(BF16))
+    query_norms, key_norms = largest_norms(query_rows, heads), largest_norms(key_rows, heads)
     blank = jnp.zeros((norm_ref.shape[1] - 2, LANES), F32)
-    norm_ref[0] = jnp.concatenate([largest_norms(queries, heads), largest_norms(keys, heads), blank], axis=0)
-
-
-def project(own, heads, gain, w_query, w_key, w_value):
+    norm_ref[0] = jnp.concatenate([query_norms, key_norms, blank], axis=0)
+
+    @pl.when(is_safe(query_norms, key_norms))
+    def _():
+        units = [(first, group) for first in range(0, blocks, 2) for group in range(heads // group_heads)]
+
+        def scores_of(first, group):
+            queries = query_ref[0, first * Q_ROWS : (first + 2) * Q_ROWS, group_lanes(group)]
+            return dot(stacked_heads(queries, head_size), key_buf[group_lanes(group), :])
+
+        scores = scores_of(*units[0])
+        for at, (first, group) in enumerate(units):
+            following = scores_of(*units[at + 1]) if at + 1 < len(units) else None
+            ranges = [(max(0, b - reach_blocks), min(blocks, b + reach_blocks + 1)) for b in (first, first + 1)]
+            spans = [(lower * Q_ROWS, upper * Q_ROWS) for lower, upper in ranges]
+
+            def bias_of(head, block):
+                shift = (reach_blocks - first - block) * Q_ROWS
+                lower, upper = spans[block]
+                return bias_buf[group * group_heads + head, :, lower + shift : upper + shift]
+
+            values = value_buf[:, 2 * group * LANES : 2 * (group + 1) * LANES]
+            mixed, totals = weighted_sums(unit_weights(scores, spans, bias_of), values, head_size)
+            here = slice(first * Q_ROWS, (first + 2) * Q_ROWS)
+            mixed_ref[0, here, group_lanes(group)] = mixed
+            total_ref[0, here, group_lanes(group)] = totals
+            scores = following
+
+
+def inner(head_window, own, gain, w_query, w_key, w_value, reach):
     members, rows, feat_width = own.shape
-    upright = (members, rows, feat_width)
-    shapes = [upright, (members, feat_width, rows), upright]
-    norm_shape = (members, 8, LANES)
+    heads = head_window.shape[0]
+    key_count = Q_ROWS + 2 * reach
+    shapes = [(own.shape, BF16), ((members, 8, LANES), F32), (own.shape, F32), (own.shape, F32)]
 
     def spec(shape):
         return pl.BlockSpec((1, *shape[1:]), lambda m: (m, 0, 0))
 
     return pl.pallas_call(
-        functools.partial(project_kernel, heads),
+        inner_kernel,
         grid=(members,),
-        out_shape=[jax.ShapeDtypeStruct(v, BF16) for v in shapes] + [jax.ShapeDtypeStruct(norm_shape, F32)],
-        in_specs=[spec(upright)] + [vmem_spec()] * 4,
-        out_specs=[spec(v) for v in (*shapes, norm_shape)],
+        out_shape=[jax.ShapeDtypeStruct(*v) for v in shapes],
+        in_specs=[smem_spec(), spec(own.shape)] + [vmem_spec()] * 4,
+        out_specs=[spec(shape) for shape, _ in shapes],
+        scratch_shapes=[
+            pltpu.VMEM((feat_width, rows), BF16),
+            pltpu.VMEM((rows, 2 * feat_width), BF16),
+            pltpu.VMEM((heads, Q_ROWS, key_count), F32),
+        ],
         compiler_params=pltpu.CompilerParams(vmem_limit_bytes=VMEM_LIMIT),
         cost_estimate=pl.CostEstimate(
-            flops=6 * own.size * feat_width, bytes_accessed=8 * own.size, transcendentals=0
+            flops=own.size * (6 * feat_width + 16 * rows), bytes_accessed=14 * own.size, transcendentals=0
         ),
-        name="project",
-    )(own, gain, w_query, w_key, w_value)
+        name="inner",
+    )(head_window, own, gain, w_query, w_key, w_value)
 
 
 def forward_kernel(
@@ -141,9 +261,9 @@
     window_ref,
     state_ref,
     query_ref,
-    key_ref,
-    value_ref,
     norm_ref,
+    inner_mixed_ref,
+    inner_total_ref,
     left_ref,
     right_ref,
     attn_gain_ref,
@@ -156,96 +276,100 @@
     down_weight_ref,
     *refs,
 ):
-    out_refs, (key_buf, value_buf, bias_buf, mixed_buf, forecast_buf) = refs[:-5], refs[-5:]
+    out_refs, (halo_key_buf, halo_value_buf, bias_buf, mixed_buf, key_buf, value_buf, forecast_buf) = (
+        refs[:-7],
+        refs[-7:],
+    )
     rows, feat_width = state_ref.shape[1:]
     reach = left_ref.shape[1]
-    head_count = window_ref.shape[0]
-    head_size = feat_width // head_count
+    heads = window_ref.shape[0]
+    head_size = feat_width // heads
     group_heads = LANES // head_size
+    groups = heads // group_heads
     blocks = rows // Q_ROWS
     key_count = Q_ROWS + 2 * reach
+    count = 2 * Q_ROWS
 
     @pl.when(pl.program_id(0) == 0)
     def _():
-        apart = jnp.abs(iota((Q_ROWS, key_count), 1) - reach - iota((Q_ROWS, key_count), 0))
-        for block in range(blocks):
-            k_pos = place_ref[0] - reach + block * Q_ROWS + iota((Q_ROWS, key_count), 1)
-            inside = (k_pos >= 0) & (k_pos < place_ref[1])
-            for head in range(head_count):
-                bias_buf[block, head] = jnp.where(inside & (apart <= window_ref[head]), 0.0, -1e30)
-        value_buf[...] = jnp.ones(value_buf.shape, BF16)
-
-    key_buf[:, reach : reach + rows] = key_ref[0]
-    groups = head_count // group_heads
-
-    def put_values(lower, values):
-        for group in range(groups):
-            lanes = slice(2 * group * LANES, (2 * group + 1) * LANES)
-            value_buf[lower : lower + values.shape[0], lanes] = values[:, group * LANES : (group + 1) * LANES]
-
-    put_values(reach, value_ref[0])
+        first_valid = place_ref[0] - reach >= 0
+        last_valid = place_ref[0] + rows + reach <= place_ref[1]
+        for head in range(heads):
+            left_bias = band_bias(window_ref[head], 0, reach, reach)
+            right_bias = band_bias(window_ref[head], key_count - reach, key_count, reach)
+            bias_buf[0, head] = jnp.where(first_valid, left_bias, -1e30)
+            bias_buf[1, head] = jnp.where(last_valid, right_bias, -1e30)
+        halo_value_buf[...] = jnp.ones(halo_value_buf.shape, BF16)
+
+    def keys_of(normed):
+        return dot(normed, w_key_ref[...])
+
+    def values_of(normed):
+        return dot(normed, w_value_ref[...]).astype(BF16)
+
     key_norms = norm_ref[0, 1:2, :]
-    for ref, lower in ((left_ref, 0), (right_ref, reach + rows)):
+    for side, ref in enumerate((left_ref, right_ref)):
         normed = rms_scaled(ref[0].astype(F32), attn_gain_ref[...]).astype(BF16)
-        keys = dot(normed, w_key_ref[...])
-        key_norms = jnp.maximum(key_norms, largest_norms(keys, head_count))
-        key_buf[:, lower : lower + reach] = keys.T.astype(BF16)
-        put_values(lower, dot(normed, w_value_ref[...]).astype(BF16))
-
-    bound = jnp.max(norm_ref[0, 0:1, :] * key_norms) * 1.05
-    safe = bound <= SAFE_SCORE * SAFE_SCORE
-
-    lane_head = iota((1, LANES), 1) // head_size
-    head_masks = [(lane_head == head).astype(F32).astype(BF16) for head in range(group_heads)]
-
-    def scores_of(start, count, group):
-        lanes = slice(group * LANES, (group + 1) * LANES)
-        queries = query_ref[0, pl.ds(start, count), lanes]
-        stacked = jnp.concatenate([queries * mask for mask in head_masks], axis=0)
-        return dot(stacked, key_buf[lanes, pl.ds(start, count + 2 * reach)])
-
-    def mix_values(start, count, group, weights):
-        lanes = slice(2 * group * LANES, 2 * (group + 1) * LANES)
-        mixed_all = dot(jnp.concatenate(weights, axis=0), value_buf[pl.ds(start, count + 2 * reach), lanes])
-        mixed, totals = mixed_all[:count, :LANES], mixed_all[:count, LANES:]
-        for head in range(1, group_heads):
-            part = mixed_all[head * count : (head + 1) * count]
-            mixed = jnp.where(lane_head == head, part[:, :LANES], mixed)
-            totals = jnp.where(lane_head == head, part[:, LANES:], totals)
-        mixed_buf[pl.ds(start, count), group * LANES : (group + 1) * LANES] = (mixed / totals).astype(BF16)
+        keys = keys_of(normed)
+        key_norms = jnp.maximum(key_norms, largest_norms(keys, heads))
+        halo_key_buf[side] = keys.T.astype(BF16)
+        put_values(halo_value_buf.at[side], 0, values_of(normed))
+    safe = is_safe(norm_ref[0, 0:1, :], key_norms)
 
     @pl.when(safe)
     def _():
-        pair = 2 * Q_ROWS
-        corner = jnp.zeros((Q_ROWS, Q_ROWS), BF16)
-        units = [(start, group) for start in range(0, rows, pair) for group in range(groups)]
-        scores = scores_of(units[0][0], pair, units[0][1])
-        for at, (start, group) in enumerate(units):
-            following = scores_of(units[at + 1][0], pair, units[at + 1][1]) if at + 1 < len(units) else None
-            weights = []
-            for head in range(group_heads):
-                top = head * pair
-                bias = [bias_buf[start // Q_ROWS + part, group * group_heads + head] for part in range(2)]
-                upper = jnp.exp2(scores[top : top + Q_ROWS, :key_count] + bias[0])
-                lower = jnp.exp2(scores[top + Q_ROWS : top + pair, Q_ROWS:] + bias[1])
-                weights.append(jnp.concatenate([upper.astype(BF16), corner], axis=1))
-                weights.append(jnp.concatenate([corner, lower.astype(BF16)], axis=1))
-            mix_values(start, pair, group, weights)
+        units = [(side, group) for side in range(2) for group in range(groups)]
+
+        def scores_of(side, group):
+            start = side * (rows - count)
+            queries = query_ref[0, start : start + count, group_lanes(group)]
+            return dot(stacked_heads(queries, head_size), halo_key_buf[side, group_lanes(group), :])
+
+        scores = scores_of(*units[0])
+        for at, (side, group) in enumerate(units):
+            following = scores_of(*units[at + 1]) if at + 1 < len(units) else None
+            spans = [(0, reach), (Q_ROWS, reach)] if side == 0 else [(0, reach - Q_ROWS), (0, reach)]
+
+            def bias_of(head, block):
+                lower, upper = spans[block]
+                shift = -block * Q_ROWS if side == 0 else (1 - block) * Q_ROWS
+                return bias_buf[side, group * group_heads + head, :, lower + shift : upper + shift]
+
+            values = halo_value_buf[side, :, 2 * group * LANES : 2 * (group + 1) * LANES]
+            mixed, totals = weighted_sums(unit_weights(scores, spans, bias_of), values, head_size)
+            here = slice(side * (rows - count), side * (rows - count) + count)
+            mixed = mixed + inner_mixed_ref[0, here, group_lanes(group)]
+            totals = totals + inner_total_ref[0, here, group_lanes(group)]
+            mixed_buf[here, group_lanes(group)] = (mixed / totals).astype(BF16)
             scores = following
 
     @pl.when(jnp.logical_not(safe))
     def _():
+        normed = rms_scaled(state_ref[0].astype(F32), attn_gain_ref[...]).astype(BF16)
+        key_buf[:, :reach] = halo_key_buf[0]
+        key_buf[:, reach : reach + rows] = keys_of(normed).T.astype(BF16)
+        key_buf[:, reach + rows :] = halo_key_buf[1]
+        value_buf[...] = jnp.ones(value_buf.shape, BF16)
+        put_values(value_buf, reach, values_of(normed))
+        value_buf[:reach] = halo_value_buf[0]
+        value_buf[reach + rows :] = halo_value_buf[1]
         for block in range(blocks):
             start = block * Q_ROWS
+            k_pos = place_ref[0] - reach + start + iota((Q_ROWS, key_count), 1)
+            inside = (k_pos >= 0) & (k_pos < place_ref[1])
             for group in range(groups):
-                scores = scores_of(start, Q_ROWS, group)
+                queries = query_ref[0, start : start + Q_ROWS, group_lanes(group)]
+                keys = key_buf[group_lanes(group), start : start + key_count]
+                scores = dot(stacked_heads(queries, head_size), keys)
                 weights = []
                 for head in range(group_heads):
-                    score_matrix = scores[head * Q_ROWS : (head + 1) * Q_ROWS]
-                    score_matrix = score_matrix + bias_buf[block, group * group_heads + head]
-                    expo = jnp.exp2(score_matrix - jnp.max(score_matrix, axis=-1, keepdims=True))
-                    weights.append(expo.astype(BF16))
-                mix_values(start, Q_ROWS, group, weights)
+                    bias = band_bias(window_ref[group * group_heads + head], 0, key_count, reach)
+                    score_matrix = scores[head * Q_ROWS : (head + 1) * Q_ROWS] + jnp.where(inside, bias, -1e30)
+                    row_top = jnp.max(score_matrix, axis=-1, keepdims=True)
+                    weights.append(jnp.exp2(score_matrix - row_top).astype(BF16))
+                values = value_buf[start : start + key_count, 2 * group * LANES : 2 * (group + 1) * LANES]
+                mixed, totals = weighted_sums(jnp.concatenate(weights, axis=0), values, head_size)
+                mixed_buf[start : start + Q_ROWS, group_lanes(group)] = (mixed / totals).astype(BF16)
 
     after = (state_ref[0].astype(F32) + dot(mixed_buf[...], w_out_ref[...])).astype(BF16)
     normed_mid = rms_scaled(after.astype(F32), ffn_gain_ref[...]).astype(BF16)
@@ -262,33 +386,37 @@
         out_ref[0] = forecast_buf[pl.ds(lower, share_rows), :]
 
 
-def forward(place, head_window, own, projected, left, right, gains, weights, shares):
+def forward(place, head_window, own, inner_parts, left, right, gains, weights, shares):
     members, row_count, feat_width = own.shape
     reach = left.shape[1]
-    key_count = Q_ROWS + 2 * reach
+    heads = head_window.shape[0]
     hidden_width = weights[3].shape[1]
-    macs = members * row_count * feat_width * (3 * feat_width + 3 * hidden_width + 8 * key_count)
-    edge_block = pl.BlockSpec((1, reach, feat_width), lambda m: (m, 0, 0))
+    macs = members * row_count * feat_width * (3 * feat_width + 3 * hidden_width + 4 * reach)
+
+    def spec(array):
+        return pl.BlockSpec((1, *array.shape[1:]), lambda m: (m, 0, 0))
+
     return pl.pallas_call(
         forward_kernel,
         grid=(members,),
         out_shape=[jax.ShapeDtypeStruct((members, row_count // shares, feat_width), BF16)] * shares,
         in_specs=[smem_spec()] * 2
-        + [pl.BlockSpec((1, *v.shape[1:]), lambda m: (m, 0, 0)) for v in (own, *projected)]
-        + [edge_block] * 2
+        + [spec(v) for v in (own, *inner_parts, left, right)]
         + [vmem_spec()] * (len(gains) + len(weights)),
         out_specs=[pl.BlockSpec((1, row_count // shares, feat_width), lambda m: (m, 0, 0))] * shares,
         scratch_shapes=[
+            pltpu.VMEM((2, feat_width, reach), BF16),
+            pltpu.VMEM((2, reach, 2 * feat_width), BF16),
+            pltpu.VMEM((2, heads, Q_ROWS, reach), F32),
+            pltpu.VMEM((row_count, feat_width), BF16),
             pltpu.VMEM((feat_width, row_count + 2 * reach), BF16),
             pltpu.VMEM((row_count + 2 * reach, 2 * feat_width), BF16),
-            pltpu.VMEM((row_count // Q_ROWS, head_window.shape[0], Q_ROWS, key_count), F32),
-            pltpu.VMEM((row_count, feat_width), BF16),
             pltpu.VMEM((row_count, feat_width), BF16),
         ],
         compiler_params=pltpu.CompilerParams(vmem_limit_bytes=VMEM_LIMIT),
         cost_estimate=pl.CostEstimate(flops=2 * macs, bytes_accessed=10 * own.size, transcendentals=0),
         name="forward",
-    )(place, head_window, own, *projected, left, right, *gains, *weights)
+    )(place, head_window, own, *inner_parts, left, right, *gains, *weights)
 
 
 def global_member(held, index, own_members):
@@ -493,9 +621,9 @@
     place = jnp.stack([first_pos, row_count * tok_count, index]).astype(jnp.int32)
     index = index.astype(jnp.int32).reshape(1)
     gains = [attn_gain.reshape(1, -1), ffn_gain.reshape(1, -1)]
-    projected = project(ens_state, head_window.shape[0], gains[0], w_query, w_key, w_value)
+    inner_parts = inner(head_window, ens_state, gains[0], w_query, w_key, w_value, WIN)
     weights = [w_key, w_value, w_out, w_gate, w_up, down_weight]
-    forecast = forward(place, head_window, ens_state, projected, left, right, gains, weights, mem_count)
+    forecast = forward(place, head_window, ens_state, inner_parts, left, right, gains, weights, mem_count)
     shares = exchanged(forecast)
     partial = gram_partial(index, shares, grid)
     partials = lax.all_to_all(

time: 87.6 us -> 88.5 us (1.010)
  Pallas kernels: 32.8 us -> 35.7 us
  local copies, waits for them, and re-layouts: 3.52 us -> 2.26 us
    pallas_call x1, Pallas kernels: 21.9 us -> 23.5 us  [forward(): pl.pallas_call(forward_kernel, grid=(members,), out_shape=[jax.ShapeDtype...]
    pallas_call x1, Pallas kernels: 2.8 us -> 4.09 us  [inner(): pl.pallas_call(inner_kernel, grid=(members,), out_shape=[jax.ShapeDtypeSt...]
    unnamed x30, local copies, waits for them, and re-layouts: 1.33 us -> 0.08 us
  transfers between devices with their start and end apart: 8 -> 8, of which waited for: 5 -> 5; matrix products, arithmetic and copies ran while one was open for 0% -> 0% of each run, Pallas kernels for 5% -> 6%
where the time goes in v12:
time: 88.5 us; the launch traced here: 88.3 us
  Pallas kernels  35.7 us (40%)
  blocking collectives  21.7 us (25%)
  waiting for transfers between devices  17.5 us (20%)
  starting transfers between devices  10.8 us (12%)
  local copies, waits for them, and re-layouts  2.26 us (3%)
    pallas_call x1, Pallas kernels, forward(): pl.pallas_call(forward_kernel, grid=(members,), out_shape=[jax.ShapeDtype...  23.5 us
    all_to_all x1, blocking collectives, local(): lax.all_to_all(jnp.broadcast_to(partial[None], (device_count, *partial.sh...  21.7 us
    ppermute x6, waiting for transfers between devices, exchanged(): lax.ppermute(v, 'mem', [(i, i ^ part) for i in range(count)])  17.1 us
    ppermute x6, starting transfers between devices, exchanged(): lax.ppermute(v, 'mem', [(i, i ^ part) for i in range(count)])  7.15 us
    pallas_call x1, Pallas kernels, inner(): pl.pallas_call(inner_kernel, grid=(members,), out_shape=[jax.ShapeDtypeSt...  4.09 us
    pallas_call x1, Pallas kernels, combine(): pl.pallas_call(combine_kernel, out_shape=[jax.ShapeDtypeStruct(v.shape, B...  3.64 us
    ppermute x1, starting transfers between devices, local(): left = lax.ppermute(ens_state[:, row_count - WIN:], 'tok', up)  2.39 us
    slice x1, local copies, waits for them, and re-layouts, local(): right = lax.ppermute(ens_state[:, :WIN], 'tok', down)  2.17 us
  transfers between devices with their start and end apart: 8, of which 5 were waited for; matrix products, arithmetic and copies ran while one was open for 0% of the time, Pallas kernels for 6%

profile of v12, /device:TPU:0, one launch (start us, length us, event | category | flops | bytes accessed | tf_op | source)
XLA Modules:
  0.0 88.3 jit_solution(18174365548920696719)
XLA Ops:
  0.0 2.2 %fusion = (bf16[4,256,256]{2,1,0:T(8,128)(2,1)S(1)}, bf16[4,256,256]{2,1,0:T(8,128)(2,1)}) fusion(bf16[4,512,256]{2,1,0:T(8,128)(2,1)} %state_ref.1), kind=kLoop, calls=%fused_computation.1 | loop fusion | bytes 2097152 | tf_op jit(solution)/shard_map/slice | solution.py:615
  2.2 2.4 %collective-permute-start = (bf16[4,256,256]{2,1,0:T(8,128)(2,1)}, bf16[4,256,256]{2,1,0:T(8,128)(2,1)S(1)}, u32[]{:S(2)}, u32[]{:S(2)}) collective-permute-start(bf16[4,256,256]{2,1,0:T(8,128)(2,1)} %get-tuple-element.30), channel_id=1, source_target_pairs={{0,1},{1,2},{2,3},{3,4},{4,5},{5,6},{6,7},{8,9},{9,10},{10,11},{11... | collective-permute-start | bytes 1572872 | tf_op jit(solution)/shard_map/ppermute | solution.py:614
  4.6 1.3 %collective-permute-start.1 = (bf16[4,256,256]{2,1,0:T(8,128)(2,1)S(1)}, bf16[4,256,256]{2,1,0:T(8,128)(2,1)S(1)}, u32[]{:S(2)}, u32[]{:S(2)}) collective-permute-start(bf16[4,256,256]{2,1,0:T(8,128)(2,1)S(1)} %get-tuple-element.29), channel_id=1, source_target_pairs={{1,0},{2,1},{3,2},{4,3},{5,4},{6,5},{7,6},{9,8},{10,9},{11,10},{12... | collective-permute-start | bytes 1572872 | tf_op jit(solution)/shard_map/ppermute | solution.py:615
  5.9 0.1 pad_add_fusion.place_ref
  6.0 0.0 copy-start.1
  6.0 0.0 copy-start.2
  6.0 0.0 copy-start.3
  6.1 0.0 copy-start.7
  6.1 0.0 copy-start.13
  6.1 4.1 %inner.1 = (bf16[4,512,256]{2,1,0:T(8,128)(2,1)S(1)}, f32[4,8,128]{2,1,0:T(8,128)S(1)}, f32[4,512,256]{2,1,0:T(8,128)S(1)}, f32[4,512,256]{2,1,0:T(8,128)S(1)}) custom-call(s32[4]{0:T(128)S(1)} %copy-done.14, bf16[4,512,256]{2,1,0:T(8,128)(2,1)S(1)} %copy-done, f32[1,256]{1,0:T(1,128)S(1)} %bitcast.13, bf16[256,256]{1,0:T(8,128)(2,1)S(1)} %copy-done.4, ...), custom_call_target="tpu_custom_call" | custom-call | flops 5100273664 | bytes 7340032 | tf_op jit(solution)/shard_map/inner/pallas_call | solution.py:240
  10.2 0.0 collective-permute-done.left_ref
  10.2 0.4 collective-permute-done.1.right_ref
  10.6 0.0 copy-start.8
  10.6 0.0 copy-start.9
  10.6 0.0 copy-start.10
  10.6 0.0 copy-start.11
  10.6 23.5 %forward.1 = (bf16[4,128,256]{2,1,0:T(8,128)(2,1)S(1)}, bf16[4,128,256]{2,1,0:T(8,128)(2,1)S(1)}, bf16[4,128,256]{2,1,0:T(8,128)(2,1)S(1)}, bf16[4,128,256]{2,1,0:T(8,128)(2,1)S(1)}) custom-call(s32[3]{0:T(128)S(1)} %pad_add_fusion.place_ref, s32[4]{0:T(128)S(1)} %copy-done.14, bf16[4,512,256]{2,1,0:T(8,128)(2,1)S(1)} %copy-done, ...), custom_call_target="tpu_custom_call" | custom-call | flops 5100273664 | bytes 5242880 | tf_op jit(solution)/shard_map/forward/pallas_call | solution.py:399
  34.1 2.1 %collective-permute-start.2 = (bf16[4,128,256]{2,1,0:T(8,128)(2,1)S(1)}, bf16[4,128,256]{2,1,0:T(8,128)(2,1)S(1)}, u32[]{:S(2)}, u32[]{:S(2)}) collective-permute-start(bf16[4,128,256]{2,1,0:T(8,128)(2,1)S(1)} %get-tuple-element.22), channel_id=1, source_target_pairs={{0,8},{8,0},{16,24},{24,16},{1,9},{9,1},{17,25},{25,17},{2,10},{10... | collective-permute-start | bytes 786440 | tf_op jit(solution)/shard_map/ppermute | solution.py:585
  36.2 1.5 %collective-permute-start.3 = (bf16[4,128,256]{2,1,0:T(8,128)(2,1)S(1)}, bf16[4,128,256]{2,1,0:T(8,128)(2,1)S(1)}, u32[]{:S(2)}, u32[]{:S(2)}) collective-permute-start(bf16[4,128,256]{2,1,0:T(8,128)(2,1)S(1)} %get-tuple-element.23), channel_id=1, source_target_pairs={{0,16},{8,24},{16,0},{24,8},{1,17},{9,25},{17,1},{25,9},{2,18},{10... | collective-permute-start | bytes 786440 | tf_op jit(solution)/shard_map/ppermute | solution.py:585
  37.7 0.0 collective-permute-start.4
  37.7 1.3 %sample_grid.1.refs_4_ = f32[2,128,256]{2,1,0:T(8,128)S(1)} custom-call(s32[1]{0:T(128)} %bitcast.4.start_ref, s32[1,4096]{1,0:T(1,128)S(1)} %bitcast.9, s32[1,4096]{1,0:T(1,128)S(1)} %bitcast.10, f32[1,4096]{1,0:T(1,128)S(1)} %bitcast.11, f32[1,4096]{1,0:T(1,128)S(1)} %bitcast.12), custom_call_target="tpu_custom_call" | custom-call | flops 1073741824 | bytes 65536 | tf_op jit(solution)/shard_map/sample_grid/pallas_call | solution.py:81
  39.0 1.5 %collective-permute-done.2.refs_1_ = bf16[4,128,256]{2,1,0:T(8,128)(2,1)S(1)} collective-permute-done((bf16[4,128,256]{2,1,0:T(8,128)(2,1)S(1)}, bf16[4,128,256]{2,1,0:T(8,128)(2,1)S(1)}, u32[]{:S(2)}, u32[]{:S(2)}) %collective-permute-start.2) | collective-permute-done | bytes 262176 | tf_op jit(solution)/shard_map/ppermute | solution.py:585
  40.5 4.9 %collective-permute-done.3.refs_2_ = bf16[4,128,256]{2,1,0:T(8,128)(2,1)S(1)} collective-permute-done((bf16[4,128,256]{2,1,0:T(8,128)(2,1)S(1)}, bf16[4,128,256]{2,1,0:T(8,128)(2,1)S(1)}, u32[]{:S(2)}, u32[]{:S(2)}) %collective-permute-start.3) | collective-permute-done | bytes 262176 | tf_op jit(solution)/shard_map/ppermute | solution.py:585
  45.4 1.7 %gram.1 = f32[8,128]{1,0:T(8,128)S(1)} custom-call(s32[1]{0:T(128)} %bitcast.index_ref, bf16[4,128,256]{2,1,0:T(8,128)(2,1)S(1)} %get-tuple-element.21.refs_0_, bf16[4,128,256]{2,1,0:T(8,128)(2,1)S(1)} %collective-permute-done.2.refs_1_, bf16[4,128,256]{2,1,0:T(8,128)(2,1)S(1)} %collective-permute-done.3.refs_2_, ...), custom_call_target="tpu_custom_call" | custom-call | flops 805306368 | bytes 1048576 | tf_op jit(solution)/shard_map/gram/pallas_call | solution.py:466
  47.1 21.7 %all_to_all.5.partial_ref = f32[32,8,128]{2,1,0:T(8,128)S(1)} all-to-all(f32[32,8,128]{2,1,0:T(8,128)S(1)} %broadcast_in_dim.2), channel_id=1, replica_groups=mesh['mem'=4,'tok'=8] {'mem','tok'}, dimensions={0} | all-to-all | bytes 262144 | tf_op jit(solution)/shard_map/all_to_all | solution.py:629
  68.8 3.6 %combine.1 = (bf16[4,128,256]{2,1,0:T(8,128)(2,1)S(1)}, bf16[4,128,256]{2,1,0:T(8,128)(2,1)S(1)}, bf16[4,128,256]{2,1,0:T(8,128)(2,1)S(1)}, bf16[4,128,256]{2,1,0:T(8,128)(2,1)S(1)}) custom-call(s32[1]{0:T(128)} %bitcast.index_ref, f32[32,8,128]{2,1,0:T(8,128)S(1)} %all_to_all.5.partial_ref, bf16[4,128,256]{2,1,0:T(8,128)(2,1)S(1)} %get-tuple-element.21.refs_0_, ...), custom_call_target="tpu_custom_call" | custom-call | flops 536870912 | bytes 2097152 | tf_op jit(solution)/shard_map/combine/pallas_call | solution.py:549
  72.5 0.9 %collective-permute-start.5 = (bf16[4,128,256]{2,1,0:T(8,128)(2,1)S(1)}, bf16[4,128,256]{2,1,0:T(8,128)(2,1)S(1)}, u32[]{:S(2)}, u32[]{:S(2)}) collective-permute-start(bf16[4,128,256]{2,1,0:T(8,128)(2,1)S(1)} %get-tuple-element.26), channel_id=1, source_target_pairs={{0,8},{8,0},{16,24},{24,16},{1,9},{9,1},{17,25},{25,17},{2,10},{10... | collective-permute-start | bytes 786440 | tf_op jit(solution)/shard_map/ppermute | solution.py:585
  73.4 0.7 collective-permute-start.6
  74.1 2.0 %collective-permute-start.7 = (bf16[4,128,256]{2,1,0:T(8,128)(2,1)S(1)}, bf16[4,128,256]{2,1,0:T(8,128)(2,1)S(1)}, u32[]{:S(2)}, u32[]{:S(2)}) collective-permute-start(bf16[4,128,256]{2,1,0:T(8,128)(2,1)S(1)} %get-tuple-element.28), channel_id=1, source_target_pairs={{0,24},{8,16},{16,8},{24,0},{1,25},{9,17},{17,9},{25,1},{2,26},{10... | collective-permute-start | bytes 786440 | tf_op jit(solution)/shard_map/ppermute | solution.py:585
  76.0 5.6 %collective-permute-done.5.refs_1_ = bf16[4,128,256]{2,1,0:T(8,128)(2,1)S(1)} collective-permute-done((bf16[4,128,256]{2,1,0:T(8,128)(2,1)S(1)}, bf16[4,128,256]{2,1,0:T(8,128)(2,1)S(1)}, u32[]{:S(2)}, u32[]{:S(2)}) %collective-permute-start.5) | collective-permute-done | bytes 262176 | tf_op jit(solution)/shard_map/ppermute | solution.py:585
  81.7 5.1 %collective-permute-done.6.refs_2_ = bf16[4,128,256]{2,1,0:T(8,128)(2,1)S(1)} collective-permute-done((bf16[4,128,256]{2,1,0:T(8,128)(2,1)S(1)}, bf16[4,128,256]{2,1,0:T(8,128)(2,1)S(1)}, u32[]{:S(2)}, u32[]{:S(2)}) %collective-permute-start.6) | collective-permute-done | bytes 262176 | tf_op jit(solution)/shard_map/ppermute | solution.py:585
  86.8 1.5 %assemble.1 = bf16[4,512,256]{2,1,0:T(8,128)(2,1)} custom-call(s32[1]{0:T(128)} %bitcast.index_ref, bf16[4,128,256]{2,1,0:T(8,128)(2,1)S(1)} %get-tuple-element.25.refs_0_, bf16[4,128,256]{2,1,0:T(8,128)(2,1)S(1)} %collective-permute-done.5.refs_1_, bf16[4,128,256]{2,1,0:T(8,128)(2,1)S(1)} %collective-permute-done.6.refs_2_, ...), custom_call_target="tpu_custom_call" | custom-call | bytes 2097152 | tf_op jit(solution)/shard_map/assemble/pallas_call | solution.py:570
  (24 shorter events, 0.1 us)
Async XLA Ops:
  0.0 6.0 %copy-start = (bf16[4,512,256]{2,1,0:T(8,128)(2,1)S(1)}, bf16[4,512,256]{2,1,0:T(8,128)(2,1)}, u32[]{:S(2)}) copy-start(bf16[4,512,256]{2,1,0:T(8,128)(2,1)} %state_ref.1) | copy-start | bytes 3145732
  0.0 6.0 %copy-start.12 = (f32[256]{0:T(256)S(1)}, f32[256]{0:T(256)}, u32[]{:S(2)}) copy-start(f32[256]{0:T(256)} %param.16) | copy-start | bytes 3076
  0.0 6.0 %copy-start.4 = (bf16[256,256]{1,0:T(8,128)(2,1)S(1)}, bf16[256,256]{1,0:T(8,128)(2,1)}, u32[]{:S(2)}) copy-start(bf16[256,256]{1,0:T(8,128)(2,1)} %w_query_ref.1) | copy-start | bytes 393220
  0.0 6.0 %copy-start.5 = (bf16[256,256]{1,0:T(8,128)(2,1)S(1)}, bf16[256,256]{1,0:T(8,128)(2,1)}, u32[]{:S(2)}) copy-start(bf16[256,256]{1,0:T(8,128)(2,1)} %w_key_ref.3) | copy-start | bytes 393220
  0.0 6.0 %copy-start.6 = (bf16[256,256]{1,0:T(8,128)(2,1)S(1)}, bf16[256,256]{1,0:T(8,128)(2,1)}, u32[]{:S(2)}) copy-start(bf16[256,256]{1,0:T(8,128)(2,1)} %w_value_ref.3) | copy-start | bytes 393220
  0.0 6.0 %copy-start.14 = (s32[4]{0:T(128)S(1)}, s32[4]{0:T(128)}, u32[]{:S(2)}) copy-start(s32[4]{0:T(128)} %window_ref.3) | copy-start | bytes 52
  2.2 8.0 %collective-permute-start = (bf16[4,256,256]{2,1,0:T(8,128)(2,1)}, bf16[4,256,256]{2,1,0:T(8,128)(2,1)S(1)}, u32[]{:S(2)}, u32[]{:S(2)}) collective-permute-start(bf16[4,256,256]{2,1,0:T(8,128)(2,1)} %get-tuple-element.30), channel_id=1, source_target_pairs={{0,1},{1,2},{2,3},{3,4},{4,5},{5,6},{6,7},{8,9},{9,10},{10,11},{11... | collective-permute-start | bytes 1572872 | tf_op jit(solution)/shard_map/ppermute | solution.py:614
  4.6 6.0 %collective-permute-start.1 = (bf16[4,256,256]{2,1,0:T(8,128)(2,1)S(1)}, bf16[4,256,256]{2,1,0:T(8,128)(2,1)S(1)}, u32[]{:S(2)}, u32[]{:S(2)}) collective-permute-start(bf16[4,256,256]{2,1,0:T(8,128)(2,1)S(1)} %get-tuple-element.29), channel_id=1, source_target_pairs={{1,0},{2,1},{3,2},{4,3},{5,4},{6,5},{7,6},{9,8},{10,9},{11,10},{12... | collective-permute-start | bytes 1572872 | tf_op jit(solution)/shard_map/ppermute | solution.py:615
  6.0 4.5 %copy-start.1 = (bf16[256,1024]{1,0:T(8,128)(2,1)S(1)}, bf16[256,1024]{1,0:T(8,128)(2,1)}, u32[]{:S(2)}) copy-start(bf16[256,1024]{1,0:T(8,128)(2,1)} %w_gate_ref.1) | copy-start | bytes 1572868
  6.0 4.5 %copy-start.2 = (bf16[256,1024]{1,0:T(8,128)(2,1)S(1)}, bf16[256,1024]{1,0:T(8,128)(2,1)}, u32[]{:S(2)}) copy-start(bf16[256,1024]{1,0:T(8,128)(2,1)} %w_up_ref.1) | copy-start | bytes 1572868
  6.0 4.5 %copy-start.3 = (bf16[1024,256]{1,0:T(8,128)(2,1)S(1)}, bf16[1024,256]{1,0:T(8,128)(2,1)}, u32[]{:S(2)}) copy-start(bf16[1024,256]{1,0:T(8,128)(2,1)} %down_weight_ref.1) | copy-start | bytes 1572868
  6.1 4.5 %copy-start.7 = (bf16[256,256]{1,0:T(8,128)(2,1)S(1)}, bf16[256,256]{1,0:T(8,128)(2,1)}, u32[]{:S(2)}) copy-start(bf16[256,256]{1,0:T(8,128)(2,1)} %w_out_ref.1) | copy-start | bytes 393220
  6.1 4.5 %copy-start.13 = (f32[256]{0:T(256)S(1)}, f32[256]{0:T(256)}, u32[]{:S(2)}) copy-start(f32[256]{0:T(256)} %param.17) | copy-start | bytes 3076
  10.6 27.1 %copy-start.8 = (s32[4096]{0:T(1024)S(1)}, s32[4096]{0:T(1024)}, u32[]{:S(2)}) copy-start(s32[4096]{0:T(1024)} %param.26) | copy-start | bytes 49156
  10.6 27.1 %copy-start.9 = (s32[4096]{0:T(1024)S(1)}, s32[4096]{0:T(1024)}, u32[]{:S(2)}) copy-start(s32[4096]{0:T(1024)} %param.27) | copy-start | bytes 49156
  10.6 27.1 %copy-start.10 = (f32[4096]{0:T(1024)S(1)}, f32[4096]{0:T(1024)}, u32[]{:S(2)}) copy-start(f32[4096]{0:T(1024)} %param.28) | copy-start | bytes 49156
  10.6 27.1 %copy-start.11 = (f32[4096]{0:T(1024)S(1)}, f32[4096]{0:T(1024)}, u32[]{:S(2)}) copy-start(f32[4096]{0:T(1024)} %param.29) | copy-start | bytes 49156
  34.1 6.4 %collective-permute-start.2 = (bf16[4,128,256]{2,1,0:T(8,128)(2,1)S(1)}, bf16[4,128,256]{2,1,0:T(8,128)(2,1)S(1)}, u32[]{:S(2)}, u32[]{:S(2)}) collective-permute-start(bf16[4,128,256]{2,1,0:T(8,128)(2,1)S(1)} %get-tuple-element.22), channel_id=1, source_target_pairs={{0,8},{8,0},{16,24},{24,16},{1,9},{9,1},{17,25},{25,17},{2,10},{10... | collective-permute-start | bytes 786440 | tf_op jit(solution)/shard_map/ppermute | solution.py:585
  36.2 9.3 %collective-permute-start.3 = (bf16[4,128,256]{2,1,0:T(8,128)(2,1)S(1)}, bf16[4,128,256]{2,1,0:T(8,128)(2,1)S(1)}, u32[]{:S(2)}, u32[]{:S(2)}) collective-permute-start(bf16[4,128,256]{2,1,0:T(8,128)(2,1)S(1)} %get-tuple-element.23), channel_id=1, source_target_pairs={{0,16},{8,24},{16,0},{24,8},{1,17},{9,25},{17,1},{25,9},{2,18},{10... | collective-permute-start | bytes 786440 | tf_op jit(solution)/shard_map/ppermute | solution.py:585
  37.7 7.8 %collective-permute-start.4 = (bf16[4,128,256]{2,1,0:T(8,128)(2,1)S(1)}, bf16[4,128,256]{2,1,0:T(8,128)(2,1)S(1)}, u32[]{:S(2)}, u32[]{:S(2)}) collective-permute-start(bf16[4,128,256]{2,1,0:T(8,128)(2,1)S(1)} %get-tuple-element.24), channel_id=1, source_target_pairs={{0,24},{8,16},{16,8},{24,0},{1,25},{9,17},{17,9},{25,1},{2,26},{10... | collective-permute-start | bytes 786440 | tf_op jit(solution)/shard_map/ppermute | solution.py:585
  72.5 9.2 %collective-permute-start.5 = (bf16[4,128,256]{2,1,0:T(8,128)(2,1)S(1)}, bf16[4,128,256]{2,1,0:T(8,128)(2,1)S(1)}, u32[]{:S(2)}, u32[]{:S(2)}) collective-permute-start(bf16[4,128,256]{2,1,0:T(8,128)(2,1)S(1)} %get-tuple-element.26), channel_id=1, source_target_pairs={{0,8},{8,0},{16,24},{24,16},{1,9},{9,1},{17,25},{25,17},{2,10},{10... | collective-permute-start | bytes 786440 | tf_op jit(solution)/shard_map/ppermute | solution.py:585
  73.4 13.4 %collective-permute-start.6 = (bf16[4,128,256]{2,1,0:T(8,128)(2,1)S(1)}, bf16[4,128,256]{2,1,0:T(8,128)(2,1)S(1)}, u32[]{:S(2)}, u32[]{:S(2)}) collective-permute-start(bf16[4,128,256]{2,1,0:T(8,128)(2,1)S(1)} %get-tuple-element.27), channel_id=1, source_target_pairs={{0,16},{8,24},{16,0},{24,8},{1,17},{9,25},{17,1},{25,9},{2,18},{10... | collective-permute-start | bytes 786440 | tf_op jit(solution)/shard_map/ppermute | solution.py:585
  74.1 12.7 %collective-permute-start.7 = (bf16[4,128,256]{2,1,0:T(8,128)(2,1)S(1)}, bf16[4,128,256]{2,1,0:T(8,128)(2,1)S(1)}, u32[]{:S(2)}, u32[]{:S(2)}) collective-permute-start(bf16[4,128,256]{2,1,0:T(8,128)(2,1)S(1)} %get-tuple-element.28), channel_id=1, source_target_pairs={{0,24},{8,16},{16,8},{24,0},{1,25},{9,17},{17,9},{25,1},{2,26},{10... | collective-permute-start | bytes 786440 | tf_op jit(solution)/shard_map/ppermute | solution.py:585

commit v13 on v12

--- a/solution.py
+++ b/solution.py
@@ -382,7 +382,8 @@
     forecast_buf[...] = forecast.astype(BF16)
     share_rows = out_refs[0].shape[1]
     for part, out_ref in enumerate(out_refs):
-        lower = pl.multiple_of((place_ref[2] ^ part) * share_rows, share_rows)
+        partner = partner_bits(part, place_ref[3] == 1, len(out_refs)) ^ place_ref[2]
+        lower = pl.multiple_of(partner * share_rows, share_rows)
         out_ref[0] = forecast_buf[pl.ds(lower, share_rows), :]
 
 
@@ -419,15 +420,24 @@
     )(place, head_window, own, *inner_parts, left, right, *gains, *weights)
 
 
-def global_member(held, index, own_members):
-    return ((held // own_members) ^ index) * own_members + held % own_members
+def partner_bits(part, odd, count):
+    fine = math.isqrt(count)
+    if fine * fine != count:
+        return part
+    turned = (part % fine) * fine + part // fine
+    return jnp.where(odd, turned, part) if isinstance(odd, jax.Array) else (turned if odd else part)
+
+
+def global_member(held, place_ref, own_members, parts):
+    bits = partner_bits(held // own_members, place_ref[1] == 1, parts)
+    return (bits ^ place_ref[0]) * own_members + held % own_members
 
 
 def gram_kernel(index_ref, *refs):
     share_refs, grid_ref, out_ref = refs[:-2], refs[-2], refs[-1]
     own_members, rows, feat_width = share_refs[0].shape
     members = own_members * len(share_refs)
-    index = index_ref[0]
+    parts = len(share_refs)
     stack = members * GROUP
     total = jnp.zeros((stack, stack), F32)
     proj = jnp.zeros((members, GROUP, feat_width), F32)
@@ -444,16 +454,16 @@
         total += dot(w_high, high, last) + dot(w_high, low, last) + dot(w_low, high, last)
     same = iota((stack, stack), 0) % GROUP == iota((stack, stack), 1) % GROUP
     by_row = jnp.sum(jnp.where(same, total, 0.0).reshape(members, GROUP, stack), axis=1)
-    column = global_member(iota((stack, LANES), 0) // GROUP, index, own_members)
+    column = global_member(iota((stack, LANES), 0) // GROUP, index_ref, own_members, parts)
     folded = (column == iota((stack, LANES), 1) % members).astype(F32)
-    held = global_member(iota((members, members), 1), index, own_members)
+    held = global_member(iota((members, members), 1), index_ref, own_members, parts)
     in_order = (held == iota((members, members), 0)).astype(F32)
     tiled = exact_dot(in_order, exact_dot(by_row, folded))
     per_row = LANES // members
     keep = iota((members, LANES), 0) % per_row == iota((members, LANES), 1) // members
     packed = jnp.sum(jnp.where(keep, tiled, 0.0).reshape(members // per_row, per_row, LANES), axis=1)
     proj_col = jnp.sum(jnp.sum(proj, axis=1), axis=1, keepdims=True)
-    at_lane = global_member(iota((members, LANES), 0), index, own_members) == iota((members, LANES), 1)
+    at_lane = global_member(iota((members, LANES), 0), index_ref, own_members, parts) == iota((members, LANES), 1)
     proj_row = jnp.sum(jnp.where(at_lane, proj_col, 0.0), axis=0, keepdims=True)
     filled = members // per_row + 1
     blank = jnp.zeros((out_ref.shape[0] - filled, LANES), F32)
@@ -526,7 +536,7 @@
     on_diagonal = iota((members, LANES), 0) == iota((members, LANES), 1)
     proj = jnp.sum(jnp.where(on_diagonal, proj_row, 0.0), axis=1, keepdims=True)
     transform = ensemble_transform(gram, proj)
-    held = global_member(iota((stack, members), 0) // GROUP, index_ref[0], own_members)
+    held = global_member(iota((stack, members), 0) // GROUP, index_ref, own_members, len(share_refs))
     pick = (held == iota((stack, members), 1)).astype(F32).astype(BF16)
     same = iota((stack, stack), 0) % GROUP == iota((stack, stack), 1) % GROUP
     mixers = []
@@ -561,7 +571,8 @@
     part_refs, out_ref = refs[:-1], refs[-1]
     rows = part_refs[0].shape[1]
     for part, ref in enumerate(part_refs):
-        lower = pl.multiple_of((index_ref[0] ^ part) * rows, rows)
+        partner = partner_bits(part, index_ref[1] == 1, len(part_refs)) ^ index_ref[0]
+        lower = pl.multiple_of(partner * rows, rows)
         out_ref[0, pl.ds(lower, rows), :] = ref[0]
 
 
@@ -580,10 +591,15 @@
 
 
 def exchanged(parts):
-    count = lax.axis_size("mem")
-    return [
-        lax.ppermute(v, "mem", [(i, i ^ part) for i in range(count)]) if part else v for part, v in enumerate(parts)
-    ]
+    mem_count, tok_count = lax.axis_size("mem"), lax.axis_size("tok")
+
+    def pairs(part):
+        for mem in range(mem_count):
+            for tok in range(tok_count):
+                target = mem ^ partner_bits(part, tok % 2 == 1, mem_count)
+                yield mem * tok_count + tok, target * tok_count + tok
+
+    return [lax.ppermute(v, ("mem", "tok"), list(pairs(part))) if part else v for part, v in enumerate(parts)]
 
 
 def local(
@@ -617,9 +633,8 @@
     grid = sample_grid(
         share_start.astype(jnp.int32).reshape(1), obs_token, obs_channel, obs_value, obs_var, share_rows, feat_width
     )
-    index = lax.axis_index("mem")
-    place = jnp.stack([first_pos, row_count * tok_count, index]).astype(jnp.int32)
-    index = index.astype(jnp.int32).reshape(1)
+    index = jnp.stack([lax.axis_index("mem"), lax.axis_index("tok") % 2]).astype(jnp.int32)
+    place = jnp.concatenate([jnp.stack([first_pos, row_count * tok_count]).astype(jnp.int32), index])
     gains = [attn_gain.reshape(1, -1), ffn_gain.reshape(1, -1)]
     inner_parts = inner(head_window, ens_state, gains[0], w_query, w_key, w_value, WIN)
     weights = [w_key, w_value, w_out, w_gate, w_up, down_weight]

time: 88.5 us -> 91 us (1.028)
  Pallas kernels: 35.7 us -> 37.4 us
where the time goes in v13:
time: 91 us; the launch traced here: 90.8 us
  Pallas kernels  37.4 us (41%)
  blocking collectives  21.8 us (24%)
  waiting for transfers between devices  18.2 us (20%)
  starting transfers between devices  10.8 us (12%)
  local copies, waits for them, and re-layouts  2.26 us (2%)
    pallas_call x1, Pallas kernels, forward(): pl.pallas_call(forward_kernel, grid=(members,), out_shape=[jax.ShapeDtype...  23.5 us
    all_to_all x1, blocking collectives, local(): lax.all_to_all(jnp.broadcast_to(partial[None], (device_count, *partial.sh...  21.8 us
    ppermute x6, waiting for transfers between devices, exchanged(): lax.ppermute(v, ('mem', 'tok'), list(pairs(part)))  17.8 us
    ppermute x6, starting transfers between devices, exchanged(): lax.ppermute(v, ('mem', 'tok'), list(pairs(part)))  7.16 us
    pallas_call x1, Pallas kernels, combine(): pl.pallas_call(combine_kernel, out_shape=[jax.ShapeDtypeStruct(v.shape, B...  4.18 us
    pallas_call x1, Pallas kernels, inner(): pl.pallas_call(inner_kernel, grid=(members,), out_shape=[jax.ShapeDtypeSt...  4.09 us
    ppermute x1, starting transfers between devices, local(): left = lax.ppermute(ens_state[:, row_count - WIN:], 'tok', up)  2.39 us
    pallas_call x1, Pallas kernels, gram_partial(): pl.pallas_call(gram_kernel, out_shape=jax.ShapeDtypeStruct((-(-filled //...  2.24 us
  transfers between devices with their start and end apart: 8, of which 5 were waited for; matrix products, arithmetic and copies ran while one was open for 0% of the time, Pallas kernels for 6%

profile of v13, /device:TPU:0, one launch (start us, length us, event | category | flops | bytes accessed | tf_op | source)
XLA Modules:
  0.0 90.8 jit_solution(18347644358090539818)
XLA Ops:
  0.0 2.2 %fusion = (bf16[4,256,256]{2,1,0:T(8,128)(2,1)S(1)}, bf16[4,256,256]{2,1,0:T(8,128)(2,1)}) fusion(bf16[4,512,256]{2,1,0:T(8,128)(2,1)} %state_ref.1), kind=kLoop, calls=%fused_computation.2 | loop fusion | bytes 2097152 | tf_op jit(solution)/shard_map/slice | solution.py:631
  2.2 2.4 %collective-permute-start = (bf16[4,256,256]{2,1,0:T(8,128)(2,1)}, bf16[4,256,256]{2,1,0:T(8,128)(2,1)S(1)}, u32[]{:S(2)}, u32[]{:S(2)}) collective-permute-start(bf16[4,256,256]{2,1,0:T(8,128)(2,1)} %get-tuple-element.30), channel_id=1, source_target_pairs={{0,1},{1,2},{2,3},{3,4},{4,5},{5,6},{6,7},{8,9},{9,10},{10,11},{11... | collective-permute-start | bytes 1572872 | tf_op jit(solution)/shard_map/ppermute | solution.py:630
  4.6 1.3 %collective-permute-start.1 = (bf16[4,256,256]{2,1,0:T(8,128)(2,1)S(1)}, bf16[4,256,256]{2,1,0:T(8,128)(2,1)S(1)}, u32[]{:S(2)}, u32[]{:S(2)}) collective-permute-start(bf16[4,256,256]{2,1,0:T(8,128)(2,1)S(1)} %get-tuple-element.29), channel_id=1, source_target_pairs={{1,0},{2,1},{3,2},{4,3},{5,4},{6,5},{7,6},{9,8},{10,9},{11,10},{12... | collective-permute-start | bytes 1572872 | tf_op jit(solution)/shard_map/ppermute | solution.py:631
  5.9 0.1 pad_add_fusion.1.place_ref
  6.0 0.0 copy-start.1
  6.0 0.0 copy-start.2
  6.1 0.0 copy-start.3
  6.1 0.0 copy-start.7
  6.1 0.0 copy-start.13
  6.1 4.1 %inner.1 = (bf16[4,512,256]{2,1,0:T(8,128)(2,1)S(1)}, f32[4,8,128]{2,1,0:T(8,128)S(1)}, f32[4,512,256]{2,1,0:T(8,128)S(1)}, f32[4,512,256]{2,1,0:T(8,128)S(1)}) custom-call(s32[4]{0:T(128)S(1)} %copy-done.14, bf16[4,512,256]{2,1,0:T(8,128)(2,1)S(1)} %copy-done, f32[1,256]{1,0:T(1,128)S(1)} %bitcast.14, bf16[256,256]{1,0:T(8,128)(2,1)S(1)} %copy-done.4, ...), custom_call_target="tpu_custom_call" | custom-call | flops 5100273664 | bytes 7340032 | tf_op jit(solution)/shard_map/inner/pallas_call | solution.py:240
  10.2 0.4 collective-permute-done.1.right_ref
  10.6 0.0 copy-start.8
  10.6 0.0 copy-start.9
  10.6 0.0 copy-start.10
  10.6 0.0 copy-start.11
  10.6 23.5 %forward.1 = (bf16[4,128,256]{2,1,0:T(8,128)(2,1)S(1)}, bf16[4,128,256]{2,1,0:T(8,128)(2,1)S(1)}, bf16[4,128,256]{2,1,0:T(8,128)(2,1)S(1)}, bf16[4,128,256]{2,1,0:T(8,128)(2,1)S(1)}) custom-call(s32[4]{0:T(128)S(1)} %pad_add_fusion.1.place_ref, s32[4]{0:T(128)S(1)} %copy-done.14, bf16[4,512,256]{2,1,0:T(8,128)(2,1)S(1)} %copy-done, ...), custom_call_target="tpu_custom_call" | custom-call | flops 5100273664 | bytes 5242880 | tf_op jit(solution)/shard_map/forward/pallas_call | solution.py:400
  34.1 2.1 %collective-permute-start.2 = (bf16[4,128,256]{2,1,0:T(8,128)(2,1)S(1)}, bf16[4,128,256]{2,1,0:T(8,128)(2,1)S(1)}, u32[]{:S(2)}, u32[]{:S(2)}) collective-permute-start(bf16[4,128,256]{2,1,0:T(8,128)(2,1)S(1)} %get-tuple-element.22), channel_id=1, source_target_pairs={{0,8},{1,17},{2,10},{3,19},{4,12},{5,21},{6,14},{7,23},{8,0},{9,25... | collective-permute-start | bytes 786440 | tf_op jit(solution)/shard_map/ppermute | solution.py:602
  36.2 1.5 %collective-permute-start.3 = (bf16[4,128,256]{2,1,0:T(8,128)(2,1)S(1)}, bf16[4,128,256]{2,1,0:T(8,128)(2,1)S(1)}, u32[]{:S(2)}, u32[]{:S(2)}) collective-permute-start(bf16[4,128,256]{2,1,0:T(8,128)(2,1)S(1)} %get-tuple-element.23), channel_id=1, source_target_pairs={{0,16},{1,9},{2,18},{3,11},{4,20},{5,13},{6,22},{7,15},{8,24},{9,1... | collective-permute-start | bytes 786440 | tf_op jit(solution)/shard_map/ppermute | solution.py:602
  37.7 0.0 collective-permute-start.4
  37.7 1.3 %sample_grid.1.refs_4_ = f32[2,128,256]{2,1,0:T(8,128)S(1)} custom-call(s32[1]{0:T(128)} %bitcast.5.start_ref, s32[1,4096]{1,0:T(1,128)S(1)} %bitcast.10, s32[1,4096]{1,0:T(1,128)S(1)} %bitcast.11, f32[1,4096]{1,0:T(1,128)S(1)} %bitcast.12, f32[1,4096]{1,0:T(1,128)S(1)} %bitcast.13), custom_call_target="tpu_custom_call" | custom-call | flops 1073741824 | bytes 65536 | tf_op jit(solution)/shard_map/sample_grid/pallas_call | solution.py:81
  39.1 0.1 pad_add_fusion.index_ref
  39.1 1.4 %collective-permute-done.2.refs_1_ = bf16[4,128,256]{2,1,0:T(8,128)(2,1)S(1)} collective-permute-done((bf16[4,128,256]{2,1,0:T(8,128)(2,1)S(1)}, bf16[4,128,256]{2,1,0:T(8,128)(2,1)S(1)}, u32[]{:S(2)}, u32[]{:S(2)}) %collective-permute-start.2) | collective-permute-done | bytes 262176 | tf_op jit(solution)/shard_map/ppermute | solution.py:602
  40.5 5.1 %collective-permute-done.3.refs_2_ = bf16[4,128,256]{2,1,0:T(8,128)(2,1)S(1)} collective-permute-done((bf16[4,128,256]{2,1,0:T(8,128)(2,1)S(1)}, bf16[4,128,256]{2,1,0:T(8,128)(2,1)S(1)}, u32[]{:S(2)}, u32[]{:S(2)}) %collective-permute-start.3) | collective-permute-done | bytes 262176 | tf_op jit(solution)/shard_map/ppermute | solution.py:602
  45.6 2.2 %gram.1 = f32[8,128]{1,0:T(8,128)S(1)} custom-call(s32[2]{0:T(128)S(1)} %pad_add_fusion.index_ref, bf16[4,128,256]{2,1,0:T(8,128)(2,1)S(1)} %get-tuple-element.21.refs_0_, bf16[4,128,256]{2,1,0:T(8,128)(2,1)S(1)} %collective-permute-done.2.refs_1_, bf16[4,128,256]{2,1,0:T(8,128)(2,1)S(1)} %collective-permute-done.3.refs_2_, ...), custom_call_target="tpu_custom_call" | custom-call | flops 805306368 | bytes 1048576 | tf_op jit(solution)/shard_map/gram/pallas_call | solution.py:476
  47.9 21.8 %all_to_all.5.partial_ref = f32[32,8,128]{2,1,0:T(8,128)S(1)} all-to-all(f32[32,8,128]{2,1,0:T(8,128)S(1)} %broadcast_in_dim.2), channel_id=1, replica_groups=mesh['mem'=4,'tok'=8] {'mem','tok'}, dimensions={0} | all-to-all | bytes 262144 | tf_op jit(solution)/shard_map/all_to_all | solution.py:644
  69.7 4.2 %combine.1 = (bf16[4,128,256]{2,1,0:T(8,128)(2,1)S(1)}, bf16[4,128,256]{2,1,0:T(8,128)(2,1)S(1)}, bf16[4,128,256]{2,1,0:T(8,128)(2,1)S(1)}, bf16[4,128,256]{2,1,0:T(8,128)(2,1)S(1)}) custom-call(s32[2]{0:T(128)S(1)} %pad_add_fusion.index_ref, f32[32,8,128]{2,1,0:T(8,128)S(1)} %all_to_all.5.partial_ref, bf16[4,128,256]{2,1,0:T(8,128)(2,1)S(1)} %get-tuple-element.21.refs_0_, ...), custom_call_target="tpu_custom_call" | custom-call | flops 536870912 | bytes 2097152 | tf_op jit(solution)/shard_map/combine/pallas_call | solution.py:559
  73.9 0.9 collective-permute-start.5
  74.8 0.7 collective-permute-start.6
  75.5 2.0 %collective-permute-start.7 = (bf16[4,128,256]{2,1,0:T(8,128)(2,1)S(1)}, bf16[4,128,256]{2,1,0:T(8,128)(2,1)S(1)}, u32[]{:S(2)}, u32[]{:S(2)}) collective-permute-start(bf16[4,128,256]{2,1,0:T(8,128)(2,1)S(1)} %get-tuple-element.28), channel_id=1, source_target_pairs={{0,24},{1,25},{2,26},{3,27},{4,28},{5,29},{6,30},{7,31},{8,16},{9,... | collective-permute-start | bytes 786440 | tf_op jit(solution)/shard_map/ppermute | solution.py:602
  77.4 5.6 %collective-permute-done.5.refs_1_ = bf16[4,128,256]{2,1,0:T(8,128)(2,1)S(1)} collective-permute-done((bf16[4,128,256]{2,1,0:T(8,128)(2,1)S(1)}, bf16[4,128,256]{2,1,0:T(8,128)(2,1)S(1)}, u32[]{:S(2)}, u32[]{:S(2)}) %collective-permute-start.5) | collective-permute-done | bytes 262176 | tf_op jit(solution)/shard_map/ppermute | solution.py:602
  83.0 5.7 %collective-permute-done.7.refs_3_ = bf16[4,128,256]{2,1,0:T(8,128)(2,1)S(1)} collective-permute-done((bf16[4,128,256]{2,1,0:T(8,128)(2,1)S(1)}, bf16[4,128,256]{2,1,0:T(8,128)(2,1)S(1)}, u32[]{:S(2)}, u32[]{:S(2)}) %collective-permute-start.7) | collective-permute-done | bytes 262176 | tf_op jit(solution)/shard_map/ppermute | solution.py:602
  88.7 2.1 %assemble.1 = bf16[4,512,256]{2,1,0:T(8,128)(2,1)} custom-call(s32[2]{0:T(128)S(1)} %pad_add_fusion.index_ref, bf16[4,128,256]{2,1,0:T(8,128)(2,1)S(1)} %get-tuple-element.25.refs_0_, bf16[4,128,256]{2,1,0:T(8,128)(2,1)S(1)} %collective-permute-done.5.refs_1_, bf16[4,128,256]{2,1,0:T(8,128)(2,1)S(1)} %collective-permute-done.6.refs_2_, ...), custom_call_target="tpu_custom_call" | custom-call | bytes 2097152 | tf_op jit(solution)/shard_map/assemble/pallas_call | solution.py:581
  (25 shorter events, 0.1 us)
Async XLA Ops:
  0.0 6.0 %copy-start = (bf16[4,512,256]{2,1,0:T(8,128)(2,1)S(1)}, bf16[4,512,256]{2,1,0:T(8,128)(2,1)}, u32[]{:S(2)}) copy-start(bf16[4,512,256]{2,1,0:T(8,128)(2,1)} %state_ref.1) | copy-start | bytes 3145732
  0.0 6.0 %copy-start.12 = (f32[256]{0:T(256)S(1)}, f32[256]{0:T(256)}, u32[]{:S(2)}) copy-start(f32[256]{0:T(256)} %param.16) | copy-start | bytes 3076
  0.0 6.0 %copy-start.4 = (bf16[256,256]{1,0:T(8,128)(2,1)S(1)}, bf16[256,256]{1,0:T(8,128)(2,1)}, u32[]{:S(2)}) copy-start(bf16[256,256]{1,0:T(8,128)(2,1)} %w_query_ref.1) | copy-start | bytes 393220
  0.0 6.0 %copy-start.5 = (bf16[256,256]{1,0:T(8,128)(2,1)S(1)}, bf16[256,256]{1,0:T(8,128)(2,1)}, u32[]{:S(2)}) copy-start(bf16[256,256]{1,0:T(8,128)(2,1)} %w_key_ref.3) | copy-start | bytes 393220
  0.0 6.0 %copy-start.6 = (bf16[256,256]{1,0:T(8,128)(2,1)S(1)}, bf16[256,256]{1,0:T(8,128)(2,1)}, u32[]{:S(2)}) copy-start(bf16[256,256]{1,0:T(8,128)(2,1)} %w_value_ref.3) | copy-start | bytes 393220
  0.0 6.0 %copy-start.14 = (s32[4]{0:T(128)S(1)}, s32[4]{0:T(128)}, u32[]{:S(2)}) copy-start(s32[4]{0:T(128)} %window_ref.3) | copy-start | bytes 52
  2.2 8.0 %collective-permute-start = (bf16[4,256,256]{2,1,0:T(8,128)(2,1)}, bf16[4,256,256]{2,1,0:T(8,128)(2,1)S(1)}, u32[]{:S(2)}, u32[]{:S(2)}) collective-permute-start(bf16[4,256,256]{2,1,0:T(8,128)(2,1)} %get-tuple-element.30), channel_id=1, source_target_pairs={{0,1},{1,2},{2,3},{3,4},{4,5},{5,6},{6,7},{8,9},{9,10},{10,11},{11... | collective-permute-start | bytes 1572872 | tf_op jit(solution)/shard_map/ppermute | solution.py:630
  4.6 6.0 %collective-permute-start.1 = (bf16[4,256,256]{2,1,0:T(8,128)(2,1)S(1)}, bf16[4,256,256]{2,1,0:T(8,128)(2,1)S(1)}, u32[]{:S(2)}, u32[]{:S(2)}) collective-permute-start(bf16[4,256,256]{2,1,0:T(8,128)(2,1)S(1)} %get-tuple-element.29), channel_id=1, source_target_pairs={{1,0},{2,1},{3,2},{4,3},{5,4},{6,5},{7,6},{9,8},{10,9},{11,10},{12... | collective-permute-start | bytes 1572872 | tf_op jit(solution)/shard_map/ppermute | solution.py:631
  6.0 4.5 %copy-start.1 = (bf16[256,1024]{1,0:T(8,128)(2,1)S(1)}, bf16[256,1024]{1,0:T(8,128)(2,1)}, u32[]{:S(2)}) copy-start(bf16[256,1024]{1,0:T(8,128)(2,1)} %w_gate_ref.1) | copy-start | bytes 1572868
  6.0 4.5 %copy-start.2 = (bf16[256,1024]{1,0:T(8,128)(2,1)S(1)}, bf16[256,1024]{1,0:T(8,128)(2,1)}, u32[]{:S(2)}) copy-start(bf16[256,1024]{1,0:T(8,128)(2,1)} %w_up_ref.1) | copy-start | bytes 1572868
  6.1 4.5 %copy-start.3 = (bf16[1024,256]{1,0:T(8,128)(2,1)S(1)}, bf16[1024,256]{1,0:T(8,128)(2,1)}, u32[]{:S(2)}) copy-start(bf16[1024,256]{1,0:T(8,128)(2,1)} %down_weight_ref.1) | copy-start | bytes 1572868
  6.1 4.5 %copy-start.7 = (bf16[256,256]{1,0:T(8,128)(2,1)S(1)}, bf16[256,256]{1,0:T(8,128)(2,1)}, u32[]{:S(2)}) copy-start(bf16[256,256]{1,0:T(8,128)(2,1)} %w_out_ref.1) | copy-start | bytes 393220
  6.1 4.5 %copy-start.13 = (f32[256]{0:T(256)S(1)}, f32[256]{0:T(256)}, u32[]{:S(2)}) copy-start(f32[256]{0:T(256)} %param.17) | copy-start | bytes 3076
  10.6 27.1 %copy-start.8 = (s32[4096]{0:T(1024)S(1)}, s32[4096]{0:T(1024)}, u32[]{:S(2)}) copy-start(s32[4096]{0:T(1024)} %param.26) | copy-start | bytes 49156
  10.6 27.1 %copy-start.9 = (s32[4096]{0:T(1024)S(1)}, s32[4096]{0:T(1024)}, u32[]{:S(2)}) copy-start(s32[4096]{0:T(1024)} %param.27) | copy-start | bytes 49156
  10.6 27.1 %copy-start.10 = (f32[4096]{0:T(1024)S(1)}, f32[4096]{0:T(1024)}, u32[]{:S(2)}) copy-start(f32[4096]{0:T(1024)} %param.28) | copy-start | bytes 49156
  10.6 27.1 %copy-start.11 = (f32[4096]{0:T(1024)S(1)}, f32[4096]{0:T(1024)}, u32[]{:S(2)}) copy-start(f32[4096]{0:T(1024)} %param.29) | copy-start | bytes 49156
  34.1 6.4 %collective-permute-start.2 = (bf16[4,128,256]{2,1,0:T(8,128)(2,1)S(1)}, bf16[4,128,256]{2,1,0:T(8,128)(2,1)S(1)}, u32[]{:S(2)}, u32[]{:S(2)}) collective-permute-start(bf16[4,128,256]{2,1,0:T(8,128)(2,1)S(1)} %get-tuple-element.22), channel_id=1, source_target_pairs={{0,8},{1,17},{2,10},{3,19},{4,12},{5,21},{6,14},{7,23},{8,0},{9,25... | collective-permute-start | bytes 786440 | tf_op jit(solution)/shard_map/ppermute | solution.py:602
  36.2 9.5 %collective-permute-start.3 = (bf16[4,128,256]{2,1,0:T(8,128)(2,1)S(1)}, bf16[4,128,256]{2,1,0:T(8,128)(2,1)S(1)}, u32[]{:S(2)}, u32[]{:S(2)}) collective-permute-start(bf16[4,128,256]{2,1,0:T(8,128)(2,1)S(1)} %get-tuple-element.23), channel_id=1, source_target_pairs={{0,16},{1,9},{2,18},{3,11},{4,20},{5,13},{6,22},{7,15},{8,24},{9,1... | collective-permute-start | bytes 786440 | tf_op jit(solution)/shard_map/ppermute | solution.py:602
  37.7 7.9 %collective-permute-start.4 = (bf16[4,128,256]{2,1,0:T(8,128)(2,1)S(1)}, bf16[4,128,256]{2,1,0:T(8,128)(2,1)S(1)}, u32[]{:S(2)}, u32[]{:S(2)}) collective-permute-start(bf16[4,128,256]{2,1,0:T(8,128)(2,1)S(1)} %get-tuple-element.24), channel_id=1, source_target_pairs={{0,24},{1,25},{2,26},{3,27},{4,28},{5,29},{6,30},{7,31},{8,16},{9,... | collective-permute-start | bytes 786440 | tf_op jit(solution)/shard_map/ppermute | solution.py:602
  73.9 9.2 %collective-permute-start.5 = (bf16[4,128,256]{2,1,0:T(8,128)(2,1)S(1)}, bf16[4,128,256]{2,1,0:T(8,128)(2,1)S(1)}, u32[]{:S(2)}, u32[]{:S(2)}) collective-permute-start(bf16[4,128,256]{2,1,0:T(8,128)(2,1)S(1)} %get-tuple-element.26), channel_id=1, source_target_pairs={{0,8},{1,17},{2,10},{3,19},{4,12},{5,21},{6,14},{7,23},{8,0},{9,25... | collective-permute-start | bytes 786440 | tf_op jit(solution)/shard_map/ppermute | solution.py:602
  74.8 8.3 %collective-permute-start.6 = (bf16[4,128,256]{2,1,0:T(8,128)(2,1)S(1)}, bf16[4,128,256]{2,1,0:T(8,128)(2,1)S(1)}, u32[]{:S(2)}, u32[]{:S(2)}) collective-permute-start(bf16[4,128,256]{2,1,0:T(8,128)(2,1)S(1)} %get-tuple-element.27), channel_id=1, source_target_pairs={{0,16},{1,9},{2,18},{3,11},{4,20},{5,13},{6,22},{7,15},{8,24},{9,1... | collective-permute-start | bytes 786440 | tf_op jit(solution)/shard_map/ppermute | solution.py:602
  75.5 13.3 %collective-permute-start.7 = (bf16[4,128,256]{2,1,0:T(8,128)(2,1)S(1)}, bf16[4,128,256]{2,1,0:T(8,128)(2,1)S(1)}, u32[]{:S(2)}, u32[]{:S(2)}) collective-permute-start(bf16[4,128,256]{2,1,0:T(8,128)(2,1)S(1)} %get-tuple-element.28), channel_id=1, source_target_pairs={{0,24},{1,25},{2,26},{3,27},{4,28},{5,29},{6,30},{7,31},{8,16},{9,... | collective-permute-start | bytes 786440 | tf_op jit(solution)/shard_map/ppermute | solution.py:602

commit v14 on v12

--- a/solution.py
+++ b/solution.py
@@ -203,28 +203,27 @@
 
     @pl.when(is_safe(query_norms, key_norms))
     def _():
-        units = [(first, group) for first in range(0, blocks, 2) for group in range(heads // group_heads)]
-
-        def scores_of(first, group):
-            queries = query_ref[0, first * Q_ROWS : (first + 2) * Q_ROWS, group_lanes(group)]
+        groups = heads // group_heads
+        ranges = [(max(0, b - reach_blocks), min(blocks, b + reach_blocks + 1)) for b in range(blocks)]
+        spans = [(lower * Q_ROWS, upper * Q_ROWS) for lower, upper in ranges]
+
+        def scores_of(group):
+            queries = query_ref[0, :, group_lanes(group)]
             return dot(stacked_heads(queries, head_size), key_buf[group_lanes(group), :])
 
-        scores = scores_of(*units[0])
-        for at, (first, group) in enumerate(units):
-            following = scores_of(*units[at + 1]) if at + 1 < len(units) else None
-            ranges = [(max(0, b - reach_blocks), min(blocks, b + reach_blocks + 1)) for b in (first, first + 1)]
-            spans = [(lower * Q_ROWS, upper * Q_ROWS) for lower, upper in ranges]
+        scores = scores_of(0)
+        for group in range(groups):
+            following = scores_of(group + 1) if group + 1 < groups else None
 
             def bias_of(head, block):
-                shift = (reach_blocks - first - block) * Q_ROWS
+                shift = (reach_blocks - block) * Q_ROWS
                 lower, upper = spans[block]
                 return bias_buf[group * group_heads + head, :, lower + shift : upper + shift]
 
             values = value_buf[:, 2 * group * LANES : 2 * (group + 1) * LANES]
             mixed, totals = weighted_sums(unit_weights(scores, spans, bias_of), values, head_size)
-            here = slice(first * Q_ROWS, (first + 2) * Q_ROWS)
-            mixed_ref[0, here, group_lanes(group)] = mixed
-            total_ref[0, here, group_lanes(group)] = totals
+            mixed_ref[0, :, group_lanes(group)] = mixed
+            total_ref[0, :, group_lanes(group)] = totals
             scores = following
 
 
@@ -257,7 +256,9 @@
 
 
 def forward_kernel(
-    place_ref,
+    total_len,
+    tok_ref,
+    mem_ref,
     window_ref,
     state_ref,
     query_ref,
@@ -289,11 +290,12 @@
     blocks = rows // Q_ROWS
     key_count = Q_ROWS + 2 * reach
     count = 2 * Q_ROWS
+    first_pos = tok_ref[0] * rows
 
     @pl.when(pl.program_id(0) == 0)
     def _():
-        first_valid = place_ref[0] - reach >= 0
-        last_valid = place_ref[0] + rows + reach <= place_ref[1]
+        first_valid = first_pos - reach >= 0
+        last_valid = first_pos + rows + reach <= total_len
         for head in range(heads):
             left_bias = band_bias(window_ref[head], 0, reach, reach)
             right_bias = band_bias(window_ref[head], key_count - reach, key_count, reach)
@@ -355,8 +357,8 @@
         value_buf[reach + rows :] = halo_value_buf[1]
         for block in range(blocks):
             start = block * Q_ROWS
-            k_pos = place_ref[0] - reach + start + iota((Q_ROWS, key_count), 1)
-            inside = (k_pos >= 0) & (k_pos < place_ref[1])
+            k_pos = first_pos - reach + start + iota((Q_ROWS, key_count), 1)
+            inside = (k_pos >= 0) & (k_pos < total_len)
             for group in range(groups):
                 queries = query_ref[0, start : start + Q_ROWS, group_lanes(group)]
                 keys = key_buf[group_lanes(group), start : start + key_count]
@@ -373,20 +375,20 @@
 
     after = (state_ref[0].astype(F32) + dot(mixed_buf[...], w_out_ref[...])).astype(BF16)
     normed_mid = rms_scaled(after.astype(F32), ffn_gain_ref[...]).astype(BF16)
-    forecast = after.astype(F32)
+    hidden = []
     for lower in range(0, w_gate_ref.shape[1], HIDDEN_CHUNK):
         part = slice(lower, lower + HIDDEN_CHUNK)
         gate = 0.5 * dot(normed_mid, w_gate_ref[:, part])
-        hidden = (gate * (1.0 + jnp.tanh(gate)) * dot(normed_mid, w_up_ref[:, part])).astype(BF16)
-        forecast += dot(hidden, down_weight_ref[part, :])
+        hidden.append((gate * (1.0 + jnp.tanh(gate)) * dot(normed_mid, w_up_ref[:, part])).astype(BF16))
+    forecast = after.astype(F32) + dot(jnp.concatenate(hidden, axis=1), down_weight_ref[...])
     forecast_buf[...] = forecast.astype(BF16)
     share_rows = out_refs[0].shape[1]
     for part, out_ref in enumerate(out_refs):
-        lower = pl.multiple_of((place_ref[2] ^ part) * share_rows, share_rows)
+        lower = pl.multiple_of((mem_ref[0] ^ part) * share_rows, share_rows)
         out_ref[0] = forecast_buf[pl.ds(lower, share_rows), :]
 
 
-def forward(place, head_window, own, inner_parts, left, right, gains, weights, shares):
+def forward(total_len, tok_index, mem_index, head_window, own, inner_parts, left, right, gains, weights, shares):
     members, row_count, feat_width = own.shape
     reach = left.shape[1]
     heads = head_window.shape[0]
@@ -397,10 +399,10 @@
         return pl.BlockSpec((1, *array.shape[1:]), lambda m: (m, 0, 0))
 
     return pl.pallas_call(
-        forward_kernel,
+        functools.partial(forward_kernel, total_len),
         grid=(members,),
         out_shape=[jax.ShapeDtypeStruct((members, row_count // shares, feat_width), BF16)] * shares,
-        in_specs=[smem_spec()] * 2
+        in_specs=[smem_spec()] * 3
         + [spec(v) for v in (own, *inner_parts, left, right)]
         + [vmem_spec()] * (len(gains) + len(weights)),
         out_specs=[pl.BlockSpec((1, row_count // shares, feat_width), lambda m: (m, 0, 0))] * shares,
@@ -416,7 +418,7 @@
         compiler_params=pltpu.CompilerParams(vmem_limit_bytes=VMEM_LIMIT),
         cost_estimate=pl.CostEstimate(flops=2 * macs, bytes_accessed=10 * own.size, transcendentals=0),
         name="forward",
-    )(place, head_window, own, *inner_parts, left, right, *gains, *weights)
+    )(tok_index, mem_index, head_window, own, *inner_parts, left, right, *gains, *weights)
 
 
 def global_member(held, index, own_members):
@@ -558,21 +560,26 @@
 
 
 def assemble_kernel(index_ref, *refs):
-    part_refs, out_ref = refs[:-1], refs[-1]
+    part_refs, out_ref, sems = refs[:-2], refs[-2], refs[-1]
     rows = part_refs[0].shape[1]
+    copies = []
     for part, ref in enumerate(part_refs):
         lower = pl.multiple_of((index_ref[0] ^ part) * rows, rows)
-        out_ref[0, pl.ds(lower, rows), :] = ref[0]
+        copies.append(pltpu.make_async_copy(ref, out_ref.at[:, pl.ds(lower, rows), :], sems.at[part]))
+    for copy in copies:
+        copy.start()
+    for copy in copies:
+        copy.wait()
 
 
 def assemble(index, parts):
     members, rows, feat_width = parts[0].shape
     return pl.pallas_call(
         assemble_kernel,
-        grid=(members,),
         out_shape=jax.ShapeDtypeStruct((members, len(parts) * rows, feat_width), BF16),
-        in_specs=[smem_spec()] + [pl.BlockSpec((1, rows, feat_width), lambda m: (m, 0, 0))] * len(parts),
-        out_specs=pl.BlockSpec((1, len(parts) * rows, feat_width), lambda m: (m, 0, 0)),
+        in_specs=[smem_spec()] + [vmem_spec()] * len(parts),
+        out_specs=pl.BlockSpec(memory_space=pl.ANY),
+        scratch_shapes=[pltpu.SemaphoreType.DMA((len(parts),))],
         compiler_params=pltpu.CompilerParams(vmem_limit_bytes=VMEM_LIMIT),
         cost_estimate=pl.CostEstimate(flops=0, bytes_accessed=4 * len(parts) * parts[0].size, transcendentals=0),
         name="assemble",
@@ -617,15 +624,17 @@
     grid = sample_grid(
         share_start.astype(jnp.int32).reshape(1), obs_token, obs_channel, obs_value, obs_var, share_rows, feat_width
     )
-    index = lax.axis_index("mem")
-    place = jnp.stack([first_pos, row_count * tok_count, index]).astype(jnp.int32)
-    index = index.astype(jnp.int32).reshape(1)
+    mem_index = lax.axis_index("mem").astype(jnp.int32).reshape(1)
+    tok_index = lax.axis_index("tok").astype(jnp.int32).reshape(1)
     gains = [attn_gain.reshape(1, -1), ffn_gain.reshape(1, -1)]
     inner_parts = inner(head_window, ens_state, gains[0], w_query, w_key, w_value, WIN)
     weights = [w_key, w_value, w_out, w_gate, w_up, down_weight]
-    forecast = forward(place, head_window, ens_state, inner_parts, left, right, gains, weights, mem_count)
+    total_len = row_count * tok_count
+    forecast = forward(
+        total_len, tok_index, mem_index, head_window, ens_state, inner_parts, left, right, gains, weights, mem_count
+    )
     shares = exchanged(forecast)
-    partial = gram_partial(index, shares, grid)
+    partial = gram_partial(mem_index, shares, grid)
     partials = lax.all_to_all(
         jnp.broadcast_to(partial[None], (device_count, *partial.shape)),
         ("mem", "tok"),
@@ -633,7 +642,7 @@
         concat_axis=0,
         tiled=True,
     )
-    return assemble(index, exchanged(combine(index, partials, shares)))
+    return assemble(mem_index, exchanged(combine(mem_index, partials, shares)))
 
 
 def solution(mesh):

time: 88.5 us -> 88.1 us (level)
  no operation moved by 1% of the time
where the time goes in v14:
time: 88.1 us; the launch traced here: 87.9 us
  Pallas kernels  35.3 us (40%)
  blocking collectives  21.8 us (25%)
  waiting for transfers between devices  17.5 us (20%)
  starting transfers between devices  10.8 us (12%)
  local copies, waits for them, and re-layouts  2.26 us (3%)
    pallas_call x1, Pallas kernels, forward(): pl.pallas_call(functools.partial(forward_kernel, total_len), grid=(member...  23.6 us
    all_to_all x1, blocking collectives, local(): lax.all_to_all(jnp.broadcast_to(partial[None], (device_count, *partial.sh...  21.8 us
    ppermute x6, waiting for transfers between devices, exchanged(): lax.ppermute(v, 'mem', [(i, i ^ part) for i in range(count)])  17.1 us
    ppermute x6, starting transfers between devices, exchanged(): lax.ppermute(v, 'mem', [(i, i ^ part) for i in range(count)])  7.11 us
    pallas_call x1, Pallas kernels, inner(): pl.pallas_call(inner_kernel, grid=(members,), out_shape=[jax.ShapeDtypeSt...  4.09 us
    pallas_call x1, Pallas kernels, combine(): pl.pallas_call(combine_kernel, out_shape=[jax.ShapeDtypeStruct(v.shape, B...  3.64 us
    ppermute x1, starting transfers between devices, local(): left = lax.ppermute(ens_state[:, row_count - WIN:], 'tok', up)  2.39 us
    slice x1, local copies, waits for them, and re-layouts, local(): right = lax.ppermute(ens_state[:, :WIN], 'tok', down)  2.17 us
  transfers between devices with their start and end apart: 8, of which 5 were waited for; matrix products, arithmetic and copies ran while one was open for 0% of the time, Pallas kernels for 6%

profile of v14, /device:TPU:0, one launch (start us, length us, event | category | flops | bytes accessed | tf_op | source)
XLA Modules:
  0.0 87.9 jit_solution(10952003839176441448)
XLA Ops:
  0.0 2.2 %fusion = (bf16[4,256,256]{2,1,0:T(8,128)(2,1)S(1)}, bf16[4,256,256]{2,1,0:T(8,128)(2,1)}) fusion(bf16[4,512,256]{2,1,0:T(8,128)(2,1)} %state_ref.1), kind=kLoop, calls=%fused_computation | loop fusion | bytes 2097152 | tf_op jit(solution)/shard_map/slice | solution.py:622
  2.2 2.4 %collective-permute-start = (bf16[4,256,256]{2,1,0:T(8,128)(2,1)}, bf16[4,256,256]{2,1,0:T(8,128)(2,1)S(1)}, u32[]{:S(2)}, u32[]{:S(2)}) collective-permute-start(bf16[4,256,256]{2,1,0:T(8,128)(2,1)} %get-tuple-element.30), channel_id=1, source_target_pairs={{0,1},{1,2},{2,3},{3,4},{4,5},{5,6},{6,7},{8,9},{9,10},{10,11},{11... | collective-permute-start | bytes 1572872 | tf_op jit(solution)/shard_map/ppermute | solution.py:621
  4.6 1.3 %collective-permute-start.1 = (bf16[4,256,256]{2,1,0:T(8,128)(2,1)S(1)}, bf16[4,256,256]{2,1,0:T(8,128)(2,1)S(1)}, u32[]{:S(2)}, u32[]{:S(2)}) collective-permute-start(bf16[4,256,256]{2,1,0:T(8,128)(2,1)S(1)} %get-tuple-element.29), channel_id=1, source_target_pairs={{1,0},{2,1},{3,2},{4,3},{5,4},{6,5},{7,6},{9,8},{10,9},{11,10},{12... | collective-permute-start | bytes 1572872 | tf_op jit(solution)/shard_map/ppermute | solution.py:622
  6.0 0.0 copy-start.1
  6.0 0.0 copy-start.2
  6.0 0.0 copy-start.3
  6.0 0.0 copy-start.7
  6.0 0.0 copy-start.13
  6.0 4.1 %inner.1 = (bf16[4,512,256]{2,1,0:T(8,128)(2,1)S(1)}, f32[4,8,128]{2,1,0:T(8,128)S(1)}, f32[4,512,256]{2,1,0:T(8,128)S(1)}, f32[4,512,256]{2,1,0:T(8,128)S(1)}) custom-call(s32[4]{0:T(128)S(1)} %copy-done.14, bf16[4,512,256]{2,1,0:T(8,128)(2,1)S(1)} %copy-done, f32[1,256]{1,0:T(1,128)S(1)} %bitcast.13, bf16[256,256]{1,0:T(8,128)(2,1)S(1)} %copy-done.4, ...), custom_call_target="tpu_custom_call" | custom-call | flops 5100273664 | bytes 7340032 | tf_op jit(solution)/shard_map/inner/pallas_call | solution.py:239
  10.1 0.0 collective-permute-done.left_ref
  10.1 0.4 collective-permute-done.1.right_ref
  10.6 0.0 copy-start.8
  10.6 0.0 copy-start.9
  10.6 0.0 copy-start.10
  10.6 0.0 copy-start.11
  10.6 23.6 %forward.1 = (bf16[4,128,256]{2,1,0:T(8,128)(2,1)S(1)}, bf16[4,128,256]{2,1,0:T(8,128)(2,1)S(1)}, bf16[4,128,256]{2,1,0:T(8,128)(2,1)S(1)}, bf16[4,128,256]{2,1,0:T(8,128)(2,1)S(1)}) custom-call(s32[1]{0:T(128)} %bitcast.1.tok_ref, s32[1]{0:T(128)} %bitcast.mem_ref.index_ref, s32[4]{0:T(128)S(1)} %copy-done.14, bf16[4,512,256]{2,1,0:T(8,128)(2,1)S(1)} %copy-done, ...), custom_call_target="tpu_custom_call" | custom-call | flops 5100273664 | bytes 5242880 | tf_op jit(solution)/shard_map/forward/pallas_call | solution.py:401
  34.2 2.0 %collective-permute-start.2 = (bf16[4,128,256]{2,1,0:T(8,128)(2,1)S(1)}, bf16[4,128,256]{2,1,0:T(8,128)(2,1)S(1)}, u32[]{:S(2)}, u32[]{:S(2)}) collective-permute-start(bf16[4,128,256]{2,1,0:T(8,128)(2,1)S(1)} %get-tuple-element.22), channel_id=1, source_target_pairs={{0,8},{8,0},{16,24},{24,16},{1,9},{9,1},{17,25},{25,17},{2,10},{10... | collective-permute-start | bytes 786440 | tf_op jit(solution)/shard_map/ppermute | solution.py:592
  36.2 1.5 %collective-permute-start.3 = (bf16[4,128,256]{2,1,0:T(8,128)(2,1)S(1)}, bf16[4,128,256]{2,1,0:T(8,128)(2,1)S(1)}, u32[]{:S(2)}, u32[]{:S(2)}) collective-permute-start(bf16[4,128,256]{2,1,0:T(8,128)(2,1)S(1)} %get-tuple-element.23), channel_id=1, source_target_pairs={{0,16},{8,24},{16,0},{24,8},{1,17},{9,25},{17,1},{25,9},{2,18},{10... | collective-permute-start | bytes 786440 | tf_op jit(solution)/shard_map/ppermute | solution.py:592
  37.7 0.0 collective-permute-start.4
  37.8 1.3 %sample_grid.1.refs_4_ = f32[2,128,256]{2,1,0:T(8,128)S(1)} custom-call(s32[1]{0:T(128)} %bitcast.4.start_ref, s32[1,4096]{1,0:T(1,128)S(1)} %bitcast.9, s32[1,4096]{1,0:T(1,128)S(1)} %bitcast.10, f32[1,4096]{1,0:T(1,128)S(1)} %bitcast.11, f32[1,4096]{1,0:T(1,128)S(1)} %bitcast.12), custom_call_target="tpu_custom_call" | custom-call | flops 1073741824 | bytes 65536 | tf_op jit(solution)/shard_map/sample_grid/pallas_call | solution.py:81
  39.1 1.5 %collective-permute-done.2.refs_1_ = bf16[4,128,256]{2,1,0:T(8,128)(2,1)S(1)} collective-permute-done((bf16[4,128,256]{2,1,0:T(8,128)(2,1)S(1)}, bf16[4,128,256]{2,1,0:T(8,128)(2,1)S(1)}, u32[]{:S(2)}, u32[]{:S(2)}) %collective-permute-start.2) | collective-permute-done | bytes 262176 | tf_op jit(solution)/shard_map/ppermute | solution.py:592
  40.6 4.8 %collective-permute-done.3.refs_2_ = bf16[4,128,256]{2,1,0:T(8,128)(2,1)S(1)} collective-permute-done((bf16[4,128,256]{2,1,0:T(8,128)(2,1)S(1)}, bf16[4,128,256]{2,1,0:T(8,128)(2,1)S(1)}, u32[]{:S(2)}, u32[]{:S(2)}) %collective-permute-start.3) | collective-permute-done | bytes 262176 | tf_op jit(solution)/shard_map/ppermute | solution.py:592
  45.4 0.0 collective-permute-done.4.refs_3_
  45.4 1.7 %gram.1 = f32[8,128]{1,0:T(8,128)S(1)} custom-call(s32[1]{0:T(128)} %bitcast.mem_ref.index_ref, bf16[4,128,256]{2,1,0:T(8,128)(2,1)S(1)} %get-tuple-element.21.refs_0_, bf16[4,128,256]{2,1,0:T(8,128)(2,1)S(1)} %collective-permute-done.2.refs_1_, bf16[4,128,256]{2,1,0:T(8,128)(2,1)S(1)} %collective-permute-done.3.refs_2_, ...), custom_call_target="tpu_custom_call" | custom-call | flops 805306368 | bytes 1048576 | tf_op jit(solution)/shard_map/gram/pallas_call | solution.py:468
  47.1 21.8 %all_to_all.5.partial_ref = f32[32,8,128]{2,1,0:T(8,128)S(1)} all-to-all(f32[32,8,128]{2,1,0:T(8,128)S(1)} %broadcast_in_dim.2), channel_id=1, replica_groups=mesh['mem'=4,'tok'=8] {'mem','tok'}, dimensions={0} | all-to-all | bytes 262144 | tf_op jit(solution)/shard_map/all_to_all | solution.py:638
  68.9 3.6 %combine.1 = (bf16[4,128,256]{2,1,0:T(8,128)(2,1)S(1)}, bf16[4,128,256]{2,1,0:T(8,128)(2,1)S(1)}, bf16[4,128,256]{2,1,0:T(8,128)(2,1)S(1)}, bf16[4,128,256]{2,1,0:T(8,128)(2,1)S(1)}) custom-call(s32[1]{0:T(128)} %bitcast.mem_ref.index_ref, f32[32,8,128]{2,1,0:T(8,128)S(1)} %all_to_all.5.partial_ref, bf16[4,128,256]{2,1,0:T(8,128)(2,1)S(1)} %get-tuple-element.21.refs_0_, ...), custom_call_target="tpu_custom_call" | custom-call | flops 536870912 | bytes 2097152 | tf_op jit(solution)/shard_map/combine/pallas_call | solution.py:551
  72.6 0.9 %collective-permute-start.5 = (bf16[4,128,256]{2,1,0:T(8,128)(2,1)S(1)}, bf16[4,128,256]{2,1,0:T(8,128)(2,1)S(1)}, u32[]{:S(2)}, u32[]{:S(2)}) collective-permute-start(bf16[4,128,256]{2,1,0:T(8,128)(2,1)S(1)} %get-tuple-element.26), channel_id=1, source_target_pairs={{0,8},{8,0},{16,24},{24,16},{1,9},{9,1},{17,25},{25,17},{2,10},{10... | collective-permute-start | bytes 786440 | tf_op jit(solution)/shard_map/ppermute | solution.py:592
  73.5 0.7 collective-permute-start.6
  74.2 2.0 %collective-permute-start.7 = (bf16[4,128,256]{2,1,0:T(8,128)(2,1)S(1)}, bf16[4,128,256]{2,1,0:T(8,128)(2,1)S(1)}, u32[]{:S(2)}, u32[]{:S(2)}) collective-permute-start(bf16[4,128,256]{2,1,0:T(8,128)(2,1)S(1)} %get-tuple-element.28), channel_id=1, source_target_pairs={{0,24},{8,16},{16,8},{24,0},{1,25},{9,17},{17,9},{25,1},{2,26},{10... | collective-permute-start | bytes 786440 | tf_op jit(solution)/shard_map/ppermute | solution.py:592
  76.1 5.6 %collective-permute-done.5.refs_1_ = bf16[4,128,256]{2,1,0:T(8,128)(2,1)S(1)} collective-permute-done((bf16[4,128,256]{2,1,0:T(8,128)(2,1)S(1)}, bf16[4,128,256]{2,1,0:T(8,128)(2,1)S(1)}, u32[]{:S(2)}, u32[]{:S(2)}) %collective-permute-start.5) | collective-permute-done | bytes 262176 | tf_op jit(solution)/shard_map/ppermute | solution.py:592
  81.8 5.1 %collective-permute-done.6.refs_2_ = bf16[4,128,256]{2,1,0:T(8,128)(2,1)S(1)} collective-permute-done((bf16[4,128,256]{2,1,0:T(8,128)(2,1)S(1)}, bf16[4,128,256]{2,1,0:T(8,128)(2,1)S(1)}, u32[]{:S(2)}, u32[]{:S(2)}) %collective-permute-start.6) | collective-permute-done | bytes 262176 | tf_op jit(solution)/shard_map/ppermute | solution.py:592
  86.9 1.0 %assemble.1 = bf16[4,512,256]{2,1,0:T(8,128)(2,1)} custom-call(s32[1]{0:T(128)} %bitcast.mem_ref.index_ref, bf16[4,128,256]{2,1,0:T(8,128)(2,1)S(1)} %get-tuple-element.25.refs_0_, bf16[4,128,256]{2,1,0:T(8,128)(2,1)S(1)} %collective-permute-done.5.refs_1_, bf16[4,128,256]{2,1,0:T(8,128)(2,1)S(1)} %collective-permute-done.6.refs_2_, ...), custom_call_target="tpu_custom_call" | custom-call | bytes 2097152 | tf_op jit(solution)/shard_map/assemble/pallas_call | solution.py:577
  (23 shorter events, 0.1 us)
Async XLA Ops:
  0.0 5.9 %copy-start = (bf16[4,512,256]{2,1,0:T(8,128)(2,1)S(1)}, bf16[4,512,256]{2,1,0:T(8,128)(2,1)}, u32[]{:S(2)}) copy-start(bf16[4,512,256]{2,1,0:T(8,128)(2,1)} %state_ref.1) | copy-start | bytes 3145732
  0.0 5.9 %copy-start.12 = (f32[256]{0:T(256)S(1)}, f32[256]{0:T(256)}, u32[]{:S(2)}) copy-start(f32[256]{0:T(256)} %param.16) | copy-start | bytes 3076
  0.0 5.9 %copy-start.4 = (bf16[256,256]{1,0:T(8,128)(2,1)S(1)}, bf16[256,256]{1,0:T(8,128)(2,1)}, u32[]{:S(2)}) copy-start(bf16[256,256]{1,0:T(8,128)(2,1)} %w_query_ref.1) | copy-start | bytes 393220
  0.0 5.9 %copy-start.5 = (bf16[256,256]{1,0:T(8,128)(2,1)S(1)}, bf16[256,256]{1,0:T(8,128)(2,1)}, u32[]{:S(2)}) copy-start(bf16[256,256]{1,0:T(8,128)(2,1)} %w_key_ref.3) | copy-start | bytes 393220
  0.0 5.9 %copy-start.6 = (bf16[256,256]{1,0:T(8,128)(2,1)S(1)}, bf16[256,256]{1,0:T(8,128)(2,1)}, u32[]{:S(2)}) copy-start(bf16[256,256]{1,0:T(8,128)(2,1)} %w_value_ref.3) | copy-start | bytes 393220
  0.0 5.9 %copy-start.14 = (s32[4]{0:T(128)S(1)}, s32[4]{0:T(128)}, u32[]{:S(2)}) copy-start(s32[4]{0:T(128)} %window_ref.3) | copy-start | bytes 52
  2.2 7.9 %collective-permute-start = (bf16[4,256,256]{2,1,0:T(8,128)(2,1)}, bf16[4,256,256]{2,1,0:T(8,128)(2,1)S(1)}, u32[]{:S(2)}, u32[]{:S(2)}) collective-permute-start(bf16[4,256,256]{2,1,0:T(8,128)(2,1)} %get-tuple-element.30), channel_id=1, source_target_pairs={{0,1},{1,2},{2,3},{3,4},{4,5},{5,6},{6,7},{8,9},{9,10},{10,11},{11... | collective-permute-start | bytes 1572872 | tf_op jit(solution)/shard_map/ppermute | solution.py:621
  4.6 6.0 %collective-permute-start.1 = (bf16[4,256,256]{2,1,0:T(8,128)(2,1)S(1)}, bf16[4,256,256]{2,1,0:T(8,128)(2,1)S(1)}, u32[]{:S(2)}, u32[]{:S(2)}) collective-permute-start(bf16[4,256,256]{2,1,0:T(8,128)(2,1)S(1)} %get-tuple-element.29), channel_id=1, source_target_pairs={{1,0},{2,1},{3,2},{4,3},{5,4},{6,5},{7,6},{9,8},{10,9},{11,10},{12... | collective-permute-start | bytes 1572872 | tf_op jit(solution)/shard_map/ppermute | solution.py:622
  6.0 4.6 %copy-start.1 = (bf16[256,1024]{1,0:T(8,128)(2,1)S(1)}, bf16[256,1024]{1,0:T(8,128)(2,1)}, u32[]{:S(2)}) copy-start(bf16[256,1024]{1,0:T(8,128)(2,1)} %w_gate_ref.1) | copy-start | bytes 1572868
  6.0 4.6 %copy-start.2 = (bf16[256,1024]{1,0:T(8,128)(2,1)S(1)}, bf16[256,1024]{1,0:T(8,128)(2,1)}, u32[]{:S(2)}) copy-start(bf16[256,1024]{1,0:T(8,128)(2,1)} %w_up_ref.1) | copy-start | bytes 1572868
  6.0 4.6 %copy-start.3 = (bf16[1024,256]{1,0:T(8,128)(2,1)S(1)}, bf16[1024,256]{1,0:T(8,128)(2,1)}, u32[]{:S(2)}) copy-start(bf16[1024,256]{1,0:T(8,128)(2,1)} %down_weight_ref.1) | copy-start | bytes 1572868
  6.0 4.6 %copy-start.7 = (bf16[256,256]{1,0:T(8,128)(2,1)S(1)}, bf16[256,256]{1,0:T(8,128)(2,1)}, u32[]{:S(2)}) copy-start(bf16[256,256]{1,0:T(8,128)(2,1)} %w_out_ref.1) | copy-start | bytes 393220
  6.0 4.6 %copy-start.13 = (f32[256]{0:T(256)S(1)}, f32[256]{0:T(256)}, u32[]{:S(2)}) copy-start(f32[256]{0:T(256)} %param.17) | copy-start | bytes 3076
  10.6 27.2 %copy-start.8 = (s32[4096]{0:T(1024)S(1)}, s32[4096]{0:T(1024)}, u32[]{:S(2)}) copy-start(s32[4096]{0:T(1024)} %param.26) | copy-start | bytes 49156
  10.6 27.2 %copy-start.9 = (s32[4096]{0:T(1024)S(1)}, s32[4096]{0:T(1024)}, u32[]{:S(2)}) copy-start(s32[4096]{0:T(1024)} %param.27) | copy-start | bytes 49156
  10.6 27.2 %copy-start.10 = (f32[4096]{0:T(1024)S(1)}, f32[4096]{0:T(1024)}, u32[]{:S(2)}) copy-start(f32[4096]{0:T(1024)} %param.28) | copy-start | bytes 49156
  10.6 27.1 %copy-start.11 = (f32[4096]{0:T(1024)S(1)}, f32[4096]{0:T(1024)}, u32[]{:S(2)}) copy-start(f32[4096]{0:T(1024)} %param.29) | copy-start | bytes 49156
  34.2 6.4 %collective-permute-start.2 = (bf16[4,128,256]{2,1,0:T(8,128)(2,1)S(1)}, bf16[4,128,256]{2,1,0:T(8,128)(2,1)S(1)}, u32[]{:S(2)}, u32[]{:S(2)}) collective-permute-start(bf16[4,128,256]{2,1,0:T(8,128)(2,1)S(1)} %get-tuple-element.22), channel_id=1, source_target_pairs={{0,8},{8,0},{16,24},{24,16},{1,9},{9,1},{17,25},{25,17},{2,10},{10... | collective-permute-start | bytes 786440 | tf_op jit(solution)/shard_map/ppermute | solution.py:592
  36.2 9.2 %collective-permute-start.3 = (bf16[4,128,256]{2,1,0:T(8,128)(2,1)S(1)}, bf16[4,128,256]{2,1,0:T(8,128)(2,1)S(1)}, u32[]{:S(2)}, u32[]{:S(2)}) collective-permute-start(bf16[4,128,256]{2,1,0:T(8,128)(2,1)S(1)} %get-tuple-element.23), channel_id=1, source_target_pairs={{0,16},{8,24},{16,0},{24,8},{1,17},{9,25},{17,1},{25,9},{2,18},{10... | collective-permute-start | bytes 786440 | tf_op jit(solution)/shard_map/ppermute | solution.py:592
  37.7 7.7 %collective-permute-start.4 = (bf16[4,128,256]{2,1,0:T(8,128)(2,1)S(1)}, bf16[4,128,256]{2,1,0:T(8,128)(2,1)S(1)}, u32[]{:S(2)}, u32[]{:S(2)}) collective-permute-start(bf16[4,128,256]{2,1,0:T(8,128)(2,1)S(1)} %get-tuple-element.24), channel_id=1, source_target_pairs={{0,24},{8,16},{16,8},{24,0},{1,25},{9,17},{17,9},{25,1},{2,26},{10... | collective-permute-start | bytes 786440 | tf_op jit(solution)/shard_map/ppermute | solution.py:592
  72.6 9.2 %collective-permute-start.5 = (bf16[4,128,256]{2,1,0:T(8,128)(2,1)S(1)}, bf16[4,128,256]{2,1,0:T(8,128)(2,1)S(1)}, u32[]{:S(2)}, u32[]{:S(2)}) collective-permute-start(bf16[4,128,256]{2,1,0:T(8,128)(2,1)S(1)} %get-tuple-element.26), channel_id=1, source_target_pairs={{0,8},{8,0},{16,24},{24,16},{1,9},{9,1},{17,25},{25,17},{2,10},{10... | collective-permute-start | bytes 786440 | tf_op jit(solution)/shard_map/ppermute | solution.py:592
  73.5 13.4 %collective-permute-start.6 = (bf16[4,128,256]{2,1,0:T(8,128)(2,1)S(1)}, bf16[4,128,256]{2,1,0:T(8,128)(2,1)S(1)}, u32[]{:S(2)}, u32[]{:S(2)}) collective-permute-start(bf16[4,128,256]{2,1,0:T(8,128)(2,1)S(1)} %get-tuple-element.27), channel_id=1, source_target_pairs={{0,16},{8,24},{16,0},{24,8},{1,17},{9,25},{17,1},{25,9},{2,18},{10... | collective-permute-start | bytes 786440 | tf_op jit(solution)/shard_map/ppermute | solution.py:592
  74.2 12.7 %collective-permute-start.7 = (bf16[4,128,256]{2,1,0:T(8,128)(2,1)S(1)}, bf16[4,128,256]{2,1,0:T(8,128)(2,1)S(1)}, u32[]{:S(2)}, u32[]{:S(2)}) collective-permute-start(bf16[4,128,256]{2,1,0:T(8,128)(2,1)S(1)} %get-tuple-element.28), channel_id=1, source_target_pairs={{0,24},{8,16},{16,8},{24,0},{1,25},{9,17},{17,9},{25,1},{2,26},{10... | collective-permute-start | bytes 786440 | tf_op jit(solution)/shard_map/ppermute | solution.py:592

commit v15 on v14

--- a/solution.py
+++ b/solution.py
@@ -53,6 +53,33 @@
 
 def smem_spec():
     return pl.BlockSpec(memory_space=pltpu.SMEM)
+
+
+def edges_kernel(own_ref, head_ref, tail_ref, sems):
+    reach = head_ref.shape[1]
+    rows = own_ref.shape[1]
+    copies = [
+        pltpu.make_async_copy(own_ref.at[:, pl.ds(lower, reach), :], ref, sems.at[which])
+        for which, (lower, ref) in enumerate(((rows - reach, tail_ref), (0, head_ref)))
+    ]
+    for copy in copies:
+        copy.start()
+    for copy in copies:
+        copy.wait()
+
+
+def edges(own, reach):
+    members, _, feat_width = own.shape
+    return pl.pallas_call(
+        edges_kernel,
+        out_shape=[jax.ShapeDtypeStruct((members, reach, feat_width), own.dtype)] * 2,
+        in_specs=[pl.BlockSpec(memory_space=pl.ANY)],
+        out_specs=[vmem_spec()] * 2,
+        scratch_shapes=[pltpu.SemaphoreType.DMA((2,))],
+        compiler_params=pltpu.CompilerParams(vmem_limit_bytes=VMEM_LIMIT),
+        cost_estimate=pl.CostEstimate(flops=0, bytes_accessed=8 * members * reach * feat_width, transcendentals=0),
+        name="edges",
+    )(own)
 
 
 def sample_grid_kernel(start_ref, token_ref, channel_ref, value_ref, var_ref, out_ref):
@@ -107,9 +134,13 @@
     return math.log2(math.e) / math.sqrt(head_size)
 
 
-def band_bias(window, lower, upper, reach):
+def in_band(window, lower, upper, reach):
     apart = jnp.abs(iota((Q_ROWS, upper - lower), 1) + (lower - reach) - iota((Q_ROWS, upper - lower), 0))
-    return jnp.where(apart <= window, 0.0, -1e30)
+    return apart <= window
+
+
+def factor(mask):
+    return jnp.where(mask, 1.0, 0.0).astype(BF16)
 
 
 def group_lanes(group):
@@ -143,21 +174,21 @@
 
 def padded_lanes(values, before, after):
     pieces = [jnp.zeros((values.shape[0], before), BF16)] if before else []
-    pieces.append(values.astype(BF16))
+    pieces.append(values)
     if after:
         pieces.append(jnp.zeros((values.shape[0], after), BF16))
     return jnp.concatenate(pieces, axis=1) if len(pieces) > 1 else pieces[0]
 
 
-def unit_weights(scores, spans, bias_of):
+def unit_weights(scores, spans, band_of):
     width = scores.shape[1]
     count = len(spans) * Q_ROWS
     weights = []
     for head in range(scores.shape[0] // count):
         for block, (lower, upper) in enumerate(spans):
             top = head * count + block * Q_ROWS
-            expo = jnp.exp2(scores[top : top + Q_ROWS, lower:upper] + bias_of(head, block))
-            weights.append(padded_lanes(expo, lower, width - upper))
+            expo = jnp.exp2(scores[top : top + Q_ROWS, lower:upper]).astype(BF16)
+            weights.append(padded_lanes(expo * band_of(head, block), lower, width - upper))
     return jnp.concatenate(weights, axis=0)
 
 
@@ -174,13 +205,13 @@
     total_ref,
     key_buf,
     value_buf,
-    bias_buf,
+    band_buf,
 ):
     rows, feat_width = own_ref.shape[1:]
     heads = window_ref.shape[0]
     head_size = feat_width // heads
     group_heads = LANES // head_size
-    key_count = bias_buf.shape[2]
+    key_count = band_buf.shape[2]
     reach = (key_count - Q_ROWS) // 2
     reach_blocks = reach // Q_ROWS
     blocks = rows // Q_ROWS
@@ -188,14 +219,14 @@
     @pl.when(pl.program_id(0) == 0)
     def _():
         for head in range(heads):
-            bias_buf[head] = band_bias(window_ref[head], 0, key_count, reach)
+            band_buf[head] = factor(in_band(window_ref[head], 0, key_count, reach))
         value_buf[...] = jnp.ones(value_buf.shape, BF16)
 
     normed = rms_scaled(own_ref[0].astype(F32), gain_ref[...]).astype(BF16)
     query_rows = dot(normed, w_query_ref[...]) * query_scale(head_size)
     key_rows = dot(normed, w_key_ref[...])
     query_ref[0] = query_rows.astype(BF16)
-    key_buf[...] = key_rows.T.astype(BF16)
+    key_buf[...] = key_rows.astype(BF16).T
     put_values(value_buf, 0, dot(normed, w_value_ref[...]).astype(BF16))
     query_norms, key_norms = largest_norms(query_rows, heads), largest_norms(key_rows, heads)
     blank = jnp.zeros((norm_ref.shape[1] - 2, LANES), F32)
@@ -203,27 +234,28 @@
 
     @pl.when(is_safe(query_norms, key_norms))
     def _():
-        groups = heads // group_heads
-        ranges = [(max(0, b - reach_blocks), min(blocks, b + reach_blocks + 1)) for b in range(blocks)]
-        spans = [(lower * Q_ROWS, upper * Q_ROWS) for lower, upper in ranges]
-
-        def scores_of(group):
-            queries = query_ref[0, :, group_lanes(group)]
+        units = [(first, group) for first in range(0, blocks, 2) for group in range(heads // group_heads)]
+
+        def scores_of(first, group):
+            queries = query_ref[0, first * Q_ROWS : (first + 2) * Q_ROWS, group_lanes(group)]
             return dot(stacked_heads(queries, head_size), key_buf[group_lanes(group), :])
 
-        scores = scores_of(0)
-        for group in range(groups):
-            following = scores_of(group + 1) if group + 1 < groups else None
-
-            def bias_of(head, block):
-                shift = (reach_blocks - block) * Q_ROWS
+        scores = scores_of(*units[0])
+        for at, (first, group) in enumerate(units):
+            following = scores_of(*units[at + 1]) if at + 1 < len(units) else None
+            ranges = [(max(0, b - reach_blocks), min(blocks, b + reach_blocks + 1)) for b in (first, first + 1)]
+            spans = [(lower * Q_ROWS, upper * Q_ROWS) for lower, upper in ranges]
+
+            def band_of(head, block):
+                shift = (reach_blocks - first - block) * Q_ROWS
                 lower, upper = spans[block]
-                return bias_buf[group * group_heads + head, :, lower + shift : upper + shift]
+                return band_buf[group * group_heads + head, :, lower + shift : upper + shift]
 
             values = value_buf[:, 2 * group * LANES : 2 * (group + 1) * LANES]
-            mixed, totals = weighted_sums(unit_weights(scores, spans, bias_of), values, head_size)
-            mixed_ref[0, :, group_lanes(group)] = mixed
-            total_ref[0, :, group_lanes(group)] = totals
+            mixed, totals = weighted_sums(unit_weights(scores, spans, band_of), values, head_size)
+            here = slice(first * Q_ROWS, (first + 2) * Q_ROWS)
+            mixed_ref[0, here, group_lanes(group)] = mixed
+            total_ref[0, here, group_lanes(group)] = totals
             scores = following
 
 
@@ -245,7 +277,7 @@
         scratch_shapes=[
             pltpu.VMEM((feat_width, rows), BF16),
             pltpu.VMEM((rows, 2 * feat_width), BF16),
-            pltpu.VMEM((heads, Q_ROWS, key_count), F32),
+            pltpu.VMEM((heads, Q_ROWS, key_count), BF16),
         ],
         compiler_params=pltpu.CompilerParams(vmem_limit_bytes=VMEM_LIMIT),
         cost_estimate=pl.CostEstimate(
@@ -277,7 +309,7 @@
     down_weight_ref,
     *refs,
 ):
-    out_refs, (halo_key_buf, halo_value_buf, bias_buf, mixed_buf, key_buf, value_buf, forecast_buf) = (
+    out_refs, (halo_key_buf, halo_value_buf, band_buf, mixed_buf, key_buf, value_buf, forecast_buf) = (
         refs[:-7],
         refs[-7:],
     )
@@ -297,10 +329,10 @@
         first_valid = first_pos - reach >= 0
         last_valid = first_pos + rows + reach <= total_len
         for head in range(heads):
-            left_bias = band_bias(window_ref[head], 0, reach, reach)
-            right_bias = band_bias(window_ref[head], key_count - reach, key_count, reach)
-            bias_buf[0, head] = jnp.where(first_valid, left_bias, -1e30)
-            bias_buf[1, head] = jnp.where(last_valid, right_bias, -1e30)
+            window = window_ref[head]
+            band_buf[0, head] = factor(in_band(jnp.where(first_valid, window, -1), 0, reach, reach))
+            right_window = jnp.where(last_valid, window, -1)
+            band_buf[1, head] = factor(in_band(right_window, key_count - reach, key_count, reach))
         halo_value_buf[...] = jnp.ones(halo_value_buf.shape, BF16)
 
     def keys_of(normed):
@@ -314,7 +346,7 @@
         normed = rms_scaled(ref[0].astype(F32), attn_gain_ref[...]).astype(BF16)
         keys = keys_of(normed)
         key_norms = jnp.maximum(key_norms, largest_norms(keys, heads))
-        halo_key_buf[side] = keys.T.astype(BF16)
+        halo_key_buf[side] = keys.astype(BF16).T
         put_values(halo_value_buf.at[side], 0, values_of(normed))
     safe = is_safe(norm_ref[0, 0:1, :], key_norms)
 
@@ -332,13 +364,13 @@
             following = scores_of(*units[at + 1]) if at + 1 < len(units) else None
             spans = [(0, reach), (Q_ROWS, reach)] if side == 0 else [(0, reach - Q_ROWS), (0, reach)]
 
-            def bias_of(head, block):
+            def band_of(head, block):
                 lower, upper = spans[block]
                 shift = -block * Q_ROWS if side == 0 else (1 - block) * Q_ROWS
-                return bias_buf[side, group * group_heads + head, :, lower + shift : upper + shift]
+                return band_buf[side, group * group_heads + head, :, lower + shift : upper + shift]
 
             values = halo_value_buf[side, :, 2 * group * LANES : 2 * (group + 1) * LANES]
-            mixed, totals = weighted_sums(unit_weights(scores, spans, bias_of), values, head_size)
+            mixed, totals = weighted_sums(unit_weights(scores, spans, band_of), values, head_size)
             here = slice(side * (rows - count), side * (rows - count) + count)
             mixed = mixed + inner_mixed_ref[0, here, group_lanes(group)]
             totals = totals + inner_total_ref[0, here, group_lanes(group)]
@@ -349,7 +381,7 @@
     def _():
         normed = rms_scaled(state_ref[0].astype(F32), attn_gain_ref[...]).astype(BF16)
         key_buf[:, :reach] = halo_key_buf[0]
-        key_buf[:, reach : reach + rows] = keys_of(normed).T.astype(BF16)
+        key_buf[:, reach : reach + rows] = keys_of(normed).astype(BF16).T
         key_buf[:, reach + rows :] = halo_key_buf[1]
         value_buf[...] = jnp.ones(value_buf.shape, BF16)
         put_values(value_buf, reach, values_of(normed))
@@ -365,8 +397,8 @@
                 scores = dot(stacked_heads(queries, head_size), keys)
                 weights = []
                 for head in range(group_heads):
-                    bias = band_bias(window_ref[group * group_heads + head], 0, key_count, reach)
-                    score_matrix = scores[head * Q_ROWS : (head + 1) * Q_ROWS] + jnp.where(inside, bias, -1e30)
+                    allowed = inside & in_band(window_ref[group * group_heads + head], 0, key_count, reach)
+                    score_matrix = jnp.where(allowed, scores[head * Q_ROWS : (head + 1) * Q_ROWS], -1e30)
                     row_top = jnp.max(score_matrix, axis=-1, keepdims=True)
                     weights.append(jnp.exp2(score_matrix - row_top).astype(BF16))
                 values = value_buf[start : start + key_count, 2 * group * LANES : 2 * (group + 1) * LANES]
@@ -375,12 +407,12 @@
 
     after = (state_ref[0].astype(F32) + dot(mixed_buf[...], w_out_ref[...])).astype(BF16)
     normed_mid = rms_scaled(after.astype(F32), ffn_gain_ref[...]).astype(BF16)
-    hidden = []
+    forecast = after.astype(F32)
     for lower in range(0, w_gate_ref.shape[1], HIDDEN_CHUNK):
         part = slice(lower, lower + HIDDEN_CHUNK)
         gate = 0.5 * dot(normed_mid, w_gate_ref[:, part])
-        hidden.append((gate * (1.0 + jnp.tanh(gate)) * dot(normed_mid, w_up_ref[:, part])).astype(BF16))
-    forecast = after.astype(F32) + dot(jnp.concatenate(hidden, axis=1), down_weight_ref[...])
+        hidden = (gate * (1.0 + jnp.tanh(gate)) * dot(normed_mid, w_up_ref[:, part])).astype(BF16)
+        forecast += dot(hidden, down_weight_ref[part, :])
     forecast_buf[...] = forecast.astype(BF16)
     share_rows = out_refs[0].shape[1]
     for part, out_ref in enumerate(out_refs):
@@ -409,7 +441,7 @@
         scratch_shapes=[
             pltpu.VMEM((2, feat_width, reach), BF16),
             pltpu.VMEM((2, reach, 2 * feat_width), BF16),
-            pltpu.VMEM((2, heads, Q_ROWS, reach), F32),
+            pltpu.VMEM((2, heads, Q_ROWS, reach), BF16),
             pltpu.VMEM((row_count, feat_width), BF16),
             pltpu.VMEM((feat_width, row_count + 2 * reach), BF16),
             pltpu.VMEM((row_count + 2 * reach, 2 * feat_width), BF16),
@@ -618,8 +650,9 @@
     first_pos = lax.axis_index("tok") * row_count
     up = [(i, i + 1) for i in range(tok_count - 1)]
     down = [(i + 1, i) for i in range(tok_count - 1)]
-    left = lax.ppermute(ens_state[:, row_count - WIN :], "tok", up)
-    right = lax.ppermute(ens_state[:, :WIN], "tok", down)
+    head, tail = edges(ens_state, WIN)
+    left = lax.ppermute(tail, "tok", up)
+    right = lax.ppermute(head, "tok", down)
     share_start = first_pos + lax.axis_index("mem") * share_rows
     grid = sample_grid(
         share_start.astype(jnp.int32).reshape(1), obs_token, obs_channel, obs_value, obs_var, share_rows, feat_width

time: 88.1 us -> 89.4 us (1.015)
  blocking collectives: 21.8 us -> 15.1 us
  local copies, waits for them, and re-layouts: 2.26 us -> 6.56 us
  waiting for transfers between devices: 17.5 us -> 20.7 us
    all_to_all x1, blocking collectives: 21.8 us -> 15.1 us  [local(): lax.all_to_all(jnp.broadcast_to(partial[None], (device_count, *partial.sh...]
    unnamed x30 -> x36, local copies, waits for them, and re-layouts: 0.08 us -> 6.55 us
    ppermute x6, waiting for transfers between devices: 17.1 us -> 20.7 us  [exchanged(): lax.ppermute(v, 'mem', [(i, i ^ part) for i in range(count)])]
    slice x1 -> x0, local copies, waits for them, and re-layouts: 2.17 us -> none  [local(): right = lax.ppermute(ens_state[:, :WIN], 'tok', down)]
where the time goes in v15:
time: 89.4 us; the launch traced here: 89.1 us
  Pallas kernels  35.4 us (40%)
  waiting for transfers between devices  20.7 us (23%)
  blocking collectives  15.1 us (17%)
  starting transfers between devices  11.2 us (13%)
  local copies, waits for them, and re-layouts  6.56 us (7%)
    pallas_call x1, Pallas kernels, forward(): pl.pallas_call(functools.partial(forward_kernel, total_len), grid=(member...  23.6 us
    ppermute x6, waiting for transfers between devices, exchanged(): lax.ppermute(v, 'mem', [(i, i ^ part) for i in range(count)])  20.7 us
    all_to_all x1, blocking collectives, local(): lax.all_to_all(jnp.broadcast_to(partial[None], (device_count, *partial.sh...  15.1 us
    ppermute x6, starting transfers between devices, exchanged(): lax.ppermute(v, 'mem', [(i, i ^ part) for i in range(count)])  7.48 us
    unnamed x36, local copies, waits for them, and re-layouts  6.55 us
    pallas_call x1, Pallas kernels, inner(): pl.pallas_call(inner_kernel, grid=(members,), out_shape=[jax.ShapeDtypeSt...  4.07 us
    pallas_call x1, Pallas kernels, combine(): pl.pallas_call(combine_kernel, out_shape=[jax.ShapeDtypeStruct(v.shape, B...  3.64 us
    ppermute x1, starting transfers between devices, local(): left = lax.ppermute(tail, 'tok', up)  2.39 us
  transfers between devices with their start and end apart: 8, of which 5 were waited for; matrix products, arithmetic and copies ran while one was open for 0% of the time, Pallas kernels for 6%

profile of v15, /device:TPU:0, one launch (start us, length us, event | category | flops | bytes accessed | tf_op | source)
XLA Modules:
  0.0 89.1 jit_solution(15329615695894086131)
XLA Ops:
  0.0 1.2 %copy-done = bf16[4,512,256]{2,1,0:T(8,128)(2,1)S(1)} copy-done((bf16[4,512,256]{2,1,0:T(8,128)(2,1)S(1)}, bf16[4,512,256]{2,1,0:T(8,128)(2,1)}, u32[]{:S(2)}) %copy-start) | copy-done | bytes 1048600
  1.2 0.1 edges.1
  1.3 2.4 %collective-permute-start = (bf16[4,256,256]{2,1,0:T(8,128)(2,1)S(1)}, bf16[4,256,256]{2,1,0:T(8,128)(2,1)S(1)}, u32[]{:S(2)}, u32[]{:S(2)}) collective-permute-start(bf16[4,256,256]{2,1,0:T(8,128)(2,1)S(1)} %get-tuple-element.23), channel_id=1, source_target_pairs={{0,1},{1,2},{2,3},{3,4},{4,5},{5,6},{6,7},{8,9},{9,10},{10,11},{11... | collective-permute-start | bytes 1572872 | tf_op jit(solution)/shard_map/ppermute | solution.py:654
  3.7 1.3 %collective-permute-start.1 = (bf16[4,256,256]{2,1,0:T(8,128)(2,1)S(1)}, bf16[4,256,256]{2,1,0:T(8,128)(2,1)S(1)}, u32[]{:S(2)}, u32[]{:S(2)}) collective-permute-start(bf16[4,256,256]{2,1,0:T(8,128)(2,1)S(1)} %get-tuple-element.24), channel_id=1, source_target_pairs={{1,0},{2,1},{3,2},{4,3},{5,4},{6,5},{7,6},{9,8},{10,9},{11,10},{12... | collective-permute-start | bytes 1572872 | tf_op jit(solution)/shard_map/ppermute | solution.py:655
  5.0 0.0 copy-start.1
  5.0 1.2 %copy-done.1 = bf16[4,512,256]{2,1,0:T(8,128)(2,1)S(1)} copy-done((bf16[4,512,256]{2,1,0:T(8,128)(2,1)S(1)}, bf16[4,512,256]{2,1,0:T(8,128)(2,1)}, u32[]{:S(2)}) %copy-start.1) | copy-done | bytes 1048600
  6.3 0.9 %copy-done.5 = bf16[256,256]{1,0:T(8,128)(2,1)S(1)} copy-done((bf16[256,256]{1,0:T(8,128)(2,1)S(1)}, bf16[256,256]{1,0:T(8,128)(2,1)}, u32[]{:S(2)}) %copy-start.5) | copy-done | bytes 131096
  7.2 0.9 %copy-done.6 = bf16[256,256]{1,0:T(8,128)(2,1)S(1)} copy-done((bf16[256,256]{1,0:T(8,128)(2,1)S(1)}, bf16[256,256]{1,0:T(8,128)(2,1)}, u32[]{:S(2)}) %copy-start.6) | copy-done | bytes 131096
  8.1 0.9 %copy-done.8 = bf16[256,256]{1,0:T(8,128)(2,1)S(1)} copy-done((bf16[256,256]{1,0:T(8,128)(2,1)S(1)}, bf16[256,256]{1,0:T(8,128)(2,1)}, u32[]{:S(2)}) %copy-start.8) | copy-done | bytes 131096
  9.0 0.7 copy-done.15
  9.7 0.7 copy-done.17
  10.3 0.0 copy-start.16
  10.4 4.1 %inner.1 = (bf16[4,512,256]{2,1,0:T(8,128)(2,1)S(1)}, f32[4,8,128]{2,1,0:T(8,128)S(1)}, f32[4,512,256]{2,1,0:T(8,128)S(1)}, f32[4,512,256]{2,1,0:T(8,128)S(1)}) custom-call(s32[4]{0:T(128)S(1)} %copy-done.17, bf16[4,512,256]{2,1,0:T(8,128)(2,1)S(1)} %copy-done.1, f32[1,256]{1,0:T(1,128)S(1)} %bitcast.13, bf16[256,256]{1,0:T(8,128)(2,1)S(1)} %copy-done.5, ...), custom_call_target="tpu_custom_call" | custom-call | flops 5100273664 | bytes 7340032 | tf_op jit(solution)/shard_map/inner/pallas_call | solution.py:271
  14.5 0.0 copy-start.12
  14.5 0.0 copy-start.13
  14.6 23.6 %forward.1 = (bf16[4,128,256]{2,1,0:T(8,128)(2,1)S(1)}, bf16[4,128,256]{2,1,0:T(8,128)(2,1)S(1)}, bf16[4,128,256]{2,1,0:T(8,128)(2,1)S(1)}, bf16[4,128,256]{2,1,0:T(8,128)(2,1)S(1)}) custom-call(s32[1]{0:T(128)} %bitcast.1.tok_ref, s32[1]{0:T(128)} %bitcast.mem_ref.index_ref, s32[4]{0:T(128)S(1)} %copy-done.17, bf16[4,512,256]{2,1,0:T(8,128)(2,1)S(1)} %copy-done.1, ...), custom_call_target="tpu_custom_call" | custom-call | flops 5100273664 | bytes 5242880 | tf_op jit(solution)/shard_map/forward/pallas_call | solution.py:433
  38.2 2.4 %collective-permute-start.2 = (bf16[4,128,256]{2,1,0:T(8,128)(2,1)S(1)}, bf16[4,128,256]{2,1,0:T(8,128)(2,1)S(1)}, u32[]{:S(2)}, u32[]{:S(2)}) collective-permute-start(bf16[4,128,256]{2,1,0:T(8,128)(2,1)S(1)} %get-tuple-element.26), channel_id=1, source_target_pairs={{0,8},{8,0},{16,24},{24,16},{1,9},{9,1},{17,25},{25,17},{2,10},{10... | collective-permute-start | bytes 786440 | tf_op jit(solution)/shard_map/ppermute | solution.py:624
  40.5 1.5 %collective-permute-start.3 = (bf16[4,128,256]{2,1,0:T(8,128)(2,1)S(1)}, bf16[4,128,256]{2,1,0:T(8,128)(2,1)S(1)}, u32[]{:S(2)}, u32[]{:S(2)}) collective-permute-start(bf16[4,128,256]{2,1,0:T(8,128)(2,1)S(1)} %get-tuple-element.27), channel_id=1, source_target_pairs={{0,16},{8,24},{16,0},{24,8},{1,17},{9,25},{17,1},{25,9},{2,18},{10... | collective-permute-start | bytes 786440 | tf_op jit(solution)/shard_map/ppermute | solution.py:624
  42.1 0.0 collective-permute-start.4
  42.1 1.3 %sample_grid.1.refs_4_ = f32[2,128,256]{2,1,0:T(8,128)S(1)} custom-call(s32[1]{0:T(128)} %bitcast.4.start_ref, s32[1,4096]{1,0:T(1,128)S(1)} %bitcast.9, s32[1,4096]{1,0:T(1,128)S(1)} %bitcast.10, f32[1,4096]{1,0:T(1,128)S(1)} %bitcast.11, f32[1,4096]{1,0:T(1,128)S(1)} %bitcast.12), custom_call_target="tpu_custom_call" | custom-call | flops 1073741824 | bytes 65536 | tf_op jit(solution)/shard_map/sample_grid/pallas_call | solution.py:108
  43.4 2.3 %collective-permute-done.2.refs_1_ = bf16[4,128,256]{2,1,0:T(8,128)(2,1)S(1)} collective-permute-done((bf16[4,128,256]{2,1,0:T(8,128)(2,1)S(1)}, bf16[4,128,256]{2,1,0:T(8,128)(2,1)S(1)}, u32[]{:S(2)}, u32[]{:S(2)}) %collective-permute-start.2) | collective-permute-done | bytes 262176 | tf_op jit(solution)/shard_map/ppermute | solution.py:624
  45.7 7.3 %collective-permute-done.3.refs_2_ = bf16[4,128,256]{2,1,0:T(8,128)(2,1)S(1)} collective-permute-done((bf16[4,128,256]{2,1,0:T(8,128)(2,1)S(1)}, bf16[4,128,256]{2,1,0:T(8,128)(2,1)S(1)}, u32[]{:S(2)}, u32[]{:S(2)}) %collective-permute-start.3) | collective-permute-done | bytes 262176 | tf_op jit(solution)/shard_map/ppermute | solution.py:624
  53.0 0.3 collective-permute-done.4.refs_3_
  53.4 1.7 %gram.1 = f32[8,128]{1,0:T(8,128)S(1)} custom-call(s32[1]{0:T(128)} %bitcast.mem_ref.index_ref, bf16[4,128,256]{2,1,0:T(8,128)(2,1)S(1)} %get-tuple-element.25.refs_0_, bf16[4,128,256]{2,1,0:T(8,128)(2,1)S(1)} %collective-permute-done.2.refs_1_, bf16[4,128,256]{2,1,0:T(8,128)(2,1)S(1)} %collective-permute-done.3.refs_2_, ...), custom_call_target="tpu_custom_call" | custom-call | flops 805306368 | bytes 1048576 | tf_op jit(solution)/shard_map/gram/pallas_call | solution.py:500
  55.0 15.1 %all_to_all.5.partial_ref = f32[32,8,128]{2,1,0:T(8,128)S(1)} all-to-all(f32[32,8,128]{2,1,0:T(8,128)S(1)} %broadcast_in_dim.2), channel_id=1, replica_groups=mesh['mem'=4,'tok'=8] {'mem','tok'}, dimensions={0} | all-to-all | bytes 262144 | tf_op jit(solution)/shard_map/all_to_all | solution.py:671
  70.1 3.6 %combine.1 = (bf16[4,128,256]{2,1,0:T(8,128)(2,1)S(1)}, bf16[4,128,256]{2,1,0:T(8,128)(2,1)S(1)}, bf16[4,128,256]{2,1,0:T(8,128)(2,1)S(1)}, bf16[4,128,256]{2,1,0:T(8,128)(2,1)S(1)}) custom-call(s32[1]{0:T(128)} %bitcast.mem_ref.index_ref, f32[32,8,128]{2,1,0:T(8,128)S(1)} %all_to_all.5.partial_ref, bf16[4,128,256]{2,1,0:T(8,128)(2,1)S(1)} %get-tuple-element.25.refs_0_, ...), custom_call_target="tpu_custom_call" | custom-call | flops 536870912 | bytes 2097152 | tf_op jit(solution)/shard_map/combine/pallas_call | solution.py:583
  73.8 0.9 collective-permute-start.5
  74.7 0.7 collective-permute-start.6
  75.4 1.9 %collective-permute-start.7 = (bf16[4,128,256]{2,1,0:T(8,128)(2,1)S(1)}, bf16[4,128,256]{2,1,0:T(8,128)(2,1)S(1)}, u32[]{:S(2)}, u32[]{:S(2)}) collective-permute-start(bf16[4,128,256]{2,1,0:T(8,128)(2,1)S(1)} %get-tuple-element.32), channel_id=1, source_target_pairs={{0,24},{8,16},{16,8},{24,0},{1,25},{9,17},{17,9},{25,1},{2,26},{10... | collective-permute-start | bytes 786440 | tf_op jit(solution)/shard_map/ppermute | solution.py:624
  77.3 5.6 %collective-permute-done.5.refs_1_ = bf16[4,128,256]{2,1,0:T(8,128)(2,1)S(1)} collective-permute-done((bf16[4,128,256]{2,1,0:T(8,128)(2,1)S(1)}, bf16[4,128,256]{2,1,0:T(8,128)(2,1)S(1)}, u32[]{:S(2)}, u32[]{:S(2)}) %collective-permute-start.5) | collective-permute-done | bytes 262176 | tf_op jit(solution)/shard_map/ppermute | solution.py:624
  83.0 5.1 %collective-permute-done.6.refs_2_ = bf16[4,128,256]{2,1,0:T(8,128)(2,1)S(1)} collective-permute-done((bf16[4,128,256]{2,1,0:T(8,128)(2,1)S(1)}, bf16[4,128,256]{2,1,0:T(8,128)(2,1)S(1)}, u32[]{:S(2)}, u32[]{:S(2)}) %collective-permute-start.6) | collective-permute-done | bytes 262176 | tf_op jit(solution)/shard_map/ppermute | solution.py:624
  88.1 1.0 %assemble.1 = bf16[4,512,256]{2,1,0:T(8,128)(2,1)} custom-call(s32[1]{0:T(128)} %bitcast.mem_ref.index_ref, bf16[4,128,256]{2,1,0:T(8,128)(2,1)S(1)} %get-tuple-element.29.refs_0_, bf16[4,128,256]{2,1,0:T(8,128)(2,1)S(1)} %collective-permute-done.5.refs_1_, bf16[4,128,256]{2,1,0:T(8,128)(2,1)S(1)} %collective-permute-done.6.refs_2_, ...), custom_call_target="tpu_custom_call" | custom-call | bytes 2097152 | tf_op jit(solution)/shard_map/assemble/pallas_call | solution.py:609
  (29 shorter events, 0.1 us)
Async XLA Ops:
  0.0 1.2 %copy-start = (bf16[4,512,256]{2,1,0:T(8,128)(2,1)S(1)}, bf16[4,512,256]{2,1,0:T(8,128)(2,1)}, u32[]{:S(2)}) copy-start(bf16[4,512,256]{2,1,0:T(8,128)(2,1)} %state_ref.1) | copy-start | bytes 3145732
  1.3 13.1 %collective-permute-start = (bf16[4,256,256]{2,1,0:T(8,128)(2,1)S(1)}, bf16[4,256,256]{2,1,0:T(8,128)(2,1)S(1)}, u32[]{:S(2)}, u32[]{:S(2)}) collective-permute-start(bf16[4,256,256]{2,1,0:T(8,128)(2,1)S(1)} %get-tuple-element.23), channel_id=1, source_target_pairs={{0,1},{1,2},{2,3},{3,4},{4,5},{5,6},{6,7},{8,9},{9,10},{10,11},{11... | collective-permute-start | bytes 1572872 | tf_op jit(solution)/shard_map/ppermute | solution.py:654
  3.7 10.7 %collective-permute-start.1 = (bf16[4,256,256]{2,1,0:T(8,128)(2,1)S(1)}, bf16[4,256,256]{2,1,0:T(8,128)(2,1)S(1)}, u32[]{:S(2)}, u32[]{:S(2)}) collective-permute-start(bf16[4,256,256]{2,1,0:T(8,128)(2,1)S(1)} %get-tuple-element.24), channel_id=1, source_target_pairs={{1,0},{2,1},{3,2},{4,3},{5,4},{6,5},{7,6},{9,8},{10,9},{11,10},{12... | collective-permute-start | bytes 1572872 | tf_op jit(solution)/shard_map/ppermute | solution.py:655
  5.0 1.2 %copy-start.1 = (bf16[4,512,256]{2,1,0:T(8,128)(2,1)S(1)}, bf16[4,512,256]{2,1,0:T(8,128)(2,1)}, u32[]{:S(2)}) copy-start(bf16[4,512,256]{2,1,0:T(8,128)(2,1)} %state_ref.1) | copy-start | bytes 3145732
  6.3 0.9 %copy-start.5 = (bf16[256,256]{1,0:T(8,128)(2,1)S(1)}, bf16[256,256]{1,0:T(8,128)(2,1)}, u32[]{:S(2)}) copy-start(bf16[256,256]{1,0:T(8,128)(2,1)} %w_query_ref.1) | copy-start | bytes 393220
  7.2 0.9 %copy-start.6 = (bf16[256,256]{1,0:T(8,128)(2,1)S(1)}, bf16[256,256]{1,0:T(8,128)(2,1)}, u32[]{:S(2)}) copy-start(bf16[256,256]{1,0:T(8,128)(2,1)} %w_key_ref.3) | copy-start | bytes 393220
  8.1 0.9 %copy-start.8 = (bf16[256,256]{1,0:T(8,128)(2,1)S(1)}, bf16[256,256]{1,0:T(8,128)(2,1)}, u32[]{:S(2)}) copy-start(bf16[256,256]{1,0:T(8,128)(2,1)} %w_value_ref.3) | copy-start | bytes 393220
  9.0 0.7 copy-start.15
  9.7 0.7 copy-start.17
  10.3 4.1 %copy-start.2 = (bf16[256,1024]{1,0:T(8,128)(2,1)S(1)}, bf16[256,1024]{1,0:T(8,128)(2,1)}, u32[]{:S(2)}) copy-start(bf16[256,1024]{1,0:T(8,128)(2,1)} %w_gate_ref.1) | copy-start | bytes 1572868
  10.3 4.2 %copy-start.3 = (bf16[256,1024]{1,0:T(8,128)(2,1)S(1)}, bf16[256,1024]{1,0:T(8,128)(2,1)}, u32[]{:S(2)}) copy-start(bf16[256,1024]{1,0:T(8,128)(2,1)} %w_up_ref.1) | copy-start | bytes 1572868
  10.3 4.2 %copy-start.4 = (bf16[1024,256]{1,0:T(8,128)(2,1)S(1)}, bf16[1024,256]{1,0:T(8,128)(2,1)}, u32[]{:S(2)}) copy-start(bf16[1024,256]{1,0:T(8,128)(2,1)} %down_weight_ref.1) | copy-start | bytes 1572868
  10.3 4.2 %copy-start.7 = (bf16[256,256]{1,0:T(8,128)(2,1)S(1)}, bf16[256,256]{1,0:T(8,128)(2,1)}, u32[]{:S(2)}) copy-start(bf16[256,256]{1,0:T(8,128)(2,1)} %w_key_ref.3) | copy-start | bytes 393220
  10.3 4.2 %copy-start.9 = (bf16[256,256]{1,0:T(8,128)(2,1)S(1)}, bf16[256,256]{1,0:T(8,128)(2,1)}, u32[]{:S(2)}) copy-start(bf16[256,256]{1,0:T(8,128)(2,1)} %w_value_ref.3) | copy-start | bytes 393220
  10.3 4.2 %copy-start.10 = (bf16[256,256]{1,0:T(8,128)(2,1)S(1)}, bf16[256,256]{1,0:T(8,128)(2,1)}, u32[]{:S(2)}) copy-start(bf16[256,256]{1,0:T(8,128)(2,1)} %w_out_ref.1) | copy-start | bytes 393220
  10.3 4.2 %copy-start.16 = (f32[256]{0:T(256)S(1)}, f32[256]{0:T(256)}, u32[]{:S(2)}) copy-start(f32[256]{0:T(256)} %param.17) | copy-start | bytes 3076
  14.5 27.6 %copy-start.11 = (s32[4096]{0:T(1024)S(1)}, s32[4096]{0:T(1024)}, u32[]{:S(2)}) copy-start(s32[4096]{0:T(1024)} %param.26) | copy-start | bytes 49156
  14.5 27.6 %copy-start.12 = (s32[4096]{0:T(1024)S(1)}, s32[4096]{0:T(1024)}, u32[]{:S(2)}) copy-start(s32[4096]{0:T(1024)} %param.27) | copy-start | bytes 49156
  14.5 27.6 %copy-start.13 = (f32[4096]{0:T(1024)S(1)}, f32[4096]{0:T(1024)}, u32[]{:S(2)}) copy-start(f32[4096]{0:T(1024)} %param.28) | copy-start | bytes 49156
  14.6 27.5 %copy-start.14 = (f32[4096]{0:T(1024)S(1)}, f32[4096]{0:T(1024)}, u32[]{:S(2)}) copy-start(f32[4096]{0:T(1024)} %param.29) | copy-start | bytes 49156
  38.2 7.5 %collective-permute-start.2 = (bf16[4,128,256]{2,1,0:T(8,128)(2,1)S(1)}, bf16[4,128,256]{2,1,0:T(8,128)(2,1)S(1)}, u32[]{:S(2)}, u32[]{:S(2)}) collective-permute-start(bf16[4,128,256]{2,1,0:T(8,128)(2,1)S(1)} %get-tuple-element.26), channel_id=1, source_target_pairs={{0,8},{8,0},{16,24},{24,16},{1,9},{9,1},{17,25},{25,17},{2,10},{10... | collective-permute-start | bytes 786440 | tf_op jit(solution)/shard_map/ppermute | solution.py:624
  40.5 12.5 %collective-permute-start.3 = (bf16[4,128,256]{2,1,0:T(8,128)(2,1)S(1)}, bf16[4,128,256]{2,1,0:T(8,128)(2,1)S(1)}, u32[]{:S(2)}, u32[]{:S(2)}) collective-permute-start(bf16[4,128,256]{2,1,0:T(8,128)(2,1)S(1)} %get-tuple-element.27), channel_id=1, source_target_pairs={{0,16},{8,24},{16,0},{24,8},{1,17},{9,25},{17,1},{25,9},{2,18},{10... | collective-permute-start | bytes 786440 | tf_op jit(solution)/shard_map/ppermute | solution.py:624
  42.1 11.3 %collective-permute-start.4 = (bf16[4,128,256]{2,1,0:T(8,128)(2,1)S(1)}, bf16[4,128,256]{2,1,0:T(8,128)(2,1)S(1)}, u32[]{:S(2)}, u32[]{:S(2)}) collective-permute-start(bf16[4,128,256]{2,1,0:T(8,128)(2,1)S(1)} %get-tuple-element.28), channel_id=1, source_target_pairs={{0,24},{8,16},{16,8},{24,0},{1,25},{9,17},{17,9},{25,1},{2,26},{10... | collective-permute-start | bytes 786440 | tf_op jit(solution)/shard_map/ppermute | solution.py:624
  73.8 9.2 %collective-permute-start.5 = (bf16[4,128,256]{2,1,0:T(8,128)(2,1)S(1)}, bf16[4,128,256]{2,1,0:T(8,128)(2,1)S(1)}, u32[]{:S(2)}, u32[]{:S(2)}) collective-permute-start(bf16[4,128,256]{2,1,0:T(8,128)(2,1)S(1)} %get-tuple-element.30), channel_id=1, source_target_pairs={{0,8},{8,0},{16,24},{24,16},{1,9},{9,1},{17,25},{25,17},{2,10},{10... | collective-permute-start | bytes 786440 | tf_op jit(solution)/shard_map/ppermute | solution.py:624
  74.7 13.4 %collective-permute-start.6 = (bf16[4,128,256]{2,1,0:T(8,128)(2,1)S(1)}, bf16[4,128,256]{2,1,0:T(8,128)(2,1)S(1)}, u32[]{:S(2)}, u32[]{:S(2)}) collective-permute-start(bf16[4,128,256]{2,1,0:T(8,128)(2,1)S(1)} %get-tuple-element.31), channel_id=1, source_target_pairs={{0,16},{8,24},{16,0},{24,8},{1,17},{9,25},{17,1},{25,9},{2,18},{10... | collective-permute-start | bytes 786440 | tf_op jit(solution)/shard_map/ppermute | solution.py:624
  75.4 12.7 %collective-permute-start.7 = (bf16[4,128,256]{2,1,0:T(8,128)(2,1)S(1)}, bf16[4,128,256]{2,1,0:T(8,128)(2,1)S(1)}, u32[]{:S(2)}, u32[]{:S(2)}) collective-permute-start(bf16[4,128,256]{2,1,0:T(8,128)(2,1)S(1)} %get-tuple-element.32), channel_id=1, source_target_pairs={{0,24},{8,16},{16,8},{24,0},{1,25},{9,17},{17,9},{25,1},{2,26},{10... | collective-permute-start | bytes 786440 | tf_op jit(solution)/shard_map/ppermute | solution.py:624

commit v16 on v15

--- a/solution.py
+++ b/solution.py
@@ -53,33 +53,6 @@
 
 def smem_spec():
     return pl.BlockSpec(memory_space=pltpu.SMEM)
-
-
-def edges_kernel(own_ref, head_ref, tail_ref, sems):
-    reach = head_ref.shape[1]
-    rows = own_ref.shape[1]
-    copies = [
-        pltpu.make_async_copy(own_ref.at[:, pl.ds(lower, reach), :], ref, sems.at[which])
-        for which, (lower, ref) in enumerate(((rows - reach, tail_ref), (0, head_ref)))
-    ]
-    for copy in copies:
-        copy.start()
-    for copy in copies:
-        copy.wait()
-
-
-def edges(own, reach):
-    members, _, feat_width = own.shape
-    return pl.pallas_call(
-        edges_kernel,
-        out_shape=[jax.ShapeDtypeStruct((members, reach, feat_width), own.dtype)] * 2,
-        in_specs=[pl.BlockSpec(memory_space=pl.ANY)],
-        out_specs=[vmem_spec()] * 2,
-        scratch_shapes=[pltpu.SemaphoreType.DMA((2,))],
-        compiler_params=pltpu.CompilerParams(vmem_limit_bytes=VMEM_LIMIT),
-        cost_estimate=pl.CostEstimate(flops=0, bytes_accessed=8 * members * reach * feat_width, transcendentals=0),
-        name="edges",
-    )(own)
 
 
 def sample_grid_kernel(start_ref, token_ref, channel_ref, value_ref, var_ref, out_ref):
@@ -411,7 +384,7 @@
     for lower in range(0, w_gate_ref.shape[1], HIDDEN_CHUNK):
         part = slice(lower, lower + HIDDEN_CHUNK)
         gate = 0.5 * dot(normed_mid, w_gate_ref[:, part])
-        hidden = (gate * (1.0 + jnp.tanh(gate)) * dot(normed_mid, w_up_ref[:, part])).astype(BF16)
+        hidden = (gate * (1.0 + jnp.tanh(gate.astype(BF16)).astype(F32)) * dot(normed_mid, w_up_ref[:, part])).astype(BF16)
         forecast += dot(hidden, down_weight_ref[part, :])
     forecast_buf[...] = forecast.astype(BF16)
     share_rows = out_refs[0].shape[1]
@@ -650,9 +623,8 @@
     first_pos = lax.axis_index("tok") * row_count
     up = [(i, i + 1) for i in range(tok_count - 1)]
     down = [(i + 1, i) for i in range(tok_count - 1)]
-    head, tail = edges(ens_state, WIN)
-    left = lax.ppermute(tail, "tok", up)
-    right = lax.ppermute(head, "tok", down)
+    left = lax.ppermute(ens_state[:, row_count - WIN :], "tok", up)
+    right = lax.ppermute(ens_state[:, :WIN], "tok", down)
     share_start = first_pos + lax.axis_index("mem") * share_rows
     grid = sample_grid(
         share_start.astype(jnp.int32).reshape(1), obs_token, obs_channel, obs_value, obs_var, share_rows, feat_width

time: 89.4 us -> 88.1 us (0.985)
  blocking collectives: 15.1 us -> 21.9 us
  local copies, waits for them, and re-layouts: 6.56 us -> 2.26 us
  waiting for transfers between devices: 20.7 us -> 17.4 us
    all_to_all x1, blocking collectives: 15.1 us -> 21.9 us  [local(): lax.all_to_all(jnp.broadcast_to(partial[None], (device_count, *partial.sh...]
    unnamed x36 -> x30, local copies, waits for them, and re-layouts: 6.55 us -> 0.08 us
    ppermute x6, waiting for transfers between devices: 20.7 us -> 17 us  [exchanged(): lax.ppermute(v, 'mem', [(i, i ^ part) for i in range(count)])]
    slice x0 -> x1, local copies, waits for them, and re-layouts: none -> 2.17 us  [local(): right = lax.ppermute(ens_state[:, :WIN], 'tok', down)]
where the time goes in v16:
time: 88.1 us; the launch traced here: 87.9 us
  Pallas kernels  35.3 us (40%)
  blocking collectives  21.9 us (25%)
  waiting for transfers between devices  17.4 us (20%)
  starting transfers between devices  10.8 us (12%)
  local copies, waits for them, and re-layouts  2.26 us (3%)
    pallas_call x1, Pallas kernels, forward(): pl.pallas_call(functools.partial(forward_kernel, total_len), grid=(member...  23.6 us
    all_to_all x1, blocking collectives, local(): lax.all_to_all(jnp.broadcast_to(partial[None], (device_count, *partial.sh...  21.9 us
    ppermute x6, waiting for transfers between devices, exchanged(): lax.ppermute(v, 'mem', [(i, i ^ part) for i in range(count)])  17 us
    ppermute x6, starting transfers between devices, exchanged(): lax.ppermute(v, 'mem', [(i, i ^ part) for i in range(count)])  7.11 us
    pallas_call x1, Pallas kernels, inner(): pl.pallas_call(inner_kernel, grid=(members,), out_shape=[jax.ShapeDtypeSt...  4.06 us
    pallas_call x1, Pallas kernels, combine(): pl.pallas_call(combine_kernel, out_shape=[jax.ShapeDtypeStruct(v.shape, B...  3.64 us
    ppermute x1, starting transfers between devices, local(): left = lax.ppermute(ens_state[:, row_count - WIN:], 'tok', up)  2.39 us
    slice x1, local copies, waits for them, and re-layouts, local(): right = lax.ppermute(ens_state[:, :WIN], 'tok', down)  2.17 us
  transfers between devices with their start and end apart: 8, of which 5 were waited for; matrix products, arithmetic and copies ran while one was open for 0% of the time, Pallas kernels for 6%

profile of v16, /device:TPU:0, one launch (start us, length us, event | category | flops | bytes accessed | tf_op | source)
XLA Modules:
  0.0 87.9 jit_solution(14181271461388087355)
XLA Ops:
  0.0 2.2 %fusion = (bf16[4,256,256]{2,1,0:T(8,128)(2,1)S(1)}, bf16[4,256,256]{2,1,0:T(8,128)(2,1)}) fusion(bf16[4,512,256]{2,1,0:T(8,128)(2,1)} %state_ref.1), kind=kLoop, calls=%fused_computation | loop fusion | bytes 2097152 | tf_op jit(solution)/shard_map/slice | solution.py:627
  2.2 2.4 %collective-permute-start = (bf16[4,256,256]{2,1,0:T(8,128)(2,1)}, bf16[4,256,256]{2,1,0:T(8,128)(2,1)S(1)}, u32[]{:S(2)}, u32[]{:S(2)}) collective-permute-start(bf16[4,256,256]{2,1,0:T(8,128)(2,1)} %get-tuple-element.30), channel_id=1, source_target_pairs={{0,1},{1,2},{2,3},{3,4},{4,5},{5,6},{6,7},{8,9},{9,10},{10,11},{11... | collective-permute-start | bytes 1572872 | tf_op jit(solution)/shard_map/ppermute | solution.py:626
  4.6 1.3 %collective-permute-start.1 = (bf16[4,256,256]{2,1,0:T(8,128)(2,1)S(1)}, bf16[4,256,256]{2,1,0:T(8,128)(2,1)S(1)}, u32[]{:S(2)}, u32[]{:S(2)}) collective-permute-start(bf16[4,256,256]{2,1,0:T(8,128)(2,1)S(1)} %get-tuple-element.29), channel_id=1, source_target_pairs={{1,0},{2,1},{3,2},{4,3},{5,4},{6,5},{7,6},{9,8},{10,9},{11,10},{12... | collective-permute-start | bytes 1572872 | tf_op jit(solution)/shard_map/ppermute | solution.py:627
  6.0 0.0 copy-start.1
  6.0 0.0 copy-start.2
  6.0 0.0 copy-start.3
  6.0 0.0 copy-start.7
  6.0 0.0 copy-start.13
  6.0 4.1 %inner.1 = (bf16[4,512,256]{2,1,0:T(8,128)(2,1)S(1)}, f32[4,8,128]{2,1,0:T(8,128)S(1)}, f32[4,512,256]{2,1,0:T(8,128)S(1)}, f32[4,512,256]{2,1,0:T(8,128)S(1)}) custom-call(s32[4]{0:T(128)S(1)} %copy-done.14, bf16[4,512,256]{2,1,0:T(8,128)(2,1)S(1)} %copy-done, f32[1,256]{1,0:T(1,128)S(1)} %bitcast.13, bf16[256,256]{1,0:T(8,128)(2,1)S(1)} %copy-done.4, ...), custom_call_target="tpu_custom_call" | custom-call | flops 5100273664 | bytes 7340032 | tf_op jit(solution)/shard_map/inner/pallas_call | solution.py:244
  10.1 0.5 collective-permute-done.1.right_ref
  10.6 0.0 copy-start.8
  10.6 0.0 copy-start.9
  10.6 0.0 copy-start.10
  10.6 0.0 copy-start.11
  10.6 23.6 %forward.1 = (bf16[4,128,256]{2,1,0:T(8,128)(2,1)S(1)}, bf16[4,128,256]{2,1,0:T(8,128)(2,1)S(1)}, bf16[4,128,256]{2,1,0:T(8,128)(2,1)S(1)}, bf16[4,128,256]{2,1,0:T(8,128)(2,1)S(1)}) custom-call(s32[1]{0:T(128)} %bitcast.1.tok_ref, s32[1]{0:T(128)} %bitcast.mem_ref.index_ref, s32[4]{0:T(128)S(1)} %copy-done.14, bf16[4,512,256]{2,1,0:T(8,128)(2,1)S(1)} %copy-done, ...), custom_call_target="tpu_custom_call" | custom-call | flops 5100273664 | bytes 5242880 | tf_op jit(solution)/shard_map/forward/pallas_call | solution.py:406
  34.2 1.9 %collective-permute-start.2 = (bf16[4,128,256]{2,1,0:T(8,128)(2,1)S(1)}, bf16[4,128,256]{2,1,0:T(8,128)(2,1)S(1)}, u32[]{:S(2)}, u32[]{:S(2)}) collective-permute-start(bf16[4,128,256]{2,1,0:T(8,128)(2,1)S(1)} %get-tuple-element.22), channel_id=1, source_target_pairs={{0,8},{8,0},{16,24},{24,16},{1,9},{9,1},{17,25},{25,17},{2,10},{10... | collective-permute-start | bytes 786440 | tf_op jit(solution)/shard_map/ppermute | solution.py:597
  36.2 1.5 %collective-permute-start.3 = (bf16[4,128,256]{2,1,0:T(8,128)(2,1)S(1)}, bf16[4,128,256]{2,1,0:T(8,128)(2,1)S(1)}, u32[]{:S(2)}, u32[]{:S(2)}) collective-permute-start(bf16[4,128,256]{2,1,0:T(8,128)(2,1)S(1)} %get-tuple-element.23), channel_id=1, source_target_pairs={{0,16},{8,24},{16,0},{24,8},{1,17},{9,25},{17,1},{25,9},{2,18},{10... | collective-permute-start | bytes 786440 | tf_op jit(solution)/shard_map/ppermute | solution.py:597
  37.7 0.1 collective-permute-start.4
  37.8 1.3 %sample_grid.1.refs_4_ = f32[2,128,256]{2,1,0:T(8,128)S(1)} custom-call(s32[1]{0:T(128)} %bitcast.4.start_ref, s32[1,4096]{1,0:T(1,128)S(1)} %bitcast.9, s32[1,4096]{1,0:T(1,128)S(1)} %bitcast.10, f32[1,4096]{1,0:T(1,128)S(1)} %bitcast.11, f32[1,4096]{1,0:T(1,128)S(1)} %bitcast.12), custom_call_target="tpu_custom_call" | custom-call | flops 1073741824 | bytes 65536 | tf_op jit(solution)/shard_map/sample_grid/pallas_call | solution.py:81
  39.1 1.5 %collective-permute-done.2.refs_1_ = bf16[4,128,256]{2,1,0:T(8,128)(2,1)S(1)} collective-permute-done((bf16[4,128,256]{2,1,0:T(8,128)(2,1)S(1)}, bf16[4,128,256]{2,1,0:T(8,128)(2,1)S(1)}, u32[]{:S(2)}, u32[]{:S(2)}) %collective-permute-start.2) | collective-permute-done | bytes 262176 | tf_op jit(solution)/shard_map/ppermute | solution.py:597
  40.7 4.7 %collective-permute-done.3.refs_2_ = bf16[4,128,256]{2,1,0:T(8,128)(2,1)S(1)} collective-permute-done((bf16[4,128,256]{2,1,0:T(8,128)(2,1)S(1)}, bf16[4,128,256]{2,1,0:T(8,128)(2,1)S(1)}, u32[]{:S(2)}, u32[]{:S(2)}) %collective-permute-start.3) | collective-permute-done | bytes 262176 | tf_op jit(solution)/shard_map/ppermute | solution.py:597
  45.4 0.0 collective-permute-done.4.refs_3_
  45.4 1.7 %gram.1 = f32[8,128]{1,0:T(8,128)S(1)} custom-call(s32[1]{0:T(128)} %bitcast.mem_ref.index_ref, bf16[4,128,256]{2,1,0:T(8,128)(2,1)S(1)} %get-tuple-element.21.refs_0_, bf16[4,128,256]{2,1,0:T(8,128)(2,1)S(1)} %collective-permute-done.2.refs_1_, bf16[4,128,256]{2,1,0:T(8,128)(2,1)S(1)} %collective-permute-done.3.refs_2_, ...), custom_call_target="tpu_custom_call" | custom-call | flops 805306368 | bytes 1048576 | tf_op jit(solution)/shard_map/gram/pallas_call | solution.py:473
  47.1 21.9 %all_to_all.5.partial_ref = f32[32,8,128]{2,1,0:T(8,128)S(1)} all-to-all(f32[32,8,128]{2,1,0:T(8,128)S(1)} %broadcast_in_dim.2), channel_id=1, replica_groups=mesh['mem'=4,'tok'=8] {'mem','tok'}, dimensions={0} | all-to-all | bytes 262144 | tf_op jit(solution)/shard_map/all_to_all | solution.py:643
  69.0 3.6 %combine.1 = (bf16[4,128,256]{2,1,0:T(8,128)(2,1)S(1)}, bf16[4,128,256]{2,1,0:T(8,128)(2,1)S(1)}, bf16[4,128,256]{2,1,0:T(8,128)(2,1)S(1)}, bf16[4,128,256]{2,1,0:T(8,128)(2,1)S(1)}) custom-call(s32[1]{0:T(128)} %bitcast.mem_ref.index_ref, f32[32,8,128]{2,1,0:T(8,128)S(1)} %all_to_all.5.partial_ref, bf16[4,128,256]{2,1,0:T(8,128)(2,1)S(1)} %get-tuple-element.21.refs_0_, ...), custom_call_target="tpu_custom_call" | custom-call | flops 536870912 | bytes 2097152 | tf_op jit(solution)/shard_map/combine/pallas_call | solution.py:556
  72.6 0.9 %collective-permute-start.5 = (bf16[4,128,256]{2,1,0:T(8,128)(2,1)S(1)}, bf16[4,128,256]{2,1,0:T(8,128)(2,1)S(1)}, u32[]{:S(2)}, u32[]{:S(2)}) collective-permute-start(bf16[4,128,256]{2,1,0:T(8,128)(2,1)S(1)} %get-tuple-element.26), channel_id=1, source_target_pairs={{0,8},{8,0},{16,24},{24,16},{1,9},{9,1},{17,25},{25,17},{2,10},{10... | collective-permute-start | bytes 786440 | tf_op jit(solution)/shard_map/ppermute | solution.py:597
  73.5 0.7 collective-permute-start.6
  74.2 2.0 %collective-permute-start.7 = (bf16[4,128,256]{2,1,0:T(8,128)(2,1)S(1)}, bf16[4,128,256]{2,1,0:T(8,128)(2,1)S(1)}, u32[]{:S(2)}, u32[]{:S(2)}) collective-permute-start(bf16[4,128,256]{2,1,0:T(8,128)(2,1)S(1)} %get-tuple-element.28), channel_id=1, source_target_pairs={{0,24},{8,16},{16,8},{24,0},{1,25},{9,17},{17,9},{25,1},{2,26},{10... | collective-permute-start | bytes 786440 | tf_op jit(solution)/shard_map/ppermute | solution.py:597
  76.2 5.6 %collective-permute-done.5.refs_1_ = bf16[4,128,256]{2,1,0:T(8,128)(2,1)S(1)} collective-permute-done((bf16[4,128,256]{2,1,0:T(8,128)(2,1)S(1)}, bf16[4,128,256]{2,1,0:T(8,128)(2,1)S(1)}, u32[]{:S(2)}, u32[]{:S(2)}) %collective-permute-start.5) | collective-permute-done | bytes 262176 | tf_op jit(solution)/shard_map/ppermute | solution.py:597
  81.8 5.1 %collective-permute-done.6.refs_2_ = bf16[4,128,256]{2,1,0:T(8,128)(2,1)S(1)} collective-permute-done((bf16[4,128,256]{2,1,0:T(8,128)(2,1)S(1)}, bf16[4,128,256]{2,1,0:T(8,128)(2,1)S(1)}, u32[]{:S(2)}, u32[]{:S(2)}) %collective-permute-start.6) | collective-permute-done | bytes 262176 | tf_op jit(solution)/shard_map/ppermute | solution.py:597
  86.9 0.0 collective-permute-done.7.refs_3_
  86.9 1.0 %assemble.1 = bf16[4,512,256]{2,1,0:T(8,128)(2,1)} custom-call(s32[1]{0:T(128)} %bitcast.mem_ref.index_ref, bf16[4,128,256]{2,1,0:T(8,128)(2,1)S(1)} %get-tuple-element.25.refs_0_, bf16[4,128,256]{2,1,0:T(8,128)(2,1)S(1)} %collective-permute-done.5.refs_1_, bf16[4,128,256]{2,1,0:T(8,128)(2,1)S(1)} %collective-permute-done.6.refs_2_, ...), custom_call_target="tpu_custom_call" | custom-call | bytes 2097152 | tf_op jit(solution)/shard_map/assemble/pallas_call | solution.py:582
  (23 shorter events, 0.1 us)
Async XLA Ops:
  0.0 5.9 %copy-start = (bf16[4,512,256]{2,1,0:T(8,128)(2,1)S(1)}, bf16[4,512,256]{2,1,0:T(8,128)(2,1)}, u32[]{:S(2)}) copy-start(bf16[4,512,256]{2,1,0:T(8,128)(2,1)} %state_ref.1) | copy-start | bytes 3145732
  0.0 5.9 %copy-start.12 = (f32[256]{0:T(256)S(1)}, f32[256]{0:T(256)}, u32[]{:S(2)}) copy-start(f32[256]{0:T(256)} %param.16) | copy-start | bytes 3076
  0.0 5.9 %copy-start.4 = (bf16[256,256]{1,0:T(8,128)(2,1)S(1)}, bf16[256,256]{1,0:T(8,128)(2,1)}, u32[]{:S(2)}) copy-start(bf16[256,256]{1,0:T(8,128)(2,1)} %w_query_ref.1) | copy-start | bytes 393220
  0.0 5.9 %copy-start.5 = (bf16[256,256]{1,0:T(8,128)(2,1)S(1)}, bf16[256,256]{1,0:T(8,128)(2,1)}, u32[]{:S(2)}) copy-start(bf16[256,256]{1,0:T(8,128)(2,1)} %w_key_ref.3) | copy-start | bytes 393220
  0.0 5.9 %copy-start.6 = (bf16[256,256]{1,0:T(8,128)(2,1)S(1)}, bf16[256,256]{1,0:T(8,128)(2,1)}, u32[]{:S(2)}) copy-start(bf16[256,256]{1,0:T(8,128)(2,1)} %w_value_ref.3) | copy-start | bytes 393220
  0.0 5.9 %copy-start.14 = (s32[4]{0:T(128)S(1)}, s32[4]{0:T(128)}, u32[]{:S(2)}) copy-start(s32[4]{0:T(128)} %window_ref.3) | copy-start | bytes 52
  2.2 7.9 %collective-permute-start = (bf16[4,256,256]{2,1,0:T(8,128)(2,1)}, bf16[4,256,256]{2,1,0:T(8,128)(2,1)S(1)}, u32[]{:S(2)}, u32[]{:S(2)}) collective-permute-start(bf16[4,256,256]{2,1,0:T(8,128)(2,1)} %get-tuple-element.30), channel_id=1, source_target_pairs={{0,1},{1,2},{2,3},{3,4},{4,5},{5,6},{6,7},{8,9},{9,10},{10,11},{11... | collective-permute-start | bytes 1572872 | tf_op jit(solution)/shard_map/ppermute | solution.py:626
  4.6 6.0 %collective-permute-start.1 = (bf16[4,256,256]{2,1,0:T(8,128)(2,1)S(1)}, bf16[4,256,256]{2,1,0:T(8,128)(2,1)S(1)}, u32[]{:S(2)}, u32[]{:S(2)}) collective-permute-start(bf16[4,256,256]{2,1,0:T(8,128)(2,1)S(1)} %get-tuple-element.29), channel_id=1, source_target_pairs={{1,0},{2,1},{3,2},{4,3},{5,4},{6,5},{7,6},{9,8},{10,9},{11,10},{12... | collective-permute-start | bytes 1572872 | tf_op jit(solution)/shard_map/ppermute | solution.py:627
  6.0 4.6 %copy-start.1 = (bf16[256,1024]{1,0:T(8,128)(2,1)S(1)}, bf16[256,1024]{1,0:T(8,128)(2,1)}, u32[]{:S(2)}) copy-start(bf16[256,1024]{1,0:T(8,128)(2,1)} %w_gate_ref.1) | copy-start | bytes 1572868
  6.0 4.6 %copy-start.2 = (bf16[256,1024]{1,0:T(8,128)(2,1)S(1)}, bf16[256,1024]{1,0:T(8,128)(2,1)}, u32[]{:S(2)}) copy-start(bf16[256,1024]{1,0:T(8,128)(2,1)} %w_up_ref.1) | copy-start | bytes 1572868
  6.0 4.6 %copy-start.3 = (bf16[1024,256]{1,0:T(8,128)(2,1)S(1)}, bf16[1024,256]{1,0:T(8,128)(2,1)}, u32[]{:S(2)}) copy-start(bf16[1024,256]{1,0:T(8,128)(2,1)} %down_weight_ref.1) | copy-start | bytes 1572868
  6.0 4.6 %copy-start.7 = (bf16[256,256]{1,0:T(8,128)(2,1)S(1)}, bf16[256,256]{1,0:T(8,128)(2,1)}, u32[]{:S(2)}) copy-start(bf16[256,256]{1,0:T(8,128)(2,1)} %w_out_ref.1) | copy-start | bytes 393220
  6.0 4.6 %copy-start.13 = (f32[256]{0:T(256)S(1)}, f32[256]{0:T(256)}, u32[]{:S(2)}) copy-start(f32[256]{0:T(256)} %param.17) | copy-start | bytes 3076
  10.6 27.2 %copy-start.8 = (s32[4096]{0:T(1024)S(1)}, s32[4096]{0:T(1024)}, u32[]{:S(2)}) copy-start(s32[4096]{0:T(1024)} %param.26) | copy-start | bytes 49156
  10.6 27.2 %copy-start.9 = (s32[4096]{0:T(1024)S(1)}, s32[4096]{0:T(1024)}, u32[]{:S(2)}) copy-start(s32[4096]{0:T(1024)} %param.27) | copy-start | bytes 49156
  10.6 27.2 %copy-start.10 = (f32[4096]{0:T(1024)S(1)}, f32[4096]{0:T(1024)}, u32[]{:S(2)}) copy-start(f32[4096]{0:T(1024)} %param.28) | copy-start | bytes 49156
  10.6 27.2 %copy-start.11 = (f32[4096]{0:T(1024)S(1)}, f32[4096]{0:T(1024)}, u32[]{:S(2)}) copy-start(f32[4096]{0:T(1024)} %param.29) | copy-start | bytes 49156
  34.2 6.4 %collective-permute-start.2 = (bf16[4,128,256]{2,1,0:T(8,128)(2,1)S(1)}, bf16[4,128,256]{2,1,0:T(8,128)(2,1)S(1)}, u32[]{:S(2)}, u32[]{:S(2)}) collective-permute-start(bf16[4,128,256]{2,1,0:T(8,128)(2,1)S(1)} %get-tuple-element.22), channel_id=1, source_target_pairs={{0,8},{8,0},{16,24},{24,16},{1,9},{9,1},{17,25},{25,17},{2,10},{10... | collective-permute-start | bytes 786440 | tf_op jit(solution)/shard_map/ppermute | solution.py:597
  36.2 9.2 %collective-permute-start.3 = (bf16[4,128,256]{2,1,0:T(8,128)(2,1)S(1)}, bf16[4,128,256]{2,1,0:T(8,128)(2,1)S(1)}, u32[]{:S(2)}, u32[]{:S(2)}) collective-permute-start(bf16[4,128,256]{2,1,0:T(8,128)(2,1)S(1)} %get-tuple-element.23), channel_id=1, source_target_pairs={{0,16},{8,24},{16,0},{24,8},{1,17},{9,25},{17,1},{25,9},{2,18},{10... | collective-permute-start | bytes 786440 | tf_op jit(solution)/shard_map/ppermute | solution.py:597
  37.7 7.7 %collective-permute-start.4 = (bf16[4,128,256]{2,1,0:T(8,128)(2,1)S(1)}, bf16[4,128,256]{2,1,0:T(8,128)(2,1)S(1)}, u32[]{:S(2)}, u32[]{:S(2)}) collective-permute-start(bf16[4,128,256]{2,1,0:T(8,128)(2,1)S(1)} %get-tuple-element.24), channel_id=1, source_target_pairs={{0,24},{8,16},{16,8},{24,0},{1,25},{9,17},{17,9},{25,1},{2,26},{10... | collective-permute-start | bytes 786440 | tf_op jit(solution)/shard_map/ppermute | solution.py:597
  72.6 9.2 %collective-permute-start.5 = (bf16[4,128,256]{2,1,0:T(8,128)(2,1)S(1)}, bf16[4,128,256]{2,1,0:T(8,128)(2,1)S(1)}, u32[]{:S(2)}, u32[]{:S(2)}) collective-permute-start(bf16[4,128,256]{2,1,0:T(8,128)(2,1)S(1)} %get-tuple-element.26), channel_id=1, source_target_pairs={{0,8},{8,0},{16,24},{24,16},{1,9},{9,1},{17,25},{25,17},{2,10},{10... | collective-permute-start | bytes 786440 | tf_op jit(solution)/shard_map/ppermute | solution.py:597
  73.5 13.4 %collective-permute-start.6 = (bf16[4,128,256]{2,1,0:T(8,128)(2,1)S(1)}, bf16[4,128,256]{2,1,0:T(8,128)(2,1)S(1)}, u32[]{:S(2)}, u32[]{:S(2)}) collective-permute-start(bf16[4,128,256]{2,1,0:T(8,128)(2,1)S(1)} %get-tuple-element.27), channel_id=1, source_target_pairs={{0,16},{8,24},{16,0},{24,8},{1,17},{9,25},{17,1},{25,9},{2,18},{10... | collective-permute-start | bytes 786440 | tf_op jit(solution)/shard_map/ppermute | solution.py:597
  74.2 12.7 %collective-permute-start.7 = (bf16[4,128,256]{2,1,0:T(8,128)(2,1)S(1)}, bf16[4,128,256]{2,1,0:T(8,128)(2,1)S(1)}, u32[]{:S(2)}, u32[]{:S(2)}) collective-permute-start(bf16[4,128,256]{2,1,0:T(8,128)(2,1)S(1)} %get-tuple-element.28), channel_id=1, source_target_pairs={{0,24},{8,16},{16,8},{24,0},{1,25},{9,17},{17,9},{25,1},{2,26},{10... | collective-permute-start | bytes 786440 | tf_op jit(solution)/shard_map/ppermute | solution.py:597

commit v17 on v16

--- a/solution.py
+++ b/solution.py
@@ -15,7 +15,8 @@
 GROUP = 16
 LANES = 128
 VMEM_LIMIT = 32 * 1024 * 1024
-SAFE_SCORE = 56.0
+SAFE_SCORE = 100.0
+FOLD = 4
 HIDDEN_CHUNK = 256
 
 F32 = jnp.float32
@@ -40,11 +41,7 @@
 
 
 def rms_scaled(values, gain):
-    rows, width = values.shape
-    ones = jnp.ones((width, LANES), BF16)
-    means = dot((values * values).astype(BF16), ones) * (1.0 / width)
-    scale = lax.rsqrt(means + EPS)
-    return values * jnp.concatenate([scale] * (width // LANES), axis=1) * gain
+    return values * lax.rsqrt(jnp.mean(values * values, axis=-1, keepdims=True) + EPS) * gain
 
 
 def vmem_spec():
@@ -94,9 +91,13 @@
     return (lane_head == iota((feat_width, LANES), 1)).astype(F32).astype(BF16)
 
 
-def largest_norms(values, heads):
-    squares = dot((values * values).astype(BF16), head_lanes(values.shape[1], heads))
-    return jnp.max(squares, axis=0, keepdims=True)
+def norm_bounds(values, heads):
+    rows = values.shape[0] // FOLD
+    squares = values * values
+    folded = squares[:rows]
+    for part in range(1, FOLD):
+        folded = jnp.maximum(folded, squares[part * rows : (part + 1) * rows])
+    return jnp.max(dot(folded.astype(BF16), head_lanes(values.shape[1], heads)), axis=0, keepdims=True)
 
 
 def is_safe(query_norms, key_norms):
@@ -201,7 +202,7 @@
     query_ref[0] = query_rows.astype(BF16)
     key_buf[...] = key_rows.astype(BF16).T
     put_values(value_buf, 0, dot(normed, w_value_ref[...]).astype(BF16))
-    query_norms, key_norms = largest_norms(query_rows, heads), largest_norms(key_rows, heads)
+    query_norms, key_norms = norm_bounds(query_rows, heads), norm_bounds(key_rows, heads)
     blank = jnp.zeros((norm_ref.shape[1] - 2, LANES), F32)
     norm_ref[0] = jnp.concatenate([query_norms, key_norms, blank], axis=0)
 
@@ -314,13 +315,15 @@
     def values_of(normed):
         return dot(normed, w_value_ref[...]).astype(BF16)
 
-    key_norms = norm_ref[0, 1:2, :]
-    for side, ref in enumerate((left_ref, right_ref)):
-        normed = rms_scaled(ref[0].astype(F32), attn_gain_ref[...]).astype(BF16)
-        keys = keys_of(normed)
-        key_norms = jnp.maximum(key_norms, largest_norms(keys, heads))
-        halo_key_buf[side] = keys.astype(BF16).T
-        put_values(halo_value_buf.at[side], 0, values_of(normed))
+    halo = jnp.concatenate([left_ref[0], right_ref[0]], axis=0)
+    normed = rms_scaled(halo.astype(F32), attn_gain_ref[...]).astype(BF16)
+    halo_keys = keys_of(normed)
+    halo_values = values_of(normed)
+    key_norms = jnp.maximum(norm_ref[0, 1:2, :], norm_bounds(halo_keys, heads))
+    for side in range(2):
+        here = slice(side * reach, (side + 1) * reach)
+        halo_key_buf[side] = halo_keys[here].astype(BF16).T
+        put_values(halo_value_buf.at[side], 0, halo_values[here])
     safe = is_safe(norm_ref[0, 0:1, :], key_norms)
 
     @pl.when(safe)
@@ -435,23 +438,27 @@
     own_members, rows, feat_width = share_refs[0].shape
     members = own_members * len(share_refs)
     index = index_ref[0]
-    stack = members * GROUP
-    total = jnp.zeros((stack, stack), F32)
-    proj = jnp.zeros((members, GROUP, feat_width), F32)
-    for lower in range(0, rows, GROUP):
-        part = slice(lower, lower + GROUP)
-        fields = jnp.concatenate([ref[:, part, :] for ref in share_refs], axis=0).astype(F32)
-        mean = jnp.sum(fields, axis=0) * (1.0 / members)
-        spread = fields - mean[None]
-        weight = grid_ref[0, part, :]
-        proj += spread * (grid_ref[1, part, :] - weight * mean)[None]
-        high, low = halves(spread.reshape(stack, feat_width))
-        w_high, w_low = halves((spread * weight[None]).reshape(stack, feat_width))
-        last = ((1,), (1,))
-        total += dot(w_high, high, last) + dot(w_high, low, last) + dot(w_low, high, last)
-    same = iota((stack, stack), 0) % GROUP == iota((stack, stack), 1) % GROUP
-    by_row = jnp.sum(jnp.where(same, total, 0.0).reshape(members, GROUP, stack), axis=1)
-    column = global_member(iota((stack, LANES), 0) // GROUP, index, own_members)
+    tokens = GROUP // 2
+    stack = members * tokens
+    total = jnp.zeros((stack, 2 * stack), F32)
+    proj = jnp.zeros((members, tokens, feat_width), F32)
+    for first in range(0, rows, GROUP):
+        loaded = jnp.concatenate([ref[:, first : first + GROUP, :] for ref in share_refs], axis=0).astype(F32)
+        for lower in range(0, GROUP, tokens):
+            fields = loaded[:, lower : lower + tokens, :]
+            mean = jnp.sum(fields, axis=0) * (1.0 / members)
+            spread = fields - mean[None]
+            part = slice(first + lower, first + lower + tokens)
+            weight = grid_ref[0, part, :]
+            proj += spread * (grid_ref[1, part, :] - weight * mean)[None]
+            both = jnp.concatenate(halves(spread.reshape(stack, feat_width)), axis=0)
+            w_high, w_low = halves((spread * weight[None]).reshape(stack, feat_width))
+            last = ((1,), (1,))
+            total += dot(w_high, both, last) + dot(w_low, both, last)
+    total = total[:, :stack] + total[:, stack:]
+    same = iota((stack, stack), 0) % tokens == iota((stack, stack), 1) % tokens
+    by_row = jnp.sum(jnp.where(same, total, 0.0).reshape(members, tokens, stack), axis=1)
+    column = global_member(iota((stack, LANES), 0) // tokens, index, own_members)
     folded = (column == iota((stack, LANES), 1) % members).astype(F32)
     held = global_member(iota((members, members), 1), index, own_members)
     in_order = (held == iota((members, members), 0)).astype(F32)

time: 88.1 us -> 86.9 us (0.986)
  Pallas kernels: 35.3 us -> 33.4 us
    pallas_call x1, Pallas kernels: 23.6 us -> 22.1 us  [forward(): pl.pallas_call(functools.partial(forward_kernel, total_len), grid=(member...]
  transfers between devices with their start and end apart: 8 -> 8, of which waited for: 5 -> 5; matrix products, arithmetic and copies ran while one was open for 0% -> 0% of each run, Pallas kernels for 6% -> 5%
where the time goes in v17:
time: 86.9 us; the launch traced here: 86.7 us
  Pallas kernels  33.4 us (38%)
  blocking collectives  22.3 us (26%)
  waiting for transfers between devices  17.7 us (20%)
  starting transfers between devices  10.8 us (12%)
  local copies, waits for them, and re-layouts  2.26 us (3%)
    all_to_all x1, blocking collectives, local(): lax.all_to_all(jnp.broadcast_to(partial[None], (device_count, *partial.sh...  22.3 us
    pallas_call x1, Pallas kernels, forward(): pl.pallas_call(functools.partial(forward_kernel, total_len), grid=(member...  22.1 us
    ppermute x6, waiting for transfers between devices, exchanged(): lax.ppermute(v, 'mem', [(i, i ^ part) for i in range(count)])  16.5 us
    ppermute x6, starting transfers between devices, exchanged(): lax.ppermute(v, 'mem', [(i, i ^ part) for i in range(count)])  7.11 us
    pallas_call x1, Pallas kernels, combine(): pl.pallas_call(combine_kernel, out_shape=[jax.ShapeDtypeStruct(v.shape, B...  3.64 us
    pallas_call x1, Pallas kernels, inner(): pl.pallas_call(inner_kernel, grid=(members,), out_shape=[jax.ShapeDtypeSt...  3.39 us
    ppermute x1, starting transfers between devices, local(): left = lax.ppermute(ens_state[:, row_count - WIN:], 'tok', up)  2.39 us
    slice x1, local copies, waits for them, and re-layouts, local(): right = lax.ppermute(ens_state[:, :WIN], 'tok', down)  2.17 us
  transfers between devices with their start and end apart: 8, of which 5 were waited for; matrix products, arithmetic and copies ran while one was open for 0% of the time, Pallas kernels for 5%

profile of v17, /device:TPU:0, one launch (start us, length us, event | category | flops | bytes accessed | tf_op | source)
XLA Modules:
  0.0 86.7 jit_solution(7855042707410157768)
XLA Ops:
  0.0 2.2 %fusion = (bf16[4,256,256]{2,1,0:T(8,128)(2,1)S(1)}, bf16[4,256,256]{2,1,0:T(8,128)(2,1)}) fusion(bf16[4,512,256]{2,1,0:T(8,128)(2,1)} %state_ref.1), kind=kLoop, calls=%fused_computation | loop fusion | bytes 2097152 | tf_op jit(solution)/shard_map/slice | solution.py:634
  2.2 2.4 %collective-permute-start = (bf16[4,256,256]{2,1,0:T(8,128)(2,1)}, bf16[4,256,256]{2,1,0:T(8,128)(2,1)S(1)}, u32[]{:S(2)}, u32[]{:S(2)}) collective-permute-start(bf16[4,256,256]{2,1,0:T(8,128)(2,1)} %get-tuple-element.30), channel_id=1, source_target_pairs={{0,1},{1,2},{2,3},{3,4},{4,5},{5,6},{6,7},{8,9},{9,10},{10,11},{11... | collective-permute-start | bytes 1572872 | tf_op jit(solution)/shard_map/ppermute | solution.py:633
  4.6 1.3 %collective-permute-start.1 = (bf16[4,256,256]{2,1,0:T(8,128)(2,1)S(1)}, bf16[4,256,256]{2,1,0:T(8,128)(2,1)S(1)}, u32[]{:S(2)}, u32[]{:S(2)}) collective-permute-start(bf16[4,256,256]{2,1,0:T(8,128)(2,1)S(1)} %get-tuple-element.29), channel_id=1, source_target_pairs={{1,0},{2,1},{3,2},{4,3},{5,4},{6,5},{7,6},{9,8},{10,9},{11,10},{12... | collective-permute-start | bytes 1572872 | tf_op jit(solution)/shard_map/ppermute | solution.py:634
  6.0 0.0 copy-start.1
  6.0 0.0 copy-start.2
  6.0 0.0 copy-start.3
  6.0 0.0 copy-start.7
  6.0 0.0 copy-start.13
  6.0 3.4 %inner.1 = (bf16[4,512,256]{2,1,0:T(8,128)(2,1)S(1)}, f32[4,8,128]{2,1,0:T(8,128)S(1)}, f32[4,512,256]{2,1,0:T(8,128)S(1)}, f32[4,512,256]{2,1,0:T(8,128)S(1)}) custom-call(s32[4]{0:T(128)S(1)} %copy-done.14, bf16[4,512,256]{2,1,0:T(8,128)(2,1)S(1)} %copy-done, f32[1,256]{1,0:T(1,128)S(1)} %bitcast.13, bf16[256,256]{1,0:T(8,128)(2,1)S(1)} %copy-done.4, ...), custom_call_target="tpu_custom_call" | custom-call | flops 5100273664 | bytes 7340032 | tf_op jit(solution)/shard_map/inner/pallas_call | solution.py:245
  9.4 0.0 collective-permute-done.left_ref
  9.4 1.1 %collective-permute-done.1.right_ref = bf16[4,256,256]{2,1,0:T(8,128)(2,1)S(1)} collective-permute-done((bf16[4,256,256]{2,1,0:T(8,128)(2,1)S(1)}, bf16[4,256,256]{2,1,0:T(8,128)(2,1)S(1)}, u32[]{:S(2)}, u32[]{:S(2)}) %collective-permute-start.1) | collective-permute-done | bytes 524320 | tf_op jit(solution)/shard_map/ppermute | solution.py:634
  10.6 0.0 copy-start.8
  10.6 0.0 copy-start.9
  10.6 0.0 copy-start.10
  10.6 0.0 copy-start.11
  10.6 22.1 %forward.1 = (bf16[4,128,256]{2,1,0:T(8,128)(2,1)S(1)}, bf16[4,128,256]{2,1,0:T(8,128)(2,1)S(1)}, bf16[4,128,256]{2,1,0:T(8,128)(2,1)S(1)}, bf16[4,128,256]{2,1,0:T(8,128)(2,1)S(1)}) custom-call(s32[1]{0:T(128)} %bitcast.1.tok_ref, s32[1]{0:T(128)} %bitcast.mem_ref.index_ref, s32[4]{0:T(128)S(1)} %copy-done.14, bf16[4,512,256]{2,1,0:T(8,128)(2,1)S(1)} %copy-done, ...), custom_call_target="tpu_custom_call" | custom-call | flops 5100273664 | bytes 5242880 | tf_op jit(solution)/shard_map/forward/pallas_call | solution.py:409
  32.7 1.5 %collective-permute-start.2 = (bf16[4,128,256]{2,1,0:T(8,128)(2,1)S(1)}, bf16[4,128,256]{2,1,0:T(8,128)(2,1)S(1)}, u32[]{:S(2)}, u32[]{:S(2)}) collective-permute-start(bf16[4,128,256]{2,1,0:T(8,128)(2,1)S(1)} %get-tuple-element.22), channel_id=1, source_target_pairs={{0,8},{8,0},{16,24},{24,16},{1,9},{9,1},{17,25},{25,17},{2,10},{10... | collective-permute-start | bytes 786440 | tf_op jit(solution)/shard_map/ppermute | solution.py:604
  34.2 1.5 %collective-permute-start.3 = (bf16[4,128,256]{2,1,0:T(8,128)(2,1)S(1)}, bf16[4,128,256]{2,1,0:T(8,128)(2,1)S(1)}, u32[]{:S(2)}, u32[]{:S(2)}) collective-permute-start(bf16[4,128,256]{2,1,0:T(8,128)(2,1)S(1)} %get-tuple-element.23), channel_id=1, source_target_pairs={{0,16},{8,24},{16,0},{24,8},{1,17},{9,25},{17,1},{25,9},{2,18},{10... | collective-permute-start | bytes 786440 | tf_op jit(solution)/shard_map/ppermute | solution.py:604
  35.8 0.5 collective-permute-start.4
  36.3 1.3 %sample_grid.1.refs_4_ = f32[2,128,256]{2,1,0:T(8,128)S(1)} custom-call(s32[1]{0:T(128)} %bitcast.4.start_ref, s32[1,4096]{1,0:T(1,128)S(1)} %bitcast.9, s32[1,4096]{1,0:T(1,128)S(1)} %bitcast.10, f32[1,4096]{1,0:T(1,128)S(1)} %bitcast.11, f32[1,4096]{1,0:T(1,128)S(1)} %bitcast.12), custom_call_target="tpu_custom_call" | custom-call | flops 1073741824 | bytes 65536 | tf_op jit(solution)/shard_map/sample_grid/pallas_call | solution.py:78
  37.6 1.5 %collective-permute-done.2.refs_1_ = bf16[4,128,256]{2,1,0:T(8,128)(2,1)S(1)} collective-permute-done((bf16[4,128,256]{2,1,0:T(8,128)(2,1)S(1)}, bf16[4,128,256]{2,1,0:T(8,128)(2,1)S(1)}, u32[]{:S(2)}, u32[]{:S(2)}) %collective-permute-start.2) | collective-permute-done | bytes 262176 | tf_op jit(solution)/shard_map/ppermute | solution.py:604
  39.2 4.3 %collective-permute-done.3.refs_2_ = bf16[4,128,256]{2,1,0:T(8,128)(2,1)S(1)} collective-permute-done((bf16[4,128,256]{2,1,0:T(8,128)(2,1)S(1)}, bf16[4,128,256]{2,1,0:T(8,128)(2,1)S(1)}, u32[]{:S(2)}, u32[]{:S(2)}) %collective-permute-start.3) | collective-permute-done | bytes 262176 | tf_op jit(solution)/shard_map/ppermute | solution.py:604
  43.4 0.0 collective-permute-done.4.refs_3_
  43.4 2.0 %gram.1 = f32[8,128]{1,0:T(8,128)S(1)} custom-call(s32[1]{0:T(128)} %bitcast.mem_ref.index_ref, bf16[4,128,256]{2,1,0:T(8,128)(2,1)S(1)} %get-tuple-element.21.refs_0_, bf16[4,128,256]{2,1,0:T(8,128)(2,1)S(1)} %collective-permute-done.2.refs_1_, bf16[4,128,256]{2,1,0:T(8,128)(2,1)S(1)} %collective-permute-done.3.refs_2_, ...), custom_call_target="tpu_custom_call" | custom-call | flops 805306368 | bytes 1048576 | tf_op jit(solution)/shard_map/gram/pallas_call | solution.py:480
  45.5 22.3 %all_to_all.5.partial_ref = f32[32,8,128]{2,1,0:T(8,128)S(1)} all-to-all(f32[32,8,128]{2,1,0:T(8,128)S(1)} %broadcast_in_dim.2), channel_id=1, replica_groups=mesh['mem'=4,'tok'=8] {'mem','tok'}, dimensions={0} | all-to-all | bytes 262144 | tf_op jit(solution)/shard_map/all_to_all | solution.py:650
  67.8 3.6 %combine.1 = (bf16[4,128,256]{2,1,0:T(8,128)(2,1)S(1)}, bf16[4,128,256]{2,1,0:T(8,128)(2,1)S(1)}, bf16[4,128,256]{2,1,0:T(8,128)(2,1)S(1)}, bf16[4,128,256]{2,1,0:T(8,128)(2,1)S(1)}) custom-call(s32[1]{0:T(128)} %bitcast.mem_ref.index_ref, f32[32,8,128]{2,1,0:T(8,128)S(1)} %all_to_all.5.partial_ref, bf16[4,128,256]{2,1,0:T(8,128)(2,1)S(1)} %get-tuple-element.21.refs_0_, ...), custom_call_target="tpu_custom_call" | custom-call | flops 536870912 | bytes 2097152 | tf_op jit(solution)/shard_map/combine/pallas_call | solution.py:563
  71.4 0.9 %collective-permute-start.5 = (bf16[4,128,256]{2,1,0:T(8,128)(2,1)S(1)}, bf16[4,128,256]{2,1,0:T(8,128)(2,1)S(1)}, u32[]{:S(2)}, u32[]{:S(2)}) collective-permute-start(bf16[4,128,256]{2,1,0:T(8,128)(2,1)S(1)} %get-tuple-element.26), channel_id=1, source_target_pairs={{0,8},{8,0},{16,24},{24,16},{1,9},{9,1},{17,25},{25,17},{2,10},{10... | collective-permute-start | bytes 786440 | tf_op jit(solution)/shard_map/ppermute | solution.py:604
  72.3 0.7 collective-permute-start.6
  73.0 2.0 %collective-permute-start.7 = (bf16[4,128,256]{2,1,0:T(8,128)(2,1)S(1)}, bf16[4,128,256]{2,1,0:T(8,128)(2,1)S(1)}, u32[]{:S(2)}, u32[]{:S(2)}) collective-permute-start(bf16[4,128,256]{2,1,0:T(8,128)(2,1)S(1)} %get-tuple-element.28), channel_id=1, source_target_pairs={{0,24},{8,16},{16,8},{24,0},{1,25},{9,17},{17,9},{25,1},{2,26},{10... | collective-permute-start | bytes 786440 | tf_op jit(solution)/shard_map/ppermute | solution.py:604
  75.0 5.6 %collective-permute-done.5.refs_1_ = bf16[4,128,256]{2,1,0:T(8,128)(2,1)S(1)} collective-permute-done((bf16[4,128,256]{2,1,0:T(8,128)(2,1)S(1)}, bf16[4,128,256]{2,1,0:T(8,128)(2,1)S(1)}, u32[]{:S(2)}, u32[]{:S(2)}) %collective-permute-start.5) | collective-permute-done | bytes 262176 | tf_op jit(solution)/shard_map/ppermute | solution.py:604
  80.6 5.1 %collective-permute-done.6.refs_2_ = bf16[4,128,256]{2,1,0:T(8,128)(2,1)S(1)} collective-permute-done((bf16[4,128,256]{2,1,0:T(8,128)(2,1)S(1)}, bf16[4,128,256]{2,1,0:T(8,128)(2,1)S(1)}, u32[]{:S(2)}, u32[]{:S(2)}) %collective-permute-start.6) | collective-permute-done | bytes 262176 | tf_op jit(solution)/shard_map/ppermute | solution.py:604
  85.7 1.0 %assemble.1 = bf16[4,512,256]{2,1,0:T(8,128)(2,1)} custom-call(s32[1]{0:T(128)} %bitcast.mem_ref.index_ref, bf16[4,128,256]{2,1,0:T(8,128)(2,1)S(1)} %get-tuple-element.25.refs_0_, bf16[4,128,256]{2,1,0:T(8,128)(2,1)S(1)} %collective-permute-done.5.refs_1_, bf16[4,128,256]{2,1,0:T(8,128)(2,1)S(1)} %collective-permute-done.6.refs_2_, ...), custom_call_target="tpu_custom_call" | custom-call | bytes 2097152 | tf_op jit(solution)/shard_map/assemble/pallas_call | solution.py:589
  (23 shorter events, 0.1 us)
Async XLA Ops:
  0.0 5.9 %copy-start = (bf16[4,512,256]{2,1,0:T(8,128)(2,1)S(1)}, bf16[4,512,256]{2,1,0:T(8,128)(2,1)}, u32[]{:S(2)}) copy-start(bf16[4,512,256]{2,1,0:T(8,128)(2,1)} %state_ref.1) | copy-start | bytes 3145732
  0.0 5.9 %copy-start.12 = (f32[256]{0:T(256)S(1)}, f32[256]{0:T(256)}, u32[]{:S(2)}) copy-start(f32[256]{0:T(256)} %param.16) | copy-start | bytes 3076
  0.0 5.9 %copy-start.4 = (bf16[256,256]{1,0:T(8,128)(2,1)S(1)}, bf16[256,256]{1,0:T(8,128)(2,1)}, u32[]{:S(2)}) copy-start(bf16[256,256]{1,0:T(8,128)(2,1)} %w_query_ref.1) | copy-start | bytes 393220
  0.0 5.9 %copy-start.5 = (bf16[256,256]{1,0:T(8,128)(2,1)S(1)}, bf16[256,256]{1,0:T(8,128)(2,1)}, u32[]{:S(2)}) copy-start(bf16[256,256]{1,0:T(8,128)(2,1)} %w_key_ref.3) | copy-start | bytes 393220
  0.0 5.9 %copy-start.6 = (bf16[256,256]{1,0:T(8,128)(2,1)S(1)}, bf16[256,256]{1,0:T(8,128)(2,1)}, u32[]{:S(2)}) copy-start(bf16[256,256]{1,0:T(8,128)(2,1)} %w_value_ref.3) | copy-start | bytes 393220
  0.0 5.9 %copy-start.14 = (s32[4]{0:T(128)S(1)}, s32[4]{0:T(128)}, u32[]{:S(2)}) copy-start(s32[4]{0:T(128)} %window_ref.3) | copy-start | bytes 52
  2.2 7.2 %collective-permute-start = (bf16[4,256,256]{2,1,0:T(8,128)(2,1)}, bf16[4,256,256]{2,1,0:T(8,128)(2,1)S(1)}, u32[]{:S(2)}, u32[]{:S(2)}) collective-permute-start(bf16[4,256,256]{2,1,0:T(8,128)(2,1)} %get-tuple-element.30), channel_id=1, source_target_pairs={{0,1},{1,2},{2,3},{3,4},{4,5},{5,6},{6,7},{8,9},{9,10},{10,11},{11... | collective-permute-start | bytes 1572872 | tf_op jit(solution)/shard_map/ppermute | solution.py:633
  4.6 6.0 %collective-permute-start.1 = (bf16[4,256,256]{2,1,0:T(8,128)(2,1)S(1)}, bf16[4,256,256]{2,1,0:T(8,128)(2,1)S(1)}, u32[]{:S(2)}, u32[]{:S(2)}) collective-permute-start(bf16[4,256,256]{2,1,0:T(8,128)(2,1)S(1)} %get-tuple-element.29), channel_id=1, source_target_pairs={{1,0},{2,1},{3,2},{4,3},{5,4},{6,5},{7,6},{9,8},{10,9},{11,10},{12... | collective-permute-start | bytes 1572872 | tf_op jit(solution)/shard_map/ppermute | solution.py:634
  6.0 4.6 %copy-start.1 = (bf16[256,1024]{1,0:T(8,128)(2,1)S(1)}, bf16[256,1024]{1,0:T(8,128)(2,1)}, u32[]{:S(2)}) copy-start(bf16[256,1024]{1,0:T(8,128)(2,1)} %w_gate_ref.1) | copy-start | bytes 1572868
  6.0 4.6 %copy-start.2 = (bf16[256,1024]{1,0:T(8,128)(2,1)S(1)}, bf16[256,1024]{1,0:T(8,128)(2,1)}, u32[]{:S(2)}) copy-start(bf16[256,1024]{1,0:T(8,128)(2,1)} %w_up_ref.1) | copy-start | bytes 1572868
  6.0 4.6 %copy-start.3 = (bf16[1024,256]{1,0:T(8,128)(2,1)S(1)}, bf16[1024,256]{1,0:T(8,128)(2,1)}, u32[]{:S(2)}) copy-start(bf16[1024,256]{1,0:T(8,128)(2,1)} %down_weight_ref.1) | copy-start | bytes 1572868
  6.0 4.6 %copy-start.7 = (bf16[256,256]{1,0:T(8,128)(2,1)S(1)}, bf16[256,256]{1,0:T(8,128)(2,1)}, u32[]{:S(2)}) copy-start(bf16[256,256]{1,0:T(8,128)(2,1)} %w_out_ref.1) | copy-start | bytes 393220
  6.0 4.6 %copy-start.13 = (f32[256]{0:T(256)S(1)}, f32[256]{0:T(256)}, u32[]{:S(2)}) copy-start(f32[256]{0:T(256)} %param.17) | copy-start | bytes 3076
  10.6 25.7 %copy-start.8 = (s32[4096]{0:T(1024)S(1)}, s32[4096]{0:T(1024)}, u32[]{:S(2)}) copy-start(s32[4096]{0:T(1024)} %param.26) | copy-start | bytes 49156
  10.6 25.7 %copy-start.9 = (s32[4096]{0:T(1024)S(1)}, s32[4096]{0:T(1024)}, u32[]{:S(2)}) copy-start(s32[4096]{0:T(1024)} %param.27) | copy-start | bytes 49156
  10.6 25.7 %copy-start.10 = (f32[4096]{0:T(1024)S(1)}, f32[4096]{0:T(1024)}, u32[]{:S(2)}) copy-start(f32[4096]{0:T(1024)} %param.28) | copy-start | bytes 49156
  10.6 25.7 %copy-start.11 = (f32[4096]{0:T(1024)S(1)}, f32[4096]{0:T(1024)}, u32[]{:S(2)}) copy-start(f32[4096]{0:T(1024)} %param.29) | copy-start | bytes 49156
  32.7 6.4 %collective-permute-start.2 = (bf16[4,128,256]{2,1,0:T(8,128)(2,1)S(1)}, bf16[4,128,256]{2,1,0:T(8,128)(2,1)S(1)}, u32[]{:S(2)}, u32[]{:S(2)}) collective-permute-start(bf16[4,128,256]{2,1,0:T(8,128)(2,1)S(1)} %get-tuple-element.22), channel_id=1, source_target_pairs={{0,8},{8,0},{16,24},{24,16},{1,9},{9,1},{17,25},{25,17},{2,10},{10... | collective-permute-start | bytes 786440 | tf_op jit(solution)/shard_map/ppermute | solution.py:604
  34.2 9.2 %collective-permute-start.3 = (bf16[4,128,256]{2,1,0:T(8,128)(2,1)S(1)}, bf16[4,128,256]{2,1,0:T(8,128)(2,1)S(1)}, u32[]{:S(2)}, u32[]{:S(2)}) collective-permute-start(bf16[4,128,256]{2,1,0:T(8,128)(2,1)S(1)} %get-tuple-element.23), channel_id=1, source_target_pairs={{0,16},{8,24},{16,0},{24,8},{1,17},{9,25},{17,1},{25,9},{2,18},{10... | collective-permute-start | bytes 786440 | tf_op jit(solution)/shard_map/ppermute | solution.py:604
  35.8 7.6 %collective-permute-start.4 = (bf16[4,128,256]{2,1,0:T(8,128)(2,1)S(1)}, bf16[4,128,256]{2,1,0:T(8,128)(2,1)S(1)}, u32[]{:S(2)}, u32[]{:S(2)}) collective-permute-start(bf16[4,128,256]{2,1,0:T(8,128)(2,1)S(1)} %get-tuple-element.24), channel_id=1, source_target_pairs={{0,24},{8,16},{16,8},{24,0},{1,25},{9,17},{17,9},{25,1},{2,26},{10... | collective-permute-start | bytes 786440 | tf_op jit(solution)/shard_map/ppermute | solution.py:604
  71.4 9.2 %collective-permute-start.5 = (bf16[4,128,256]{2,1,0:T(8,128)(2,1)S(1)}, bf16[4,128,256]{2,1,0:T(8,128)(2,1)S(1)}, u32[]{:S(2)}, u32[]{:S(2)}) collective-permute-start(bf16[4,128,256]{2,1,0:T(8,128)(2,1)S(1)} %get-tuple-element.26), channel_id=1, source_target_pairs={{0,8},{8,0},{16,24},{24,16},{1,9},{9,1},{17,25},{25,17},{2,10},{10... | collective-permute-start | bytes 786440 | tf_op jit(solution)/shard_map/ppermute | solution.py:604
  72.3 13.4 %collective-permute-start.6 = (bf16[4,128,256]{2,1,0:T(8,128)(2,1)S(1)}, bf16[4,128,256]{2,1,0:T(8,128)(2,1)S(1)}, u32[]{:S(2)}, u32[]{:S(2)}) collective-permute-start(bf16[4,128,256]{2,1,0:T(8,128)(2,1)S(1)} %get-tuple-element.27), channel_id=1, source_target_pairs={{0,16},{8,24},{16,0},{24,8},{1,17},{9,25},{17,1},{25,9},{2,18},{10... | collective-permute-start | bytes 786440 | tf_op jit(solution)/shard_map/ppermute | solution.py:604
  73.0 12.7 %collective-permute-start.7 = (bf16[4,128,256]{2,1,0:T(8,128)(2,1)S(1)}, bf16[4,128,256]{2,1,0:T(8,128)(2,1)S(1)}, u32[]{:S(2)}, u32[]{:S(2)}) collective-permute-start(bf16[4,128,256]{2,1,0:T(8,128)(2,1)S(1)} %get-tuple-element.28), channel_id=1, source_target_pairs={{0,24},{8,16},{16,8},{24,0},{1,25},{9,17},{17,9},{25,1},{2,26},{10... | collective-permute-start | bytes 786440 | tf_op jit(solution)/shard_map/ppermute | solution.py:604

commit v18 on v16

--- a/solution.py
+++ b/solution.py
@@ -15,7 +15,8 @@
 GROUP = 16
 LANES = 128
 VMEM_LIMIT = 32 * 1024 * 1024
-SAFE_SCORE = 56.0
+SAFE_SCORE = 100.0
+FOLD = 4
 HIDDEN_CHUNK = 256
 
 F32 = jnp.float32
@@ -40,11 +41,7 @@
 
 
 def rms_scaled(values, gain):
-    rows, width = values.shape
-    ones = jnp.ones((width, LANES), BF16)
-    means = dot((values * values).astype(BF16), ones) * (1.0 / width)
-    scale = lax.rsqrt(means + EPS)
-    return values * jnp.concatenate([scale] * (width // LANES), axis=1) * gain
+    return values * lax.rsqrt(jnp.mean(values * values, axis=-1, keepdims=True) + EPS) * gain
 
 
 def vmem_spec():
@@ -94,9 +91,13 @@
     return (lane_head == iota((feat_width, LANES), 1)).astype(F32).astype(BF16)
 
 
-def largest_norms(values, heads):
-    squares = dot((values * values).astype(BF16), head_lanes(values.shape[1], heads))
-    return jnp.max(squares, axis=0, keepdims=True)
+def norm_bounds(values, heads):
+    rows = values.shape[0] // FOLD
+    squares = values * values
+    folded = squares[:rows]
+    for part in range(1, FOLD):
+        folded = jnp.maximum(folded, squares[part * rows : (part + 1) * rows])
+    return jnp.max(dot(folded.astype(BF16), head_lanes(values.shape[1], heads)), axis=0, keepdims=True)
 
 
 def is_safe(query_norms, key_norms):
@@ -201,7 +202,7 @@
     query_ref[0] = query_rows.astype(BF16)
     key_buf[...] = key_rows.astype(BF16).T
     put_values(value_buf, 0, dot(normed, w_value_ref[...]).astype(BF16))
-    query_norms, key_norms = largest_norms(query_rows, heads), largest_norms(key_rows, heads)
+    query_norms, key_norms = norm_bounds(query_rows, heads), norm_bounds(key_rows, heads)
     blank = jnp.zeros((norm_ref.shape[1] - 2, LANES), F32)
     norm_ref[0] = jnp.concatenate([query_norms, key_norms, blank], axis=0)
 
@@ -270,8 +271,8 @@
     norm_ref,
     inner_mixed_ref,
     inner_total_ref,
-    left_ref,
-    right_ref,
+    near_ref,
+    far_ref,
     attn_gain_ref,
     ffn_gain_ref,
     w_key_ref,
@@ -287,7 +288,7 @@
         refs[-7:],
     )
     rows, feat_width = state_ref.shape[1:]
-    reach = left_ref.shape[1]
+    reach = near_ref.shape[1]
     heads = window_ref.shape[0]
     head_size = feat_width // heads
     group_heads = LANES // head_size
@@ -314,13 +315,17 @@
     def values_of(normed):
         return dot(normed, w_value_ref[...]).astype(BF16)
 
-    key_norms = norm_ref[0, 1:2, :]
-    for side, ref in enumerate((left_ref, right_ref)):
-        normed = rms_scaled(ref[0].astype(F32), attn_gain_ref[...]).astype(BF16)
-        keys = keys_of(normed)
-        key_norms = jnp.maximum(key_norms, largest_norms(keys, heads))
-        halo_key_buf[side] = keys.astype(BF16).T
-        put_values(halo_value_buf.at[side], 0, values_of(normed))
+    odd = tok_ref[0] % 2 == 1
+    near, far = near_ref[0].astype(F32), far_ref[0].astype(F32)
+    halo = jnp.concatenate([jnp.where(odd, near, far), jnp.where(odd, far, near)], axis=0)
+    normed = rms_scaled(halo, attn_gain_ref[...]).astype(BF16)
+    halo_keys = keys_of(normed)
+    halo_values = values_of(normed)
+    key_norms = jnp.maximum(norm_ref[0, 1:2, :], norm_bounds(halo_keys, heads))
+    for side in range(2):
+        here = slice(side * reach, (side + 1) * reach)
+        halo_key_buf[side] = halo_keys[here].astype(BF16).T
+        put_values(halo_value_buf.at[side], 0, halo_values[here])
     safe = is_safe(norm_ref[0, 0:1, :], key_norms)
 
     @pl.when(safe)
@@ -393,9 +398,9 @@
         out_ref[0] = forecast_buf[pl.ds(lower, share_rows), :]
 
 
-def forward(total_len, tok_index, mem_index, head_window, own, inner_parts, left, right, gains, weights, shares):
+def forward(total_len, tok_index, mem_index, head_window, own, inner_parts, near, far, gains, weights, shares):
     members, row_count, feat_width = own.shape
-    reach = left.shape[1]
+    reach = near.shape[1]
     heads = head_window.shape[0]
     hidden_width = weights[3].shape[1]
     macs = members * row_count * feat_width * (3 * feat_width + 3 * hidden_width + 4 * reach)
@@ -408,7 +413,7 @@
         grid=(members,),
         out_shape=[jax.ShapeDtypeStruct((members, row_count // shares, feat_width), BF16)] * shares,
         in_specs=[smem_spec()] * 3
-        + [spec(v) for v in (own, *inner_parts, left, right)]
+        + [spec(v) for v in (own, *inner_parts, near, far)]
         + [vmem_spec()] * (len(gains) + len(weights)),
         out_specs=[pl.BlockSpec((1, row_count // shares, feat_width), lambda m: (m, 0, 0))] * shares,
         scratch_shapes=[
@@ -423,7 +428,7 @@
         compiler_params=pltpu.CompilerParams(vmem_limit_bytes=VMEM_LIMIT),
         cost_estimate=pl.CostEstimate(flops=2 * macs, bytes_accessed=10 * own.size, transcendentals=0),
         name="forward",
-    )(tok_index, mem_index, head_window, own, *inner_parts, left, right, *gains, *weights)
+    )(tok_index, mem_index, head_window, own, *inner_parts, near, far, *gains, *weights)
 
 
 def global_member(held, index, own_members):
@@ -598,6 +603,17 @@
     ]
 
 
+def halos(own, reach):
+    count = lax.axis_size("tok")
+    odd = lax.axis_index("tok") % 2
+    last = own.shape[1] - reach
+    near = lax.dynamic_slice_in_dim(own, (1 - odd) * last, reach, axis=1)
+    far = lax.dynamic_slice_in_dim(own, odd * last, reach, axis=1)
+    near_pairs = [(i, i ^ 1) for i in range(count)]
+    far_pairs = [pair for i in range(1, count - 1, 2) for pair in ((i, i + 1), (i + 1, i))]
+    return lax.ppermute(near, "tok", near_pairs), lax.ppermute(far, "tok", far_pairs)
+
+
 def local(
     ens_state,
     attn_gain,
@@ -621,10 +637,7 @@
     device_count = mem_count * tok_count
     share_rows = row_count // mem_count
     first_pos = lax.axis_index("tok") * row_count
-    up = [(i, i + 1) for i in range(tok_count - 1)]
-    down = [(i + 1, i) for i in range(tok_count - 1)]
-    left = lax.ppermute(ens_state[:, row_count - WIN :], "tok", up)
-    right = lax.ppermute(ens_state[:, :WIN], "tok", down)
+    near_halo, far_halo = halos(ens_state, WIN)
     share_start = first_pos + lax.axis_index("mem") * share_rows
     grid = sample_grid(
         share_start.astype(jnp.int32).reshape(1), obs_token, obs_channel, obs_value, obs_var, share_rows, feat_width
@@ -636,7 +649,7 @@
     weights = [w_key, w_value, w_out, w_gate, w_up, down_weight]
     total_len = row_count * tok_count
     forecast = forward(
-        total_len, tok_index, mem_index, head_window, ens_state, inner_parts, left, right, gains, weights, mem_count
+        total_len, tok_index, mem_index, head_window, ens_state, inner_parts, near_halo, far_halo, gains, weights, mem_count
     )
     shares = exchanged(forecast)
     partial = gram_partial(mem_index, shares, grid)

time: 88.1 us -> 84.7 us (0.961)
  Pallas kernels: 35.3 us -> 33.1 us
  starting transfers between devices: 10.8 us -> 8.8 us
  blocking collectives: 21.9 us -> 22.9 us
    ppermute x2, starting transfers between devices: 3.68 us -> 1.15 us  [the longest x1 0.68 us: halos(): lax.ppermute(far, 'tok', far_pairs)]
    slice x1 -> x0, local copies, waits for them, and re-layouts: 2.17 us -> none  [local(): right = lax.ppermute(ens_state[:, :WIN], 'tok', down)]
    dynamic_slice x0 -> x1, local copies, waits for them, and re-layouts: none -> 2.17 us  [halos(): far = lax.dynamic_slice_in_dim(own, odd * last, reach, axis=1)]
    pallas_call x1, Pallas kernels: 23.6 us -> 22.1 us  [forward(): pl.pallas_call(functools.partial(forward_kernel, total_len), grid=(member...]
    all_to_all x1, blocking collectives: 21.9 us -> 22.9 us  [local(): lax.all_to_all(jnp.broadcast_to(partial[None], (device_count, *partial.sh...]
  transfers between devices with their start and end apart: 8 -> 8, of which waited for: 5 -> 4; matrix products, arithmetic and copies ran while one was open for 0% -> 0% of each run, Pallas kernels for 6% -> 6%
where the time goes in v18:
time: 84.7 us; the launch traced here: 84.5 us
  Pallas kernels  33.1 us (39%)
  blocking collectives  22.9 us (27%)
  waiting for transfers between devices  17.1 us (20%)
  starting transfers between devices  8.8 us (10%)
  local copies, waits for them, and re-layouts  2.26 us (3%)
    all_to_all x1, blocking collectives, local(): lax.all_to_all(jnp.broadcast_to(partial[None], (device_count, *partial.sh...  22.9 us
    pallas_call x1, Pallas kernels, forward(): pl.pallas_call(functools.partial(forward_kernel, total_len), grid=(member...  22.1 us
    ppermute x6, waiting for transfers between devices, exchanged(): lax.ppermute(v, 'mem', [(i, i ^ part) for i in range(count)])  17.1 us
    ppermute x6, starting transfers between devices, exchanged(): lax.ppermute(v, 'mem', [(i, i ^ part) for i in range(count)])  7.65 us
    pallas_call x1, Pallas kernels, combine(): pl.pallas_call(combine_kernel, out_shape=[jax.ShapeDtypeStruct(v.shape, B...  3.64 us
    pallas_call x1, Pallas kernels, inner(): pl.pallas_call(inner_kernel, grid=(members,), out_shape=[jax.ShapeDtypeSt...  3.39 us
    dynamic_slice x1, local copies, waits for them, and re-layouts, halos(): far = lax.dynamic_slice_in_dim(own, odd * last, reach, axis=1)  2.17 us
  transfers between devices with their start and end apart: 8, of which 4 were waited for; matrix products, arithmetic and copies ran while one was open for 0% of the time, Pallas kernels for 6%

profile of v18, /device:TPU:0, one launch (start us, length us, event | category | flops | bytes accessed | tf_op | source)
XLA Modules:
  0.0 84.5 jit_solution(6761813157602227632)
XLA Ops:
  0.0 2.2 %constant_dynamic-slice_fusion = (bf16[4,256,256]{2,1,0:T(8,128)(2,1)S(1)}, bf16[4,256,256]{2,1,0:T(8,128)(2,1)}) fusion(bf16[4,512,256]{2,1,0:T(8,128)(2,1)} %state_ref.1, s32[]{:T(128)S(6)} %select_n.15, s32[]{:T(128)S(6)} %select_n.14), kind=kLoop, calls=%fused_computation | loop fusion | bytes 2097160 | tf_op jit(solution)/shard_map/dynamic_slice | solution.py:611
  2.2 0.5 collective-permute-start
  2.7 0.7 collective-permute-start.1
  3.4 0.0 copy-start.1
  3.5 0.0 copy-start.2
  3.5 0.0 copy-start.3
  3.5 0.0 copy-start.7
  3.5 0.0 copy-start.13
  3.5 3.4 %inner.1 = (bf16[4,512,256]{2,1,0:T(8,128)(2,1)S(1)}, f32[4,8,128]{2,1,0:T(8,128)S(1)}, f32[4,512,256]{2,1,0:T(8,128)S(1)}, f32[4,512,256]{2,1,0:T(8,128)S(1)}) custom-call(s32[4]{0:T(128)S(1)} %copy-done.14, bf16[4,512,256]{2,1,0:T(8,128)(2,1)S(1)} %copy-done, f32[1,256]{1,0:T(1,128)S(1)} %bitcast.13, bf16[256,256]{1,0:T(8,128)(2,1)S(1)} %copy-done.4, ...), custom_call_target="tpu_custom_call" | custom-call | flops 5100273664 | bytes 7340032 | tf_op jit(solution)/shard_map/inner/pallas_call | solution.py:245
  6.9 0.0 collective-permute-done.near_ref
  6.9 0.0 collective-permute-done.1.far_ref
  7.0 0.0 copy-start.8
  7.0 0.0 copy-start.9
  7.0 0.0 copy-start.10
  7.0 0.0 copy-start.11
  7.0 22.1 %forward.1 = (bf16[4,128,256]{2,1,0:T(8,128)(2,1)S(1)}, bf16[4,128,256]{2,1,0:T(8,128)(2,1)S(1)}, bf16[4,128,256]{2,1,0:T(8,128)(2,1)S(1)}, bf16[4,128,256]{2,1,0:T(8,128)(2,1)S(1)}) custom-call(s32[1]{0:T(128)} %bitcast.1.tok_ref, s32[1]{0:T(128)} %bitcast.mem_ref.index_ref, s32[4]{0:T(128)S(1)} %copy-done.14, bf16[4,512,256]{2,1,0:T(8,128)(2,1)S(1)} %copy-done, ...), custom_call_target="tpu_custom_call" | custom-call | flops 5100273664 | bytes 5242880 | tf_op jit(solution)/shard_map/forward/pallas_call | solution.py:411
  29.1 2.6 %collective-permute-start.2 = (bf16[4,128,256]{2,1,0:T(8,128)(2,1)S(1)}, bf16[4,128,256]{2,1,0:T(8,128)(2,1)S(1)}, u32[]{:S(2)}, u32[]{:S(2)}) collective-permute-start(bf16[4,128,256]{2,1,0:T(8,128)(2,1)S(1)} %get-tuple-element.22), channel_id=1, source_target_pairs={{0,8},{8,0},{16,24},{24,16},{1,9},{9,1},{17,25},{25,17},{2,10},{10... | collective-permute-start | bytes 786440 | tf_op jit(solution)/shard_map/ppermute | solution.py:602
  31.7 1.5 %collective-permute-start.3 = (bf16[4,128,256]{2,1,0:T(8,128)(2,1)S(1)}, bf16[4,128,256]{2,1,0:T(8,128)(2,1)S(1)}, u32[]{:S(2)}, u32[]{:S(2)}) collective-permute-start(bf16[4,128,256]{2,1,0:T(8,128)(2,1)S(1)} %get-tuple-element.23), channel_id=1, source_target_pairs={{0,16},{8,24},{16,0},{24,8},{1,17},{9,25},{17,1},{25,9},{2,18},{10... | collective-permute-start | bytes 786440 | tf_op jit(solution)/shard_map/ppermute | solution.py:602
  33.2 0.0 collective-permute-start.4
  33.2 1.3 %sample_grid.1.refs_4_ = f32[2,128,256]{2,1,0:T(8,128)S(1)} custom-call(s32[1]{0:T(128)} %bitcast.4.start_ref, s32[1,4096]{1,0:T(1,128)S(1)} %bitcast.9, s32[1,4096]{1,0:T(1,128)S(1)} %bitcast.10, f32[1,4096]{1,0:T(1,128)S(1)} %bitcast.11, f32[1,4096]{1,0:T(1,128)S(1)} %bitcast.12), custom_call_target="tpu_custom_call" | custom-call | flops 1073741824 | bytes 65536 | tf_op jit(solution)/shard_map/sample_grid/pallas_call | solution.py:78
  34.6 1.5 %collective-permute-done.2.refs_1_ = bf16[4,128,256]{2,1,0:T(8,128)(2,1)S(1)} collective-permute-done((bf16[4,128,256]{2,1,0:T(8,128)(2,1)S(1)}, bf16[4,128,256]{2,1,0:T(8,128)(2,1)S(1)}, u32[]{:S(2)}, u32[]{:S(2)}) %collective-permute-start.2) | collective-permute-done | bytes 262176 | tf_op jit(solution)/shard_map/ppermute | solution.py:602
  36.0 4.9 %collective-permute-done.3.refs_2_ = bf16[4,128,256]{2,1,0:T(8,128)(2,1)S(1)} collective-permute-done((bf16[4,128,256]{2,1,0:T(8,128)(2,1)S(1)}, bf16[4,128,256]{2,1,0:T(8,128)(2,1)S(1)}, u32[]{:S(2)}, u32[]{:S(2)}) %collective-permute-start.3) | collective-permute-done | bytes 262176 | tf_op jit(solution)/shard_map/ppermute | solution.py:602
  40.9 1.7 %gram.1 = f32[8,128]{1,0:T(8,128)S(1)} custom-call(s32[1]{0:T(128)} %bitcast.mem_ref.index_ref, bf16[4,128,256]{2,1,0:T(8,128)(2,1)S(1)} %get-tuple-element.21.refs_0_, bf16[4,128,256]{2,1,0:T(8,128)(2,1)S(1)} %collective-permute-done.2.refs_1_, bf16[4,128,256]{2,1,0:T(8,128)(2,1)S(1)} %collective-permute-done.3.refs_2_, ...), custom_call_target="tpu_custom_call" | custom-call | flops 805306368 | bytes 1048576 | tf_op jit(solution)/shard_map/gram/pallas_call | solution.py:478
  42.6 22.9 %all_to_all.5.partial_ref = f32[32,8,128]{2,1,0:T(8,128)S(1)} all-to-all(f32[32,8,128]{2,1,0:T(8,128)S(1)} %broadcast_in_dim.2), channel_id=1, replica_groups=mesh['mem'=4,'tok'=8] {'mem','tok'}, dimensions={0} | all-to-all | bytes 262144 | tf_op jit(solution)/shard_map/all_to_all | solution.py:656
  65.6 3.6 %combine.1 = (bf16[4,128,256]{2,1,0:T(8,128)(2,1)S(1)}, bf16[4,128,256]{2,1,0:T(8,128)(2,1)S(1)}, bf16[4,128,256]{2,1,0:T(8,128)(2,1)S(1)}, bf16[4,128,256]{2,1,0:T(8,128)(2,1)S(1)}) custom-call(s32[1]{0:T(128)} %bitcast.mem_ref.index_ref, f32[32,8,128]{2,1,0:T(8,128)S(1)} %all_to_all.5.partial_ref, bf16[4,128,256]{2,1,0:T(8,128)(2,1)S(1)} %get-tuple-element.21.refs_0_, ...), custom_call_target="tpu_custom_call" | custom-call | flops 536870912 | bytes 2097152 | tf_op jit(solution)/shard_map/combine/pallas_call | solution.py:561
  69.2 0.9 %collective-permute-start.5 = (bf16[4,128,256]{2,1,0:T(8,128)(2,1)S(1)}, bf16[4,128,256]{2,1,0:T(8,128)(2,1)S(1)}, u32[]{:S(2)}, u32[]{:S(2)}) collective-permute-start(bf16[4,128,256]{2,1,0:T(8,128)(2,1)S(1)} %get-tuple-element.26), channel_id=1, source_target_pairs={{0,8},{8,0},{16,24},{24,16},{1,9},{9,1},{17,25},{25,17},{2,10},{10... | collective-permute-start | bytes 786440 | tf_op jit(solution)/shard_map/ppermute | solution.py:602
  70.1 0.7 collective-permute-start.6
  70.8 2.0 %collective-permute-start.7 = (bf16[4,128,256]{2,1,0:T(8,128)(2,1)S(1)}, bf16[4,128,256]{2,1,0:T(8,128)(2,1)S(1)}, u32[]{:S(2)}, u32[]{:S(2)}) collective-permute-start(bf16[4,128,256]{2,1,0:T(8,128)(2,1)S(1)} %get-tuple-element.28), channel_id=1, source_target_pairs={{0,24},{8,16},{16,8},{24,0},{1,25},{9,17},{17,9},{25,1},{2,26},{10... | collective-permute-start | bytes 786440 | tf_op jit(solution)/shard_map/ppermute | solution.py:602
  72.8 5.6 %collective-permute-done.5.refs_1_ = bf16[4,128,256]{2,1,0:T(8,128)(2,1)S(1)} collective-permute-done((bf16[4,128,256]{2,1,0:T(8,128)(2,1)S(1)}, bf16[4,128,256]{2,1,0:T(8,128)(2,1)S(1)}, u32[]{:S(2)}, u32[]{:S(2)}) %collective-permute-start.5) | collective-permute-done | bytes 262176 | tf_op jit(solution)/shard_map/ppermute | solution.py:602
  78.4 5.1 %collective-permute-done.6.refs_2_ = bf16[4,128,256]{2,1,0:T(8,128)(2,1)S(1)} collective-permute-done((bf16[4,128,256]{2,1,0:T(8,128)(2,1)S(1)}, bf16[4,128,256]{2,1,0:T(8,128)(2,1)S(1)}, u32[]{:S(2)}, u32[]{:S(2)}) %collective-permute-start.6) | collective-permute-done | bytes 262176 | tf_op jit(solution)/shard_map/ppermute | solution.py:602
  83.5 0.0 collective-permute-done.7.refs_3_
  83.5 1.0 %assemble.1 = bf16[4,512,256]{2,1,0:T(8,128)(2,1)} custom-call(s32[1]{0:T(128)} %bitcast.mem_ref.index_ref, bf16[4,128,256]{2,1,0:T(8,128)(2,1)S(1)} %get-tuple-element.25.refs_0_, bf16[4,128,256]{2,1,0:T(8,128)(2,1)S(1)} %collective-permute-done.5.refs_1_, bf16[4,128,256]{2,1,0:T(8,128)(2,1)S(1)} %collective-permute-done.6.refs_2_, ...), custom_call_target="tpu_custom_call" | custom-call | bytes 2097152 | tf_op jit(solution)/shard_map/assemble/pallas_call | solution.py:587
  (23 shorter events, 0.1 us)
Async XLA Ops:
  0.0 3.4 %copy-start = (bf16[4,512,256]{2,1,0:T(8,128)(2,1)S(1)}, bf16[4,512,256]{2,1,0:T(8,128)(2,1)}, u32[]{:S(2)}) copy-start(bf16[4,512,256]{2,1,0:T(8,128)(2,1)} %state_ref.1) | copy-start | bytes 3145732
  0.0 3.4 %copy-start.12 = (f32[256]{0:T(256)S(1)}, f32[256]{0:T(256)}, u32[]{:S(2)}) copy-start(f32[256]{0:T(256)} %param.16) | copy-start | bytes 3076
  0.0 3.4 %copy-start.4 = (bf16[256,256]{1,0:T(8,128)(2,1)S(1)}, bf16[256,256]{1,0:T(8,128)(2,1)}, u32[]{:S(2)}) copy-start(bf16[256,256]{1,0:T(8,128)(2,1)} %w_query_ref.1) | copy-start | bytes 393220
  0.0 3.4 %copy-start.5 = (bf16[256,256]{1,0:T(8,128)(2,1)S(1)}, bf16[256,256]{1,0:T(8,128)(2,1)}, u32[]{:S(2)}) copy-start(bf16[256,256]{1,0:T(8,128)(2,1)} %w_key_ref.3) | copy-start | bytes 393220
  0.0 3.4 %copy-start.6 = (bf16[256,256]{1,0:T(8,128)(2,1)S(1)}, bf16[256,256]{1,0:T(8,128)(2,1)}, u32[]{:S(2)}) copy-start(bf16[256,256]{1,0:T(8,128)(2,1)} %w_value_ref.3) | copy-start | bytes 393220
  0.0 3.4 %copy-start.14 = (s32[4]{0:T(128)S(1)}, s32[4]{0:T(128)}, u32[]{:S(2)}) copy-start(s32[4]{0:T(128)} %window_ref.3) | copy-start | bytes 52
  2.2 4.7 %collective-permute-start = (bf16[4,256,256]{2,1,0:T(8,128)(2,1)}, bf16[4,256,256]{2,1,0:T(8,128)(2,1)S(1)}, u32[]{:S(2)}, u32[]{:S(2)}) collective-permute-start(bf16[4,256,256]{2,1,0:T(8,128)(2,1)} %get-tuple-element.30), channel_id=1, source_target_pairs={{0,1},{1,0},{2,3},{3,2},{4,5},{5,4},{6,7},{7,6},{8,9},{9,8},{10,11... | collective-permute-start | bytes 1572872 | tf_op jit(solution)/shard_map/ppermute | solution.py:614
  2.7 4.2 %collective-permute-start.1 = (bf16[4,256,256]{2,1,0:T(8,128)(2,1)S(1)}, bf16[4,256,256]{2,1,0:T(8,128)(2,1)S(1)}, u32[]{:S(2)}, u32[]{:S(2)}) collective-permute-start(bf16[4,256,256]{2,1,0:T(8,128)(2,1)S(1)} %get-tuple-element.29), channel_id=1, source_target_pairs={{1,2},{2,1},{3,4},{4,3},{5,6},{6,5},{9,10},{10,9},{11,12},{12,11},... | collective-permute-start | bytes 1572872 | tf_op jit(solution)/shard_map/ppermute | solution.py:614
  3.4 3.5 %copy-start.1 = (bf16[256,1024]{1,0:T(8,128)(2,1)S(1)}, bf16[256,1024]{1,0:T(8,128)(2,1)}, u32[]{:S(2)}) copy-start(bf16[256,1024]{1,0:T(8,128)(2,1)} %w_gate_ref.1) | copy-start | bytes 1572868
  3.5 3.5 %copy-start.2 = (bf16[256,1024]{1,0:T(8,128)(2,1)S(1)}, bf16[256,1024]{1,0:T(8,128)(2,1)}, u32[]{:S(2)}) copy-start(bf16[256,1024]{1,0:T(8,128)(2,1)} %w_up_ref.1) | copy-start | bytes 1572868
  3.5 3.5 %copy-start.3 = (bf16[1024,256]{1,0:T(8,128)(2,1)S(1)}, bf16[1024,256]{1,0:T(8,128)(2,1)}, u32[]{:S(2)}) copy-start(bf16[1024,256]{1,0:T(8,128)(2,1)} %down_weight_ref.1) | copy-start | bytes 1572868
  3.5 3.5 %copy-start.7 = (bf16[256,256]{1,0:T(8,128)(2,1)S(1)}, bf16[256,256]{1,0:T(8,128)(2,1)}, u32[]{:S(2)}) copy-start(bf16[256,256]{1,0:T(8,128)(2,1)} %w_out_ref.1) | copy-start | bytes 393220
  3.5 3.5 %copy-start.13 = (f32[256]{0:T(256)S(1)}, f32[256]{0:T(256)}, u32[]{:S(2)}) copy-start(f32[256]{0:T(256)} %param.17) | copy-start | bytes 3076
  7.0 26.3 %copy-start.8 = (s32[4096]{0:T(1024)S(1)}, s32[4096]{0:T(1024)}, u32[]{:S(2)}) copy-start(s32[4096]{0:T(1024)} %param.26) | copy-start | bytes 49156
  7.0 26.3 %copy-start.9 = (s32[4096]{0:T(1024)S(1)}, s32[4096]{0:T(1024)}, u32[]{:S(2)}) copy-start(s32[4096]{0:T(1024)} %param.27) | copy-start | bytes 49156
  7.0 26.2 %copy-start.10 = (f32[4096]{0:T(1024)S(1)}, f32[4096]{0:T(1024)}, u32[]{:S(2)}) copy-start(f32[4096]{0:T(1024)} %param.28) | copy-start | bytes 49156
  7.0 26.2 %copy-start.11 = (f32[4096]{0:T(1024)S(1)}, f32[4096]{0:T(1024)}, u32[]{:S(2)}) copy-start(f32[4096]{0:T(1024)} %param.29) | copy-start | bytes 49156
  29.1 6.9 %collective-permute-start.2 = (bf16[4,128,256]{2,1,0:T(8,128)(2,1)S(1)}, bf16[4,128,256]{2,1,0:T(8,128)(2,1)S(1)}, u32[]{:S(2)}, u32[]{:S(2)}) collective-permute-start(bf16[4,128,256]{2,1,0:T(8,128)(2,1)S(1)} %get-tuple-element.22), channel_id=1, source_target_pairs={{0,8},{8,0},{16,24},{24,16},{1,9},{9,1},{17,25},{25,17},{2,10},{10... | collective-permute-start | bytes 786440 | tf_op jit(solution)/shard_map/ppermute | solution.py:602
  31.7 9.2 %collective-permute-start.3 = (bf16[4,128,256]{2,1,0:T(8,128)(2,1)S(1)}, bf16[4,128,256]{2,1,0:T(8,128)(2,1)S(1)}, u32[]{:S(2)}, u32[]{:S(2)}) collective-permute-start(bf16[4,128,256]{2,1,0:T(8,128)(2,1)S(1)} %get-tuple-element.23), channel_id=1, source_target_pairs={{0,16},{8,24},{16,0},{24,8},{1,17},{9,25},{17,1},{25,9},{2,18},{10... | collective-permute-start | bytes 786440 | tf_op jit(solution)/shard_map/ppermute | solution.py:602
  33.2 7.7 %collective-permute-start.4 = (bf16[4,128,256]{2,1,0:T(8,128)(2,1)S(1)}, bf16[4,128,256]{2,1,0:T(8,128)(2,1)S(1)}, u32[]{:S(2)}, u32[]{:S(2)}) collective-permute-start(bf16[4,128,256]{2,1,0:T(8,128)(2,1)S(1)} %get-tuple-element.24), channel_id=1, source_target_pairs={{0,24},{8,16},{16,8},{24,0},{1,25},{9,17},{17,9},{25,1},{2,26},{10... | collective-permute-start | bytes 786440 | tf_op jit(solution)/shard_map/ppermute | solution.py:602
  69.2 9.2 %collective-permute-start.5 = (bf16[4,128,256]{2,1,0:T(8,128)(2,1)S(1)}, bf16[4,128,256]{2,1,0:T(8,128)(2,1)S(1)}, u32[]{:S(2)}, u32[]{:S(2)}) collective-permute-start(bf16[4,128,256]{2,1,0:T(8,128)(2,1)S(1)} %get-tuple-element.26), channel_id=1, source_target_pairs={{0,8},{8,0},{16,24},{24,16},{1,9},{9,1},{17,25},{25,17},{2,10},{10... | collective-permute-start | bytes 786440 | tf_op jit(solution)/shard_map/ppermute | solution.py:602
  70.1 13.4 %collective-permute-start.6 = (bf16[4,128,256]{2,1,0:T(8,128)(2,1)S(1)}, bf16[4,128,256]{2,1,0:T(8,128)(2,1)S(1)}, u32[]{:S(2)}, u32[]{:S(2)}) collective-permute-start(bf16[4,128,256]{2,1,0:T(8,128)(2,1)S(1)} %get-tuple-element.27), channel_id=1, source_target_pairs={{0,16},{8,24},{16,0},{24,8},{1,17},{9,25},{17,1},{25,9},{2,18},{10... | collective-permute-start | bytes 786440 | tf_op jit(solution)/shard_map/ppermute | solution.py:602
  70.8 12.7 %collective-permute-start.7 = (bf16[4,128,256]{2,1,0:T(8,128)(2,1)S(1)}, bf16[4,128,256]{2,1,0:T(8,128)(2,1)S(1)}, u32[]{:S(2)}, u32[]{:S(2)}) collective-permute-start(bf16[4,128,256]{2,1,0:T(8,128)(2,1)S(1)} %get-tuple-element.28), channel_id=1, source_target_pairs={{0,24},{8,16},{16,8},{24,0},{1,25},{9,17},{17,9},{25,1},{2,26},{10... | collective-permute-start | bytes 786440 | tf_op jit(solution)/shard_map/ppermute | solution.py:602

commit v19 on v18

--- a/solution.py
+++ b/solution.py
@@ -17,6 +17,7 @@
 VMEM_LIMIT = 32 * 1024 * 1024
 SAFE_SCORE = 100.0
 FOLD = 4
+BATCH = 2
 HIDDEN_CHUNK = 256
 
 F32 = jnp.float32
@@ -316,29 +317,33 @@
         return dot(normed, w_value_ref[...]).astype(BF16)
 
     odd = tok_ref[0] % 2 == 1
-    near, far = near_ref[0].astype(F32), far_ref[0].astype(F32)
-    halo = jnp.concatenate([jnp.where(odd, near, far), jnp.where(odd, far, near)], axis=0)
-    normed = rms_scaled(halo, attn_gain_ref[...]).astype(BF16)
+    batch = state_ref.shape[0]
+    halo = []
+    for member in range(batch):
+        near, far = near_ref[member].astype(F32), far_ref[member].astype(F32)
+        halo += [jnp.where(odd, near, far), jnp.where(odd, far, near)]
+    normed = rms_scaled(jnp.concatenate(halo, axis=0), attn_gain_ref[...]).astype(BF16)
     halo_keys = keys_of(normed)
     halo_values = values_of(normed)
-    key_norms = jnp.maximum(norm_ref[0, 1:2, :], norm_bounds(halo_keys, heads))
-    for side in range(2):
-        here = slice(side * reach, (side + 1) * reach)
-        halo_key_buf[side] = halo_keys[here].astype(BF16).T
-        put_values(halo_value_buf.at[side], 0, halo_values[here])
-    safe = is_safe(norm_ref[0, 0:1, :], key_norms)
+    query_norms = jnp.max(norm_ref[:, 0, :], axis=0, keepdims=True)
+    key_norms = jnp.maximum(jnp.max(norm_ref[:, 1, :], axis=0, keepdims=True), norm_bounds(halo_keys, heads))
+    for at in range(2 * batch):
+        here = slice(at * reach, (at + 1) * reach)
+        halo_key_buf[at] = halo_keys[here].astype(BF16).T
+        put_values(halo_value_buf.at[at], 0, halo_values[here])
+    safe = is_safe(query_norms, key_norms)
 
     @pl.when(safe)
     def _():
-        units = [(side, group) for side in range(2) for group in range(groups)]
-
-        def scores_of(side, group):
+        units = [(member, side, group) for member in range(batch) for side in range(2) for group in range(groups)]
+
+        def scores_of(member, side, group):
             start = side * (rows - count)
-            queries = query_ref[0, start : start + count, group_lanes(group)]
-            return dot(stacked_heads(queries, head_size), halo_key_buf[side, group_lanes(group), :])
+            queries = query_ref[member, start : start + count, group_lanes(group)]
+            return dot(stacked_heads(queries, head_size), halo_key_buf[2 * member + side, group_lanes(group), :])
 
         scores = scores_of(*units[0])
-        for at, (side, group) in enumerate(units):
+        for at, (member, side, group) in enumerate(units):
             following = scores_of(*units[at + 1]) if at + 1 < len(units) else None
             spans = [(0, reach), (Q_ROWS, reach)] if side == 0 else [(0, reach - Q_ROWS), (0, reach)]
 
@@ -347,43 +352,48 @@
                 shift = -block * Q_ROWS if side == 0 else (1 - block) * Q_ROWS
                 return band_buf[side, group * group_heads + head, :, lower + shift : upper + shift]
 
-            values = halo_value_buf[side, :, 2 * group * LANES : 2 * (group + 1) * LANES]
+            values = halo_value_buf[2 * member + side, :, 2 * group * LANES : 2 * (group + 1) * LANES]
             mixed, totals = weighted_sums(unit_weights(scores, spans, band_of), values, head_size)
-            here = slice(side * (rows - count), side * (rows - count) + count)
-            mixed = mixed + inner_mixed_ref[0, here, group_lanes(group)]
-            totals = totals + inner_total_ref[0, here, group_lanes(group)]
-            mixed_buf[here, group_lanes(group)] = (mixed / totals).astype(BF16)
+            start = side * (rows - count)
+            here = slice(start, start + count)
+            mixed = mixed + inner_mixed_ref[member, here, group_lanes(group)]
+            totals = totals + inner_total_ref[member, here, group_lanes(group)]
+            start += member * rows
+            mixed_buf[start : start + count, group_lanes(group)] = (mixed / totals).astype(BF16)
             scores = following
 
     @pl.when(jnp.logical_not(safe))
     def _():
-        normed = rms_scaled(state_ref[0].astype(F32), attn_gain_ref[...]).astype(BF16)
-        key_buf[:, :reach] = halo_key_buf[0]
-        key_buf[:, reach : reach + rows] = keys_of(normed).astype(BF16).T
-        key_buf[:, reach + rows :] = halo_key_buf[1]
-        value_buf[...] = jnp.ones(value_buf.shape, BF16)
-        put_values(value_buf, reach, values_of(normed))
-        value_buf[:reach] = halo_value_buf[0]
-        value_buf[reach + rows :] = halo_value_buf[1]
-        for block in range(blocks):
-            start = block * Q_ROWS
-            k_pos = first_pos - reach + start + iota((Q_ROWS, key_count), 1)
-            inside = (k_pos >= 0) & (k_pos < total_len)
-            for group in range(groups):
-                queries = query_ref[0, start : start + Q_ROWS, group_lanes(group)]
-                keys = key_buf[group_lanes(group), start : start + key_count]
-                scores = dot(stacked_heads(queries, head_size), keys)
-                weights = []
-                for head in range(group_heads):
-                    allowed = inside & in_band(window_ref[group * group_heads + head], 0, key_count, reach)
-                    score_matrix = jnp.where(allowed, scores[head * Q_ROWS : (head + 1) * Q_ROWS], -1e30)
-                    row_top = jnp.max(score_matrix, axis=-1, keepdims=True)
-                    weights.append(jnp.exp2(score_matrix - row_top).astype(BF16))
-                values = value_buf[start : start + key_count, 2 * group * LANES : 2 * (group + 1) * LANES]
-                mixed, totals = weighted_sums(jnp.concatenate(weights, axis=0), values, head_size)
-                mixed_buf[start : start + Q_ROWS, group_lanes(group)] = (mixed / totals).astype(BF16)
-
-    after = (state_ref[0].astype(F32) + dot(mixed_buf[...], w_out_ref[...])).astype(BF16)
+        for member in range(batch):
+            normed = rms_scaled(state_ref[member].astype(F32), attn_gain_ref[...]).astype(BF16)
+            key_buf[:, :reach] = halo_key_buf[2 * member]
+            key_buf[:, reach : reach + rows] = keys_of(normed).astype(BF16).T
+            key_buf[:, reach + rows :] = halo_key_buf[2 * member + 1]
+            value_buf[...] = jnp.ones(value_buf.shape, BF16)
+            put_values(value_buf, reach, values_of(normed))
+            value_buf[:reach] = halo_value_buf[2 * member]
+            value_buf[reach + rows :] = halo_value_buf[2 * member + 1]
+            for block in range(blocks):
+                start = block * Q_ROWS
+                k_pos = first_pos - reach + start + iota((Q_ROWS, key_count), 1)
+                inside = (k_pos >= 0) & (k_pos < total_len)
+                for group in range(groups):
+                    queries = query_ref[member, start : start + Q_ROWS, group_lanes(group)]
+                    keys = key_buf[group_lanes(group), start : start + key_count]
+                    scores = dot(stacked_heads(queries, head_size), keys)
+                    weights = []
+                    for head in range(group_heads):
+                        allowed = inside & in_band(window_ref[group * group_heads + head], 0, key_count, reach)
+                        score_matrix = jnp.where(allowed, scores[head * Q_ROWS : (head + 1) * Q_ROWS], -1e30)
+                        row_top = jnp.max(score_matrix, axis=-1, keepdims=True)
+                        weights.append(jnp.exp2(score_matrix - row_top).astype(BF16))
+                    values = value_buf[start : start + key_count, 2 * group * LANES : 2 * (group + 1) * LANES]
+                    mixed, totals = weighted_sums(jnp.concatenate(weights, axis=0), values, head_size)
+                    here = slice(member * rows + start, member * rows + start + Q_ROWS)
+                    mixed_buf[here, group_lanes(group)] = (mixed / totals).astype(BF16)
+
+    state = state_ref[...].reshape(batch * rows, feat_width).astype(F32)
+    after = (state + dot(mixed_buf[...], w_out_ref[...])).astype(BF16)
     normed_mid = rms_scaled(after.astype(F32), ffn_gain_ref[...]).astype(BF16)
     forecast = after.astype(F32)
     for lower in range(0, w_gate_ref.shape[1], HIDDEN_CHUNK):
@@ -395,7 +405,8 @@
     share_rows = out_refs[0].shape[1]
     for part, out_ref in enumerate(out_refs):
         lower = pl.multiple_of((mem_ref[0] ^ part) * share_rows, share_rows)
-        out_ref[0] = forecast_buf[pl.ds(lower, share_rows), :]
+        for member in range(batch):
+            out_ref[member] = forecast_buf[pl.ds(member * rows + lower, share_rows), :]
 
 
 def forward(total_len, tok_index, mem_index, head_window, own, inner_parts, near, far, gains, weights, shares):
@@ -404,26 +415,28 @@
     heads = head_window.shape[0]
     hidden_width = weights[3].shape[1]
     macs = members * row_count * feat_width * (3 * feat_width + 3 * hidden_width + 4 * reach)
+    batch = BATCH if members % BATCH == 0 else 1
+    share_rows = row_count // shares
 
     def spec(array):
-        return pl.BlockSpec((1, *array.shape[1:]), lambda m: (m, 0, 0))
+        return pl.BlockSpec((batch, *array.shape[1:]), lambda m: (m, 0, 0))
 
     return pl.pallas_call(
         functools.partial(forward_kernel, total_len),
-        grid=(members,),
-        out_shape=[jax.ShapeDtypeStruct((members, row_count // shares, feat_width), BF16)] * shares,
+        grid=(members // batch,),
+        out_shape=[jax.ShapeDtypeStruct((members, share_rows, feat_width), BF16)] * shares,
         in_specs=[smem_spec()] * 3
         + [spec(v) for v in (own, *inner_parts, near, far)]
         + [vmem_spec()] * (len(gains) + len(weights)),
-        out_specs=[pl.BlockSpec((1, row_count // shares, feat_width), lambda m: (m, 0, 0))] * shares,
+        out_specs=[pl.BlockSpec((batch, share_rows, feat_width), lambda m: (m, 0, 0))] * shares,
         scratch_shapes=[
-            pltpu.VMEM((2, feat_width, reach), BF16),
-            pltpu.VMEM((2, reach, 2 * feat_width), BF16),
+            pltpu.VMEM((2 * batch, feat_width, reach), BF16),
+            pltpu.VMEM((2 * batch, reach, 2 * feat_width), BF16),
             pltpu.VMEM((2, heads, Q_ROWS, reach), BF16),
-            pltpu.VMEM((row_count, feat_width), BF16),
+            pltpu.VMEM((batch * row_count, feat_width), BF16),
             pltpu.VMEM((feat_width, row_count + 2 * reach), BF16),
             pltpu.VMEM((row_count + 2 * reach, 2 * feat_width), BF16),
-            pltpu.VMEM((row_count, feat_width), BF16),
+            pltpu.VMEM((batch * row_count, feat_width), BF16),
         ],
         compiler_params=pltpu.CompilerParams(vmem_limit_bytes=VMEM_LIMIT),
         cost_estimate=pl.CostEstimate(flops=2 * macs, bytes_accessed=10 * own.size, transcendentals=0),

time: 84.7 us -> 82.8 us (0.978)
  Pallas kernels: 33.1 us -> 31.1 us
    pallas_call x1, Pallas kernels: 22.1 us -> 20 us  [forward(): pl.pallas_call(functools.partial(forward_kernel, total_len), grid=(member...]
where the time goes in v19:
time: 82.8 us; the launch traced here: 82.6 us
  Pallas kernels  31.1 us (38%)
  blocking collectives  22.9 us (28%)
  waiting for transfers between devices  17.1 us (21%)
  starting transfers between devices  8.8 us (11%)
  local copies, waits for them, and re-layouts  2.26 us (3%)
    all_to_all x1, blocking collectives, local(): lax.all_to_all(jnp.broadcast_to(partial[None], (device_count, *partial.sh...  22.9 us
    pallas_call x1, Pallas kernels, forward(): pl.pallas_call(functools.partial(forward_kernel, total_len), grid=(member...  20 us
    ppermute x6, waiting for transfers between devices, exchanged(): lax.ppermute(v, 'mem', [(i, i ^ part) for i in range(count)])  17.1 us
    ppermute x6, starting transfers between devices, exchanged(): lax.ppermute(v, 'mem', [(i, i ^ part) for i in range(count)])  7.65 us
    pallas_call x1, Pallas kernels, combine(): pl.pallas_call(combine_kernel, out_shape=[jax.ShapeDtypeStruct(v.shape, B...  3.64 us
    pallas_call x1, Pallas kernels, inner(): pl.pallas_call(inner_kernel, grid=(members,), out_shape=[jax.ShapeDtypeSt...  3.39 us
    dynamic_slice x1, local copies, waits for them, and re-layouts, halos(): far = lax.dynamic_slice_in_dim(own, odd * last, reach, axis=1)  2.17 us
    pallas_call x1, Pallas kernels, gram_partial(): pl.pallas_call(gram_kernel, out_shape=jax.ShapeDtypeStruct((-(-filled //...  1.67 us
  transfers between devices with their start and end apart: 8, of which 4 were waited for; matrix products, arithmetic and copies ran while one was open for 0% of the time, Pallas kernels for 6%

profile of v19, /device:TPU:0, one launch (start us, length us, event | category | flops | bytes accessed | tf_op | source)
XLA Modules:
  0.0 82.6 jit_solution(12975978968958253384)
XLA Ops:
  0.0 2.2 %constant_dynamic-slice_fusion = (bf16[4,256,256]{2,1,0:T(8,128)(2,1)S(1)}, bf16[4,256,256]{2,1,0:T(8,128)(2,1)}) fusion(bf16[4,512,256]{2,1,0:T(8,128)(2,1)} %state_ref.1, s32[]{:T(128)S(6)} %select_n.15, s32[]{:T(128)S(6)} %select_n.14), kind=kLoop, calls=%fused_computation | loop fusion | bytes 2097160 | tf_op jit(solution)/shard_map/dynamic_slice | solution.py:624
  2.2 0.5 collective-permute-start
  2.7 0.7 collective-permute-start.1
  3.4 0.0 copy-start.1
  3.5 0.0 copy-start.2
  3.5 0.0 copy-start.3
  3.5 0.0 copy-start.7
  3.5 0.0 copy-start.13
  3.5 3.4 %inner.1 = (bf16[4,512,256]{2,1,0:T(8,128)(2,1)S(1)}, f32[4,8,128]{2,1,0:T(8,128)S(1)}, f32[4,512,256]{2,1,0:T(8,128)S(1)}, f32[4,512,256]{2,1,0:T(8,128)S(1)}) custom-call(s32[4]{0:T(128)S(1)} %copy-done.14, bf16[4,512,256]{2,1,0:T(8,128)(2,1)S(1)} %copy-done, f32[1,256]{1,0:T(1,128)S(1)} %bitcast.13, bf16[256,256]{1,0:T(8,128)(2,1)S(1)} %copy-done.4, ...), custom_call_target="tpu_custom_call" | custom-call | flops 5100273664 | bytes 7340032 | tf_op jit(solution)/shard_map/inner/pallas_call | solution.py:246
  6.9 0.0 collective-permute-done.near_ref
  6.9 0.0 collective-permute-done.1.far_ref
  7.0 0.0 copy-start.8
  7.0 0.0 copy-start.9
  7.0 0.0 copy-start.10
  7.0 0.0 copy-start.11
  7.0 20.0 %forward.1 = (bf16[4,128,256]{2,1,0:T(8,128)(2,1)S(1)}, bf16[4,128,256]{2,1,0:T(8,128)(2,1)S(1)}, bf16[4,128,256]{2,1,0:T(8,128)(2,1)S(1)}, bf16[4,128,256]{2,1,0:T(8,128)(2,1)S(1)}) custom-call(s32[1]{0:T(128)} %bitcast.1.tok_ref, s32[1]{0:T(128)} %bitcast.mem_ref.index_ref, s32[4]{0:T(128)S(1)} %copy-done.14, bf16[4,512,256]{2,1,0:T(8,128)(2,1)S(1)} %copy-done, ...), custom_call_target="tpu_custom_call" | custom-call | flops 5100273664 | bytes 5242880 | tf_op jit(solution)/shard_map/forward/pallas_call | solution.py:424
  27.1 2.6 %collective-permute-start.2 = (bf16[4,128,256]{2,1,0:T(8,128)(2,1)S(1)}, bf16[4,128,256]{2,1,0:T(8,128)(2,1)S(1)}, u32[]{:S(2)}, u32[]{:S(2)}) collective-permute-start(bf16[4,128,256]{2,1,0:T(8,128)(2,1)S(1)} %get-tuple-element.22), channel_id=1, source_target_pairs={{0,8},{8,0},{16,24},{24,16},{1,9},{9,1},{17,25},{25,17},{2,10},{10... | collective-permute-start | bytes 786440 | tf_op jit(solution)/shard_map/ppermute | solution.py:615
  29.6 1.5 %collective-permute-start.3 = (bf16[4,128,256]{2,1,0:T(8,128)(2,1)S(1)}, bf16[4,128,256]{2,1,0:T(8,128)(2,1)S(1)}, u32[]{:S(2)}, u32[]{:S(2)}) collective-permute-start(bf16[4,128,256]{2,1,0:T(8,128)(2,1)S(1)} %get-tuple-element.23), channel_id=1, source_target_pairs={{0,16},{8,24},{16,0},{24,8},{1,17},{9,25},{17,1},{25,9},{2,18},{10... | collective-permute-start | bytes 786440 | tf_op jit(solution)/shard_map/ppermute | solution.py:615
  31.1 0.0 collective-permute-start.4
  31.2 1.3 %sample_grid.1.refs_4_ = f32[2,128,256]{2,1,0:T(8,128)S(1)} custom-call(s32[1]{0:T(128)} %bitcast.4.start_ref, s32[1,4096]{1,0:T(1,128)S(1)} %bitcast.9, s32[1,4096]{1,0:T(1,128)S(1)} %bitcast.10, f32[1,4096]{1,0:T(1,128)S(1)} %bitcast.11, f32[1,4096]{1,0:T(1,128)S(1)} %bitcast.12), custom_call_target="tpu_custom_call" | custom-call | flops 1073741824 | bytes 65536 | tf_op jit(solution)/shard_map/sample_grid/pallas_call | solution.py:79
  32.5 1.5 %collective-permute-done.2.refs_1_ = bf16[4,128,256]{2,1,0:T(8,128)(2,1)S(1)} collective-permute-done((bf16[4,128,256]{2,1,0:T(8,128)(2,1)S(1)}, bf16[4,128,256]{2,1,0:T(8,128)(2,1)S(1)}, u32[]{:S(2)}, u32[]{:S(2)}) %collective-permute-start.2) | collective-permute-done | bytes 262176 | tf_op jit(solution)/shard_map/ppermute | solution.py:615
  34.0 4.9 %collective-permute-done.3.refs_2_ = bf16[4,128,256]{2,1,0:T(8,128)(2,1)S(1)} collective-permute-done((bf16[4,128,256]{2,1,0:T(8,128)(2,1)S(1)}, bf16[4,128,256]{2,1,0:T(8,128)(2,1)S(1)}, u32[]{:S(2)}, u32[]{:S(2)}) %collective-permute-start.3) | collective-permute-done | bytes 262176 | tf_op jit(solution)/shard_map/ppermute | solution.py:615
  38.9 0.0 collective-permute-done.4.refs_3_
  38.9 1.7 %gram.1 = f32[8,128]{1,0:T(8,128)S(1)} custom-call(s32[1]{0:T(128)} %bitcast.mem_ref.index_ref, bf16[4,128,256]{2,1,0:T(8,128)(2,1)S(1)} %get-tuple-element.21.refs_0_, bf16[4,128,256]{2,1,0:T(8,128)(2,1)S(1)} %collective-permute-done.2.refs_1_, bf16[4,128,256]{2,1,0:T(8,128)(2,1)S(1)} %collective-permute-done.3.refs_2_, ...), custom_call_target="tpu_custom_call" | custom-call | flops 805306368 | bytes 1048576 | tf_op jit(solution)/shard_map/gram/pallas_call | solution.py:491
  40.6 22.9 %all_to_all.5.partial_ref = f32[32,8,128]{2,1,0:T(8,128)S(1)} all-to-all(f32[32,8,128]{2,1,0:T(8,128)S(1)} %broadcast_in_dim.2), channel_id=1, replica_groups=mesh['mem'=4,'tok'=8] {'mem','tok'}, dimensions={0} | all-to-all | bytes 262144 | tf_op jit(solution)/shard_map/all_to_all | solution.py:669
  63.5 3.6 %combine.1 = (bf16[4,128,256]{2,1,0:T(8,128)(2,1)S(1)}, bf16[4,128,256]{2,1,0:T(8,128)(2,1)S(1)}, bf16[4,128,256]{2,1,0:T(8,128)(2,1)S(1)}, bf16[4,128,256]{2,1,0:T(8,128)(2,1)S(1)}) custom-call(s32[1]{0:T(128)} %bitcast.mem_ref.index_ref, f32[32,8,128]{2,1,0:T(8,128)S(1)} %all_to_all.5.partial_ref, bf16[4,128,256]{2,1,0:T(8,128)(2,1)S(1)} %get-tuple-element.21.refs_0_, ...), custom_call_target="tpu_custom_call" | custom-call | flops 536870912 | bytes 2097152 | tf_op jit(solution)/shard_map/combine/pallas_call | solution.py:574
  67.1 0.9 %collective-permute-start.5 = (bf16[4,128,256]{2,1,0:T(8,128)(2,1)S(1)}, bf16[4,128,256]{2,1,0:T(8,128)(2,1)S(1)}, u32[]{:S(2)}, u32[]{:S(2)}) collective-permute-start(bf16[4,128,256]{2,1,0:T(8,128)(2,1)S(1)} %get-tuple-element.26), channel_id=1, source_target_pairs={{0,8},{8,0},{16,24},{24,16},{1,9},{9,1},{17,25},{25,17},{2,10},{10... | collective-permute-start | bytes 786440 | tf_op jit(solution)/shard_map/ppermute | solution.py:615
  68.0 0.7 collective-permute-start.6
  68.7 2.0 %collective-permute-start.7 = (bf16[4,128,256]{2,1,0:T(8,128)(2,1)S(1)}, bf16[4,128,256]{2,1,0:T(8,128)(2,1)S(1)}, u32[]{:S(2)}, u32[]{:S(2)}) collective-permute-start(bf16[4,128,256]{2,1,0:T(8,128)(2,1)S(1)} %get-tuple-element.28), channel_id=1, source_target_pairs={{0,24},{8,16},{16,8},{24,0},{1,25},{9,17},{17,9},{25,1},{2,26},{10... | collective-permute-start | bytes 786440 | tf_op jit(solution)/shard_map/ppermute | solution.py:615
  70.7 5.6 %collective-permute-done.5.refs_1_ = bf16[4,128,256]{2,1,0:T(8,128)(2,1)S(1)} collective-permute-done((bf16[4,128,256]{2,1,0:T(8,128)(2,1)S(1)}, bf16[4,128,256]{2,1,0:T(8,128)(2,1)S(1)}, u32[]{:S(2)}, u32[]{:S(2)}) %collective-permute-start.5) | collective-permute-done | bytes 262176 | tf_op jit(solution)/shard_map/ppermute | solution.py:615
  76.3 5.1 %collective-permute-done.6.refs_2_ = bf16[4,128,256]{2,1,0:T(8,128)(2,1)S(1)} collective-permute-done((bf16[4,128,256]{2,1,0:T(8,128)(2,1)S(1)}, bf16[4,128,256]{2,1,0:T(8,128)(2,1)S(1)}, u32[]{:S(2)}, u32[]{:S(2)}) %collective-permute-start.6) | collective-permute-done | bytes 262176 | tf_op jit(solution)/shard_map/ppermute | solution.py:615
  81.4 1.0 %assemble.1 = bf16[4,512,256]{2,1,0:T(8,128)(2,1)} custom-call(s32[1]{0:T(128)} %bitcast.mem_ref.index_ref, bf16[4,128,256]{2,1,0:T(8,128)(2,1)S(1)} %get-tuple-element.25.refs_0_, bf16[4,128,256]{2,1,0:T(8,128)(2,1)S(1)} %collective-permute-done.5.refs_1_, bf16[4,128,256]{2,1,0:T(8,128)(2,1)S(1)} %collective-permute-done.6.refs_2_, ...), custom_call_target="tpu_custom_call" | custom-call | bytes 2097152 | tf_op jit(solution)/shard_map/assemble/pallas_call | solution.py:600
  (23 shorter events, 0.1 us)
Async XLA Ops:
  0.0 3.4 %copy-start = (bf16[4,512,256]{2,1,0:T(8,128)(2,1)S(1)}, bf16[4,512,256]{2,1,0:T(8,128)(2,1)}, u32[]{:S(2)}) copy-start(bf16[4,512,256]{2,1,0:T(8,128)(2,1)} %state_ref.1) | copy-start | bytes 3145732
  0.0 3.4 %copy-start.12 = (f32[256]{0:T(256)S(1)}, f32[256]{0:T(256)}, u32[]{:S(2)}) copy-start(f32[256]{0:T(256)} %param.16) | copy-start | bytes 3076
  0.0 3.4 %copy-start.4 = (bf16[256,256]{1,0:T(8,128)(2,1)S(1)}, bf16[256,256]{1,0:T(8,128)(2,1)}, u32[]{:S(2)}) copy-start(bf16[256,256]{1,0:T(8,128)(2,1)} %w_query_ref.1) | copy-start | bytes 393220
  0.0 3.4 %copy-start.5 = (bf16[256,256]{1,0:T(8,128)(2,1)S(1)}, bf16[256,256]{1,0:T(8,128)(2,1)}, u32[]{:S(2)}) copy-start(bf16[256,256]{1,0:T(8,128)(2,1)} %w_key_ref.3) | copy-start | bytes 393220
  0.0 3.4 %copy-start.6 = (bf16[256,256]{1,0:T(8,128)(2,1)S(1)}, bf16[256,256]{1,0:T(8,128)(2,1)}, u32[]{:S(2)}) copy-start(bf16[256,256]{1,0:T(8,128)(2,1)} %w_value_ref.3) | copy-start | bytes 393220
  0.0 3.4 %copy-start.14 = (s32[4]{0:T(128)S(1)}, s32[4]{0:T(128)}, u32[]{:S(2)}) copy-start(s32[4]{0:T(128)} %window_ref.3) | copy-start | bytes 52
  2.2 4.7 %collective-permute-start = (bf16[4,256,256]{2,1,0:T(8,128)(2,1)}, bf16[4,256,256]{2,1,0:T(8,128)(2,1)S(1)}, u32[]{:S(2)}, u32[]{:S(2)}) collective-permute-start(bf16[4,256,256]{2,1,0:T(8,128)(2,1)} %get-tuple-element.30), channel_id=1, source_target_pairs={{0,1},{1,0},{2,3},{3,2},{4,5},{5,4},{6,7},{7,6},{8,9},{9,8},{10,11... | collective-permute-start | bytes 1572872 | tf_op jit(solution)/shard_map/ppermute | solution.py:627
  2.7 4.2 %collective-permute-start.1 = (bf16[4,256,256]{2,1,0:T(8,128)(2,1)S(1)}, bf16[4,256,256]{2,1,0:T(8,128)(2,1)S(1)}, u32[]{:S(2)}, u32[]{:S(2)}) collective-permute-start(bf16[4,256,256]{2,1,0:T(8,128)(2,1)S(1)} %get-tuple-element.29), channel_id=1, source_target_pairs={{1,2},{2,1},{3,4},{4,3},{5,6},{6,5},{9,10},{10,9},{11,12},{12,11},... | collective-permute-start | bytes 1572872 | tf_op jit(solution)/shard_map/ppermute | solution.py:627
  3.4 3.5 %copy-start.1 = (bf16[256,1024]{1,0:T(8,128)(2,1)S(1)}, bf16[256,1024]{1,0:T(8,128)(2,1)}, u32[]{:S(2)}) copy-start(bf16[256,1024]{1,0:T(8,128)(2,1)} %w_gate_ref.1) | copy-start | bytes 1572868
  3.5 3.5 %copy-start.2 = (bf16[256,1024]{1,0:T(8,128)(2,1)S(1)}, bf16[256,1024]{1,0:T(8,128)(2,1)}, u32[]{:S(2)}) copy-start(bf16[256,1024]{1,0:T(8,128)(2,1)} %w_up_ref.1) | copy-start | bytes 1572868
  3.5 3.5 %copy-start.3 = (bf16[1024,256]{1,0:T(8,128)(2,1)S(1)}, bf16[1024,256]{1,0:T(8,128)(2,1)}, u32[]{:S(2)}) copy-start(bf16[1024,256]{1,0:T(8,128)(2,1)} %down_weight_ref.1) | copy-start | bytes 1572868
  3.5 3.5 %copy-start.7 = (bf16[256,256]{1,0:T(8,128)(2,1)S(1)}, bf16[256,256]{1,0:T(8,128)(2,1)}, u32[]{:S(2)}) copy-start(bf16[256,256]{1,0:T(8,128)(2,1)} %w_out_ref.1) | copy-start | bytes 393220
  3.5 3.5 %copy-start.13 = (f32[256]{0:T(256)S(1)}, f32[256]{0:T(256)}, u32[]{:S(2)}) copy-start(f32[256]{0:T(256)} %param.17) | copy-start | bytes 3076
  7.0 24.2 %copy-start.8 = (s32[4096]{0:T(1024)S(1)}, s32[4096]{0:T(1024)}, u32[]{:S(2)}) copy-start(s32[4096]{0:T(1024)} %param.26) | copy-start | bytes 49156
  7.0 24.2 %copy-start.9 = (s32[4096]{0:T(1024)S(1)}, s32[4096]{0:T(1024)}, u32[]{:S(2)}) copy-start(s32[4096]{0:T(1024)} %param.27) | copy-start | bytes 49156
  7.0 24.2 %copy-start.10 = (f32[4096]{0:T(1024)S(1)}, f32[4096]{0:T(1024)}, u32[]{:S(2)}) copy-start(f32[4096]{0:T(1024)} %param.28) | copy-start | bytes 49156
  7.0 24.2 %copy-start.11 = (f32[4096]{0:T(1024)S(1)}, f32[4096]{0:T(1024)}, u32[]{:S(2)}) copy-start(f32[4096]{0:T(1024)} %param.29) | copy-start | bytes 49156
  27.1 6.9 %collective-permute-start.2 = (bf16[4,128,256]{2,1,0:T(8,128)(2,1)S(1)}, bf16[4,128,256]{2,1,0:T(8,128)(2,1)S(1)}, u32[]{:S(2)}, u32[]{:S(2)}) collective-permute-start(bf16[4,128,256]{2,1,0:T(8,128)(2,1)S(1)} %get-tuple-element.22), channel_id=1, source_target_pairs={{0,8},{8,0},{16,24},{24,16},{1,9},{9,1},{17,25},{25,17},{2,10},{10... | collective-permute-start | bytes 786440 | tf_op jit(solution)/shard_map/ppermute | solution.py:615
  29.6 9.2 %collective-permute-start.3 = (bf16[4,128,256]{2,1,0:T(8,128)(2,1)S(1)}, bf16[4,128,256]{2,1,0:T(8,128)(2,1)S(1)}, u32[]{:S(2)}, u32[]{:S(2)}) collective-permute-start(bf16[4,128,256]{2,1,0:T(8,128)(2,1)S(1)} %get-tuple-element.23), channel_id=1, source_target_pairs={{0,16},{8,24},{16,0},{24,8},{1,17},{9,25},{17,1},{25,9},{2,18},{10... | collective-permute-start | bytes 786440 | tf_op jit(solution)/shard_map/ppermute | solution.py:615
  31.1 7.7 %collective-permute-start.4 = (bf16[4,128,256]{2,1,0:T(8,128)(2,1)S(1)}, bf16[4,128,256]{2,1,0:T(8,128)(2,1)S(1)}, u32[]{:S(2)}, u32[]{:S(2)}) collective-permute-start(bf16[4,128,256]{2,1,0:T(8,128)(2,1)S(1)} %get-tuple-element.24), channel_id=1, source_target_pairs={{0,24},{8,16},{16,8},{24,0},{1,25},{9,17},{17,9},{25,1},{2,26},{10... | collective-permute-start | bytes 786440 | tf_op jit(solution)/shard_map/ppermute | solution.py:615
  67.1 9.2 %collective-permute-start.5 = (bf16[4,128,256]{2,1,0:T(8,128)(2,1)S(1)}, bf16[4,128,256]{2,1,0:T(8,128)(2,1)S(1)}, u32[]{:S(2)}, u32[]{:S(2)}) collective-permute-start(bf16[4,128,256]{2,1,0:T(8,128)(2,1)S(1)} %get-tuple-element.26), channel_id=1, source_target_pairs={{0,8},{8,0},{16,24},{24,16},{1,9},{9,1},{17,25},{25,17},{2,10},{10... | collective-permute-start | bytes 786440 | tf_op jit(solution)/shard_map/ppermute | solution.py:615
  68.0 13.4 %collective-permute-start.6 = (bf16[4,128,256]{2,1,0:T(8,128)(2,1)S(1)}, bf16[4,128,256]{2,1,0:T(8,128)(2,1)S(1)}, u32[]{:S(2)}, u32[]{:S(2)}) collective-permute-start(bf16[4,128,256]{2,1,0:T(8,128)(2,1)S(1)} %get-tuple-element.27), channel_id=1, source_target_pairs={{0,16},{8,24},{16,0},{24,8},{1,17},{9,25},{17,1},{25,9},{2,18},{10... | collective-permute-start | bytes 786440 | tf_op jit(solution)/shard_map/ppermute | solution.py:615
  68.7 12.7 %collective-permute-start.7 = (bf16[4,128,256]{2,1,0:T(8,128)(2,1)S(1)}, bf16[4,128,256]{2,1,0:T(8,128)(2,1)S(1)}, u32[]{:S(2)}, u32[]{:S(2)}) collective-permute-start(bf16[4,128,256]{2,1,0:T(8,128)(2,1)S(1)} %get-tuple-element.28), channel_id=1, source_target_pairs={{0,24},{8,16},{16,8},{24,0},{1,25},{9,17},{17,9},{25,1},{2,26},{10... | collective-permute-start | bytes 786440 | tf_op jit(solution)/shard_map/ppermute | solution.py:615

commit v20 on v19

--- a/solution.py
+++ b/solution.py
@@ -18,6 +18,7 @@
 SAFE_SCORE = 100.0
 FOLD = 4
 BATCH = 2
+PASSES = 6
 HIDDEN_CHUNK = 256
 
 F32 = jnp.float32
@@ -197,26 +198,33 @@
             band_buf[head] = factor(in_band(window_ref[head], 0, key_count, reach))
         value_buf[...] = jnp.ones(value_buf.shape, BF16)
 
-    normed = rms_scaled(own_ref[0].astype(F32), gain_ref[...]).astype(BF16)
+    batch = own_ref.shape[0]
+    own = own_ref[...].reshape(batch * rows, feat_width).astype(F32)
+    normed = rms_scaled(own, gain_ref[...]).astype(BF16)
     query_rows = dot(normed, w_query_ref[...]) * query_scale(head_size)
     key_rows = dot(normed, w_key_ref[...])
-    query_ref[0] = query_rows.astype(BF16)
-    key_buf[...] = key_rows.astype(BF16).T
-    put_values(value_buf, 0, dot(normed, w_value_ref[...]).astype(BF16))
+    value_rows = dot(normed, w_value_ref[...]).astype(BF16)
     query_norms, key_norms = norm_bounds(query_rows, heads), norm_bounds(key_rows, heads)
     blank = jnp.zeros((norm_ref.shape[1] - 2, LANES), F32)
-    norm_ref[0] = jnp.concatenate([query_norms, key_norms, blank], axis=0)
+    for member in range(batch):
+        here = slice(member * rows, (member + 1) * rows)
+        query_ref[member] = query_rows[here].astype(BF16)
+        key_buf[member] = key_rows[here].astype(BF16).T
+        put_values(value_buf.at[member], 0, value_rows[here])
+        norm_ref[member] = jnp.concatenate([query_norms, key_norms, blank], axis=0)
 
     @pl.when(is_safe(query_norms, key_norms))
     def _():
-        units = [(first, group) for first in range(0, blocks, 2) for group in range(heads // group_heads)]
-
-        def scores_of(first, group):
-            queries = query_ref[0, first * Q_ROWS : (first + 2) * Q_ROWS, group_lanes(group)]
-            return dot(stacked_heads(queries, head_size), key_buf[group_lanes(group), :])
+        pairs = range(0, blocks, 2)
+        groups = range(heads // group_heads)
+        units = [(member, first, group) for member in range(batch) for first in pairs for group in groups]
+
+        def scores_of(member, first, group):
+            queries = query_ref[member, first * Q_ROWS : (first + 2) * Q_ROWS, group_lanes(group)]
+            return dot(stacked_heads(queries, head_size), key_buf[member, group_lanes(group), :])
 
         scores = scores_of(*units[0])
-        for at, (first, group) in enumerate(units):
+        for at, (member, first, group) in enumerate(units):
             following = scores_of(*units[at + 1]) if at + 1 < len(units) else None
             ranges = [(max(0, b - reach_blocks), min(blocks, b + reach_blocks + 1)) for b in (first, first + 1)]
             spans = [(lower * Q_ROWS, upper * Q_ROWS) for lower, upper in ranges]
@@ -226,12 +234,16 @@
                 lower, upper = spans[block]
                 return band_buf[group * group_heads + head, :, lower + shift : upper + shift]
 
-            values = value_buf[:, 2 * group * LANES : 2 * (group + 1) * LANES]
+            values = value_buf[member, :, 2 * group * LANES : 2 * (group + 1) * LANES]
             mixed, totals = weighted_sums(unit_weights(scores, spans, band_of), values, head_size)
             here = slice(first * Q_ROWS, (first + 2) * Q_ROWS)
-            mixed_ref[0, here, group_lanes(group)] = mixed
-            total_ref[0, here, group_lanes(group)] = totals
+            mixed_ref[member, here, group_lanes(group)] = mixed
+            total_ref[member, here, group_lanes(group)] = totals
             scores = following
+
+
+def batch_of(members):
+    return BATCH if members % BATCH == 0 else 1
 
 
 def inner(head_window, own, gain, w_query, w_key, w_value, reach):
@@ -240,18 +252,20 @@
     key_count = Q_ROWS + 2 * reach
     shapes = [(own.shape, BF16), ((members, 8, LANES), F32), (own.shape, F32), (own.shape, F32)]
 
+    batch = batch_of(members)
+
     def spec(shape):
-        return pl.BlockSpec((1, *shape[1:]), lambda m: (m, 0, 0))
+        return pl.BlockSpec((batch, *shape[1:]), lambda m: (m, 0, 0))
 
     return pl.pallas_call(
         inner_kernel,
-        grid=(members,),
+        grid=(members // batch,),
         out_shape=[jax.ShapeDtypeStruct(*v) for v in shapes],
         in_specs=[smem_spec(), spec(own.shape)] + [vmem_spec()] * 4,
         out_specs=[spec(shape) for shape, _ in shapes],
         scratch_shapes=[
-            pltpu.VMEM((feat_width, rows), BF16),
-            pltpu.VMEM((rows, 2 * feat_width), BF16),
+            pltpu.VMEM((batch, feat_width, rows), BF16),
+            pltpu.VMEM((batch, rows, 2 * feat_width), BF16),
             pltpu.VMEM((heads, Q_ROWS, key_count), BF16),
         ],
         compiler_params=pltpu.CompilerParams(vmem_limit_bytes=VMEM_LIMIT),
@@ -415,7 +429,7 @@
     heads = head_window.shape[0]
     hidden_width = weights[3].shape[1]
     macs = members * row_count * feat_width * (3 * feat_width + 3 * hidden_width + 4 * reach)
-    batch = BATCH if members % BATCH == 0 else 1
+    batch = batch_of(members)
     share_rows = row_count // shares
 
     def spec(array):
@@ -501,6 +515,23 @@
     )(index, *shares, grid)
 
 
+def repeated_dot(a, b):
+    size = a.shape[0]
+
+    def pieces(values):
+        first = values.astype(BF16).astype(F32)
+        rest = values - first
+        second = rest.astype(BF16).astype(F32)
+        return first, second, rest - second
+
+    block = iota(a.shape, 1) // size
+    a_first, a_second, a_third = pieces(a)
+    b_first, b_second, b_third = (piece.astype(BF16) for piece in pieces(b))
+    left = jnp.where((block == 2) | (block == 4), a_second, jnp.where(block == 5, a_third, a_first))
+    right = jnp.concatenate([b_first, b_second, b_first, b_third, b_second, b_first], axis=0)
+    return dot(left.astype(BF16), right)
+
+
 def ensemble_transform(gram, proj):
     members = gram.shape[0]
     row, column = iota((members, members), 0), iota((members, members), 1)
@@ -519,14 +550,17 @@
     mean_level = jnp.sum(jnp.sum(system * identity, axis=1, keepdims=True), axis=0, keepdims=True) / members
     lifted = system + (mean_level - (members - 1.0)) * (1.0 / members)
     frobenius = jnp.sqrt(jnp.sum(jnp.sum(lifted * lifted, axis=1, keepdims=True), axis=0, keepdims=True))
-    root_iter = lifted / frobenius
-    inv_iter = identity
+    root_iter = jnp.concatenate([lifted / frobenius] * PASSES, axis=1)
+    repeated = iota((members, PASSES * members), 1) % members == iota((members, PASSES * members), 0)
+    repeated = repeated.astype(F32)
+    inv_iter = repeated
     for sweep in range(NS_STEPS):
-        product = root_iter if sweep == 0 else exact_dot(inv_iter, root_iter)
-        correction = 1.5 * identity - 0.5 * product
-        inv_iter = correction if sweep == 0 else exact_dot(correction, inv_iter)
+        product = root_iter if sweep == 0 else repeated_dot(inv_iter, root_iter)
+        correction = 1.5 * repeated - 0.5 * product
+        inv_iter = correction if sweep == 0 else repeated_dot(correction, inv_iter)
         if sweep < NS_STEPS - 1:
-            root_iter = exact_dot(root_iter, correction)
+            root_iter = repeated_dot(root_iter, correction)
+    inv_iter = inv_iter[:, :members]
     inv_root = inv_iter / jnp.sqrt(frobenius) + (1.0 / math.sqrt(members - 1.0) - 1.0 / jnp.sqrt(mean_level)) * (
         1.0 / members
     )

time: 82.8 us -> 82.9 us (level)
  blocking collectives: 22.9 us -> 23.8 us
    all_to_all x1, blocking collectives: 22.9 us -> 23.8 us  [local(): lax.all_to_all(jnp.broadcast_to(partial[None], (device_count, *partial.sh...]
    pallas_call x1, Pallas kernels: 3.39 us -> 2.55 us  [inner(): pl.pallas_call(inner_kernel, grid=(members // batch,), out_shape=[jax.Sha...]
  transfers between devices with their start and end apart: 8 -> 8, of which waited for: 4 -> 4; matrix products, arithmetic and copies ran while one was open for 0% -> 0% of each run, Pallas kernels for 6% -> 5%
where the time goes in v20:
time: 82.9 us; the launch traced here: 82.7 us
  Pallas kernels  30.3 us (37%)
  blocking collectives  23.8 us (29%)
  waiting for transfers between devices  17 us (21%)
  starting transfers between devices  8.79 us (11%)
  local copies, waits for them, and re-layouts  2.26 us (3%)
    all_to_all x1, blocking collectives, local(): lax.all_to_all(jnp.broadcast_to(partial[None], (device_count, *partial.sh...  23.8 us
    pallas_call x1, Pallas kernels, forward(): pl.pallas_call(functools.partial(forward_kernel, total_len), grid=(member...  20 us
    ppermute x6, waiting for transfers between devices, exchanged(): lax.ppermute(v, 'mem', [(i, i ^ part) for i in range(count)])  17 us
    ppermute x6, starting transfers between devices, exchanged(): lax.ppermute(v, 'mem', [(i, i ^ part) for i in range(count)])  7.64 us
    pallas_call x1, Pallas kernels, combine(): pl.pallas_call(combine_kernel, out_shape=[jax.ShapeDtypeStruct(v.shape, B...  3.75 us
    pallas_call x1, Pallas kernels, inner(): pl.pallas_call(inner_kernel, grid=(members // batch,), out_shape=[jax.Sha...  2.55 us
    dynamic_slice x1, local copies, waits for them, and re-layouts, halos(): far = lax.dynamic_slice_in_dim(own, odd * last, reach, axis=1)  2.17 us
    pallas_call x1, Pallas kernels, gram_partial(): pl.pallas_call(gram_kernel, out_shape=jax.ShapeDtypeStruct((-(-filled //...  1.67 us
  transfers between devices with their start and end apart: 8, of which 4 were waited for; matrix products, arithmetic and copies ran while one was open for 0% of the time, Pallas kernels for 5%

profile of v20, /device:TPU:0, one launch (start us, length us, event | category | flops | bytes accessed | tf_op | source)
XLA Modules:
  0.0 82.7 jit_solution(4855060063270420425)
XLA Ops:
  0.0 2.2 %constant_dynamic-slice_fusion = (bf16[4,256,256]{2,1,0:T(8,128)(2,1)S(1)}, bf16[4,256,256]{2,1,0:T(8,128)(2,1)}) fusion(bf16[4,512,256]{2,1,0:T(8,128)(2,1)} %state_ref.1, s32[]{:T(128)S(6)} %select_n.15, s32[]{:T(128)S(6)} %select_n.14), kind=kLoop, calls=%fused_computation | loop fusion | bytes 2097160 | tf_op jit(solution)/shard_map/dynamic_slice | solution.py:658
  2.2 0.5 collective-permute-start
  2.7 0.7 collective-permute-start.1
  3.4 0.0 copy-start.1
  3.5 0.0 copy-start.2
  3.5 0.0 copy-start.3
  3.5 0.0 copy-start.7
  3.5 0.0 copy-start.13
  3.5 2.6 %inner.1 = (bf16[4,512,256]{2,1,0:T(8,128)(2,1)S(1)}, f32[4,8,128]{2,1,0:T(8,128)S(1)}, f32[4,512,256]{2,1,0:T(8,128)S(1)}, f32[4,512,256]{2,1,0:T(8,128)S(1)}) custom-call(s32[4]{0:T(128)S(1)} %copy-done.14, bf16[4,512,256]{2,1,0:T(8,128)(2,1)S(1)} %copy-done, f32[1,256]{1,0:T(1,128)S(1)} %bitcast.13, bf16[256,256]{1,0:T(8,128)(2,1)S(1)} %copy-done.4, ...), custom_call_target="tpu_custom_call" | custom-call | flops 5100273664 | bytes 7340032 | tf_op jit(solution)/shard_map/inner/pallas_call | solution.py:260
  6.1 0.0 collective-permute-done.near_ref
  6.1 0.0 collective-permute-done.1.far_ref
  6.1 0.0 copy-start.8
  6.1 0.0 copy-start.9
  6.2 0.0 copy-start.10
  6.2 0.0 copy-start.11
  6.2 20.0 %forward.1 = (bf16[4,128,256]{2,1,0:T(8,128)(2,1)S(1)}, bf16[4,128,256]{2,1,0:T(8,128)(2,1)S(1)}, bf16[4,128,256]{2,1,0:T(8,128)(2,1)S(1)}, bf16[4,128,256]{2,1,0:T(8,128)(2,1)S(1)}) custom-call(s32[1]{0:T(128)} %bitcast.1.tok_ref, s32[1]{0:T(128)} %bitcast.mem_ref.index_ref, s32[4]{0:T(128)S(1)} %copy-done.14, bf16[4,512,256]{2,1,0:T(8,128)(2,1)S(1)} %copy-done, ...), custom_call_target="tpu_custom_call" | custom-call | flops 5100273664 | bytes 5242880 | tf_op jit(solution)/shard_map/forward/pallas_call | solution.py:438
  26.2 2.5 %collective-permute-start.2 = (bf16[4,128,256]{2,1,0:T(8,128)(2,1)S(1)}, bf16[4,128,256]{2,1,0:T(8,128)(2,1)S(1)}, u32[]{:S(2)}, u32[]{:S(2)}) collective-permute-start(bf16[4,128,256]{2,1,0:T(8,128)(2,1)S(1)} %get-tuple-element.22), channel_id=1, source_target_pairs={{0,8},{8,0},{16,24},{24,16},{1,9},{9,1},{17,25},{25,17},{2,10},{10... | collective-permute-start | bytes 786440 | tf_op jit(solution)/shard_map/ppermute | solution.py:649
  28.8 1.5 %collective-permute-start.3 = (bf16[4,128,256]{2,1,0:T(8,128)(2,1)S(1)}, bf16[4,128,256]{2,1,0:T(8,128)(2,1)S(1)}, u32[]{:S(2)}, u32[]{:S(2)}) collective-permute-start(bf16[4,128,256]{2,1,0:T(8,128)(2,1)S(1)} %get-tuple-element.23), channel_id=1, source_target_pairs={{0,16},{8,24},{16,0},{24,8},{1,17},{9,25},{17,1},{25,9},{2,18},{10... | collective-permute-start | bytes 786440 | tf_op jit(solution)/shard_map/ppermute | solution.py:649
  30.3 0.0 collective-permute-start.4
  30.3 1.3 %sample_grid.1.refs_4_ = f32[2,128,256]{2,1,0:T(8,128)S(1)} custom-call(s32[1]{0:T(128)} %bitcast.4.start_ref, s32[1,4096]{1,0:T(1,128)S(1)} %bitcast.9, s32[1,4096]{1,0:T(1,128)S(1)} %bitcast.10, f32[1,4096]{1,0:T(1,128)S(1)} %bitcast.11, f32[1,4096]{1,0:T(1,128)S(1)} %bitcast.12), custom_call_target="tpu_custom_call" | custom-call | flops 1073741824 | bytes 65536 | tf_op jit(solution)/shard_map/sample_grid/pallas_call | solution.py:80
  31.7 1.5 %collective-permute-done.2.refs_1_ = bf16[4,128,256]{2,1,0:T(8,128)(2,1)S(1)} collective-permute-done((bf16[4,128,256]{2,1,0:T(8,128)(2,1)S(1)}, bf16[4,128,256]{2,1,0:T(8,128)(2,1)S(1)}, u32[]{:S(2)}, u32[]{:S(2)}) %collective-permute-start.2) | collective-permute-done | bytes 262176 | tf_op jit(solution)/shard_map/ppermute | solution.py:649
  33.1 4.8 %collective-permute-done.3.refs_2_ = bf16[4,128,256]{2,1,0:T(8,128)(2,1)S(1)} collective-permute-done((bf16[4,128,256]{2,1,0:T(8,128)(2,1)S(1)}, bf16[4,128,256]{2,1,0:T(8,128)(2,1)S(1)}, u32[]{:S(2)}, u32[]{:S(2)}) %collective-permute-start.3) | collective-permute-done | bytes 262176 | tf_op jit(solution)/shard_map/ppermute | solution.py:649
  38.0 1.7 %gram.1 = f32[8,128]{1,0:T(8,128)S(1)} custom-call(s32[1]{0:T(128)} %bitcast.mem_ref.index_ref, bf16[4,128,256]{2,1,0:T(8,128)(2,1)S(1)} %get-tuple-element.21.refs_0_, bf16[4,128,256]{2,1,0:T(8,128)(2,1)S(1)} %collective-permute-done.2.refs_1_, bf16[4,128,256]{2,1,0:T(8,128)(2,1)S(1)} %collective-permute-done.3.refs_2_, ...), custom_call_target="tpu_custom_call" | custom-call | flops 805306368 | bytes 1048576 | tf_op jit(solution)/shard_map/gram/pallas_call | solution.py:505
  39.7 23.8 %all_to_all.5.partial_ref = f32[32,8,128]{2,1,0:T(8,128)S(1)} all-to-all(f32[32,8,128]{2,1,0:T(8,128)S(1)} %broadcast_in_dim.2), channel_id=1, replica_groups=mesh['mem'=4,'tok'=8] {'mem','tok'}, dimensions={0} | all-to-all | bytes 262144 | tf_op jit(solution)/shard_map/all_to_all | solution.py:703
  63.5 3.7 %combine.1 = (bf16[4,128,256]{2,1,0:T(8,128)(2,1)S(1)}, bf16[4,128,256]{2,1,0:T(8,128)(2,1)S(1)}, bf16[4,128,256]{2,1,0:T(8,128)(2,1)S(1)}, bf16[4,128,256]{2,1,0:T(8,128)(2,1)S(1)}) custom-call(s32[1]{0:T(128)} %bitcast.mem_ref.index_ref, f32[32,8,128]{2,1,0:T(8,128)S(1)} %all_to_all.5.partial_ref, bf16[4,128,256]{2,1,0:T(8,128)(2,1)S(1)} %get-tuple-element.21.refs_0_, ...), custom_call_target="tpu_custom_call" | custom-call | flops 536870912 | bytes 2097152 | tf_op jit(solution)/shard_map/combine/pallas_call | solution.py:608
  67.3 0.9 %collective-permute-start.5 = (bf16[4,128,256]{2,1,0:T(8,128)(2,1)S(1)}, bf16[4,128,256]{2,1,0:T(8,128)(2,1)S(1)}, u32[]{:S(2)}, u32[]{:S(2)}) collective-permute-start(bf16[4,128,256]{2,1,0:T(8,128)(2,1)S(1)} %get-tuple-element.26), channel_id=1, source_target_pairs={{0,8},{8,0},{16,24},{24,16},{1,9},{9,1},{17,25},{25,17},{2,10},{10... | collective-permute-start | bytes 786440 | tf_op jit(solution)/shard_map/ppermute | solution.py:649
  68.1 0.7 collective-permute-start.6
  68.9 2.0 %collective-permute-start.7 = (bf16[4,128,256]{2,1,0:T(8,128)(2,1)S(1)}, bf16[4,128,256]{2,1,0:T(8,128)(2,1)S(1)}, u32[]{:S(2)}, u32[]{:S(2)}) collective-permute-start(bf16[4,128,256]{2,1,0:T(8,128)(2,1)S(1)} %get-tuple-element.28), channel_id=1, source_target_pairs={{0,24},{8,16},{16,8},{24,0},{1,25},{9,17},{17,9},{25,1},{2,26},{10... | collective-permute-start | bytes 786440 | tf_op jit(solution)/shard_map/ppermute | solution.py:649
  70.8 5.6 %collective-permute-done.5.refs_1_ = bf16[4,128,256]{2,1,0:T(8,128)(2,1)S(1)} collective-permute-done((bf16[4,128,256]{2,1,0:T(8,128)(2,1)S(1)}, bf16[4,128,256]{2,1,0:T(8,128)(2,1)S(1)}, u32[]{:S(2)}, u32[]{:S(2)}) %collective-permute-start.5) | collective-permute-done | bytes 262176 | tf_op jit(solution)/shard_map/ppermute | solution.py:649
  76.4 5.1 %collective-permute-done.6.refs_2_ = bf16[4,128,256]{2,1,0:T(8,128)(2,1)S(1)} collective-permute-done((bf16[4,128,256]{2,1,0:T(8,128)(2,1)S(1)}, bf16[4,128,256]{2,1,0:T(8,128)(2,1)S(1)}, u32[]{:S(2)}, u32[]{:S(2)}) %collective-permute-start.6) | collective-permute-done | bytes 262176 | tf_op jit(solution)/shard_map/ppermute | solution.py:649
  81.5 0.0 collective-permute-done.7.refs_3_
  81.5 1.0 %assemble.1 = bf16[4,512,256]{2,1,0:T(8,128)(2,1)} custom-call(s32[1]{0:T(128)} %bitcast.mem_ref.index_ref, bf16[4,128,256]{2,1,0:T(8,128)(2,1)S(1)} %get-tuple-element.25.refs_0_, bf16[4,128,256]{2,1,0:T(8,128)(2,1)S(1)} %collective-permute-done.5.refs_1_, bf16[4,128,256]{2,1,0:T(8,128)(2,1)S(1)} %collective-permute-done.6.refs_2_, ...), custom_call_target="tpu_custom_call" | custom-call | bytes 2097152 | tf_op jit(solution)/shard_map/assemble/pallas_call | solution.py:634
  (23 shorter events, 0.1 us)
Async XLA Ops:
  0.0 3.4 %copy-start = (bf16[4,512,256]{2,1,0:T(8,128)(2,1)S(1)}, bf16[4,512,256]{2,1,0:T(8,128)(2,1)}, u32[]{:S(2)}) copy-start(bf16[4,512,256]{2,1,0:T(8,128)(2,1)} %state_ref.1) | copy-start | bytes 3145732
  0.0 3.4 %copy-start.12 = (f32[256]{0:T(256)S(1)}, f32[256]{0:T(256)}, u32[]{:S(2)}) copy-start(f32[256]{0:T(256)} %param.16) | copy-start | bytes 3076
  0.0 3.4 %copy-start.4 = (bf16[256,256]{1,0:T(8,128)(2,1)S(1)}, bf16[256,256]{1,0:T(8,128)(2,1)}, u32[]{:S(2)}) copy-start(bf16[256,256]{1,0:T(8,128)(2,1)} %w_query_ref.1) | copy-start | bytes 393220
  0.0 3.4 %copy-start.5 = (bf16[256,256]{1,0:T(8,128)(2,1)S(1)}, bf16[256,256]{1,0:T(8,128)(2,1)}, u32[]{:S(2)}) copy-start(bf16[256,256]{1,0:T(8,128)(2,1)} %w_key_ref.3) | copy-start | bytes 393220
  0.0 3.4 %copy-start.6 = (bf16[256,256]{1,0:T(8,128)(2,1)S(1)}, bf16[256,256]{1,0:T(8,128)(2,1)}, u32[]{:S(2)}) copy-start(bf16[256,256]{1,0:T(8,128)(2,1)} %w_value_ref.3) | copy-start | bytes 393220
  0.0 3.4 %copy-start.14 = (s32[4]{0:T(128)S(1)}, s32[4]{0:T(128)}, u32[]{:S(2)}) copy-start(s32[4]{0:T(128)} %window_ref.3) | copy-start | bytes 52
  2.2 3.8 %collective-permute-start = (bf16[4,256,256]{2,1,0:T(8,128)(2,1)}, bf16[4,256,256]{2,1,0:T(8,128)(2,1)S(1)}, u32[]{:S(2)}, u32[]{:S(2)}) collective-permute-start(bf16[4,256,256]{2,1,0:T(8,128)(2,1)} %get-tuple-element.30), channel_id=1, source_target_pairs={{0,1},{1,0},{2,3},{3,2},{4,5},{5,4},{6,7},{7,6},{8,9},{9,8},{10,11... | collective-permute-start | bytes 1572872 | tf_op jit(solution)/shard_map/ppermute | solution.py:661
  2.7 3.4 %collective-permute-start.1 = (bf16[4,256,256]{2,1,0:T(8,128)(2,1)S(1)}, bf16[4,256,256]{2,1,0:T(8,128)(2,1)S(1)}, u32[]{:S(2)}, u32[]{:S(2)}) collective-permute-start(bf16[4,256,256]{2,1,0:T(8,128)(2,1)S(1)} %get-tuple-element.29), channel_id=1, source_target_pairs={{1,2},{2,1},{3,4},{4,3},{5,6},{6,5},{9,10},{10,9},{11,12},{12,11},... | collective-permute-start | bytes 1572872 | tf_op jit(solution)/shard_map/ppermute | solution.py:661
  3.4 2.6 %copy-start.1 = (bf16[256,1024]{1,0:T(8,128)(2,1)S(1)}, bf16[256,1024]{1,0:T(8,128)(2,1)}, u32[]{:S(2)}) copy-start(bf16[256,1024]{1,0:T(8,128)(2,1)} %w_gate_ref.1) | copy-start | bytes 1572868
  3.5 2.6 %copy-start.2 = (bf16[256,1024]{1,0:T(8,128)(2,1)S(1)}, bf16[256,1024]{1,0:T(8,128)(2,1)}, u32[]{:S(2)}) copy-start(bf16[256,1024]{1,0:T(8,128)(2,1)} %w_up_ref.1) | copy-start | bytes 1572868
  3.5 2.6 %copy-start.3 = (bf16[1024,256]{1,0:T(8,128)(2,1)S(1)}, bf16[1024,256]{1,0:T(8,128)(2,1)}, u32[]{:S(2)}) copy-start(bf16[1024,256]{1,0:T(8,128)(2,1)} %down_weight_ref.1) | copy-start | bytes 1572868
  3.5 2.6 %copy-start.7 = (bf16[256,256]{1,0:T(8,128)(2,1)S(1)}, bf16[256,256]{1,0:T(8,128)(2,1)}, u32[]{:S(2)}) copy-start(bf16[256,256]{1,0:T(8,128)(2,1)} %w_out_ref.1) | copy-start | bytes 393220
  3.5 2.6 %copy-start.13 = (f32[256]{0:T(256)S(1)}, f32[256]{0:T(256)}, u32[]{:S(2)}) copy-start(f32[256]{0:T(256)} %param.17) | copy-start | bytes 3076
  6.1 24.2 %copy-start.8 = (s32[4096]{0:T(1024)S(1)}, s32[4096]{0:T(1024)}, u32[]{:S(2)}) copy-start(s32[4096]{0:T(1024)} %param.26) | copy-start | bytes 49156
  6.1 24.2 %copy-start.9 = (s32[4096]{0:T(1024)S(1)}, s32[4096]{0:T(1024)}, u32[]{:S(2)}) copy-start(s32[4096]{0:T(1024)} %param.27) | copy-start | bytes 49156
  6.2 24.2 %copy-start.10 = (f32[4096]{0:T(1024)S(1)}, f32[4096]{0:T(1024)}, u32[]{:S(2)}) copy-start(f32[4096]{0:T(1024)} %param.28) | copy-start | bytes 49156
  6.2 24.2 %copy-start.11 = (f32[4096]{0:T(1024)S(1)}, f32[4096]{0:T(1024)}, u32[]{:S(2)}) copy-start(f32[4096]{0:T(1024)} %param.29) | copy-start | bytes 49156
  26.2 6.9 %collective-permute-start.2 = (bf16[4,128,256]{2,1,0:T(8,128)(2,1)S(1)}, bf16[4,128,256]{2,1,0:T(8,128)(2,1)S(1)}, u32[]{:S(2)}, u32[]{:S(2)}) collective-permute-start(bf16[4,128,256]{2,1,0:T(8,128)(2,1)S(1)} %get-tuple-element.22), channel_id=1, source_target_pairs={{0,8},{8,0},{16,24},{24,16},{1,9},{9,1},{17,25},{25,17},{2,10},{10... | collective-permute-start | bytes 786440 | tf_op jit(solution)/shard_map/ppermute | solution.py:649
  28.8 9.2 %collective-permute-start.3 = (bf16[4,128,256]{2,1,0:T(8,128)(2,1)S(1)}, bf16[4,128,256]{2,1,0:T(8,128)(2,1)S(1)}, u32[]{:S(2)}, u32[]{:S(2)}) collective-permute-start(bf16[4,128,256]{2,1,0:T(8,128)(2,1)S(1)} %get-tuple-element.23), channel_id=1, source_target_pairs={{0,16},{8,24},{16,0},{24,8},{1,17},{9,25},{17,1},{25,9},{2,18},{10... | collective-permute-start | bytes 786440 | tf_op jit(solution)/shard_map/ppermute | solution.py:649
  30.3 7.7 %collective-permute-start.4 = (bf16[4,128,256]{2,1,0:T(8,128)(2,1)S(1)}, bf16[4,128,256]{2,1,0:T(8,128)(2,1)S(1)}, u32[]{:S(2)}, u32[]{:S(2)}) collective-permute-start(bf16[4,128,256]{2,1,0:T(8,128)(2,1)S(1)} %get-tuple-element.24), channel_id=1, source_target_pairs={{0,24},{8,16},{16,8},{24,0},{1,25},{9,17},{17,9},{25,1},{2,26},{10... | collective-permute-start | bytes 786440 | tf_op jit(solution)/shard_map/ppermute | solution.py:649
  67.3 9.2 %collective-permute-start.5 = (bf16[4,128,256]{2,1,0:T(8,128)(2,1)S(1)}, bf16[4,128,256]{2,1,0:T(8,128)(2,1)S(1)}, u32[]{:S(2)}, u32[]{:S(2)}) collective-permute-start(bf16[4,128,256]{2,1,0:T(8,128)(2,1)S(1)} %get-tuple-element.26), channel_id=1, source_target_pairs={{0,8},{8,0},{16,24},{24,16},{1,9},{9,1},{17,25},{25,17},{2,10},{10... | collective-permute-start | bytes 786440 | tf_op jit(solution)/shard_map/ppermute | solution.py:649
  68.1 13.4 %collective-permute-start.6 = (bf16[4,128,256]{2,1,0:T(8,128)(2,1)S(1)}, bf16[4,128,256]{2,1,0:T(8,128)(2,1)S(1)}, u32[]{:S(2)}, u32[]{:S(2)}) collective-permute-start(bf16[4,128,256]{2,1,0:T(8,128)(2,1)S(1)} %get-tuple-element.27), channel_id=1, source_target_pairs={{0,16},{8,24},{16,0},{24,8},{1,17},{9,25},{17,1},{25,9},{2,18},{10... | collective-permute-start | bytes 786440 | tf_op jit(solution)/shard_map/ppermute | solution.py:649
  68.9 12.7 %collective-permute-start.7 = (bf16[4,128,256]{2,1,0:T(8,128)(2,1)S(1)}, bf16[4,128,256]{2,1,0:T(8,128)(2,1)S(1)}, u32[]{:S(2)}, u32[]{:S(2)}) collective-permute-start(bf16[4,128,256]{2,1,0:T(8,128)(2,1)S(1)} %get-tuple-element.28), channel_id=1, source_target_pairs={{0,24},{8,16},{16,8},{24,0},{1,25},{9,17},{17,9},{25,1},{2,26},{10... | collective-permute-start | bytes 786440 | tf_op jit(solution)/shard_map/ppermute | solution.py:649

commit v21 on v20

--- a/solution.py
+++ b/solution.py
@@ -410,11 +410,18 @@
     after = (state + dot(mixed_buf[...], w_out_ref[...])).astype(BF16)
     normed_mid = rms_scaled(after.astype(F32), ffn_gain_ref[...]).astype(BF16)
     forecast = after.astype(F32)
-    for lower in range(0, w_gate_ref.shape[1], HIDDEN_CHUNK):
-        part = slice(lower, lower + HIDDEN_CHUNK)
-        gate = 0.5 * dot(normed_mid, w_gate_ref[:, part])
-        hidden = (gate * (1.0 + jnp.tanh(gate.astype(BF16)).astype(F32)) * dot(normed_mid, w_up_ref[:, part])).astype(BF16)
+    chunks = [slice(lower, lower + HIDDEN_CHUNK) for lower in range(0, w_gate_ref.shape[1], HIDDEN_CHUNK)]
+
+    def gate_and_up(part):
+        return dot(normed_mid, w_gate_ref[:, part]), dot(normed_mid, w_up_ref[:, part])
+
+    gate, up = gate_and_up(chunks[0])
+    for at, part in enumerate(chunks):
+        following = gate_and_up(chunks[at + 1]) if at + 1 < len(chunks) else (None, None)
+        gate = 0.5 * gate
+        hidden = (gate * (1.0 + jnp.tanh(gate.astype(BF16)).astype(F32)) * up).astype(BF16)
         forecast += dot(hidden, down_weight_ref[part, :])
+        gate, up = following
     forecast_buf[...] = forecast.astype(BF16)
     share_rows = out_refs[0].shape[1]
     for part, out_ref in enumerate(out_refs):
@@ -469,6 +476,7 @@
     index = index_ref[0]
     stack = members * GROUP
     total = jnp.zeros((stack, stack), F32)
+    crossed = jnp.zeros((stack, stack), F32)
     proj = jnp.zeros((members, GROUP, feat_width), F32)
     for lower in range(0, rows, GROUP):
         part = slice(lower, lower + GROUP)
@@ -477,10 +485,11 @@
         spread = fields - mean[None]
         weight = grid_ref[0, part, :]
         proj += spread * (grid_ref[1, part, :] - weight * mean)[None]
-        high, low = halves(spread.reshape(stack, feat_width))
-        w_high, w_low = halves((spread * weight[None]).reshape(stack, feat_width))
-        last = ((1,), (1,))
-        total += dot(w_high, high, last) + dot(w_high, low, last) + dot(w_low, high, last)
+        scaled = spread * jnp.sqrt(jnp.maximum(weight, 0.0))[None]
+        high, low = halves(scaled.reshape(stack, feat_width))
+        total += dot(high, high, ((1,), (1,)))
+        crossed += dot(high, low, ((1,), (1,)))
+    total += crossed + crossed.T
     same = iota((stack, stack), 0) % GROUP == iota((stack, stack), 1) % GROUP
     by_row = jnp.sum(jnp.where(same, total, 0.0).reshape(members, GROUP, stack), axis=1)
     column = global_member(iota((stack, LANES), 0) // GROUP, index, own_members)
@@ -654,11 +663,13 @@
     count = lax.axis_size("tok")
     odd = lax.axis_index("tok") % 2
     last = own.shape[1] - reach
-    near = lax.dynamic_slice_in_dim(own, (1 - odd) * last, reach, axis=1)
-    far = lax.dynamic_slice_in_dim(own, odd * last, reach, axis=1)
     near_pairs = [(i, i ^ 1) for i in range(count)]
     far_pairs = [pair for i in range(1, count - 1, 2) for pair in ((i, i + 1), (i + 1, i))]
-    return lax.ppermute(near, "tok", near_pairs), lax.ppermute(far, "tok", far_pairs)
+    far = lax.dynamic_slice_in_dim(own, odd * last, reach, axis=1)
+    far, own = lax.optimization_barrier((far, own))
+    far_halo = lax.ppermute(far, "tok", far_pairs)
+    near = lax.dynamic_slice_in_dim(own, (1 - odd) * last, reach, axis=1)
+    return lax.ppermute(near, "tok", near_pairs), far_halo
 
 
 def local(

time: 82.9 us -> 83.6 us (level)
  local copies, waits for them, and re-layouts: 2.26 us -> 3.15 us
    dynamic_slice x0 -> x1, local copies, waits for them, and re-layouts: none -> 1.88 us  [halos(): near = lax.dynamic_slice_in_dim(own, (1 - odd) * last, reach, axis=1)]
    dynamic_slice x1, local copies, waits for them, and re-layouts: 2.17 us -> 1.19 us  [halos(): far = lax.dynamic_slice_in_dim(own, odd * last, reach, axis=1)]
where the time goes in v21:
time: 83.6 us; the launch traced here: 83.4 us
  Pallas kernels  30.1 us (36%)
  blocking collectives  23.8 us (28%)
  waiting for transfers between devices  17 us (20%)
  starting transfers between devices  8.79 us (11%)
  local copies, waits for them, and re-layouts  3.15 us (4%)
    all_to_all x1, blocking collectives, local(): lax.all_to_all(jnp.broadcast_to(partial[None], (device_count, *partial.sh...  23.8 us
    pallas_call x1, Pallas kernels, forward(): pl.pallas_call(functools.partial(forward_kernel, total_len), grid=(member...  20 us
    ppermute x6, waiting for transfers between devices, exchanged(): lax.ppermute(v, 'mem', [(i, i ^ part) for i in range(count)])  17 us
    ppermute x6, starting transfers between devices, exchanged(): lax.ppermute(v, 'mem', [(i, i ^ part) for i in range(count)])  7.64 us
    pallas_call x1, Pallas kernels, combine(): pl.pallas_call(combine_kernel, out_shape=[jax.ShapeDtypeStruct(v.shape, B...  3.74 us
    pallas_call x1, Pallas kernels, inner(): pl.pallas_call(inner_kernel, grid=(members // batch,), out_shape=[jax.Sha...  2.55 us
    dynamic_slice x1, local copies, waits for them, and re-layouts, halos(): near = lax.dynamic_slice_in_dim(own, (1 - odd) * last, reach, axis=1)  1.88 us
  transfers between devices with their start and end apart: 8, of which 4 were waited for; matrix products, arithmetic and copies ran while one was open for 0% of the time, Pallas kernels for 5%

profile of v21, /device:TPU:0, one launch (start us, length us, event | category | flops | bytes accessed | tf_op | source)
XLA Modules:
  0.0 83.4 jit_solution(1079019802874430686)
XLA Ops:
  0.0 1.2 %constant_dynamic-slice_fusion.1 = bf16[4,256,256]{2,1,0:T(8,128)(2,1)S(1)} fusion(bf16[4,512,256]{2,1,0:T(8,128)(2,1)} %state_ref.1, s32[]{:T(128)S(6)} %select_n.14), kind=kLoop, calls=%fused_computation.1 | loop fusion | bytes 1048580 | tf_op jit(solution)/shard_map/dynamic_slice | solution.py:668
  1.2 1.9 %constant_dynamic-slice_fusion = bf16[4,256,256]{2,1,0:T(8,128)(2,1)} fusion(bf16[4,512,256]{2,1,0:T(8,128)(2,1)} %state_ref.1, s32[]{:T(128)S(6)} %select_n.15), kind=kLoop, calls=%fused_computation | loop fusion | bytes 1048580 | tf_op jit(solution)/shard_map/dynamic_slice | solution.py:671
  3.1 0.5 collective-permute-start
  3.6 0.7 collective-permute-start.1
  4.3 0.0 copy-start.1
  4.4 0.0 copy-start.2
  4.4 0.0 copy-start.3
  4.4 0.0 copy-start.7
  4.4 0.0 copy-start.13
  4.4 2.6 %inner.1 = (bf16[4,512,256]{2,1,0:T(8,128)(2,1)S(1)}, f32[4,8,128]{2,1,0:T(8,128)S(1)}, f32[4,512,256]{2,1,0:T(8,128)S(1)}, f32[4,512,256]{2,1,0:T(8,128)S(1)}) custom-call(s32[4]{0:T(128)S(1)} %copy-done.14, bf16[4,512,256]{2,1,0:T(8,128)(2,1)S(1)} %copy-done, f32[1,256]{1,0:T(1,128)S(1)} %bitcast.13, bf16[256,256]{1,0:T(8,128)(2,1)S(1)} %copy-done.4, ...), custom_call_target="tpu_custom_call" | custom-call | flops 5100273664 | bytes 7340032 | tf_op jit(solution)/shard_map/inner/pallas_call | solution.py:260
  7.0 0.0 collective-permute-done.near_ref
  7.0 0.0 collective-permute-done.1.far_ref
  7.0 0.0 copy-start.8
  7.0 0.0 copy-start.9
  7.1 0.0 copy-start.10
  7.1 0.0 copy-start.11
  7.1 20.0 %forward.1 = (bf16[4,128,256]{2,1,0:T(8,128)(2,1)S(1)}, bf16[4,128,256]{2,1,0:T(8,128)(2,1)S(1)}, bf16[4,128,256]{2,1,0:T(8,128)(2,1)S(1)}, bf16[4,128,256]{2,1,0:T(8,128)(2,1)S(1)}) custom-call(s32[1]{0:T(128)} %bitcast.1.tok_ref, s32[1]{0:T(128)} %bitcast.mem_ref.index_ref, s32[4]{0:T(128)S(1)} %copy-done.14, bf16[4,512,256]{2,1,0:T(8,128)(2,1)S(1)} %copy-done, ...), custom_call_target="tpu_custom_call" | custom-call | flops 5100273664 | bytes 5242880 | tf_op jit(solution)/shard_map/forward/pallas_call | solution.py:445
  27.1 2.5 %collective-permute-start.2 = (bf16[4,128,256]{2,1,0:T(8,128)(2,1)S(1)}, bf16[4,128,256]{2,1,0:T(8,128)(2,1)S(1)}, u32[]{:S(2)}, u32[]{:S(2)}) collective-permute-start(bf16[4,128,256]{2,1,0:T(8,128)(2,1)S(1)} %get-tuple-element.26), channel_id=1, source_target_pairs={{0,8},{8,0},{16,24},{24,16},{1,9},{9,1},{17,25},{25,17},{2,10},{10... | collective-permute-start | bytes 786440 | tf_op jit(solution)/shard_map/ppermute | solution.py:658
  29.6 1.5 %collective-permute-start.3 = (bf16[4,128,256]{2,1,0:T(8,128)(2,1)S(1)}, bf16[4,128,256]{2,1,0:T(8,128)(2,1)S(1)}, u32[]{:S(2)}, u32[]{:S(2)}) collective-permute-start(bf16[4,128,256]{2,1,0:T(8,128)(2,1)S(1)} %get-tuple-element.27), channel_id=1, source_target_pairs={{0,16},{8,24},{16,0},{24,8},{1,17},{9,25},{17,1},{25,9},{2,18},{10... | collective-permute-start | bytes 786440 | tf_op jit(solution)/shard_map/ppermute | solution.py:658
  31.2 0.0 collective-permute-start.4
  31.2 1.3 %sample_grid.1.refs_4_ = f32[2,128,256]{2,1,0:T(8,128)S(1)} custom-call(s32[1]{0:T(128)} %bitcast.4.start_ref, s32[1,4096]{1,0:T(1,128)S(1)} %bitcast.9, s32[1,4096]{1,0:T(1,128)S(1)} %bitcast.10, f32[1,4096]{1,0:T(1,128)S(1)} %bitcast.11, f32[1,4096]{1,0:T(1,128)S(1)} %bitcast.12), custom_call_target="tpu_custom_call" | custom-call | flops 1073741824 | bytes 65536 | tf_op jit(solution)/shard_map/sample_grid/pallas_call | solution.py:80
  32.5 1.5 %collective-permute-done.2.refs_1_ = bf16[4,128,256]{2,1,0:T(8,128)(2,1)S(1)} collective-permute-done((bf16[4,128,256]{2,1,0:T(8,128)(2,1)S(1)}, bf16[4,128,256]{2,1,0:T(8,128)(2,1)S(1)}, u32[]{:S(2)}, u32[]{:S(2)}) %collective-permute-start.2) | collective-permute-done | bytes 262176 | tf_op jit(solution)/shard_map/ppermute | solution.py:658
  34.0 4.8 %collective-permute-done.3.refs_2_ = bf16[4,128,256]{2,1,0:T(8,128)(2,1)S(1)} collective-permute-done((bf16[4,128,256]{2,1,0:T(8,128)(2,1)S(1)}, bf16[4,128,256]{2,1,0:T(8,128)(2,1)S(1)}, u32[]{:S(2)}, u32[]{:S(2)}) %collective-permute-start.3) | collective-permute-done | bytes 262176 | tf_op jit(solution)/shard_map/ppermute | solution.py:658
  38.8 1.5 %gram.1 = f32[8,128]{1,0:T(8,128)S(1)} custom-call(s32[1]{0:T(128)} %bitcast.mem_ref.index_ref, bf16[4,128,256]{2,1,0:T(8,128)(2,1)S(1)} %get-tuple-element.25.refs_0_, bf16[4,128,256]{2,1,0:T(8,128)(2,1)S(1)} %collective-permute-done.2.refs_1_, bf16[4,128,256]{2,1,0:T(8,128)(2,1)S(1)} %collective-permute-done.3.refs_2_, ...), custom_call_target="tpu_custom_call" | custom-call | flops 805306368 | bytes 1048576 | tf_op jit(solution)/shard_map/gram/pallas_call | solution.py:514
  40.3 23.8 %all_to_all.5.partial_ref = f32[32,8,128]{2,1,0:T(8,128)S(1)} all-to-all(f32[32,8,128]{2,1,0:T(8,128)S(1)} %broadcast_in_dim.2), channel_id=1, replica_groups=mesh['mem'=4,'tok'=8] {'mem','tok'}, dimensions={0} | all-to-all | bytes 262144 | tf_op jit(solution)/shard_map/all_to_all | solution.py:714
  64.2 3.7 %combine.1 = (bf16[4,128,256]{2,1,0:T(8,128)(2,1)S(1)}, bf16[4,128,256]{2,1,0:T(8,128)(2,1)S(1)}, bf16[4,128,256]{2,1,0:T(8,128)(2,1)S(1)}, bf16[4,128,256]{2,1,0:T(8,128)(2,1)S(1)}) custom-call(s32[1]{0:T(128)} %bitcast.mem_ref.index_ref, f32[32,8,128]{2,1,0:T(8,128)S(1)} %all_to_all.5.partial_ref, bf16[4,128,256]{2,1,0:T(8,128)(2,1)S(1)} %get-tuple-element.25.refs_0_, ...), custom_call_target="tpu_custom_call" | custom-call | flops 536870912 | bytes 2097152 | tf_op jit(solution)/shard_map/combine/pallas_call | solution.py:617
  67.9 0.9 %collective-permute-start.5 = (bf16[4,128,256]{2,1,0:T(8,128)(2,1)S(1)}, bf16[4,128,256]{2,1,0:T(8,128)(2,1)S(1)}, u32[]{:S(2)}, u32[]{:S(2)}) collective-permute-start(bf16[4,128,256]{2,1,0:T(8,128)(2,1)S(1)} %get-tuple-element.30), channel_id=1, source_target_pairs={{0,8},{8,0},{16,24},{24,16},{1,9},{9,1},{17,25},{25,17},{2,10},{10... | collective-permute-start | bytes 786440 | tf_op jit(solution)/shard_map/ppermute | solution.py:658
  68.8 0.7 collective-permute-start.6
  69.5 2.0 %collective-permute-start.7 = (bf16[4,128,256]{2,1,0:T(8,128)(2,1)S(1)}, bf16[4,128,256]{2,1,0:T(8,128)(2,1)S(1)}, u32[]{:S(2)}, u32[]{:S(2)}) collective-permute-start(bf16[4,128,256]{2,1,0:T(8,128)(2,1)S(1)} %get-tuple-element.32), channel_id=1, source_target_pairs={{0,24},{8,16},{16,8},{24,0},{1,25},{9,17},{17,9},{25,1},{2,26},{10... | collective-permute-start | bytes 786440 | tf_op jit(solution)/shard_map/ppermute | solution.py:658
  71.5 5.6 %collective-permute-done.5.refs_1_ = bf16[4,128,256]{2,1,0:T(8,128)(2,1)S(1)} collective-permute-done((bf16[4,128,256]{2,1,0:T(8,128)(2,1)S(1)}, bf16[4,128,256]{2,1,0:T(8,128)(2,1)S(1)}, u32[]{:S(2)}, u32[]{:S(2)}) %collective-permute-start.5) | collective-permute-done | bytes 262176 | tf_op jit(solution)/shard_map/ppermute | solution.py:658
  77.1 5.1 %collective-permute-done.6.refs_2_ = bf16[4,128,256]{2,1,0:T(8,128)(2,1)S(1)} collective-permute-done((bf16[4,128,256]{2,1,0:T(8,128)(2,1)S(1)}, bf16[4,128,256]{2,1,0:T(8,128)(2,1)S(1)}, u32[]{:S(2)}, u32[]{:S(2)}) %collective-permute-start.6) | collective-permute-done | bytes 262176 | tf_op jit(solution)/shard_map/ppermute | solution.py:658
  82.2 1.0 %assemble.1 = bf16[4,512,256]{2,1,0:T(8,128)(2,1)} custom-call(s32[1]{0:T(128)} %bitcast.mem_ref.index_ref, bf16[4,128,256]{2,1,0:T(8,128)(2,1)S(1)} %get-tuple-element.29.refs_0_, bf16[4,128,256]{2,1,0:T(8,128)(2,1)S(1)} %collective-permute-done.5.refs_1_, bf16[4,128,256]{2,1,0:T(8,128)(2,1)S(1)} %collective-permute-done.6.refs_2_, ...), custom_call_target="tpu_custom_call" | custom-call | bytes 2097152 | tf_op jit(solution)/shard_map/assemble/pallas_call | solution.py:643
  (24 shorter events, 0.1 us)
Async XLA Ops:
  0.0 4.3 %copy-start = (bf16[4,512,256]{2,1,0:T(8,128)(2,1)S(1)}, bf16[4,512,256]{2,1,0:T(8,128)(2,1)}, u32[]{:S(2)}) copy-start(bf16[4,512,256]{2,1,0:T(8,128)(2,1)} %state_ref.1) | copy-start | bytes 3145732
  0.0 4.3 %copy-start.12 = (f32[256]{0:T(256)S(1)}, f32[256]{0:T(256)}, u32[]{:S(2)}) copy-start(f32[256]{0:T(256)} %param.16) | copy-start | bytes 3076
  0.0 4.3 %copy-start.4 = (bf16[256,256]{1,0:T(8,128)(2,1)S(1)}, bf16[256,256]{1,0:T(8,128)(2,1)}, u32[]{:S(2)}) copy-start(bf16[256,256]{1,0:T(8,128)(2,1)} %w_query_ref.1) | copy-start | bytes 393220
  0.0 4.3 %copy-start.5 = (bf16[256,256]{1,0:T(8,128)(2,1)S(1)}, bf16[256,256]{1,0:T(8,128)(2,1)}, u32[]{:S(2)}) copy-start(bf16[256,256]{1,0:T(8,128)(2,1)} %w_key_ref.3) | copy-start | bytes 393220
  0.0 4.3 %copy-start.6 = (bf16[256,256]{1,0:T(8,128)(2,1)S(1)}, bf16[256,256]{1,0:T(8,128)(2,1)}, u32[]{:S(2)}) copy-start(bf16[256,256]{1,0:T(8,128)(2,1)} %w_value_ref.3) | copy-start | bytes 393220
  0.0 4.3 %copy-start.14 = (s32[4]{0:T(128)S(1)}, s32[4]{0:T(128)}, u32[]{:S(2)}) copy-start(s32[4]{0:T(128)} %window_ref.3) | copy-start | bytes 52
  3.1 3.8 %collective-permute-start = (bf16[4,256,256]{2,1,0:T(8,128)(2,1)}, bf16[4,256,256]{2,1,0:T(8,128)(2,1)S(1)}, u32[]{:S(2)}, u32[]{:S(2)}) collective-permute-start(bf16[4,256,256]{2,1,0:T(8,128)(2,1)} %constant_dynamic-slice_fusion), channel_id=1, source_target_pairs={{0,1},{1,0},{2,3},{3,2},{4,5},{5,4},{6,7},{7,6},{8,9},{9,8},{10,11... | collective-permute-start | bytes 1572872 | tf_op jit(solution)/shard_map/ppermute | solution.py:672
  3.6 3.4 %collective-permute-start.1 = (bf16[4,256,256]{2,1,0:T(8,128)(2,1)S(1)}, bf16[4,256,256]{2,1,0:T(8,128)(2,1)S(1)}, u32[]{:S(2)}, u32[]{:S(2)}) collective-permute-start(bf16[4,256,256]{2,1,0:T(8,128)(2,1)S(1)} %constant_dynamic-slice_fusion.1), channel_id=1, source_target_pairs={{1,2},{2,1},{3,4},{4,3},{5,6},{6,5},{9,10},{10,9},{11,12},{12,11},... | collective-permute-start | bytes 1572872 | tf_op jit(solution)/shard_map/ppermute | solution.py:670
  4.3 2.6 %copy-start.1 = (bf16[256,1024]{1,0:T(8,128)(2,1)S(1)}, bf16[256,1024]{1,0:T(8,128)(2,1)}, u32[]{:S(2)}) copy-start(bf16[256,1024]{1,0:T(8,128)(2,1)} %w_gate_ref.1) | copy-start | bytes 1572868
  4.4 2.6 %copy-start.2 = (bf16[256,1024]{1,0:T(8,128)(2,1)S(1)}, bf16[256,1024]{1,0:T(8,128)(2,1)}, u32[]{:S(2)}) copy-start(bf16[256,1024]{1,0:T(8,128)(2,1)} %w_up_ref.1) | copy-start | bytes 1572868
  4.4 2.6 %copy-start.3 = (bf16[1024,256]{1,0:T(8,128)(2,1)S(1)}, bf16[1024,256]{1,0:T(8,128)(2,1)}, u32[]{:S(2)}) copy-start(bf16[1024,256]{1,0:T(8,128)(2,1)} %down_weight_ref.1) | copy-start | bytes 1572868
  4.4 2.6 %copy-start.7 = (bf16[256,256]{1,0:T(8,128)(2,1)S(1)}, bf16[256,256]{1,0:T(8,128)(2,1)}, u32[]{:S(2)}) copy-start(bf16[256,256]{1,0:T(8,128)(2,1)} %w_out_ref.1) | copy-start | bytes 393220
  4.4 2.6 %copy-start.13 = (f32[256]{0:T(256)S(1)}, f32[256]{0:T(256)}, u32[]{:S(2)}) copy-start(f32[256]{0:T(256)} %param.17) | copy-start | bytes 3076
  7.0 24.1 %copy-start.8 = (s32[4096]{0:T(1024)S(1)}, s32[4096]{0:T(1024)}, u32[]{:S(2)}) copy-start(s32[4096]{0:T(1024)} %param.26) | copy-start | bytes 49156
  7.0 24.1 %copy-start.9 = (s32[4096]{0:T(1024)S(1)}, s32[4096]{0:T(1024)}, u32[]{:S(2)}) copy-start(s32[4096]{0:T(1024)} %param.27) | copy-start | bytes 49156
  7.1 24.1 %copy-start.10 = (f32[4096]{0:T(1024)S(1)}, f32[4096]{0:T(1024)}, u32[]{:S(2)}) copy-start(f32[4096]{0:T(1024)} %param.28) | copy-start | bytes 49156
  7.1 24.1 %copy-start.11 = (f32[4096]{0:T(1024)S(1)}, f32[4096]{0:T(1024)}, u32[]{:S(2)}) copy-start(f32[4096]{0:T(1024)} %param.29) | copy-start | bytes 49156
  27.1 6.9 %collective-permute-start.2 = (bf16[4,128,256]{2,1,0:T(8,128)(2,1)S(1)}, bf16[4,128,256]{2,1,0:T(8,128)(2,1)S(1)}, u32[]{:S(2)}, u32[]{:S(2)}) collective-permute-start(bf16[4,128,256]{2,1,0:T(8,128)(2,1)S(1)} %get-tuple-element.26), channel_id=1, source_target_pairs={{0,8},{8,0},{16,24},{24,16},{1,9},{9,1},{17,25},{25,17},{2,10},{10... | collective-permute-start | bytes 786440 | tf_op jit(solution)/shard_map/ppermute | solution.py:658
  29.6 9.2 %collective-permute-start.3 = (bf16[4,128,256]{2,1,0:T(8,128)(2,1)S(1)}, bf16[4,128,256]{2,1,0:T(8,128)(2,1)S(1)}, u32[]{:S(2)}, u32[]{:S(2)}) collective-permute-start(bf16[4,128,256]{2,1,0:T(8,128)(2,1)S(1)} %get-tuple-element.27), channel_id=1, source_target_pairs={{0,16},{8,24},{16,0},{24,8},{1,17},{9,25},{17,1},{25,9},{2,18},{10... | collective-permute-start | bytes 786440 | tf_op jit(solution)/shard_map/ppermute | solution.py:658
  31.2 7.7 %collective-permute-start.4 = (bf16[4,128,256]{2,1,0:T(8,128)(2,1)S(1)}, bf16[4,128,256]{2,1,0:T(8,128)(2,1)S(1)}, u32[]{:S(2)}, u32[]{:S(2)}) collective-permute-start(bf16[4,128,256]{2,1,0:T(8,128)(2,1)S(1)} %get-tuple-element.28), channel_id=1, source_target_pairs={{0,24},{8,16},{16,8},{24,0},{1,25},{9,17},{17,9},{25,1},{2,26},{10... | collective-permute-start | bytes 786440 | tf_op jit(solution)/shard_map/ppermute | solution.py:658
  67.9 9.2 %collective-permute-start.5 = (bf16[4,128,256]{2,1,0:T(8,128)(2,1)S(1)}, bf16[4,128,256]{2,1,0:T(8,128)(2,1)S(1)}, u32[]{:S(2)}, u32[]{:S(2)}) collective-permute-start(bf16[4,128,256]{2,1,0:T(8,128)(2,1)S(1)} %get-tuple-element.30), channel_id=1, source_target_pairs={{0,8},{8,0},{16,24},{24,16},{1,9},{9,1},{17,25},{25,17},{2,10},{10... | collective-permute-start | bytes 786440 | tf_op jit(solution)/shard_map/ppermute | solution.py:658
  68.8 13.4 %collective-permute-start.6 = (bf16[4,128,256]{2,1,0:T(8,128)(2,1)S(1)}, bf16[4,128,256]{2,1,0:T(8,128)(2,1)S(1)}, u32[]{:S(2)}, u32[]{:S(2)}) collective-permute-start(bf16[4,128,256]{2,1,0:T(8,128)(2,1)S(1)} %get-tuple-element.31), channel_id=1, source_target_pairs={{0,16},{8,24},{16,0},{24,8},{1,17},{9,25},{17,1},{25,9},{2,18},{10... | collective-permute-start | bytes 786440 | tf_op jit(solution)/shard_map/ppermute | solution.py:658
  69.5 12.7 %collective-permute-start.7 = (bf16[4,128,256]{2,1,0:T(8,128)(2,1)S(1)}, bf16[4,128,256]{2,1,0:T(8,128)(2,1)S(1)}, u32[]{:S(2)}, u32[]{:S(2)}) collective-permute-start(bf16[4,128,256]{2,1,0:T(8,128)(2,1)S(1)} %get-tuple-element.32), channel_id=1, source_target_pairs={{0,24},{8,16},{16,8},{24,0},{1,25},{9,17},{17,9},{25,1},{2,26},{10... | collective-permute-start | bytes 786440 | tf_op jit(solution)/shard_map/ppermute | solution.py:658

commit v22 on v21

--- a/solution.py
+++ b/solution.py
@@ -625,31 +625,38 @@
     )(index, partials, *shares)
 
 
-def assemble_kernel(index_ref, *refs):
-    part_refs, out_ref, sems = refs[:-2], refs[-2], refs[-1]
+def place_kernel(first, count, index_ref, *refs):
+    part_refs, out_ref, sems = refs[:count], refs[-2], refs[-1]
     rows = part_refs[0].shape[1]
     copies = []
-    for part, ref in enumerate(part_refs):
-        lower = pl.multiple_of((index_ref[0] ^ part) * rows, rows)
-        copies.append(pltpu.make_async_copy(ref, out_ref.at[:, pl.ds(lower, rows), :], sems.at[part]))
+    for at, ref in enumerate(part_refs):
+        lower = pl.multiple_of((index_ref[0] ^ (first + at)) * rows, rows)
+        copies.append(pltpu.make_async_copy(ref, out_ref.at[:, pl.ds(lower, rows), :], sems.at[at]))
     for copy in copies:
         copy.start()
     for copy in copies:
         copy.wait()
 
 
-def assemble(index, parts):
+def place(index, parts, first, shares, result=()):
     members, rows, feat_width = parts[0].shape
+    anywhere = pl.BlockSpec(memory_space=pl.ANY)
     return pl.pallas_call(
-        assemble_kernel,
-        out_shape=jax.ShapeDtypeStruct((members, len(parts) * rows, feat_width), BF16),
-        in_specs=[smem_spec()] + [vmem_spec()] * len(parts),
-        out_specs=pl.BlockSpec(memory_space=pl.ANY),
+        functools.partial(place_kernel, first, len(parts)),
+        out_shape=jax.ShapeDtypeStruct((members, shares * rows, feat_width), BF16),
+        in_specs=[smem_spec()] + [vmem_spec()] * len(parts) + [anywhere] * len(result),
+        out_specs=anywhere,
+        input_output_aliases={1 + len(parts): 0} if result else {},
         scratch_shapes=[pltpu.SemaphoreType.DMA((len(parts),))],
         compiler_params=pltpu.CompilerParams(vmem_limit_bytes=VMEM_LIMIT),
         cost_estimate=pl.CostEstimate(flops=0, bytes_accessed=4 * len(parts) * parts[0].size, transcendentals=0),
-        name="assemble",
-    )(index, *parts)
+        name="place",
+    )(index, *parts, *result)
+
+
+def assemble(index, parts):
+    result = place(index, parts[:-1], 0, len(parts))
+    return place(index, parts[-1:], len(parts) - 1, len(parts), (result,))
 
 
 def exchanged(parts):
@@ -663,12 +670,11 @@
     count = lax.axis_size("tok")
     odd = lax.axis_index("tok") % 2
     last = own.shape[1] - reach
+    near = lax.dynamic_slice_in_dim(own, (1 - odd) * last, reach, axis=1)
+    far = lax.dynamic_slice_in_dim(own, odd * last, reach, axis=1)
     near_pairs = [(i, i ^ 1) for i in range(count)]
     far_pairs = [pair for i in range(1, count - 1, 2) for pair in ((i, i + 1), (i + 1, i))]
-    far = lax.dynamic_slice_in_dim(own, odd * last, reach, axis=1)
-    far, own = lax.optimization_barrier((far, own))
     far_halo = lax.ppermute(far, "tok", far_pairs)
-    near = lax.dynamic_slice_in_dim(own, (1 - odd) * last, reach, axis=1)
     return lax.ppermute(near, "tok", near_pairs), far_halo
 
 

time: 83.6 us -> 83.3 us (level)
  local copies, waits for them, and re-layouts: 3.15 us -> 2.26 us
    dynamic_slice x1 -> x0, local copies, waits for them, and re-layouts: 1.88 us -> none  [halos(): near = lax.dynamic_slice_in_dim(own, (1 - odd) * last, reach, axis=1)]
    dynamic_slice x1, local copies, waits for them, and re-layouts: 1.19 us -> 2.17 us  [halos(): far = lax.dynamic_slice_in_dim(own, odd * last, reach, axis=1)]
  transfers between devices with their start and end apart: 8 -> 8, of which waited for: 4 -> 4; matrix products, arithmetic and copies ran while one was open for 0% -> 0% of each run, Pallas kernels for 5% -> 6%
where the time goes in v22:
time: 83.3 us; the launch traced here: 83.1 us
  Pallas kernels  30.7 us (37%)
  blocking collectives  23.8 us (29%)
  waiting for transfers between devices  17 us (20%)
  starting transfers between devices  8.79 us (11%)
  local copies, waits for them, and re-layouts  2.26 us (3%)
    all_to_all x1, blocking collectives, local(): lax.all_to_all(jnp.broadcast_to(partial[None], (device_count, *partial.sh...  23.8 us
    pallas_call x1, Pallas kernels, forward(): pl.pallas_call(functools.partial(forward_kernel, total_len), grid=(member...  20 us
    ppermute x6, waiting for transfers between devices, exchanged(): lax.ppermute(v, 'mem', [(i, i ^ part) for i in range(count)])  17 us
    ppermute x6, starting transfers between devices, exchanged(): lax.ppermute(v, 'mem', [(i, i ^ part) for i in range(count)])  7.64 us
    pallas_call x1, Pallas kernels, combine(): pl.pallas_call(combine_kernel, out_shape=[jax.ShapeDtypeStruct(v.shape, B...  3.74 us
    pallas_call x1, Pallas kernels, inner(): pl.pallas_call(inner_kernel, grid=(members // batch,), out_shape=[jax.Sha...  2.55 us
    dynamic_slice x1, local copies, waits for them, and re-layouts, halos(): far = lax.dynamic_slice_in_dim(own, odd * last, reach, axis=1)  2.17 us
  transfers between devices with their start and end apart: 8, of which 4 were waited for; matrix products, arithmetic and copies ran while one was open for 0% of the time, Pallas kernels for 6%

profile of v22, /device:TPU:0, one launch (start us, length us, event | category | flops | bytes accessed | tf_op | source)
XLA Modules:
  0.0 83.1 jit_solution(3218367865950451632)
XLA Ops:
  0.0 2.2 %constant_dynamic-slice_fusion = (bf16[4,256,256]{2,1,0:T(8,128)(2,1)S(1)}, bf16[4,256,256]{2,1,0:T(8,128)(2,1)}) fusion(bf16[4,512,256]{2,1,0:T(8,128)(2,1)} %state_ref.1, s32[]{:T(128)S(6)} %select_n.15, s32[]{:T(128)S(6)} %select_n.14), kind=kLoop, calls=%fused_computation | loop fusion | bytes 2097160 | tf_op jit(solution)/shard_map/dynamic_slice | solution.py:674
  2.2 0.5 collective-permute-start
  2.7 0.7 collective-permute-start.1
  3.4 0.0 copy-start.1
  3.5 0.0 copy-start.2
  3.5 0.0 copy-start.3
  3.5 0.0 copy-start.7
  3.5 0.0 copy-start.13
  3.5 2.6 %inner.1 = (bf16[4,512,256]{2,1,0:T(8,128)(2,1)S(1)}, f32[4,8,128]{2,1,0:T(8,128)S(1)}, f32[4,512,256]{2,1,0:T(8,128)S(1)}, f32[4,512,256]{2,1,0:T(8,128)S(1)}) custom-call(s32[4]{0:T(128)S(1)} %copy-done.14, bf16[4,512,256]{2,1,0:T(8,128)(2,1)S(1)} %copy-done, f32[1,256]{1,0:T(1,128)S(1)} %bitcast.13, bf16[256,256]{1,0:T(8,128)(2,1)S(1)} %copy-done.4, ...), custom_call_target="tpu_custom_call" | custom-call | flops 5100273664 | bytes 7340032 | tf_op jit(solution)/shard_map/inner/pallas_call | solution.py:260
  6.1 0.0 copy-start.8
  6.1 0.0 copy-start.9
  6.2 0.0 copy-start.10
  6.2 0.0 copy-start.11
  6.2 20.0 %forward.1 = (bf16[4,128,256]{2,1,0:T(8,128)(2,1)S(1)}, bf16[4,128,256]{2,1,0:T(8,128)(2,1)S(1)}, bf16[4,128,256]{2,1,0:T(8,128)(2,1)S(1)}, bf16[4,128,256]{2,1,0:T(8,128)(2,1)S(1)}) custom-call(s32[1]{0:T(128)} %bitcast.1.tok_ref, s32[1]{0:T(128)} %bitcast.mem_ref.index_ref, s32[4]{0:T(128)S(1)} %copy-done.14, bf16[4,512,256]{2,1,0:T(8,128)(2,1)S(1)} %copy-done, ...), custom_call_target="tpu_custom_call" | custom-call | flops 5100273664 | bytes 5242880 | tf_op jit(solution)/shard_map/forward/pallas_call | solution.py:445
  26.2 2.5 %collective-permute-start.2 = (bf16[4,128,256]{2,1,0:T(8,128)(2,1)S(1)}, bf16[4,128,256]{2,1,0:T(8,128)(2,1)S(1)}, u32[]{:S(2)}, u32[]{:S(2)}) collective-permute-start(bf16[4,128,256]{2,1,0:T(8,128)(2,1)S(1)} %get-tuple-element.22), channel_id=1, source_target_pairs={{0,8},{8,0},{16,24},{24,16},{1,9},{9,1},{17,25},{25,17},{2,10},{10... | collective-permute-start | bytes 786440 | tf_op jit(solution)/shard_map/ppermute | solution.py:665
  28.7 1.5 %collective-permute-start.3 = (bf16[4,128,256]{2,1,0:T(8,128)(2,1)S(1)}, bf16[4,128,256]{2,1,0:T(8,128)(2,1)S(1)}, u32[]{:S(2)}, u32[]{:S(2)}) collective-permute-start(bf16[4,128,256]{2,1,0:T(8,128)(2,1)S(1)} %get-tuple-element.23), channel_id=1, source_target_pairs={{0,16},{8,24},{16,0},{24,8},{1,17},{9,25},{17,1},{25,9},{2,18},{10... | collective-permute-start | bytes 786440 | tf_op jit(solution)/shard_map/ppermute | solution.py:665
  30.3 0.0 collective-permute-start.4
  30.3 1.3 %sample_grid.1.refs_4_ = f32[2,128,256]{2,1,0:T(8,128)S(1)} custom-call(s32[1]{0:T(128)} %bitcast.4.start_ref, s32[1,4096]{1,0:T(1,128)S(1)} %bitcast.9, s32[1,4096]{1,0:T(1,128)S(1)} %bitcast.10, f32[1,4096]{1,0:T(1,128)S(1)} %bitcast.11, f32[1,4096]{1,0:T(1,128)S(1)} %bitcast.12), custom_call_target="tpu_custom_call" | custom-call | flops 1073741824 | bytes 65536 | tf_op jit(solution)/shard_map/sample_grid/pallas_call | solution.py:80
  31.6 1.5 %collective-permute-done.2.refs_1_ = bf16[4,128,256]{2,1,0:T(8,128)(2,1)S(1)} collective-permute-done((bf16[4,128,256]{2,1,0:T(8,128)(2,1)S(1)}, bf16[4,128,256]{2,1,0:T(8,128)(2,1)S(1)}, u32[]{:S(2)}, u32[]{:S(2)}) %collective-permute-start.2) | collective-permute-done | bytes 262176 | tf_op jit(solution)/shard_map/ppermute | solution.py:665
  33.1 4.8 %collective-permute-done.3.refs_2_ = bf16[4,128,256]{2,1,0:T(8,128)(2,1)S(1)} collective-permute-done((bf16[4,128,256]{2,1,0:T(8,128)(2,1)S(1)}, bf16[4,128,256]{2,1,0:T(8,128)(2,1)S(1)}, u32[]{:S(2)}, u32[]{:S(2)}) %collective-permute-start.3) | collective-permute-done | bytes 262176 | tf_op jit(solution)/shard_map/ppermute | solution.py:665
  37.9 0.0 collective-permute-done.4.refs_3_
  37.9 1.5 %gram.1 = f32[8,128]{1,0:T(8,128)S(1)} custom-call(s32[1]{0:T(128)} %bitcast.mem_ref.index_ref, bf16[4,128,256]{2,1,0:T(8,128)(2,1)S(1)} %get-tuple-element.21.refs_0_, bf16[4,128,256]{2,1,0:T(8,128)(2,1)S(1)} %collective-permute-done.2.refs_1_, bf16[4,128,256]{2,1,0:T(8,128)(2,1)S(1)} %collective-permute-done.3.refs_2_, ...), custom_call_target="tpu_custom_call" | custom-call | flops 805306368 | bytes 1048576 | tf_op jit(solution)/shard_map/gram/pallas_call | solution.py:514
  39.4 23.8 %all_to_all.5.partial_ref = f32[32,8,128]{2,1,0:T(8,128)S(1)} all-to-all(f32[32,8,128]{2,1,0:T(8,128)S(1)} %broadcast_in_dim.2), channel_id=1, replica_groups=mesh['mem'=4,'tok'=8] {'mem','tok'}, dimensions={0} | all-to-all | bytes 262144 | tf_op jit(solution)/shard_map/all_to_all | solution.py:720
  63.3 3.7 %combine.1 = (bf16[4,128,256]{2,1,0:T(8,128)(2,1)S(1)}, bf16[4,128,256]{2,1,0:T(8,128)(2,1)S(1)}, bf16[4,128,256]{2,1,0:T(8,128)(2,1)S(1)}, bf16[4,128,256]{2,1,0:T(8,128)(2,1)S(1)}) custom-call(s32[1]{0:T(128)} %bitcast.mem_ref.index_ref, f32[32,8,128]{2,1,0:T(8,128)S(1)} %all_to_all.5.partial_ref, bf16[4,128,256]{2,1,0:T(8,128)(2,1)S(1)} %get-tuple-element.21.refs_0_, ...), custom_call_target="tpu_custom_call" | custom-call | flops 536870912 | bytes 2097152 | tf_op jit(solution)/shard_map/combine/pallas_call | solution.py:617
  67.0 0.9 %collective-permute-start.6 = (bf16[4,128,256]{2,1,0:T(8,128)(2,1)S(1)}, bf16[4,128,256]{2,1,0:T(8,128)(2,1)S(1)}, u32[]{:S(2)}, u32[]{:S(2)}) collective-permute-start(bf16[4,128,256]{2,1,0:T(8,128)(2,1)S(1)} %get-tuple-element.27), channel_id=1, source_target_pairs={{0,8},{8,0},{16,24},{24,16},{1,9},{9,1},{17,25},{25,17},{2,10},{10... | collective-permute-start | bytes 786440 | tf_op jit(solution)/shard_map/ppermute | solution.py:665
  67.9 0.7 collective-permute-start.7
  68.6 2.0 %collective-permute-start.5 = (bf16[4,128,256]{2,1,0:T(8,128)(2,1)S(1)}, bf16[4,128,256]{2,1,0:T(8,128)(2,1)S(1)}, u32[]{:S(2)}, u32[]{:S(2)}) collective-permute-start(bf16[4,128,256]{2,1,0:T(8,128)(2,1)S(1)} %get-tuple-element.25), channel_id=1, source_target_pairs={{0,24},{8,16},{16,8},{24,0},{1,25},{9,17},{17,9},{25,1},{2,26},{10... | collective-permute-start | bytes 786440 | tf_op jit(solution)/shard_map/ppermute | solution.py:665
  70.6 5.6 %collective-permute-done.6.refs_1_ = bf16[4,128,256]{2,1,0:T(8,128)(2,1)S(1)} collective-permute-done((bf16[4,128,256]{2,1,0:T(8,128)(2,1)S(1)}, bf16[4,128,256]{2,1,0:T(8,128)(2,1)S(1)}, u32[]{:S(2)}, u32[]{:S(2)}) %collective-permute-start.6) | collective-permute-done | bytes 262176 | tf_op jit(solution)/shard_map/ppermute | solution.py:665
  76.2 5.1 %collective-permute-done.7.refs_2_ = bf16[4,128,256]{2,1,0:T(8,128)(2,1)S(1)} collective-permute-done((bf16[4,128,256]{2,1,0:T(8,128)(2,1)S(1)}, bf16[4,128,256]{2,1,0:T(8,128)(2,1)S(1)}, u32[]{:S(2)}, u32[]{:S(2)}) %collective-permute-start.7) | collective-permute-done | bytes 262176 | tf_op jit(solution)/shard_map/ppermute | solution.py:665
  81.3 0.9 %place.2.refs_1_ = bf16[4,512,256]{2,1,0:T(8,128)(2,1)} custom-call(s32[1]{0:T(128)} %bitcast.mem_ref.index_ref, bf16[4,128,256]{2,1,0:T(8,128)(2,1)S(1)} %get-tuple-element.26.refs_0_, bf16[4,128,256]{2,1,0:T(8,128)(2,1)S(1)} %collective-permute-done.6.refs_1_, bf16[4,128,256]{2,1,0:T(8,128)(2,1)S(1)} %collective-permute-done.7.refs_2_), custom_call_target="tpu_custom_call" | custom-call | bytes 1572864 | tf_op jit(solution)/shard_map/place/pallas_call | solution.py:644
  82.2 0.0 collective-permute-done.5.refs_0_
  82.2 0.7 place.3
  (24 shorter events, 0.1 us)
Async XLA Ops:
  0.0 3.4 %copy-start = (bf16[4,512,256]{2,1,0:T(8,128)(2,1)S(1)}, bf16[4,512,256]{2,1,0:T(8,128)(2,1)}, u32[]{:S(2)}) copy-start(bf16[4,512,256]{2,1,0:T(8,128)(2,1)} %state_ref.1) | copy-start | bytes 3145732
  0.0 3.4 %copy-start.12 = (f32[256]{0:T(256)S(1)}, f32[256]{0:T(256)}, u32[]{:S(2)}) copy-start(f32[256]{0:T(256)} %param.16) | copy-start | bytes 3076
  0.0 3.4 %copy-start.4 = (bf16[256,256]{1,0:T(8,128)(2,1)S(1)}, bf16[256,256]{1,0:T(8,128)(2,1)}, u32[]{:S(2)}) copy-start(bf16[256,256]{1,0:T(8,128)(2,1)} %w_query_ref.1) | copy-start | bytes 393220
  0.0 3.4 %copy-start.5 = (bf16[256,256]{1,0:T(8,128)(2,1)S(1)}, bf16[256,256]{1,0:T(8,128)(2,1)}, u32[]{:S(2)}) copy-start(bf16[256,256]{1,0:T(8,128)(2,1)} %w_key_ref.3) | copy-start | bytes 393220
  0.0 3.4 %copy-start.6 = (bf16[256,256]{1,0:T(8,128)(2,1)S(1)}, bf16[256,256]{1,0:T(8,128)(2,1)}, u32[]{:S(2)}) copy-start(bf16[256,256]{1,0:T(8,128)(2,1)} %w_value_ref.3) | copy-start | bytes 393220
  0.0 3.4 %copy-start.14 = (s32[4]{0:T(128)S(1)}, s32[4]{0:T(128)}, u32[]{:S(2)}) copy-start(s32[4]{0:T(128)} %window_ref.3) | copy-start | bytes 52
  2.2 3.8 %collective-permute-start = (bf16[4,256,256]{2,1,0:T(8,128)(2,1)}, bf16[4,256,256]{2,1,0:T(8,128)(2,1)S(1)}, u32[]{:S(2)}, u32[]{:S(2)}) collective-permute-start(bf16[4,256,256]{2,1,0:T(8,128)(2,1)} %get-tuple-element.30), channel_id=1, source_target_pairs={{0,1},{1,0},{2,3},{3,2},{4,5},{5,4},{6,7},{7,6},{8,9},{9,8},{10,11... | collective-permute-start | bytes 1572872 | tf_op jit(solution)/shard_map/ppermute | solution.py:678
  2.7 3.4 %collective-permute-start.1 = (bf16[4,256,256]{2,1,0:T(8,128)(2,1)S(1)}, bf16[4,256,256]{2,1,0:T(8,128)(2,1)S(1)}, u32[]{:S(2)}, u32[]{:S(2)}) collective-permute-start(bf16[4,256,256]{2,1,0:T(8,128)(2,1)S(1)} %get-tuple-element.29), channel_id=1, source_target_pairs={{1,2},{2,1},{3,4},{4,3},{5,6},{6,5},{9,10},{10,9},{11,12},{12,11},... | collective-permute-start | bytes 1572872 | tf_op jit(solution)/shard_map/ppermute | solution.py:677
  3.4 2.6 %copy-start.1 = (bf16[256,1024]{1,0:T(8,128)(2,1)S(1)}, bf16[256,1024]{1,0:T(8,128)(2,1)}, u32[]{:S(2)}) copy-start(bf16[256,1024]{1,0:T(8,128)(2,1)} %w_gate_ref.1) | copy-start | bytes 1572868
  3.5 2.6 %copy-start.2 = (bf16[256,1024]{1,0:T(8,128)(2,1)S(1)}, bf16[256,1024]{1,0:T(8,128)(2,1)}, u32[]{:S(2)}) copy-start(bf16[256,1024]{1,0:T(8,128)(2,1)} %w_up_ref.1) | copy-start | bytes 1572868
  3.5 2.6 %copy-start.3 = (bf16[1024,256]{1,0:T(8,128)(2,1)S(1)}, bf16[1024,256]{1,0:T(8,128)(2,1)}, u32[]{:S(2)}) copy-start(bf16[1024,256]{1,0:T(8,128)(2,1)} %down_weight_ref.1) | copy-start | bytes 1572868
  3.5 2.6 %copy-start.7 = (bf16[256,256]{1,0:T(8,128)(2,1)S(1)}, bf16[256,256]{1,0:T(8,128)(2,1)}, u32[]{:S(2)}) copy-start(bf16[256,256]{1,0:T(8,128)(2,1)} %w_out_ref.1) | copy-start | bytes 393220
  3.5 2.6 %copy-start.13 = (f32[256]{0:T(256)S(1)}, f32[256]{0:T(256)}, u32[]{:S(2)}) copy-start(f32[256]{0:T(256)} %param.17) | copy-start | bytes 3076
  6.1 24.1 %copy-start.8 = (s32[4096]{0:T(1024)S(1)}, s32[4096]{0:T(1024)}, u32[]{:S(2)}) copy-start(s32[4096]{0:T(1024)} %param.26) | copy-start | bytes 49156
  6.1 24.1 %copy-start.9 = (s32[4096]{0:T(1024)S(1)}, s32[4096]{0:T(1024)}, u32[]{:S(2)}) copy-start(s32[4096]{0:T(1024)} %param.27) | copy-start | bytes 49156
  6.2 24.1 %copy-start.10 = (f32[4096]{0:T(1024)S(1)}, f32[4096]{0:T(1024)}, u32[]{:S(2)}) copy-start(f32[4096]{0:T(1024)} %param.28) | copy-start | bytes 49156
  6.2 24.1 %copy-start.11 = (f32[4096]{0:T(1024)S(1)}, f32[4096]{0:T(1024)}, u32[]{:S(2)}) copy-start(f32[4096]{0:T(1024)} %param.29) | copy-start | bytes 49156
  26.2 6.9 %collective-permute-start.2 = (bf16[4,128,256]{2,1,0:T(8,128)(2,1)S(1)}, bf16[4,128,256]{2,1,0:T(8,128)(2,1)S(1)}, u32[]{:S(2)}, u32[]{:S(2)}) collective-permute-start(bf16[4,128,256]{2,1,0:T(8,128)(2,1)S(1)} %get-tuple-element.22), channel_id=1, source_target_pairs={{0,8},{8,0},{16,24},{24,16},{1,9},{9,1},{17,25},{25,17},{2,10},{10... | collective-permute-start | bytes 786440 | tf_op jit(solution)/shard_map/ppermute | solution.py:665
  28.7 9.2 %collective-permute-start.3 = (bf16[4,128,256]{2,1,0:T(8,128)(2,1)S(1)}, bf16[4,128,256]{2,1,0:T(8,128)(2,1)S(1)}, u32[]{:S(2)}, u32[]{:S(2)}) collective-permute-start(bf16[4,128,256]{2,1,0:T(8,128)(2,1)S(1)} %get-tuple-element.23), channel_id=1, source_target_pairs={{0,16},{8,24},{16,0},{24,8},{1,17},{9,25},{17,1},{25,9},{2,18},{10... | collective-permute-start | bytes 786440 | tf_op jit(solution)/shard_map/ppermute | solution.py:665
  30.3 7.7 %collective-permute-start.4 = (bf16[4,128,256]{2,1,0:T(8,128)(2,1)S(1)}, bf16[4,128,256]{2,1,0:T(8,128)(2,1)S(1)}, u32[]{:S(2)}, u32[]{:S(2)}) collective-permute-start(bf16[4,128,256]{2,1,0:T(8,128)(2,1)S(1)} %get-tuple-element.24), channel_id=1, source_target_pairs={{0,24},{8,16},{16,8},{24,0},{1,25},{9,17},{17,9},{25,1},{2,26},{10... | collective-permute-start | bytes 786440 | tf_op jit(solution)/shard_map/ppermute | solution.py:665
  67.0 9.2 %collective-permute-start.6 = (bf16[4,128,256]{2,1,0:T(8,128)(2,1)S(1)}, bf16[4,128,256]{2,1,0:T(8,128)(2,1)S(1)}, u32[]{:S(2)}, u32[]{:S(2)}) collective-permute-start(bf16[4,128,256]{2,1,0:T(8,128)(2,1)S(1)} %get-tuple-element.27), channel_id=1, source_target_pairs={{0,8},{8,0},{16,24},{24,16},{1,9},{9,1},{17,25},{25,17},{2,10},{10... | collective-permute-start | bytes 786440 | tf_op jit(solution)/shard_map/ppermute | solution.py:665
  67.9 13.4 %collective-permute-start.7 = (bf16[4,128,256]{2,1,0:T(8,128)(2,1)S(1)}, bf16[4,128,256]{2,1,0:T(8,128)(2,1)S(1)}, u32[]{:S(2)}, u32[]{:S(2)}) collective-permute-start(bf16[4,128,256]{2,1,0:T(8,128)(2,1)S(1)} %get-tuple-element.28), channel_id=1, source_target_pairs={{0,16},{8,24},{16,0},{24,8},{1,17},{9,25},{17,1},{25,9},{2,18},{10... | collective-permute-start | bytes 786440 | tf_op jit(solution)/shard_map/ppermute | solution.py:665
  68.6 13.6 %collective-permute-start.5 = (bf16[4,128,256]{2,1,0:T(8,128)(2,1)S(1)}, bf16[4,128,256]{2,1,0:T(8,128)(2,1)S(1)}, u32[]{:S(2)}, u32[]{:S(2)}) collective-permute-start(bf16[4,128,256]{2,1,0:T(8,128)(2,1)S(1)} %get-tuple-element.25), channel_id=1, source_target_pairs={{0,24},{8,16},{16,8},{24,0},{1,25},{9,17},{17,9},{25,1},{2,26},{10... | collective-permute-start | bytes 786440 | tf_op jit(solution)/shard_map/ppermute | solution.py:665

commit v23 on v21

--- a/solution.py
+++ b/solution.py
@@ -663,12 +663,11 @@
     count = lax.axis_size("tok")
     odd = lax.axis_index("tok") % 2
     last = own.shape[1] - reach
+    near = lax.dynamic_slice_in_dim(own, (1 - odd) * last, reach, axis=1)
+    far = lax.dynamic_slice_in_dim(own, odd * last, reach, axis=1)
     near_pairs = [(i, i ^ 1) for i in range(count)]
     far_pairs = [pair for i in range(1, count - 1, 2) for pair in ((i, i + 1), (i + 1, i))]
-    far = lax.dynamic_slice_in_dim(own, odd * last, reach, axis=1)
-    far, own = lax.optimization_barrier((far, own))
     far_halo = lax.ppermute(far, "tok", far_pairs)
-    near = lax.dynamic_slice_in_dim(own, (1 - odd) * last, reach, axis=1)
     return lax.ppermute(near, "tok", near_pairs), far_halo
 
 

time: 83.6 us -> 82.6 us (0.988)
  local copies, waits for them, and re-layouts: 3.15 us -> 2.26 us
    dynamic_slice x1 -> x0, local copies, waits for them, and re-layouts: 1.88 us -> none  [halos(): near = lax.dynamic_slice_in_dim(own, (1 - odd) * last, reach, axis=1)]
    dynamic_slice x1, local copies, waits for them, and re-layouts: 1.19 us -> 2.17 us  [halos(): far = lax.dynamic_slice_in_dim(own, odd * last, reach, axis=1)]
where the time goes in v23:
time: 82.6 us; the launch traced here: 82.5 us
  Pallas kernels  30.1 us (36%)
  blocking collectives  23.8 us (29%)
  waiting for transfers between devices  17 us (21%)
  starting transfers between devices  8.79 us (11%)
  local copies, waits for them, and re-layouts  2.26 us (3%)
    all_to_all x1, blocking collectives, local(): lax.all_to_all(jnp.broadcast_to(partial[None], (device_count, *partial.sh...  23.8 us
    pallas_call x1, Pallas kernels, forward(): pl.pallas_call(functools.partial(forward_kernel, total_len), grid=(member...  20 us
    ppermute x6, waiting for transfers between devices, exchanged(): lax.ppermute(v, 'mem', [(i, i ^ part) for i in range(count)])  17 us
    ppermute x6, starting transfers between devices, exchanged(): lax.ppermute(v, 'mem', [(i, i ^ part) for i in range(count)])  7.64 us
    pallas_call x1, Pallas kernels, combine(): pl.pallas_call(combine_kernel, out_shape=[jax.ShapeDtypeStruct(v.shape, B...  3.74 us
    pallas_call x1, Pallas kernels, inner(): pl.pallas_call(inner_kernel, grid=(members // batch,), out_shape=[jax.Sha...  2.55 us
    dynamic_slice x1, local copies, waits for them, and re-layouts, halos(): far = lax.dynamic_slice_in_dim(own, odd * last, reach, axis=1)  2.17 us
  transfers between devices with their start and end apart: 8, of which 4 were waited for; matrix products, arithmetic and copies ran while one was open for 0% of the time, Pallas kernels for 5%

profile of v23, /device:TPU:0, one launch (start us, length us, event | category | flops | bytes accessed | tf_op | source)
XLA Modules:
  0.0 82.5 jit_solution(2670682178640820460)
XLA Ops:
  0.0 2.2 %constant_dynamic-slice_fusion = (bf16[4,256,256]{2,1,0:T(8,128)(2,1)S(1)}, bf16[4,256,256]{2,1,0:T(8,128)(2,1)}) fusion(bf16[4,512,256]{2,1,0:T(8,128)(2,1)} %state_ref.1, s32[]{:T(128)S(6)} %select_n.15, s32[]{:T(128)S(6)} %select_n.14), kind=kLoop, calls=%fused_computation | loop fusion | bytes 2097160 | tf_op jit(solution)/shard_map/dynamic_slice | solution.py:667
  2.2 0.5 collective-permute-start
  2.7 0.7 collective-permute-start.1
  3.4 0.0 copy-start.1
  3.5 0.0 copy-start.2
  3.5 0.0 copy-start.3
  3.5 0.0 copy-start.7
  3.5 0.0 copy-start.13
  3.5 2.6 %inner.1 = (bf16[4,512,256]{2,1,0:T(8,128)(2,1)S(1)}, f32[4,8,128]{2,1,0:T(8,128)S(1)}, f32[4,512,256]{2,1,0:T(8,128)S(1)}, f32[4,512,256]{2,1,0:T(8,128)S(1)}) custom-call(s32[4]{0:T(128)S(1)} %copy-done.14, bf16[4,512,256]{2,1,0:T(8,128)(2,1)S(1)} %copy-done, f32[1,256]{1,0:T(1,128)S(1)} %bitcast.13, bf16[256,256]{1,0:T(8,128)(2,1)S(1)} %copy-done.4, ...), custom_call_target="tpu_custom_call" | custom-call | flops 5100273664 | bytes 7340032 | tf_op jit(solution)/shard_map/inner/pallas_call | solution.py:260
  6.1 0.0 collective-permute-done.near_ref
  6.1 0.0 copy-start.8
  6.1 0.0 copy-start.9
  6.2 0.0 copy-start.10
  6.2 0.0 copy-start.11
  6.2 20.0 %forward.1 = (bf16[4,128,256]{2,1,0:T(8,128)(2,1)S(1)}, bf16[4,128,256]{2,1,0:T(8,128)(2,1)S(1)}, bf16[4,128,256]{2,1,0:T(8,128)(2,1)S(1)}, bf16[4,128,256]{2,1,0:T(8,128)(2,1)S(1)}) custom-call(s32[1]{0:T(128)} %bitcast.1.tok_ref, s32[1]{0:T(128)} %bitcast.mem_ref.index_ref, s32[4]{0:T(128)S(1)} %copy-done.14, bf16[4,512,256]{2,1,0:T(8,128)(2,1)S(1)} %copy-done, ...), custom_call_target="tpu_custom_call" | custom-call | flops 5100273664 | bytes 5242880 | tf_op jit(solution)/shard_map/forward/pallas_call | solution.py:445
  26.2 2.5 %collective-permute-start.2 = (bf16[4,128,256]{2,1,0:T(8,128)(2,1)S(1)}, bf16[4,128,256]{2,1,0:T(8,128)(2,1)S(1)}, u32[]{:S(2)}, u32[]{:S(2)}) collective-permute-start(bf16[4,128,256]{2,1,0:T(8,128)(2,1)S(1)} %get-tuple-element.22), channel_id=1, source_target_pairs={{0,8},{8,0},{16,24},{24,16},{1,9},{9,1},{17,25},{25,17},{2,10},{10... | collective-permute-start | bytes 786440 | tf_op jit(solution)/shard_map/ppermute | solution.py:658
  28.7 1.5 %collective-permute-start.3 = (bf16[4,128,256]{2,1,0:T(8,128)(2,1)S(1)}, bf16[4,128,256]{2,1,0:T(8,128)(2,1)S(1)}, u32[]{:S(2)}, u32[]{:S(2)}) collective-permute-start(bf16[4,128,256]{2,1,0:T(8,128)(2,1)S(1)} %get-tuple-element.23), channel_id=1, source_target_pairs={{0,16},{8,24},{16,0},{24,8},{1,17},{9,25},{17,1},{25,9},{2,18},{10... | collective-permute-start | bytes 786440 | tf_op jit(solution)/shard_map/ppermute | solution.py:658
  30.3 0.0 collective-permute-start.4
  30.3 1.3 %sample_grid.1.refs_4_ = f32[2,128,256]{2,1,0:T(8,128)S(1)} custom-call(s32[1]{0:T(128)} %bitcast.4.start_ref, s32[1,4096]{1,0:T(1,128)S(1)} %bitcast.9, s32[1,4096]{1,0:T(1,128)S(1)} %bitcast.10, f32[1,4096]{1,0:T(1,128)S(1)} %bitcast.11, f32[1,4096]{1,0:T(1,128)S(1)} %bitcast.12), custom_call_target="tpu_custom_call" | custom-call | flops 1073741824 | bytes 65536 | tf_op jit(solution)/shard_map/sample_grid/pallas_call | solution.py:80
  31.6 1.5 %collective-permute-done.2.refs_1_ = bf16[4,128,256]{2,1,0:T(8,128)(2,1)S(1)} collective-permute-done((bf16[4,128,256]{2,1,0:T(8,128)(2,1)S(1)}, bf16[4,128,256]{2,1,0:T(8,128)(2,1)S(1)}, u32[]{:S(2)}, u32[]{:S(2)}) %collective-permute-start.2) | collective-permute-done | bytes 262176 | tf_op jit(solution)/shard_map/ppermute | solution.py:658
  33.1 4.8 %collective-permute-done.3.refs_2_ = bf16[4,128,256]{2,1,0:T(8,128)(2,1)S(1)} collective-permute-done((bf16[4,128,256]{2,1,0:T(8,128)(2,1)S(1)}, bf16[4,128,256]{2,1,0:T(8,128)(2,1)S(1)}, u32[]{:S(2)}, u32[]{:S(2)}) %collective-permute-start.3) | collective-permute-done | bytes 262176 | tf_op jit(solution)/shard_map/ppermute | solution.py:658
  37.9 0.0 collective-permute-done.4.refs_3_
  37.9 1.5 %gram.1 = f32[8,128]{1,0:T(8,128)S(1)} custom-call(s32[1]{0:T(128)} %bitcast.mem_ref.index_ref, bf16[4,128,256]{2,1,0:T(8,128)(2,1)S(1)} %get-tuple-element.21.refs_0_, bf16[4,128,256]{2,1,0:T(8,128)(2,1)S(1)} %collective-permute-done.2.refs_1_, bf16[4,128,256]{2,1,0:T(8,128)(2,1)S(1)} %collective-permute-done.3.refs_2_, ...), custom_call_target="tpu_custom_call" | custom-call | flops 805306368 | bytes 1048576 | tf_op jit(solution)/shard_map/gram/pallas_call | solution.py:514
  39.4 23.8 %all_to_all.5.partial_ref = f32[32,8,128]{2,1,0:T(8,128)S(1)} all-to-all(f32[32,8,128]{2,1,0:T(8,128)S(1)} %broadcast_in_dim.2), channel_id=1, replica_groups=mesh['mem'=4,'tok'=8] {'mem','tok'}, dimensions={0} | all-to-all | bytes 262144 | tf_op jit(solution)/shard_map/all_to_all | solution.py:713
  63.3 3.7 %combine.1 = (bf16[4,128,256]{2,1,0:T(8,128)(2,1)S(1)}, bf16[4,128,256]{2,1,0:T(8,128)(2,1)S(1)}, bf16[4,128,256]{2,1,0:T(8,128)(2,1)S(1)}, bf16[4,128,256]{2,1,0:T(8,128)(2,1)S(1)}) custom-call(s32[1]{0:T(128)} %bitcast.mem_ref.index_ref, f32[32,8,128]{2,1,0:T(8,128)S(1)} %all_to_all.5.partial_ref, bf16[4,128,256]{2,1,0:T(8,128)(2,1)S(1)} %get-tuple-element.21.refs_0_, ...), custom_call_target="tpu_custom_call" | custom-call | flops 536870912 | bytes 2097152 | tf_op jit(solution)/shard_map/combine/pallas_call | solution.py:617
  67.0 0.9 %collective-permute-start.5 = (bf16[4,128,256]{2,1,0:T(8,128)(2,1)S(1)}, bf16[4,128,256]{2,1,0:T(8,128)(2,1)S(1)}, u32[]{:S(2)}, u32[]{:S(2)}) collective-permute-start(bf16[4,128,256]{2,1,0:T(8,128)(2,1)S(1)} %get-tuple-element.26), channel_id=1, source_target_pairs={{0,8},{8,0},{16,24},{24,16},{1,9},{9,1},{17,25},{25,17},{2,10},{10... | collective-permute-start | bytes 786440 | tf_op jit(solution)/shard_map/ppermute | solution.py:658
  67.9 0.7 collective-permute-start.6
  68.6 2.0 %collective-permute-start.7 = (bf16[4,128,256]{2,1,0:T(8,128)(2,1)S(1)}, bf16[4,128,256]{2,1,0:T(8,128)(2,1)S(1)}, u32[]{:S(2)}, u32[]{:S(2)}) collective-permute-start(bf16[4,128,256]{2,1,0:T(8,128)(2,1)S(1)} %get-tuple-element.28), channel_id=1, source_target_pairs={{0,24},{8,16},{16,8},{24,0},{1,25},{9,17},{17,9},{25,1},{2,26},{10... | collective-permute-start | bytes 786440 | tf_op jit(solution)/shard_map/ppermute | solution.py:658
  70.6 5.6 %collective-permute-done.5.refs_1_ = bf16[4,128,256]{2,1,0:T(8,128)(2,1)S(1)} collective-permute-done((bf16[4,128,256]{2,1,0:T(8,128)(2,1)S(1)}, bf16[4,128,256]{2,1,0:T(8,128)(2,1)S(1)}, u32[]{:S(2)}, u32[]{:S(2)}) %collective-permute-start.5) | collective-permute-done | bytes 262176 | tf_op jit(solution)/shard_map/ppermute | solution.py:658
  76.2 5.1 %collective-permute-done.6.refs_2_ = bf16[4,128,256]{2,1,0:T(8,128)(2,1)S(1)} collective-permute-done((bf16[4,128,256]{2,1,0:T(8,128)(2,1)S(1)}, bf16[4,128,256]{2,1,0:T(8,128)(2,1)S(1)}, u32[]{:S(2)}, u32[]{:S(2)}) %collective-permute-start.6) | collective-permute-done | bytes 262176 | tf_op jit(solution)/shard_map/ppermute | solution.py:658
  81.3 0.0 collective-permute-done.7.refs_3_
  81.3 1.0 %assemble.1 = bf16[4,512,256]{2,1,0:T(8,128)(2,1)} custom-call(s32[1]{0:T(128)} %bitcast.mem_ref.index_ref, bf16[4,128,256]{2,1,0:T(8,128)(2,1)S(1)} %get-tuple-element.25.refs_0_, bf16[4,128,256]{2,1,0:T(8,128)(2,1)S(1)} %collective-permute-done.5.refs_1_, bf16[4,128,256]{2,1,0:T(8,128)(2,1)S(1)} %collective-permute-done.6.refs_2_, ...), custom_call_target="tpu_custom_call" | custom-call | bytes 2097152 | tf_op jit(solution)/shard_map/assemble/pallas_call | solution.py:643
  (23 shorter events, 0.1 us)
Async XLA Ops:
  0.0 3.4 %copy-start = (bf16[4,512,256]{2,1,0:T(8,128)(2,1)S(1)}, bf16[4,512,256]{2,1,0:T(8,128)(2,1)}, u32[]{:S(2)}) copy-start(bf16[4,512,256]{2,1,0:T(8,128)(2,1)} %state_ref.1) | copy-start | bytes 3145732
  0.0 3.4 %copy-start.12 = (f32[256]{0:T(256)S(1)}, f32[256]{0:T(256)}, u32[]{:S(2)}) copy-start(f32[256]{0:T(256)} %param.16) | copy-start | bytes 3076
  0.0 3.4 %copy-start.4 = (bf16[256,256]{1,0:T(8,128)(2,1)S(1)}, bf16[256,256]{1,0:T(8,128)(2,1)}, u32[]{:S(2)}) copy-start(bf16[256,256]{1,0:T(8,128)(2,1)} %w_query_ref.1) | copy-start | bytes 393220
  0.0 3.4 %copy-start.5 = (bf16[256,256]{1,0:T(8,128)(2,1)S(1)}, bf16[256,256]{1,0:T(8,128)(2,1)}, u32[]{:S(2)}) copy-start(bf16[256,256]{1,0:T(8,128)(2,1)} %w_key_ref.3) | copy-start | bytes 393220
  0.0 3.4 %copy-start.6 = (bf16[256,256]{1,0:T(8,128)(2,1)S(1)}, bf16[256,256]{1,0:T(8,128)(2,1)}, u32[]{:S(2)}) copy-start(bf16[256,256]{1,0:T(8,128)(2,1)} %w_value_ref.3) | copy-start | bytes 393220
  0.0 3.4 %copy-start.14 = (s32[4]{0:T(128)S(1)}, s32[4]{0:T(128)}, u32[]{:S(2)}) copy-start(s32[4]{0:T(128)} %window_ref.3) | copy-start | bytes 52
  2.2 3.8 %collective-permute-start = (bf16[4,256,256]{2,1,0:T(8,128)(2,1)}, bf16[4,256,256]{2,1,0:T(8,128)(2,1)S(1)}, u32[]{:S(2)}, u32[]{:S(2)}) collective-permute-start(bf16[4,256,256]{2,1,0:T(8,128)(2,1)} %get-tuple-element.30), channel_id=1, source_target_pairs={{0,1},{1,0},{2,3},{3,2},{4,5},{5,4},{6,7},{7,6},{8,9},{9,8},{10,11... | collective-permute-start | bytes 1572872 | tf_op jit(solution)/shard_map/ppermute | solution.py:671
  2.7 3.4 %collective-permute-start.1 = (bf16[4,256,256]{2,1,0:T(8,128)(2,1)S(1)}, bf16[4,256,256]{2,1,0:T(8,128)(2,1)S(1)}, u32[]{:S(2)}, u32[]{:S(2)}) collective-permute-start(bf16[4,256,256]{2,1,0:T(8,128)(2,1)S(1)} %get-tuple-element.29), channel_id=1, source_target_pairs={{1,2},{2,1},{3,4},{4,3},{5,6},{6,5},{9,10},{10,9},{11,12},{12,11},... | collective-permute-start | bytes 1572872 | tf_op jit(solution)/shard_map/ppermute | solution.py:670
  3.4 2.6 %copy-start.1 = (bf16[256,1024]{1,0:T(8,128)(2,1)S(1)}, bf16[256,1024]{1,0:T(8,128)(2,1)}, u32[]{:S(2)}) copy-start(bf16[256,1024]{1,0:T(8,128)(2,1)} %w_gate_ref.1) | copy-start | bytes 1572868
  3.5 2.6 %copy-start.2 = (bf16[256,1024]{1,0:T(8,128)(2,1)S(1)}, bf16[256,1024]{1,0:T(8,128)(2,1)}, u32[]{:S(2)}) copy-start(bf16[256,1024]{1,0:T(8,128)(2,1)} %w_up_ref.1) | copy-start | bytes 1572868
  3.5 2.6 %copy-start.3 = (bf16[1024,256]{1,0:T(8,128)(2,1)S(1)}, bf16[1024,256]{1,0:T(8,128)(2,1)}, u32[]{:S(2)}) copy-start(bf16[1024,256]{1,0:T(8,128)(2,1)} %down_weight_ref.1) | copy-start | bytes 1572868
  3.5 2.6 %copy-start.7 = (bf16[256,256]{1,0:T(8,128)(2,1)S(1)}, bf16[256,256]{1,0:T(8,128)(2,1)}, u32[]{:S(2)}) copy-start(bf16[256,256]{1,0:T(8,128)(2,1)} %w_out_ref.1) | copy-start | bytes 393220
  3.5 2.6 %copy-start.13 = (f32[256]{0:T(256)S(1)}, f32[256]{0:T(256)}, u32[]{:S(2)}) copy-start(f32[256]{0:T(256)} %param.17) | copy-start | bytes 3076
  6.1 24.1 %copy-start.8 = (s32[4096]{0:T(1024)S(1)}, s32[4096]{0:T(1024)}, u32[]{:S(2)}) copy-start(s32[4096]{0:T(1024)} %param.26) | copy-start | bytes 49156
  6.1 24.1 %copy-start.9 = (s32[4096]{0:T(1024)S(1)}, s32[4096]{0:T(1024)}, u32[]{:S(2)}) copy-start(s32[4096]{0:T(1024)} %param.27) | copy-start | bytes 49156
  6.2 24.1 %copy-start.10 = (f32[4096]{0:T(1024)S(1)}, f32[4096]{0:T(1024)}, u32[]{:S(2)}) copy-start(f32[4096]{0:T(1024)} %param.28) | copy-start | bytes 49156
  6.2 24.1 %copy-start.11 = (f32[4096]{0:T(1024)S(1)}, f32[4096]{0:T(1024)}, u32[]{:S(2)}) copy-start(f32[4096]{0:T(1024)} %param.29) | copy-start | bytes 49156
  26.2 6.9 %collective-permute-start.2 = (bf16[4,128,256]{2,1,0:T(8,128)(2,1)S(1)}, bf16[4,128,256]{2,1,0:T(8,128)(2,1)S(1)}, u32[]{:S(2)}, u32[]{:S(2)}) collective-permute-start(bf16[4,128,256]{2,1,0:T(8,128)(2,1)S(1)} %get-tuple-element.22), channel_id=1, source_target_pairs={{0,8},{8,0},{16,24},{24,16},{1,9},{9,1},{17,25},{25,17},{2,10},{10... | collective-permute-start | bytes 786440 | tf_op jit(solution)/shard_map/ppermute | solution.py:658
  28.7 9.2 %collective-permute-start.3 = (bf16[4,128,256]{2,1,0:T(8,128)(2,1)S(1)}, bf16[4,128,256]{2,1,0:T(8,128)(2,1)S(1)}, u32[]{:S(2)}, u32[]{:S(2)}) collective-permute-start(bf16[4,128,256]{2,1,0:T(8,128)(2,1)S(1)} %get-tuple-element.23), channel_id=1, source_target_pairs={{0,16},{8,24},{16,0},{24,8},{1,17},{9,25},{17,1},{25,9},{2,18},{10... | collective-permute-start | bytes 786440 | tf_op jit(solution)/shard_map/ppermute | solution.py:658
  30.3 7.7 %collective-permute-start.4 = (bf16[4,128,256]{2,1,0:T(8,128)(2,1)S(1)}, bf16[4,128,256]{2,1,0:T(8,128)(2,1)S(1)}, u32[]{:S(2)}, u32[]{:S(2)}) collective-permute-start(bf16[4,128,256]{2,1,0:T(8,128)(2,1)S(1)} %get-tuple-element.24), channel_id=1, source_target_pairs={{0,24},{8,16},{16,8},{24,0},{1,25},{9,17},{17,9},{25,1},{2,26},{10... | collective-permute-start | bytes 786440 | tf_op jit(solution)/shard_map/ppermute | solution.py:658
  67.0 9.2 %collective-permute-start.5 = (bf16[4,128,256]{2,1,0:T(8,128)(2,1)S(1)}, bf16[4,128,256]{2,1,0:T(8,128)(2,1)S(1)}, u32[]{:S(2)}, u32[]{:S(2)}) collective-permute-start(bf16[4,128,256]{2,1,0:T(8,128)(2,1)S(1)} %get-tuple-element.26), channel_id=1, source_target_pairs={{0,8},{8,0},{16,24},{24,16},{1,9},{9,1},{17,25},{25,17},{2,10},{10... | collective-permute-start | bytes 786440 | tf_op jit(solution)/shard_map/ppermute | solution.py:658
  67.9 13.4 %collective-permute-start.6 = (bf16[4,128,256]{2,1,0:T(8,128)(2,1)S(1)}, bf16[4,128,256]{2,1,0:T(8,128)(2,1)S(1)}, u32[]{:S(2)}, u32[]{:S(2)}) collective-permute-start(bf16[4,128,256]{2,1,0:T(8,128)(2,1)S(1)} %get-tuple-element.27), channel_id=1, source_target_pairs={{0,16},{8,24},{16,0},{24,8},{1,17},{9,25},{17,1},{25,9},{2,18},{10... | collective-permute-start | bytes 786440 | tf_op jit(solution)/shard_map/ppermute | solution.py:658
  68.6 12.7 %collective-permute-start.7 = (bf16[4,128,256]{2,1,0:T(8,128)(2,1)S(1)}, bf16[4,128,256]{2,1,0:T(8,128)(2,1)S(1)}, u32[]{:S(2)}, u32[]{:S(2)}) collective-permute-start(bf16[4,128,256]{2,1,0:T(8,128)(2,1)S(1)} %get-tuple-element.28), channel_id=1, source_target_pairs={{0,24},{8,16},{16,8},{24,0},{1,25},{9,17},{17,9},{25,1},{2,26},{10... | collective-permute-start | bytes 786440 | tf_op jit(solution)/shard_map/ppermute | solution.py:658
